TPU v7x, 32 devices: a whole 2x2x4 slice. The times are simulated.
32 devices in a mesh: lon: 32 (over z, y, x, core), lat: 1.
Axes of the slice: x: 2, y: 2, z: 4, core: 2. Of those that a mesh axis runs over, the one named last changes fastest.
Arguments:
- inputs: bfloat16 [32, 1024, 192], P('lat', 'lon'), may hold values from -6 to 6
- cotangent: bfloat16 [32, 1024, 192], P('lat', 'lon'), may hold values from -6 to 6
- first_weight: bfloat16 [3, 3, 192, 192], replicated, may hold values from -0.15625 to 0.15625
- second_weight: bfloat16 [3, 3, 192, 192], replicated, may hold values from -0.15625 to 0.15625
Outputs:
- input_gradient: bfloat16 [32, 1024, 192], P('lat', 'lon')
- first_kernel_gradient: float32 [3, 3, 192, 192], replicated
- second_kernel_gradient: float32 [3, 3, 192, 192], replicated
All inputs are finite; a program needn't handle non-finite values.
Results may differ from a plain program's by a relative error of at most 0.0049.
Values may be sent and summed in bfloat16 or wider, within the bound.
No kernel may reach another device: no remote copies, remote signals or barrier semaphores. Data moves between devices by JAX's collectives and lax.ppermute only.
A program may use at most 128 MiB of HBM per device.

v0:
```python
import math

import jax
import jax.numpy as jnp
from jax import lax
from jax.sharding import PartitionSpec as P

FIRST_SPREAD = 32
SECOND_SPREAD = 64


def with_halo(cells, sides, width):
    for axis, dim in sides:
        count = lax.axis_size(axis)
        ends = count - 1
        head = lax.slice_in_dim(cells, 0, width, axis=dim)
        tail = lax.slice_in_dim(cells, cells.shape[dim] - width, cells.shape[dim], axis=dim)
        cells = jnp.concatenate(
            [
                lax.ppermute(tail, axis, [(i, (i + 1) % count) for i in range(ends)]),
                cells,
                lax.ppermute(head, axis, [((i + 1) % count, i) for i in range(ends)]),
            ],
            axis=dim,
        )
    return cells


def from_behind(value, axis, steps):
    count = lax.axis_size(axis)
    pairs = [(source, (source + steps) % count) for source in range(count)]
    return lax.ppermute(value, axis, pairs)


def widened_field(field, dilation):
    rimmed = with_halo(field, (("lat", 0),), 1)
    border_width = field.shape[1]
    reach = -(-dilation // border_width)
    behind = []
    ahead_list = []
    back_piece = rimmed
    front_piece = rimmed
    for distance in range(reach):
        back_piece = from_behind(back_piece, "lon", 1)
        front_piece = from_behind(front_piece, "lon", -1)
        behind.insert(0, back_piece)
        ahead_list.append(front_piece)
    offset = reach * border_width
    return (jnp.concatenate(behind + [rimmed] + ahead_list, axis=1), offset)


def gather_taps(extended, offset, dilation, border_width):
    height = extended.shape[0] - 2
    pieces = []
    for row_off in range(3):
        for col_off in (-1, 0, 1):
            start = offset + col_off * dilation
            pieces.append(extended[row_off : row_off + height, start : start + border_width])
    return jnp.concatenate(pieces, axis=2).reshape(height * border_width, -1)


def flipped_kernel(weight):
    return jnp.transpose(weight[::-1, ::-1], (0, 1, 3, 2))


def contract_cells(stacked, other):
    return lax.dot_general(
        stacked, other, (((0,), (0,)), ((), ())), preferred_element_type=jnp.float32
    )


def shards(inputs, cotangent, first_weight, second_weight):
    height, border_width, channels = inputs.shape
    gradient_scale = 1.0 / math.sqrt(
        height * lax.axis_size("lat") * border_width * lax.axis_size("lon")
    )
    extended_input, input_shift = widened_field(inputs, FIRST_SPREAD)
    input_taps = gather_taps(extended_input, input_shift, FIRST_SPREAD, border_width)
    pre_activation = jnp.dot(
        input_taps, first_weight.reshape(-1, channels), preferred_element_type=jnp.float32
    )
    hidden_state = (
        jax.nn.silu(pre_activation).astype(jnp.bfloat16).reshape(height, border_width, channels)
    )
    extended_hidden, hidden_shift = widened_field(hidden_state, SECOND_SPREAD)
    hidden_taps = gather_taps(extended_hidden, hidden_shift, SECOND_SPREAD, border_width)
    extended_cotangent, cotangent_shift = widened_field(cotangent, SECOND_SPREAD)
    cotangent_taps = gather_taps(extended_cotangent, cotangent_shift, SECOND_SPREAD, border_width)
    hidden_gradient = jnp.dot(
        cotangent_taps,
        flipped_kernel(second_weight).reshape(-1, channels),
        preferred_element_type=jnp.float32,
    )
    part_two = contract_cells(hidden_taps, cotangent.reshape(-1, channels))
    sigma = jax.nn.sigmoid(pre_activation)
    pre_flat = (hidden_gradient * sigma * (1.0 + pre_activation * (1.0 - sigma))).astype(
        jnp.bfloat16
    )
    pre_activation_gradient = pre_flat.reshape(height, border_width, channels)
    extended_pre_gradient, pre_gradient_shift = widened_field(pre_activation_gradient, FIRST_SPREAD)
    pre_gradient_taps = gather_taps(
        extended_pre_gradient, pre_gradient_shift, FIRST_SPREAD, border_width
    )
    input_gradient = jnp.dot(
        pre_gradient_taps,
        flipped_kernel(first_weight).reshape(-1, channels),
        preferred_element_type=jnp.float32,
    )
    input_gradient = input_gradient.astype(jnp.bfloat16).reshape(height, border_width, channels)
    part_one = contract_cells(input_taps, pre_flat)
    summed_one, summed_two = lax.psum((part_one, part_two), ("lon", "lat"))
    first_kernel_gradient = (summed_one * gradient_scale).reshape(3, 3, channels, channels)
    second_kernel_gradient = (summed_two * gradient_scale).reshape(3, 3, channels, channels)
    return (input_gradient, first_kernel_gradient, second_kernel_gradient)


def solution(mesh):
    placed = (P("lat", "lon", None), P("lat", "lon", None), P(), P())
    return jax.shard_map(
        shards,
        mesh=mesh,
        in_specs=placed,
        out_specs=(P("lat", "lon", None), P(), P()),
        check_vma=False,
    )
```

profile of v0, /device:TPU:0, one launch (start us, length us, event | category | flops | bytes accessed | tf_op | source)
XLA Modules:
  0.0 282.5 jit_solution(18257873843777672325)
XLA Ops:
  11.4 1.8 pad_maximum_fusion.6
  13.2 6.4 %collective-permute-start.9 = (bf16[34,32,192]{2,1,0:T(8,128)(2,1)S(1)}, bf16[34,32,192]{2,1,0:T(8,128)(2,1)S(1)}, u32[]{:S(2)}, u32[]{:S(2)}) collective-permute-start(bf16[34,32,192]{2,1,0:T(8,128)(2,1)S(1)} %constant_dynamic-update-slice_fusion.3), channel_id=1, source_target_pairs={{0,31},{1,0},{2,1},{3,2},{4,3},{5,4},{6,5},{7,6},{8,7},{9,8},{10,9... | collective-permute-start | bytes 1253384 | tf_op jit(solution)/shard_map/ppermute | solution.py:32
  23.4 5.3 %collective-permute-start.4 = (bf16[34,32,192]{2,1,0:T(8,128)(2,1)}, bf16[34,32,192]{2,1,0:T(8,128)(2,1)}, u32[]{:S(2)}, u32[]{:S(2)}) collective-permute-start(bf16[34,32,192]{2,1,0:T(8,128)(2,1)} %constant_dynamic-update-slice_fusion), channel_id=1, source_target_pairs={{0,31},{1,0},{2,1},{3,2},{4,3},{5,4},{6,5},{7,6},{8,7},{9,8},{10,9... | collective-permute-start | bytes 1253384 | tf_op jit(solution)/shard_map/ppermute | solution.py:32
  30.0 3.6 %collective-permute-done.8 = bf16[34,32,192]{2,1,0:T(8,128)(2,1)S(1)} collective-permute-done((bf16[34,32,192]{2,1,0:T(8,128)(2,1)S(1)}, bf16[34,32,192]{2,1,0:T(8,128)(2,1)S(1)}, u32[]{:S(2)}, u32[]{:S(2)}) %collective-permute-start.8) | collective-permute-done | bytes 417824 | tf_op jit(solution)/shard_map/ppermute | solution.py:32
  34.8 6.8 %concatenate.72 = bf16[32,32,1728]{2,1,0:T(8,128)(2,1)} concatenate(bf16[32,32,192]{2,1,0:T(8,128)(2,1)} %get-tuple-element.25, bf16[32,32,192]{2,1,0:T(8,128)(2,1)S(1)} %get-tuple-element.38, bf16[32,32,192]{2,1,0:T(8,128)(2,1)} %get-tuple-element.22, bf16[32,32,192]{2,1,0:T(8,128)(2,1)} %get-tuple-element.24, bf16[32,32,192]{2,1,0:T(8,128)(2,1)S(1)} %copy-done.3, ...), dimensions={2} | concatenate | bytes 7077888 | tf_op jit(solution)/shard_map/concatenate | solution.py:59
  41.6 4.6 %multiply_convert_fusion = (bf16[1024,192]{0,1:T(8,128)(2,1)S(1)}, f32[1024,192]{0,1:T(8,128)}) fusion(bf16[1024,1728]{1,0:T(8,128)(2,1)} %bitcast.42, bf16[1728,192]{1,0:T(8,128)(2,1)} %bitcast.60), kind=kOutput, calls=%fused_computation.7 | convolution fusion | flops 680460288 | bytes 5382144 | tf_op jit(solution)/shard_map/dot_general | solution.py:79
  46.2 1.7 collective-permute-start.5
  50.9 1.4 copy.22
  52.2 1.4 copy.36
  56.0 4.5 %collective-permute-start.18 = (bf16[34,32,192]{2,1,0:T(8,128)(2,1)}, bf16[34,32,192]{2,1,0:T(8,128)(2,1)}, u32[]{:S(2)}, u32[]{:S(2)}) collective-permute-start(bf16[34,32,192]{2,1,0:T(8,128)(2,1)} %pad_maximum_fusion.1), channel_id=1, source_target_pairs={{0,31},{1,0},{2,1},{3,2},{4,3},{5,4},{6,5},{7,6},{8,7},{9,8},{10,9... | collective-permute-start | bytes 1253384 | tf_op jit(solution)/shard_map/ppermute | solution.py:32
  64.1 7.0 %concatenate.68 = bf16[32,32,1728]{2,1,0:T(8,128)(2,1)} concatenate(bf16[32,32,192]{2,1,0:T(8,128)(2,1)} %get-tuple-element.31, bf16[32,32,192]{2,1,0:T(8,128)(2,1)} %get-tuple-element.42, bf16[32,32,192]{2,1,0:T(8,128)(2,1)} %get-tuple-element.28, bf16[32,32,192]{2,1,0:T(8,128)(2,1)} %get-tuple-element.30, bf16[32,32,192]{2,1,0:T(8,128)(2,1)S(1)} %copy-done, ...), dimensions={2} | concatenate | bytes 7077888 | tf_op jit(solution)/shard_map/concatenate | solution.py:59
  71.0 3.7 %fusion.1 = bf16[1024,192]{0,1:T(8,128)(2,1)S(1)} fusion(bf16[1024,1728]{1,0:T(8,128)(2,1)} %bitcast.49, bf16[1728,192]{1,0:T(8,128)(2,1)S(1)} %bitcast.62, f32[1024,192]{0,1:T(8,128)} %get-tuple-element.51), kind=kOutput, calls=%fused_computation.3 | convolution fusion | flops 681246720 | bytes 5382144 | tf_op jit(solution)/shard_map/dot_general | solution.py:89
  77.3 3.2 %collective-permute-start.16 = (bf16[34,32,192]{2,1,0:T(8,128)(2,1)}, bf16[34,32,192]{2,1,0:T(8,128)(2,1)}, u32[]{:S(2)}, u32[]{:S(2)}) collective-permute-start(bf16[34,32,192]{2,1,0:T(8,128)(2,1)} %pad_maximum_fusion.1), channel_id=1, source_target_pairs={{0,1},{1,2},{2,3},{3,4},{4,5},{5,6},{6,7},{7,8},{8,9},{9,10},{10,1... | collective-permute-start | bytes 1253384 | tf_op jit(solution)/shard_map/ppermute | solution.py:32
  81.8 2.4 collective-permute-start.12
  84.2 3.0 %collective-permute-start.19 = (bf16[34,32,192]{2,1,0:T(8,128)(2,1)}, bf16[34,32,192]{2,1,0:T(8,128)(2,1)S(1)}, u32[]{:S(2)}, u32[]{:S(2)}) collective-permute-start(bf16[34,32,192]{2,1,0:T(8,128)(2,1)} %collective-permute-done.18), channel_id=1, source_target_pairs={{0,31},{1,0},{2,1},{3,2},{4,3},{5,4},{6,5},{7,6},{8,7},{9,8},{10,9... | collective-permute-start | bytes 1253384 | tf_op jit(solution)/shard_map/ppermute | solution.py:32
  87.2 4.0 %fusion.12 = f32[1728,192]{0,1:T(8,128)} fusion(bf16[1024,192]{0,1:T(8,128)(2,1)S(1)} %fusion.1, bf16[1024,1728]{1,0:T(8,128)(2,1)} %bitcast.43), kind=kOutput, calls=%fused_computation.50 | convolution fusion | flops 679477248 | bytes 5259264 | tf_op jit(solution)/shard_map/dot_general | solution.py:67
  92.3 2.0 copy.29
  94.3 2.0 copy.34
  96.3 5.3 %collective-permute-start.17 = (bf16[34,32,192]{2,1,0:T(8,128)(2,1)}, bf16[34,32,192]{2,1,0:T(8,128)(2,1)}, u32[]{:S(2)}, u32[]{:S(2)}) collective-permute-start(bf16[34,32,192]{2,1,0:T(8,128)(2,1)} %collective-permute-done.16), channel_id=1, source_target_pairs={{0,1},{1,2},{2,3},{3,4},{4,5},{5,6},{6,7},{7,8},{8,9},{9,10},{10,1... | collective-permute-start | bytes 1253384 | tf_op jit(solution)/shard_map/ppermute | solution.py:32
  102.8 2.1 copy.28
  106.1 3.2 %collective-permute-done.17 = bf16[34,32,192]{2,1,0:T(8,128)(2,1)} collective-permute-done((bf16[34,32,192]{2,1,0:T(8,128)(2,1)}, bf16[34,32,192]{2,1,0:T(8,128)(2,1)}, u32[]{:S(2)}, u32[]{:S(2)}) %collective-permute-start.17) | collective-permute-done | bytes 417824 | tf_op jit(solution)/shard_map/ppermute | solution.py:32
  109.3 2.5 fusion.3
  111.7 6.8 %concatenate.88 = bf16[32,32,1728]{2,1,0:T(8,128)(2,1)} concatenate(bf16[32,32,192]{2,1,0:T(8,128)(2,1)} %get-tuple-element.13, bf16[32,32,192]{2,1,0:T(8,128)(2,1)S(1)} %copy-done.5, bf16[32,32,192]{2,1,0:T(8,128)(2,1)} %get-tuple-element.10, bf16[32,32,192]{2,1,0:T(8,128)(2,1)} %get-tuple-element.12, bf16[32,32,192]{2,1,0:T(8,128)(2,1)S(1)} %bitcast.46, ...), dimensions={2} | concatenate | bytes 7077888 | tf_op jit(solution)/shard_map/concatenate | solution.py:59
  118.5 1.8 constant_dynamic-update-slice_fusion.14
  120.3 4.0 %convolution_bitcast_fusion = f32[1728,192]{0,1:T(8,128)} fusion(bf16[32,32,1728]{2,1,0:T(8,128)(2,1)} %concatenate.88, bf16[32,32,192]{2,1,0:T(8,128)(2,1)S(1)} %copy-done), kind=kOutput, calls=%fused_computation | convolution fusion | flops 679477248 | bytes 5259264 | tf_op jit(solution)/shard_map/dot_general | solution.py:67
  127.8 1.8 constant_dynamic-update-slice_fusion.12
  129.6 1.8 constant_dynamic-update-slice_fusion.11
  135.3 2.9 %convolution_convert_fusion = bf16[1024,192]{0,1:T(8,128)(2,1)S(1)} fusion(bf16[1024,1728]{0,1:T(8,128)(2,1)} %constant_dynamic-update-slice_fusion.6, bf16[1728,192]{1,0:T(8,128)(2,1)S(1)} %bitcast.61), kind=kOutput, calls=%fused_computation.4 | convolution fusion | flops 679673856 | bytes 4595712 | tf_op jit(solution)/shard_map/dot_general | solution.py:104
  139.2 130.9 %all-reduce.3.cloned.1.call-done = (f32[1728,192]{0,1:T(8,128)}, f32[1728,192]{0,1:T(8,128)}) async-done(((f32[1728,192]{0,1:T(8,128)}, f32[1728,192]{0,1:T(8,128)}), (f32[1728,192]{0,1:T(8,128)}, f32[1728,192]{0,1:T(8,128)})) %all-reduce.3.cloned.1.call-update) | async-done | bytes 2654224 | tf_op jit(solution)/shard_map/psum | solution.py:111
  270.2 2.0 broadcast_multiply_fusion
  272.2 1.7 copy.38
  273.9 1.7 copy.44
  (102 shorter events, 34.9 us)
Async XLA Ops:
  7.2 14.4 %copy-start = (bf16[32,32,192]{2,1,0:T(8,128)(2,1)S(1)}, bf16[32,32,192]{2,1,0:T(8,128)(2,1)}, u32[]{:S(2)}) copy-start(bf16[32,32,192]{2,1,0:T(8,128)(2,1)} %param.5) | copy-start | bytes 1179652
  7.2 263.0 %all-reduce.3.cloned.1.call-start = ((), (), s32[]{:S(2)}) async-start(), calls=%async_computation | async-start | bytes 5505024 | tf_op jit(solution)/shard_map/psum | solution.py:111
  8.0 3.4 %collective-permute-start.6 = (bf16[1,32,192]{2,1,0:T(8,128)(2,1)S(1)}, bf16[1,32,192]{2,1,0:T(8,128)(2,1)S(1)}, u32[]{:S(2)}, u32[]{:S(2)}) collective-permute-start(bf16[1,32,192]{2,1,0:T(8,128)(2,1)S(1)} %get-tuple-element.40), channel_id=1, source_target_pairs={} | collective-permute-start | bytes 36872 | tf_op jit(solution)/shard_map/ppermute | solution.py:20
  8.7 2.7 collective-permute-start.7
  10.1 10.9 %collective-permute-start = (bf16[1,32,192]{2,1,0:T(8,128)(2,1)S(1)}, bf16[1,32,192]{2,1,0:T(8,128)(2,1)S(1)}, u32[]{:S(2)}, u32[]{:S(2)}) collective-permute-start(bf16[1,32,192]{2,1,0:T(8,128)(2,1)S(1)} %get-tuple-element.45), channel_id=1, source_target_pairs={} | collective-permute-start | bytes 36872 | tf_op jit(solution)/shard_map/ppermute | solution.py:20
  10.7 10.8 %collective-permute-start.1 = (bf16[1,32,192]{2,1,0:T(8,128)(2,1)S(1)}, bf16[1,32,192]{2,1,0:T(8,128)(2,1)S(1)}, u32[]{:S(2)}, u32[]{:S(2)}) collective-permute-start(bf16[1,32,192]{2,1,0:T(8,128)(2,1)S(1)} %get-tuple-element.44), channel_id=1, source_target_pairs={} | collective-permute-start | bytes 36872 | tf_op jit(solution)/shard_map/ppermute | solution.py:22
  13.2 15.5 %collective-permute-start.9 = (bf16[34,32,192]{2,1,0:T(8,128)(2,1)S(1)}, bf16[34,32,192]{2,1,0:T(8,128)(2,1)S(1)}, u32[]{:S(2)}, u32[]{:S(2)}) collective-permute-start(bf16[34,32,192]{2,1,0:T(8,128)(2,1)S(1)} %constant_dynamic-update-slice_fusion.3), channel_id=1, source_target_pairs={{0,31},{1,0},{2,1},{3,2},{4,3},{5,4},{6,5},{7,6},{8,7},{9,8},{10,9... | collective-permute-start | bytes 1253384 | tf_op jit(solution)/shard_map/ppermute | solution.py:32
  20.9 12.7 %collective-permute-start.8 = (bf16[34,32,192]{2,1,0:T(8,128)(2,1)S(1)}, bf16[34,32,192]{2,1,0:T(8,128)(2,1)S(1)}, u32[]{:S(2)}, u32[]{:S(2)}) collective-permute-start(bf16[34,32,192]{2,1,0:T(8,128)(2,1)S(1)} %constant_dynamic-update-slice_fusion.3), channel_id=1, source_target_pairs={{0,1},{1,2},{2,3},{3,4},{4,5},{5,6},{6,7},{7,8},{8,9},{9,10},{10,1... | collective-permute-start | bytes 1253384 | tf_op jit(solution)/shard_map/ppermute | solution.py:32
  22.8 11.9 %copy-start.3 = (bf16[32,32,192]{2,1,0:T(8,128)(2,1)S(1)}, bf16[32,32,192]{2,1,0:T(8,128)(2,1)}, u32[]{:S(2)}) copy-start(bf16[32,32,192]{2,1,0:T(8,128)(2,1)} %param.4) | copy-start | bytes 1179652
  23.4 22.7 %collective-permute-start.4 = (bf16[34,32,192]{2,1,0:T(8,128)(2,1)}, bf16[34,32,192]{2,1,0:T(8,128)(2,1)}, u32[]{:S(2)}, u32[]{:S(2)}) collective-permute-start(bf16[34,32,192]{2,1,0:T(8,128)(2,1)} %constant_dynamic-update-slice_fusion), channel_id=1, source_target_pairs={{0,31},{1,0},{2,1},{3,2},{4,3},{5,4},{6,5},{7,6},{8,7},{9,8},{10,9... | collective-permute-start | bytes 1253384 | tf_op jit(solution)/shard_map/ppermute | solution.py:32
  28.8 21.2 %collective-permute-start.2 = (bf16[34,32,192]{2,1,0:T(8,128)(2,1)}, bf16[34,32,192]{2,1,0:T(8,128)(2,1)}, u32[]{:S(2)}, u32[]{:S(2)}) collective-permute-start(bf16[34,32,192]{2,1,0:T(8,128)(2,1)} %constant_dynamic-update-slice_fusion), channel_id=1, source_target_pairs={{0,1},{1,2},{2,3},{3,4},{4,5},{5,6},{6,7},{7,8},{8,9},{9,10},{10,1... | collective-permute-start | bytes 1253384 | tf_op jit(solution)/shard_map/ppermute | solution.py:32
  41.5 9.2 %copy-start.11 = (bf16[3,3,192,192]{3,2,1,0:T(8,128)(2,1)S(1)}, bf16[3,3,192,192]{3,2,1,0:T(8,128)(2,1)}, u32[]{:S(2)}) copy-start(bf16[3,3,192,192]{3,2,1,0:T(8,128)(2,1)} %param.7) | copy-start | bytes 1990660
  46.2 14.3 %collective-permute-start.5 = (bf16[34,32,192]{2,1,0:T(8,128)(2,1)}, bf16[34,32,192]{2,1,0:T(8,128)(2,1)S(1)}, u32[]{:S(2)}, u32[]{:S(2)}) collective-permute-start(bf16[34,32,192]{2,1,0:T(8,128)(2,1)} %collective-permute-done.4), channel_id=1, source_target_pairs={{0,31},{1,0},{2,1},{3,2},{4,3},{5,4},{6,5},{7,6},{8,7},{9,8},{10,9... | collective-permute-start | bytes 1253384 | tf_op jit(solution)/shard_map/ppermute | solution.py:32
  48.6 6.2 %collective-permute-start.14 = (bf16[1,32,192]{1,2,0:T(8,128)(2,1)}, bf16[1,32,192]{1,2,0:T(8,128)(2,1)S(1)}, u32[]{:S(2)}, u32[]{:S(2)}) collective-permute-start(bf16[1,32,192]{1,2,0:T(8,128)(2,1)} %get-tuple-element.46), channel_id=1, source_target_pairs={} | collective-permute-start | bytes 36872 | tf_op jit(solution)/shard_map/ppermute | solution.py:20
  49.2 5.7 %collective-permute-start.15 = (bf16[1,32,192]{1,2,0:T(8,128)(2,1)S(1)}, bf16[1,32,192]{1,2,0:T(8,128)(2,1)S(1)}, u32[]{:S(2)}, u32[]{:S(2)}) collective-permute-start(bf16[1,32,192]{1,2,0:T(8,128)(2,1)S(1)} %get-tuple-element.47), channel_id=1, source_target_pairs={} | collective-permute-start | bytes 36872 | tf_op jit(solution)/shard_map/ppermute | solution.py:22
  49.9 12.9 %collective-permute-start.3 = (bf16[34,32,192]{2,1,0:T(8,128)(2,1)}, bf16[34,32,192]{2,1,0:T(8,128)(2,1)S(1)}, u32[]{:S(2)}, u32[]{:S(2)}) collective-permute-start(bf16[34,32,192]{2,1,0:T(8,128)(2,1)} %collective-permute-done.2), channel_id=1, source_target_pairs={{0,1},{1,2},{2,3},{3,4},{4,5},{5,6},{6,7},{7,8},{8,9},{9,10},{10,1... | collective-permute-start | bytes 1253384 | tf_op jit(solution)/shard_map/ppermute | solution.py:32
  55.0 9.1 %copy-start.6 = (bf16[32,32,192]{2,1,0:T(8,128)(2,1)S(1)}, bf16[32,32,192]{2,1,0:T(8,128)(2,1)}, u32[]{:S(2)}) copy-start(bf16[32,32,192]{2,1,0:T(8,128)(2,1)} %get-tuple-element.41) | copy-start | bytes 1179652
  56.0 28.3 %collective-permute-start.18 = (bf16[34,32,192]{2,1,0:T(8,128)(2,1)}, bf16[34,32,192]{2,1,0:T(8,128)(2,1)}, u32[]{:S(2)}, u32[]{:S(2)}) collective-permute-start(bf16[34,32,192]{2,1,0:T(8,128)(2,1)} %pad_maximum_fusion.1), channel_id=1, source_target_pairs={{0,31},{1,0},{2,1},{3,2},{4,3},{5,4},{6,5},{7,6},{8,7},{9,8},{10,9... | collective-permute-start | bytes 1253384 | tf_op jit(solution)/shard_map/ppermute | solution.py:32
  64.1 7.0 %copy-start.13 = (bf16[3,3,192,192]{3,2,1,0:T(8,128)(2,1)S(1)}, bf16[3,3,192,192]{3,2,1,0:T(8,128)(2,1)}, u32[]{:S(2)}) copy-start(bf16[3,3,192,192]{3,2,1,0:T(8,128)(2,1)} %copy.22) | copy-start | bytes 1990660
  74.7 12.4 %copy-start.1 = (bf16[1024,192]{0,1:T(8,128)(2,1)}, bf16[1024,192]{0,1:T(8,128)(2,1)S(1)}, u32[]{:S(2)}) copy-start(bf16[1024,192]{0,1:T(8,128)(2,1)S(1)} %fusion.1) | copy-start | bytes 1179652
  74.8 5.9 %collective-permute-start.10 = (bf16[1,32,192]{1,2,0:T(8,128)(2,1)S(1)}, bf16[1,32,192]{1,2,0:T(8,128)(2,1)S(1)}, u32[]{:S(2)}, u32[]{:S(2)}) collective-permute-start(bf16[1,32,192]{1,2,0:T(8,128)(2,1)S(1)} %get-tuple-element.48), channel_id=1, source_target_pairs={} | collective-permute-start | bytes 36872 | tf_op jit(solution)/shard_map/ppermute | solution.py:20
  75.5 5.3 %collective-permute-start.11 = (bf16[1,32,192]{1,2,0:T(8,128)(2,1)S(1)}, bf16[1,32,192]{1,2,0:T(8,128)(2,1)S(1)}, u32[]{:S(2)}, u32[]{:S(2)}) collective-permute-start(bf16[1,32,192]{1,2,0:T(8,128)(2,1)S(1)} %get-tuple-element.49), channel_id=1, source_target_pairs={} | collective-permute-start | bytes 36872 | tf_op jit(solution)/shard_map/ppermute | solution.py:22
  77.3 19.0 %collective-permute-start.16 = (bf16[34,32,192]{2,1,0:T(8,128)(2,1)}, bf16[34,32,192]{2,1,0:T(8,128)(2,1)}, u32[]{:S(2)}, u32[]{:S(2)}) collective-permute-start(bf16[34,32,192]{2,1,0:T(8,128)(2,1)} %pad_maximum_fusion.1), channel_id=1, source_target_pairs={{0,1},{1,2},{2,3},{3,4},{4,5},{5,6},{6,7},{7,8},{8,9},{9,10},{10,1... | collective-permute-start | bytes 1253384 | tf_op jit(solution)/shard_map/ppermute | solution.py:32
  81.8 19.8 %collective-permute-start.12 = (bf16[34,32,192]{2,1,0:T(8,128)(2,1)}, bf16[34,32,192]{2,1,0:T(8,128)(2,1)S(1)}, u32[]{:S(2)}, u32[]{:S(2)}) collective-permute-start(bf16[34,32,192]{2,1,0:T(8,128)(2,1)} %pad_maximum_fusion), channel_id=1, source_target_pairs={{0,1},{1,2},{2,3},{3,4},{4,5},{5,6},{6,7},{7,8},{8,9},{9,10},{10,1... | collective-permute-start | bytes 1253384 | tf_op jit(solution)/shard_map/ppermute | solution.py:32
  84.2 20.6 %collective-permute-start.19 = (bf16[34,32,192]{2,1,0:T(8,128)(2,1)}, bf16[34,32,192]{2,1,0:T(8,128)(2,1)S(1)}, u32[]{:S(2)}, u32[]{:S(2)}) collective-permute-start(bf16[34,32,192]{2,1,0:T(8,128)(2,1)} %collective-permute-done.18), channel_id=1, source_target_pairs={{0,31},{1,0},{2,1},{3,2},{4,3},{5,4},{6,5},{7,6},{8,7},{9,8},{10,9... | collective-permute-start | bytes 1253384 | tf_op jit(solution)/shard_map/ppermute | solution.py:32
  91.2 33.2 %collective-permute-start.13 = (bf16[34,32,192]{2,1,0:T(8,128)(2,1)}, bf16[34,32,192]{2,1,0:T(8,128)(2,1)S(1)}, u32[]{:S(2)}, u32[]{:S(2)}) collective-permute-start(bf16[34,32,192]{2,1,0:T(8,128)(2,1)} %pad_maximum_fusion), channel_id=1, source_target_pairs={{0,31},{1,0},{2,1},{3,2},{4,3},{5,4},{6,5},{7,6},{8,7},{9,8},{10,9... | collective-permute-start | bytes 1253384 | tf_op jit(solution)/shard_map/ppermute | solution.py:32
  96.3 13.0 %collective-permute-start.17 = (bf16[34,32,192]{2,1,0:T(8,128)(2,1)}, bf16[34,32,192]{2,1,0:T(8,128)(2,1)}, u32[]{:S(2)}, u32[]{:S(2)}) collective-permute-start(bf16[34,32,192]{2,1,0:T(8,128)(2,1)} %collective-permute-done.16), channel_id=1, source_target_pairs={{0,1},{1,2},{2,3},{3,4},{4,5},{5,6},{6,7},{7,8},{8,9},{9,10},{10,1... | collective-permute-start | bytes 1253384 | tf_op jit(solution)/shard_map/ppermute | solution.py:32
  102.8 8.9 %copy-start.4 = (bf16[32,32,192]{2,1,0:T(8,128)(2,1)S(1)}, bf16[32,32,192]{2,1,0:T(8,128)(2,1)}, u32[]{:S(2)}) copy-start(bf16[32,32,192]{2,1,0:T(8,128)(2,1)} %get-tuple-element.32) | copy-start | bytes 1179652
  102.8 8.9 %copy-start.5 = (bf16[32,32,192]{2,1,0:T(8,128)(2,1)S(1)}, bf16[32,32,192]{2,1,0:T(8,128)(2,1)}, u32[]{:S(2)}) copy-start(bf16[32,32,192]{2,1,0:T(8,128)(2,1)} %get-tuple-element.33) | copy-start | bytes 1179652
  126.6 4.8 %copy-start.2 = (bf16[1024,192]{0,1:T(8,128)(2,1)S(1)}, bf16[1024,192]{0,1:T(8,128)(2,1)}, u32[]{:S(2)}) copy-start(bf16[1024,192]{0,1:T(8,128)(2,1)} %copy-done.1) | copy-start | bytes 1179652
  127.0 6.7 %copy-start.9 = (bf16[1024,192]{0,1:T(8,128)(2,1)S(1)}, bf16[1024,192]{0,1:T(8,128)(2,1)}, u32[]{:S(2)}) copy-start(bf16[1024,192]{0,1:T(8,128)(2,1)} %copy.34) | copy-start | bytes 1179652
  127.1 8.2 %copy-start.12 = (bf16[3,3,192,192]{3,2,1,0:T(8,128)(2,1)S(1)}, bf16[3,3,192,192]{3,2,1,0:T(8,128)(2,1)}, u32[]{:S(2)}) copy-start(bf16[3,3,192,192]{3,2,1,0:T(8,128)(2,1)} %copy.36) | copy-start | bytes 1990660
  (4 other events, 9.7 us)
Sparse Core Ops, SparseCore 0:
  127.2 142.9 all-reduce.2
where the time goes:
time: 284 us; the launch traced here: 282 us
  waiting for transfers between devices  139 us (49%)
  local copies, waits for them, and re-layouts  62.6 us (22%)
  starting transfers between devices  38 us (13%)
  matrix products  19.3 us (7%)
  between operations  14.4 us (5%)
  other arithmetic  9.23 us (3%)
    psum x1, waiting for transfers between devices, shards(): summed_one, summed_two = lax.psum((part_one, part_two), ('lon', 'lat'))  131 us
    ppermute x12, starting transfers between devices, from_behind(): return lax.ppermute(value, axis, pairs)  32.8 us
    concatenate x12, local copies, waits for them, and re-layouts, gather_taps(): return jnp.concatenate(pieces, axis=2).reshape(height * border_width, -1)  29.8 us
    unnamed x40, local copies, waits for them, and re-layouts  9.88 us
    slice x8, local copies, waits for them, and re-layouts, gather_taps(): extended[row_off:row_off + height, start:start + border_width]  9.8 us
    dot_general x2, matrix products, contract_cells(): lax.dot_general(stacked, other, (((0,), (0,)), ((), ())), preferred_eleme...  8.04 us
    ppermute x12, waiting for transfers between devices, from_behind(): return lax.ppermute(value, axis, pairs)  8.01 us
    concatenate x6, other arithmetic, with_halo(): jnp.concatenate([lax.ppermute(tail, axis, [(i, (i + 1) % count) for i in...  7.24 us
  transfers between devices with their start and end apart: 21, of which 4 were waited for; matrix products, arithmetic and copies ran while one was open for 29% of the time, Pallas kernels for 0%

commit v1 on v0

v1 whole, which is shorter than its diff:
```python
import math

import jax
import jax.numpy as jnp
from jax import lax
from jax.experimental import pallas as pl
from jax.experimental.pallas import tpu as pltpu
from jax.sharding import PartitionSpec as P

FIRST_SPREAD = 32
SECOND_SPREAD = 64
LANES = 128
ROW_TILE = 16
VMEM_LIMIT = 48 * 1024 * 1024


def call(body, outs, args, scratch=(), flops=0, name=None):
    moved = sum(a.size * a.dtype.itemsize for a in list(args) + list(outs))
    return pl.pallas_call(
        body,
        out_shape=list(outs),
        in_specs=[pl.BlockSpec(memory_space=pltpu.VMEM)] * len(args),
        out_specs=[pl.BlockSpec(memory_space=pltpu.VMEM)] * len(outs),
        scratch_shapes=list(scratch),
        compiler_params=pltpu.CompilerParams(vmem_limit_bytes=VMEM_LIMIT),
        cost_estimate=pl.CostEstimate(flops=flops, bytes_accessed=moved, transcendentals=0),
        name=name,
    )(*args)


def shape_of(shape, dtype):
    return jax.ShapeDtypeStruct(shape, dtype)


def packs(rows, channels):
    return channels % LANES * 2 == LANES and rows % (2 * ROW_TILE) == 0


def packed_shape(rows, channels):
    if not packs(rows, channels):
        return (rows, channels)
    full = channels // LANES
    return (rows * full + rows // 2, LANES)


def pack_into(ref, value):
    rows, channels = value.shape
    if not packs(rows, channels):
        ref[...] = value
        return
    full = channels // LANES
    for tile in range(full):
        ref[tile * rows : (tile + 1) * rows, :] = value[:, tile * LANES : (tile + 1) * LANES]
    rest = value[:, full * LANES :]
    half = rows // 2
    ref[full * rows :, :] = jnp.concatenate([rest[:half], rest[half:]], axis=1)


def unpacked(ref, rows, channels):
    if not packs(rows, channels):
        return ref[...]
    full = channels // LANES
    rest = ref[full * rows :, :]
    width = channels - full * LANES
    tail = jnp.concatenate([rest[:, :width], rest[:, width:]], axis=0)
    return jnp.concatenate([ref[t * rows : (t + 1) * rows, :] for t in range(full)] + [tail], axis=1)


def extend(scratch, value, rim, width):
    rows = value.shape[0]
    scratch[width : width + rows, :] = value
    if rim is None:
        blank = jnp.zeros((width, value.shape[1]), value.dtype)
        scratch[:width, :] = blank
        scratch[width + rows :, :] = blank
    else:
        scratch[:width, :] = rim[:width, :]
        scratch[width + rows :, :] = rim[width:, :]


def row_blocks(rows):
    size = rows
    while size > 256 and size % 2 == 0 and size // 2 % ROW_TILE == 0:
        size //= 2
    return [(start, size) for start in range(0, rows, size)]


NT = (((1,), (1,)), ((), ()))
NN = (((1,), (0,)), ((), ()))


def conv_block(terms, start, size, width):
    total = None
    for ext, weight, b, flipped in terms:
        for a in (-1, 0, 1):
            tap = ext[start + (1 + a) * width : start + (1 + a) * width + size, :]
            kernel = weight[1 - a, 1 - b] if flipped else weight[1 + a, 1 + b]
            part = lax.dot_general(tap, kernel, NT if flipped else NN, preferred_element_type=jnp.float32)
            total = part if total is None else total + part
    return total


def flat_rows(channels, pieces):
    if channels % LANES * 2 != LANES:
        rows = 9 * channels * (-(-channels // LANES))
    else:
        rows = 9 * channels * channels // LANES
    unit = pieces * ROW_TILE
    return -(-rows // unit) * unit


def store_flat(ref, lead, blocks):
    channels = blocks[0].shape[0]
    full = channels // LANES
    row = 0
    for block in blocks:
        for tile in range(full):
            ref[lead, row : row + channels, :] = block[:, tile * LANES : (tile + 1) * LANES]
            row += channels
    width = channels - full * LANES
    if width == 0:
        return
    rests = [block[:, full * LANES :] for block in blocks]
    if width * 2 != LANES:
        for rest in rests:
            ref[lead, row : row + channels, :width] = rest
            row += channels
        return
    for pair in range(0, 8, 2):
        ref[lead, row : row + channels, :] = jnp.concatenate([rests[pair], rests[pair + 1]], axis=1)
        row += channels
    half = channels // 2
    ref[lead, row : row + half, :] = jnp.concatenate([rests[8][:half], rests[8][half:]], axis=1)


def load_flat(ref, lead, channels):
    full = channels // LANES
    row = 0
    parts = []
    for _ in range(9):
        tiles = []
        for _ in range(full):
            tiles.append(ref[lead, row : row + channels, :])
            row += channels
        parts.append(tiles)
    width = channels - full * LANES
    if width == 0:
        pass
    elif width * 2 != LANES:
        for tap in range(9):
            parts[tap].append(ref[lead, row : row + channels, :width])
            row += channels
    else:
        for pair in range(0, 8, 2):
            both = ref[lead, row : row + channels, :]
            parts[pair].append(both[:, :width])
            parts[pair + 1].append(both[:, width:])
            row += channels
        both = ref[lead, row : row + channels // 2, :]
        parts[8].append(jnp.concatenate([both[:, :width], both[:, width:]], axis=0))
    return [jnp.concatenate(p, axis=1) if len(p) > 1 else p[0] for p in parts]


def radices(count):
    found = []
    if count % 2 == 0:
        found.append(2)
        count //= 2
    while count % 4 == 0:
        found.append(4)
        count //= 4
    while count % 2 == 0:
        found.append(2)
        count //= 2
    return found if count == 1 else None


def swapped(value, count, stride, k):
    return lax.ppermute(value, "lon", [(i, i ^ (k * stride)) for i in range(count)])


def moved(value, steps):
    count = lax.axis_size("lon")
    if steps % count == 0:
        return value
    return lax.ppermute(value, "lon", [(i, (i + steps) % count) for i in range(count)])


def lat_rim(field):
    count = lax.axis_size("lat")
    if count == 1:
        return None
    north = lax.ppermute(field[-1], "lat", [(i, i + 1) for i in range(count - 1)])
    south = lax.ppermute(field[0], "lat", [(i + 1, i) for i in range(count - 1)])
    return jnp.stack([north, south])


def beside(field, packed, spread, pack):
    width = field.shape[1]
    steps, rest = divmod(spread, width)
    if rest == 0:
        return moved(packed, steps), moved(packed, -steps)
    cut = width - rest
    west = jnp.concatenate([moved(field[:, cut:], steps + 1), moved(field[:, :cut], steps)], axis=1)
    east = jnp.concatenate([moved(field[:, rest:], -steps), moved(field[:, :rest], -steps - 1)], axis=1)
    return pack(west), pack(east)


def shards(inputs, cotangent, first_weight, second_weight):
    height, width, channels = inputs.shape
    rows = height * width
    count = lax.axis_size("lon")
    scale = 1.0 / math.sqrt(rows * lax.axis_size("lat") * count)
    bf16, f32 = jnp.bfloat16, jnp.float32
    pshape = packed_shape(rows, channels)
    ext_shape = (rows + 2 * width, channels)
    ext = pltpu.VMEM(ext_shape, bf16)
    tap_flops = 2 * rows * channels * channels
    blocks = row_blocks(rows)

    def pack_body(*refs):
        half = len(refs) // 2
        for source, target in zip(refs[:half], refs[half:]):
            pack_into(target, source[...])

    def pack(*fields):
        flat = [f.reshape(rows, channels) for f in fields]
        return call(pack_body, [shape_of(pshape, bf16)] * len(flat), flat, name="pack")

    def pack_one(field):
        return pack(field)[0]

    def rims_of(field, spread):
        rim = lat_rim(field)
        if rim is None:
            return []
        west, east = beside(rim, rim, spread, lambda r: r)
        return [r.reshape(2 * width, channels) for r in (rim, west, east)]

    x = inputs.reshape(rows, channels)
    g = cotangent.reshape(rows, channels)
    x_rims = rims_of(inputs, FIRST_SPREAD)
    g_rims = rims_of(cotangent, SECOND_SPREAD)
    rimmed = bool(x_rims)

    x_packed, g_packed = pack(inputs, cotangent)
    x_west, x_east = beside(inputs, x_packed, FIRST_SPREAD, pack_one)
    g_west, g_east = beside(cotangent, g_packed, SECOND_SPREAD, pack_one)

    def own_body(x_ref, g_ref, w1_ref, w2_ref, *rest):
        rims, (part1, part2, xe, ge) = (rest[:2], rest[2:]) if rimmed else ((None, None), rest)
        extend(xe, x_ref[...], rims[0], width)
        extend(ge, g_ref[...], rims[1], width)
        for start, size in blocks:
            part1[start : start + size, :] = conv_block([(xe, w1_ref, 0, False)], start, size, width)
        for start, size in blocks:
            part2[start : start + size, :] = conv_block([(ge, w2_ref, 0, True)], start, size, width)

    part1, part2 = call(
        own_body,
        [shape_of((rows, channels), f32)] * 2,
        [x, g, first_weight, second_weight] + x_rims[:1] + g_rims[:1],
        [ext, ext],
        flops=6 * tap_flops,
        name="own_columns",
    )

    def hidden_body(part_ref, west_ref, east_ref, w_ref, *rest):
        rims, (hidden_t, slope, we, ee, hid) = (rest[:2], rest[2:]) if rimmed else ((None, None), rest)
        extend(we, unpacked(west_ref, rows, channels), rims[0], width)
        extend(ee, unpacked(east_ref, rows, channels), rims[1], width)
        for start, size in blocks:
            act = part_ref[start : start + size, :] + conv_block(
                [(we, w_ref, -1, False), (ee, w_ref, 1, False)], start, size, width
            )
            sigma = jax.nn.sigmoid(act)
            slope[start : start + size, :] = sigma * (1.0 + act * (1.0 - sigma))
            hid[start : start + size, :] = (act * sigma).astype(bf16).astype(f32)
        hidden_t[...] = hid[...].T.astype(bf16)

    hidden_t, slope = call(
        hidden_body,
        [shape_of((channels, rows), bf16), shape_of((rows, channels), f32)],
        [part1, x_west, x_east, first_weight] + x_rims[1:],
        [ext, ext, pltpu.VMEM((rows, channels), f32)],
        flops=6 * tap_flops,
        name="hidden",
    )

    def grad_body(part_ref, slope_ref, west_ref, east_ref, w_ref, *rest):
        rims, (pre_grad, packed, we, ee) = (rest[:2], rest[2:]) if rimmed else ((None, None), rest)
        extend(we, unpacked(west_ref, rows, channels), rims[0], width)
        extend(ee, unpacked(east_ref, rows, channels), rims[1], width)
        for start, size in blocks:
            grad = part_ref[start : start + size, :] + conv_block(
                [(we, w_ref, -1, True), (ee, w_ref, 1, True)], start, size, width
            )
            pre_grad[start : start + size, :] = (grad * slope_ref[start : start + size, :]).astype(bf16)
        pack_into(packed, pre_grad[...])

    pre_grad, pre_packed = call(
        grad_body,
        [shape_of((rows, channels), bf16), shape_of(pshape, bf16)],
        [part2, slope, g_west, g_east, second_weight] + g_rims[1:],
        [ext, ext],
        flops=6 * tap_flops,
        name="pre_grad",
    )
    pre_field = pre_grad.reshape(height, width, channels)
    p_west, p_east = beside(pre_field, pre_packed, FIRST_SPREAD, pack_one)
    p_rims = rims_of(pre_field, FIRST_SPREAD)

    stages = radices(count)
    pieces = count // 2 if stages else 1
    flat = flat_rows(channels, pieces)

    def kernels_body(hidden_t, pre_ref, x_ref, xw_ref, xe_ref, g_ref, gw_ref, ge_ref, *rest):
        rims, rest = (rest[:6], rest[6:]) if rimmed else ((None,) * 6, rest)
        own, send, both, e0, e1, e2, f0, f1, f2 = rest
        extend(e0, unpacked(gw_ref, rows, channels), rims[4], width)
        extend(e1, g_ref[...], rims[3], width)
        extend(e2, unpacked(ge_ref, rows, channels), rims[5], width)
        extend(f0, unpacked(xw_ref, rows, channels), rims[1], width)
        extend(f1, x_ref[...], rims[0], width)
        extend(f2, unpacked(xe_ref, rows, channels), rims[2], width)

        def window(field, a):
            return field[(1 + a) * width : (1 + a) * width + rows, :]

        second = []
        for a in (-1, 0, 1):
            for b in (-1, 0, 1):
                tap = window((e0, e1, e2)[1 - b], -a)
                second.append(jnp.dot(hidden_t[...], tap, preferred_element_type=f32))
        used = flat_rows(channels, 1) // ROW_TILE * ROW_TILE
        if used < flat:
            both[:, used - ROW_TILE :, :] = jnp.zeros((2, flat - used + ROW_TILE, LANES), f32)
        store_flat(both, 0, second)
        pre_t = pre_ref[...].astype(f32).T.astype(bf16)
        first = []
        for a in (-1, 0, 1):
            for b in (-1, 0, 1):
                first.append(jnp.dot(pre_t, window((f0, f1, f2)[1 + b], a), preferred_element_type=f32))
        store_flat(both, 1, first)
        mine = lax.rem(lax.axis_index("lon"), 2)
        own[...] = both[mine]
        send[...] = both[1 - mine].astype(bf16)

    own, send = call(
        kernels_body,
        [shape_of((flat, LANES), f32), shape_of((flat, LANES), bf16)],
        [hidden_t, pre_grad, x, x_west, x_east, g, g_west, g_east] + x_rims + g_rims,
        [pltpu.VMEM((2, flat, LANES), f32)] + [ext] * 6,
        flops=18 * tap_flops,
        name="kernel_gradients",
    )

    index = lax.axis_index("lon")
    total = own + swapped(send, count, 1, 1).astype(f32)
    stride = 2
    for radix in stages[1:]:
        digit = index // stride % radix
        split = total.reshape(radix, -1, LANES)
        parts = [
            swapped(
                lax.dynamic_index_in_dim(split, digit ^ k, 0, keepdims=False).astype(bf16), count, stride, k
            )
            for k in range(1, radix)
        ]
        total = lax.dynamic_index_in_dim(split, digit, 0, keepdims=False)
        for part in parts:
            total = total + part.astype(f32)
        stride *= radix
    if lax.axis_size("lat") > 1:
        total = lax.psum(total, "lat")
    held = total.astype(bf16)
    for radix in reversed(stages[2:]):
        stride //= radix
        held = jnp.concatenate([held] + [swapped(held, count, stride, k) for k in range(1, radix)], axis=0)
    group = stages[1]
    quarter = [held] + [swapped(held, count, 2, k) for k in range(1, group)]
    sibling = [swapped(q, count, 1, 1) for q in quarter]

    def own_grad_body(p_ref, w_ref, *rest):
        rim, (part, pe) = (rest[0], rest[1:]) if rimmed else (None, rest)
        extend(pe, p_ref[...], rim, width)
        for start, size in blocks:
            part[start : start + size, :] = conv_block([(pe, w_ref, 0, True)], start, size, width)

    (part3,) = call(
        own_grad_body,
        [shape_of((rows, channels), f32)],
        [pre_grad, first_weight] + p_rims[:1],
        [ext],
        flops=3 * tap_flops,
        name="own_input_gradient",
    )

    def input_body(part_ref, west_ref, east_ref, w_ref, *rest):
        rims, (out, we, ee) = (rest[:2], rest[2:]) if rimmed else ((None, None), rest)
        extend(we, unpacked(west_ref, rows, channels), rims[0], width)
        extend(ee, unpacked(east_ref, rows, channels), rims[1], width)
        for start, size in blocks:
            grad = part_ref[start : start + size, :] + conv_block(
                [(we, w_ref, -1, True), (ee, w_ref, 1, True)], start, size, width
            )
            out[start : start + size, :] = grad.astype(bf16)

    (input_gradient,) = call(
        input_body,
        [shape_of((rows, channels), bf16)],
        [part3, p_west, p_east, first_weight] + p_rims[1:],
        [ext, ext],
        flops=6 * tap_flops,
        name="input_gradient",
    )

    rest_radices = stages[2:]
    unit = flat // pieces

    def final_body(*refs):
        quarters, (first_out, second_out, both) = refs[: 2 * group], refs[2 * group :]
        place = lax.axis_index("lon")
        mine = lax.rem(place, 2)
        for side in range(2):
            lead = mine if side == 0 else 1 - mine
            for k in range(group):
                begin = (lax.rem(place // 2, group) ^ k) * (pieces // group)
                parts = [(begin, 0)]
                stride, span = 2 * group, pieces // group
                offset_parts = [(begin, 0, span)]
                walk = [(begin, 0)]
                for radix in rest_radices:
                    digit = lax.rem(place // stride, radix)
                    span //= radix
                    walk = [
                        (at + (digit ^ j) * span, order + j * span) for at, order in walk for j in range(radix)
                    ]
                    stride *= radix
                for at, order in walk:
                    both[lead, pl.ds(pl.multiple_of(at * unit, unit), unit), :] = quarters[side * group + k][
                        order * unit : (order + 1) * unit, :
                    ].astype(f32)
        second = load_flat(both, 0, channels)
        first = load_flat(both, 1, channels)
        for tap in range(9):
            second_out[tap // 3, tap % 3] = second[tap] * scale
            first_out[tap // 3, tap % 3] = first[tap].T * scale

    first_gradient, second_gradient = call(
        final_body,
        [shape_of((3, 3, channels, channels), f32)] * 2,
        quarter + sibling,
        [pltpu.VMEM((2, flat, LANES), f32)],
        name="unpack_gradients",
    )
    return (input_gradient.reshape(height, width, channels), first_gradient, second_gradient)


def solution(mesh):
    placed = (P("lat", "lon", None), P("lat", "lon", None), P(), P())
    return jax.shard_map(
        shards,
        mesh=mesh,
        in_specs=placed,
        out_specs=(P("lat", "lon", None), P(), P()),
        check_vma=False,
    )
```

time: 284 us -> 94.8 us (0.33)
  waiting for transfers between devices: 139 us -> 44.5 us
  local copies, waits for them, and re-layouts: 62.6 us -> 4.57 us
  matrix products: 19.3 us -> 0 us
  between operations: 14.4 us -> 0.79 us
  Pallas kernels: 0 us -> 12.2 us
  starting transfers between devices: 38 us -> 30.2 us
  other arithmetic: 9.23 us -> 2.32 us
    psum x1 -> x0, waiting for transfers between devices: 131 us -> none  [shards(): summed_one, summed_two = lax.psum((part_one, part_two), ('lon', 'lat'))]
    ppermute x20 -> x23, waiting for transfers between devices: 8.06 us -> 44.5 us  [the longest x17 29.7 us: swapped(): lax.ppermute(value, 'lon', [(i, i ^ k * stride) for i in range(count)])]
    concatenate x14 -> x0, local copies, waits for them, and re-layouts: 30.4 us -> none  [the longest x12 29.8 us: gather_taps(): return jnp.concatenate(pieces, axis=2).reshape(height * border_width, -1)]
    dot_general x5 -> x0, matrix products: 19.3 us -> none  [the longest x2 8.04 us: contract_cells(): lax.dot_general(stacked, other, (((0,), (0,)), ((), ())), preferred_eleme...]
    pallas_call x0 -> x8, Pallas kernels: none -> 12.2 us  [call(): pl.pallas_call(body, out_shape=list(outs), in_specs=[pl.BlockSpec(memory_...]
    slice x12 -> x0, local copies, waits for them, and re-layouts: 12.1 us -> none  [the longest x8 9.8 us: gather_taps(): extended[row_off:row_off + height, start:start + border_width]]
    ppermute x20 -> x23, starting transfers between devices: 38 us -> 30.2 us  [the longest x17 20.5 us: swapped(): lax.ppermute(value, 'lon', [(i, i ^ k * stride) for i in range(count)])]
    concatenate x6 -> x1, other arithmetic: 7.24 us -> 0.01 us  [shards(): jnp.concatenate([held] + [swapped(held, count, stride, k) for k in range(...]
  transfers between devices with their start and end apart: 21 -> 23, of which waited for: 4 -> 13; matrix products, arithmetic and copies ran while one was open for 29% -> 0% of each run, Pallas kernels for 0% -> 5%
where the time goes in v1:
time: 94.8 us; the launch traced here: 94.5 us
  waiting for transfers between devices  44.5 us (47%)
  starting transfers between devices  30.2 us (32%)
  Pallas kernels  12.2 us (13%)
  local copies, waits for them, and re-layouts  4.57 us (5%)
  other arithmetic  2.32 us (2%)
    ppermute x17, waiting for transfers between devices, swapped(): lax.ppermute(value, 'lon', [(i, i ^ k * stride) for i in range(count)])  29.7 us
    ppermute x17, starting transfers between devices, swapped(): lax.ppermute(value, 'lon', [(i, i ^ k * stride) for i in range(count)])  20.5 us
    ppermute x6, waiting for transfers between devices, moved(): lax.ppermute(value, 'lon', [(i, (i + steps) % count) for i in range(count)])  14.7 us
    pallas_call x8, Pallas kernels, call(): pl.pallas_call(body, out_shape=list(outs), in_specs=[pl.BlockSpec(memory_...  12.2 us
    ppermute x6, starting transfers between devices, moved(): lax.ppermute(value, 'lon', [(i, (i + steps) % count) for i in range(count)])  9.64 us
    unnamed x16, local copies, waits for them, and re-layouts  4.47 us
  transfers between devices with their start and end apart: 23, of which 13 were waited for; matrix products, arithmetic and copies ran while one was open for 0% of the time, Pallas kernels for 5%

profile of v1, /device:TPU:0, one launch (start us, length us, event | category | flops | bytes accessed | tf_op | source)
XLA Modules:
  0.0 94.5 jit_solution(13502243344780672163)
XLA Ops:
  0.7 1.1 %copy-done.3 = bf16[32,32,192]{2,1,0:T(8,128)(2,1)S(1)} copy-done((bf16[32,32,192]{2,1,0:T(8,128)(2,1)S(1)}, bf16[32,32,192]{2,1,0:T(8,128)(2,1)}, u32[]{:S(2)}) %copy-start.3) | copy-done | bytes 393240
  3.0 6.4 %collective-permute-start.1 = (bf16[1536,128]{1,0:T(8,128)(2,1)S(1)}, bf16[1536,128]{1,0:T(8,128)(2,1)S(1)}, u32[]{:S(2)}, u32[]{:S(2)}) collective-permute-start(bf16[1536,128]{1,0:T(8,128)(2,1)S(1)} %get-tuple-element.17), channel_id=1, source_target_pairs={{0,31},{1,0},{2,1},{3,2},{4,3},{5,4},{6,5},{7,6},{8,7},{9,8},{10,9... | collective-permute-start | bytes 1179656 | tf_op jit(solution)/shard_map/ppermute | solution.py:186
  9.4 1.1 %collective-permute-start.3 = (bf16[1536,128]{1,0:T(8,128)(2,1)S(1)}, bf16[1536,128]{1,0:T(8,128)(2,1)S(1)}, u32[]{:S(2)}, u32[]{:S(2)}) collective-permute-start(bf16[1536,128]{1,0:T(8,128)(2,1)S(1)} %get-tuple-element.19), channel_id=1, source_target_pairs={{0,30},{1,31},{2,0},{3,1},{4,2},{5,3},{6,4},{7,5},{8,6},{9,7},{10,... | collective-permute-start | bytes 1179656 | tf_op jit(solution)/shard_map/ppermute | solution.py:186
  11.4 1.2 %copy-done.1 = bf16[3,3,192,192]{3,2,1,0:T(8,128)(2,1)S(1)} copy-done((bf16[3,3,192,192]{3,2,1,0:T(8,128)(2,1)S(1)}, bf16[3,3,192,192]{3,2,1,0:T(8,128)(2,1)}, u32[]{:S(2)}) %copy-start.1) | copy-done | bytes 663576
  13.6 1.1 %collective-permute-done.1.east_ref.xe_ref = bf16[1536,128]{1,0:T(8,128)(2,1)S(1)} collective-permute-done((bf16[1536,128]{1,0:T(8,128)(2,1)S(1)}, bf16[1536,128]{1,0:T(8,128)(2,1)S(1)}, u32[]{:S(2)}, u32[]{:S(2)}) %collective-permute-start.1) | collective-permute-done | bytes 393248 | tf_op jit(solution)/shard_map/ppermute | solution.py:186
  14.7 8.1 %collective-permute-done.west_ref.xw_ref = bf16[1536,128]{1,0:T(8,128)(2,1)S(1)} collective-permute-done((bf16[1536,128]{1,0:T(8,128)(2,1)S(1)}, bf16[1536,128]{1,0:T(8,128)(2,1)S(1)}, u32[]{:S(2)}, u32[]{:S(2)}) %collective-permute-start) | collective-permute-done | bytes 393248 | tf_op jit(solution)/shard_map/ppermute | solution.py:186
  22.8 1.3 %hidden.1 = (bf16[192,1024]{1,0:T(8,128)(2,1)S(1)}, f32[1024,192]{1,0:T(8,128)S(1)}) custom-call(f32[1024,192]{1,0:T(8,128)S(1)} %get-tuple-element.16.part_ref, bf16[1536,128]{1,0:T(8,128)(2,1)S(1)} %collective-permute-done.west_ref.xw_ref, bf16[1536,128]{1,0:T(8,128)(2,1)S(1)} %collective-permute-done.1.east_ref.xe_ref, bf16[3,3,192,192]{3,2,1,0:T(8,128)(2,1)S(1)} %copy-done), custom_call_target="tpu_custom_call" | custom-call | flops 452984832 | bytes 3416064 | tf_op jit(solution)/shard_map/hidden/pallas_call | solution.py:19
  24.1 5.5 %collective-permute-done.2.west_ref.gw_ref = bf16[1536,128]{1,0:T(8,128)(2,1)S(1)} collective-permute-done((bf16[1536,128]{1,0:T(8,128)(2,1)S(1)}, bf16[1536,128]{1,0:T(8,128)(2,1)S(1)}, u32[]{:S(2)}, u32[]{:S(2)}) %collective-permute-start.2) | collective-permute-done | bytes 393248 | tf_op jit(solution)/shard_map/ppermute | solution.py:186
  29.6 1.1 %pre_grad.1 = (bf16[1024,192]{1,0:T(8,128)(2,1)S(1)}, bf16[1536,128]{1,0:T(8,128)(2,1)S(1)}) custom-call(f32[1024,192]{1,0:T(8,128)S(1)} %get-tuple-element.15.part_ref, f32[1024,192]{1,0:T(8,128)S(1)} %get-tuple-element.18.slope_ref, bf16[1536,128]{1,0:T(8,128)(2,1)S(1)} %collective-permute-done.2.west_ref.gw_ref, ...), custom_call_target="tpu_custom_call" | custom-call | flops 452984832 | bytes 3809280 | tf_op jit(solution)/shard_map/pre_grad/pallas_call | solution.py:19
  30.8 3.4 %kernel_gradients.1 = (f32[2816,128]{1,0:T(8,128)S(1)}, bf16[2816,128]{1,0:T(8,128)(2,1)}) custom-call(bf16[192,1024]{1,0:T(8,128)(2,1)S(1)} %get-tuple-element.22.hidden_t, bf16[1024,192]{1,0:T(8,128)(2,1)S(1)} %get-tuple-element.20.p_ref.pre_ref, bf16[1024,192]{1,0:T(8,128)(2,1)S(1)} %bitcast.33, ...), custom_call_target="tpu_custom_call" | custom-call | flops 1358954496 | bytes 5308416 | tf_op jit(solution)/shard_map/kernel_gradients/pallas_call | solution.py:19
  34.2 2.4 %collective-permute-start.6 = (bf16[2816,128]{1,0:T(8,128)(2,1)}, bf16[2816,128]{1,0:T(8,128)(2,1)}, u32[]{:S(2)}, u32[]{:S(2)}) collective-permute-start(bf16[2816,128]{1,0:T(8,128)(2,1)} %get-tuple-element.24), channel_id=1, source_target_pairs={{0,1},{1,0},{2,3},{3,2},{4,5},{5,4},{6,7},{7,6},{8,9},{9,8},{10,11... | collective-permute-start | bytes 2162696 | tf_op jit(solution)/shard_map/ppermute | solution.py:179
  36.6 2.2 %collective-permute-done.6 = bf16[2816,128]{1,0:T(8,128)(2,1)} collective-permute-done((bf16[2816,128]{1,0:T(8,128)(2,1)}, bf16[2816,128]{1,0:T(8,128)(2,1)}, u32[]{:S(2)}, u32[]{:S(2)}) %collective-permute-start.6) | collective-permute-done | bytes 720928 | tf_op jit(solution)/shard_map/ppermute | solution.py:179
  38.7 1.2 %convert_add_fusion = f32[2816,128]{1,0:T(8,128)S(1)} fusion(f32[2816,128]{1,0:T(8,128)S(1)} %get-tuple-element.23, bf16[2816,128]{1,0:T(8,128)(2,1)} %collective-permute-done.6), kind=kLoop, calls=%fused_computation | loop fusion | flops 720896 | bytes 3604480 | tf_op jit(solution)/shard_map/add | solution.py:359
  40.0 1.1 %copy-done.7 = f32[2816,128]{1,0:T(8,128)} copy-done((f32[2816,128]{1,0:T(8,128)}, f32[2816,128]{1,0:T(8,128)S(1)}, u32[]{:S(2)}) %copy-start.7) | copy-done | bytes 1441816
  41.1 2.3 %collective-permute-start.7 = (bf16[704,128]{1,0:T(8,128)(2,1)S(1)}, bf16[704,128]{1,0:T(8,128)(2,1)S(1)}, u32[]{:S(2)}, u32[]{:S(2)}) collective-permute-start(bf16[704,128]{1,0:T(8,128)(2,1)S(1)} %get-tuple-element.27), channel_id=1, source_target_pairs={{0,2},{1,3},{2,0},{3,1},{4,6},{5,7},{6,4},{7,5},{8,10},{9,11},{10,... | collective-permute-start | bytes 540680 | tf_op jit(solution)/shard_map/ppermute | solution.py:179
  43.4 2.0 %collective-permute-start.9 = (bf16[704,128]{1,0:T(8,128)(2,1)S(1)}, bf16[704,128]{1,0:T(8,128)(2,1)S(1)}, u32[]{:S(2)}, u32[]{:S(2)}) collective-permute-start(bf16[704,128]{1,0:T(8,128)(2,1)S(1)} %get-tuple-element.28), channel_id=1, source_target_pairs={{0,6},{1,7},{2,4},{3,5},{4,2},{5,3},{6,0},{7,1},{8,14},{9,15},{10,... | collective-permute-start | bytes 540680 | tf_op jit(solution)/shard_map/ppermute | solution.py:179
  45.4 3.4 %collective-permute-done.7 = bf16[704,128]{1,0:T(8,128)(2,1)S(1)} collective-permute-done((bf16[704,128]{1,0:T(8,128)(2,1)S(1)}, bf16[704,128]{1,0:T(8,128)(2,1)S(1)}, u32[]{:S(2)}, u32[]{:S(2)}) %collective-permute-start.7) | collective-permute-done | bytes 180256 | tf_op jit(solution)/shard_map/ppermute | solution.py:179
  48.8 5.1 %collective-permute-done.9 = bf16[704,128]{1,0:T(8,128)(2,1)S(1)} collective-permute-done((bf16[704,128]{1,0:T(8,128)(2,1)S(1)}, bf16[704,128]{1,0:T(8,128)(2,1)S(1)}, u32[]{:S(2)}, u32[]{:S(2)}) %collective-permute-start.9) | collective-permute-done | bytes 180256 | tf_op jit(solution)/shard_map/ppermute | solution.py:179
  53.9 1.4 %collective-permute-done.8 = bf16[704,128]{1,0:T(8,128)(2,1)S(1)} collective-permute-done((bf16[704,128]{1,0:T(8,128)(2,1)S(1)}, bf16[704,128]{1,0:T(8,128)(2,1)S(1)}, u32[]{:S(2)}, u32[]{:S(2)}) %collective-permute-start.8) | collective-permute-done | bytes 180256 | tf_op jit(solution)/shard_map/ppermute | solution.py:179
  56.4 1.6 %collective-permute-start.10 = (bf16[176,128]{1,0:T(8,128)(2,1)S(1)}, bf16[176,128]{1,0:T(8,128)(2,1)S(1)}, u32[]{:S(2)}, u32[]{:S(2)}) collective-permute-start(bf16[176,128]{1,0:T(8,128)(2,1)S(1)} %get-tuple-element.30), channel_id=1, source_target_pairs={{0,8},{1,9},{2,10},{3,11},{4,12},{5,13},{6,14},{7,15},{8,0},{9,1},... | collective-permute-start | bytes 135176 | tf_op jit(solution)/shard_map/ppermute | solution.py:179
  58.0 2.5 %collective-permute-start.12 = (bf16[176,128]{1,0:T(8,128)(2,1)S(1)}, bf16[176,128]{1,0:T(8,128)(2,1)S(1)}, u32[]{:S(2)}, u32[]{:S(2)}) collective-permute-start(bf16[176,128]{1,0:T(8,128)(2,1)S(1)} %get-tuple-element.31), channel_id=1, source_target_pairs={{0,24},{1,25},{2,26},{3,27},{4,28},{5,29},{6,30},{7,31},{8,16},{9,... | collective-permute-start | bytes 135176 | tf_op jit(solution)/shard_map/ppermute | solution.py:179
  60.6 1.2 %collective-permute-start.5 = (bf16[1536,128]{1,0:T(8,128)(2,1)S(1)}, bf16[1536,128]{1,0:T(8,128)(2,1)S(1)}, u32[]{:S(2)}, u32[]{:S(2)}) collective-permute-start(bf16[1536,128]{1,0:T(8,128)(2,1)S(1)} %get-tuple-element.21), channel_id=1, source_target_pairs={{0,31},{1,0},{2,1},{3,2},{4,3},{5,4},{6,5},{7,6},{8,7},{9,8},{10,9... | collective-permute-start | bytes 1179656 | tf_op jit(solution)/shard_map/ppermute | solution.py:186
  61.8 2.1 %collective-permute-done.12 = bf16[176,128]{1,0:T(8,128)(2,1)S(1)} collective-permute-done((bf16[176,128]{1,0:T(8,128)(2,1)S(1)}, bf16[176,128]{1,0:T(8,128)(2,1)S(1)}, u32[]{:S(2)}, u32[]{:S(2)}) %collective-permute-start.12) | collective-permute-done | bytes 45088 | tf_op jit(solution)/shard_map/ppermute | solution.py:179
  63.9 2.4 %collective-permute-done.11 = bf16[176,128]{1,0:T(8,128)(2,1)S(1)} collective-permute-done((bf16[176,128]{1,0:T(8,128)(2,1)S(1)}, bf16[176,128]{1,0:T(8,128)(2,1)S(1)}, u32[]{:S(2)}, u32[]{:S(2)}) %collective-permute-start.11) | collective-permute-done | bytes 45088 | tf_op jit(solution)/shard_map/ppermute | solution.py:179
  66.4 5.0 %collective-permute-start.15 = (bf16[176,128]{1,0:T(8,128)(2,1)S(1)}, bf16[176,128]{1,0:T(8,128)(2,1)S(1)}, u32[]{:S(2)}, u32[]{:S(2)}) collective-permute-start(bf16[176,128]{1,0:T(8,128)(2,1)S(1)} %fusion.7), channel_id=1, source_target_pairs={{0,24},{1,25},{2,26},{3,27},{4,28},{5,29},{6,30},{7,31},{8,16},{9,... | collective-permute-start | bytes 135176 | tf_op jit(solution)/shard_map/ppermute | solution.py:179
  72.0 1.4 %collective-permute-done.15 = bf16[176,128]{1,0:T(8,128)(2,1)S(1)} collective-permute-done((bf16[176,128]{1,0:T(8,128)(2,1)S(1)}, bf16[176,128]{1,0:T(8,128)(2,1)S(1)}, u32[]{:S(2)}, u32[]{:S(2)}) %collective-permute-start.15) | collective-permute-done | bytes 45088 | tf_op jit(solution)/shard_map/ppermute | solution.py:179
  73.3 2.9 %collective-permute-done.14 = bf16[176,128]{1,0:T(8,128)(2,1)S(1)} collective-permute-done((bf16[176,128]{1,0:T(8,128)(2,1)S(1)}, bf16[176,128]{1,0:T(8,128)(2,1)S(1)}, u32[]{:S(2)}, u32[]{:S(2)}) %collective-permute-start.14) | collective-permute-done | bytes 45088 | tf_op jit(solution)/shard_map/ppermute | solution.py:179
  76.4 3.4 %collective-permute-start.16 = (bf16[704,128]{1,0:T(8,128)(2,1)S(1)}, bf16[704,128]{1,0:T(8,128)(2,1)S(1)}, u32[]{:S(2)}, u32[]{:S(2)}) collective-permute-start(bf16[704,128]{1,0:T(8,128)(2,1)S(1)} %pad_maximum_fusion.refs_0_), channel_id=1, source_target_pairs={{0,2},{1,3},{2,0},{3,1},{4,6},{5,7},{6,4},{7,5},{8,10},{9,11},{10,... | collective-permute-start | bytes 540680 | tf_op jit(solution)/shard_map/ppermute | solution.py:179
  79.8 7.0 %collective-permute-done.18.refs_3_ = bf16[704,128]{1,0:T(8,128)(2,1)S(1)} collective-permute-done((bf16[704,128]{1,0:T(8,128)(2,1)S(1)}, bf16[704,128]{1,0:T(8,128)(2,1)S(1)}, u32[]{:S(2)}, u32[]{:S(2)}) %collective-permute-start.18) | collective-permute-done | bytes 180256 | tf_op jit(solution)/shard_map/ppermute | solution.py:179
  86.8 1.9 %collective-permute-done.17.refs_2_ = bf16[704,128]{1,0:T(8,128)(2,1)S(1)} collective-permute-done((bf16[704,128]{1,0:T(8,128)(2,1)S(1)}, bf16[704,128]{1,0:T(8,128)(2,1)S(1)}, u32[]{:S(2)}, u32[]{:S(2)}) %collective-permute-start.17) | collective-permute-done | bytes 180256 | tf_op jit(solution)/shard_map/ppermute | solution.py:179
  89.8 1.8 %input_gradient.1 = bf16[1024,192]{1,0:T(8,128)(2,1)} custom-call(f32[1024,192]{1,0:T(8,128)S(1)} %own_input_gradient.1.part_ref, bf16[1536,128]{1,0:T(8,128)(2,1)S(1)} %collective-permute-done.4.west_ref, bf16[1536,128]{1,0:T(8,128)(2,1)S(1)} %collective-permute-done.5.east_ref, bf16[3,3,192,192]{3,2,1,0:T(8,128)(2,1)S(1)} %copy-done), custom_call_target="tpu_custom_call" | custom-call | flops 452984832 | bytes 2629632 | tf_op jit(solution)/shard_map/input_gradient/pallas_call | solution.py:19
  91.6 2.9 %unpack_gradients.1 = (f32[3,3,192,192]{3,2,1,0:T(8,128)}, f32[3,3,192,192]{3,2,1,0:T(8,128)}) custom-call(bf16[704,128]{1,0:T(8,128)(2,1)S(1)} %pad_maximum_fusion.refs_0_, bf16[704,128]{1,0:T(8,128)(2,1)S(1)} %collective-permute-done.16.refs_1_, bf16[704,128]{1,0:T(8,128)(2,1)S(1)} %collective-permute-done.17.refs_2_, ...), custom_call_target="tpu_custom_call" | custom-call | bytes 4096000 | tf_op jit(solution)/shard_map/unpack_gradients/pallas_call | solution.py:19
  (44 shorter events, 6.4 us)
Async XLA Ops:
  0.6 10.8 %copy-start = (bf16[3,3,192,192]{3,2,1,0:T(8,128)(2,1)S(1)}, bf16[3,3,192,192]{3,2,1,0:T(8,128)(2,1)}, u32[]{:S(2)}) copy-start(bf16[3,3,192,192]{3,2,1,0:T(8,128)(2,1)} %w_ref.7) | copy-start | bytes 1990660
  0.6 1.1 %copy-start.3 = (bf16[32,32,192]{2,1,0:T(8,128)(2,1)S(1)}, bf16[32,32,192]{2,1,0:T(8,128)(2,1)}, u32[]{:S(2)}) copy-start(bf16[32,32,192]{2,1,0:T(8,128)(2,1)} %param.4) | copy-start | bytes 1179652
  1.8 1.0 %copy-start.5 = (bf16[32,32,192]{2,1,0:T(8,128)(2,1)S(1)}, bf16[32,32,192]{2,1,0:T(8,128)(2,1)}, u32[]{:S(2)}) copy-start(bf16[32,32,192]{2,1,0:T(8,128)(2,1)} %param.5) | copy-start | bytes 1179652
  3.0 11.7 %collective-permute-start.1 = (bf16[1536,128]{1,0:T(8,128)(2,1)S(1)}, bf16[1536,128]{1,0:T(8,128)(2,1)S(1)}, u32[]{:S(2)}, u32[]{:S(2)}) collective-permute-start(bf16[1536,128]{1,0:T(8,128)(2,1)S(1)} %get-tuple-element.17), channel_id=1, source_target_pairs={{0,31},{1,0},{2,1},{3,2},{4,3},{5,4},{6,5},{7,6},{8,7},{9,8},{10,9... | collective-permute-start | bytes 1179656 | tf_op jit(solution)/shard_map/ppermute | solution.py:186
  9.4 13.4 %collective-permute-start = (bf16[1536,128]{1,0:T(8,128)(2,1)S(1)}, bf16[1536,128]{1,0:T(8,128)(2,1)S(1)}, u32[]{:S(2)}, u32[]{:S(2)}) collective-permute-start(bf16[1536,128]{1,0:T(8,128)(2,1)S(1)} %get-tuple-element.17), channel_id=1, source_target_pairs={{0,1},{1,2},{2,3},{3,4},{4,5},{5,6},{6,7},{7,8},{8,9},{9,10},{10,1... | collective-permute-start | bytes 1179656 | tf_op jit(solution)/shard_map/ppermute | solution.py:186
  9.4 14.7 %collective-permute-start.3 = (bf16[1536,128]{1,0:T(8,128)(2,1)S(1)}, bf16[1536,128]{1,0:T(8,128)(2,1)S(1)}, u32[]{:S(2)}, u32[]{:S(2)}) collective-permute-start(bf16[1536,128]{1,0:T(8,128)(2,1)S(1)} %get-tuple-element.19), channel_id=1, source_target_pairs={{0,30},{1,31},{2,0},{3,1},{4,2},{5,3},{6,4},{7,5},{8,6},{9,7},{10,... | collective-permute-start | bytes 1179656 | tf_op jit(solution)/shard_map/ppermute | solution.py:186
  10.5 19.1 %collective-permute-start.2 = (bf16[1536,128]{1,0:T(8,128)(2,1)S(1)}, bf16[1536,128]{1,0:T(8,128)(2,1)S(1)}, u32[]{:S(2)}, u32[]{:S(2)}) collective-permute-start(bf16[1536,128]{1,0:T(8,128)(2,1)S(1)} %get-tuple-element.19), channel_id=1, source_target_pairs={{0,2},{1,3},{2,4},{3,5},{4,6},{5,7},{6,8},{7,9},{8,10},{9,11},{10,... | collective-permute-start | bytes 1179656 | tf_op jit(solution)/shard_map/ppermute | solution.py:186
  11.4 1.2 %copy-start.1 = (bf16[3,3,192,192]{3,2,1,0:T(8,128)(2,1)S(1)}, bf16[3,3,192,192]{3,2,1,0:T(8,128)(2,1)}, u32[]{:S(2)}) copy-start(bf16[3,3,192,192]{3,2,1,0:T(8,128)(2,1)} %w_ref.5) | copy-start | bytes 1990660
  13.6 16.0 %copy-start.2 = (bf16[3,3,192,192]{3,2,1,0:T(8,128)(2,1)S(1)}, bf16[3,3,192,192]{3,2,1,0:T(8,128)(2,1)}, u32[]{:S(2)}) copy-start(bf16[3,3,192,192]{3,2,1,0:T(8,128)(2,1)} %w_ref.5) | copy-start | bytes 1990660
  29.6 1.2 %copy-start.4 = (bf16[32,32,192]{2,1,0:T(8,128)(2,1)S(1)}, bf16[32,32,192]{2,1,0:T(8,128)(2,1)}, u32[]{:S(2)}) copy-start(bf16[32,32,192]{2,1,0:T(8,128)(2,1)} %param.4) | copy-start | bytes 1179652
  29.6 1.2 %copy-start.6 = (bf16[32,32,192]{2,1,0:T(8,128)(2,1)S(1)}, bf16[32,32,192]{2,1,0:T(8,128)(2,1)}, u32[]{:S(2)}) copy-start(bf16[32,32,192]{2,1,0:T(8,128)(2,1)} %param.5) | copy-start | bytes 1179652
  34.2 4.5 %collective-permute-start.6 = (bf16[2816,128]{1,0:T(8,128)(2,1)}, bf16[2816,128]{1,0:T(8,128)(2,1)}, u32[]{:S(2)}, u32[]{:S(2)}) collective-permute-start(bf16[2816,128]{1,0:T(8,128)(2,1)} %get-tuple-element.24), channel_id=1, source_target_pairs={{0,1},{1,0},{2,3},{3,2},{4,5},{5,4},{6,7},{7,6},{8,9},{9,8},{10,11... | collective-permute-start | bytes 2162696 | tf_op jit(solution)/shard_map/ppermute | solution.py:179
  40.0 1.1 %copy-start.7 = (f32[2816,128]{1,0:T(8,128)}, f32[2816,128]{1,0:T(8,128)S(1)}, u32[]{:S(2)}) copy-start(f32[2816,128]{1,0:T(8,128)S(1)} %convert_add_fusion) | copy-start | bytes 4325380
  41.1 7.7 %collective-permute-start.7 = (bf16[704,128]{1,0:T(8,128)(2,1)S(1)}, bf16[704,128]{1,0:T(8,128)(2,1)S(1)}, u32[]{:S(2)}, u32[]{:S(2)}) collective-permute-start(bf16[704,128]{1,0:T(8,128)(2,1)S(1)} %get-tuple-element.27), channel_id=1, source_target_pairs={{0,2},{1,3},{2,0},{3,1},{4,6},{5,7},{6,4},{7,5},{8,10},{9,11},{10,... | collective-permute-start | bytes 540680 | tf_op jit(solution)/shard_map/ppermute | solution.py:179
  43.4 10.5 %collective-permute-start.9 = (bf16[704,128]{1,0:T(8,128)(2,1)S(1)}, bf16[704,128]{1,0:T(8,128)(2,1)S(1)}, u32[]{:S(2)}, u32[]{:S(2)}) collective-permute-start(bf16[704,128]{1,0:T(8,128)(2,1)S(1)} %get-tuple-element.28), channel_id=1, source_target_pairs={{0,6},{1,7},{2,4},{3,5},{4,2},{5,3},{6,0},{7,1},{8,14},{9,15},{10,... | collective-permute-start | bytes 540680 | tf_op jit(solution)/shard_map/ppermute | solution.py:179
  45.4 9.9 %collective-permute-start.8 = (bf16[704,128]{1,0:T(8,128)(2,1)S(1)}, bf16[704,128]{1,0:T(8,128)(2,1)S(1)}, u32[]{:S(2)}, u32[]{:S(2)}) collective-permute-start(bf16[704,128]{1,0:T(8,128)(2,1)S(1)} %get-tuple-element.29), channel_id=1, source_target_pairs={{0,4},{1,5},{2,6},{3,7},{4,0},{5,1},{6,2},{7,3},{8,12},{9,13},{10,... | collective-permute-start | bytes 540680 | tf_op jit(solution)/shard_map/ppermute | solution.py:179
  56.4 5.4 %collective-permute-start.10 = (bf16[176,128]{1,0:T(8,128)(2,1)S(1)}, bf16[176,128]{1,0:T(8,128)(2,1)S(1)}, u32[]{:S(2)}, u32[]{:S(2)}) collective-permute-start(bf16[176,128]{1,0:T(8,128)(2,1)S(1)} %get-tuple-element.30), channel_id=1, source_target_pairs={{0,8},{1,9},{2,10},{3,11},{4,12},{5,13},{6,14},{7,15},{8,0},{9,1},... | collective-permute-start | bytes 135176 | tf_op jit(solution)/shard_map/ppermute | solution.py:179
  58.0 5.8 %collective-permute-start.12 = (bf16[176,128]{1,0:T(8,128)(2,1)S(1)}, bf16[176,128]{1,0:T(8,128)(2,1)S(1)}, u32[]{:S(2)}, u32[]{:S(2)}) collective-permute-start(bf16[176,128]{1,0:T(8,128)(2,1)S(1)} %get-tuple-element.31), channel_id=1, source_target_pairs={{0,24},{1,25},{2,26},{3,27},{4,28},{5,29},{6,30},{7,31},{8,16},{9,... | collective-permute-start | bytes 135176 | tf_op jit(solution)/shard_map/ppermute | solution.py:179
  60.5 5.8 %collective-permute-start.11 = (bf16[176,128]{1,0:T(8,128)(2,1)S(1)}, bf16[176,128]{1,0:T(8,128)(2,1)S(1)}, u32[]{:S(2)}, u32[]{:S(2)}) collective-permute-start(bf16[176,128]{1,0:T(8,128)(2,1)S(1)} %get-tuple-element.32), channel_id=1, source_target_pairs={{0,16},{1,17},{2,18},{3,19},{4,20},{5,21},{6,22},{7,23},{8,24},{9,... | collective-permute-start | bytes 135176 | tf_op jit(solution)/shard_map/ppermute | solution.py:179
  60.6 19.2 %collective-permute-start.5 = (bf16[1536,128]{1,0:T(8,128)(2,1)S(1)}, bf16[1536,128]{1,0:T(8,128)(2,1)S(1)}, u32[]{:S(2)}, u32[]{:S(2)}) collective-permute-start(bf16[1536,128]{1,0:T(8,128)(2,1)S(1)} %get-tuple-element.21), channel_id=1, source_target_pairs={{0,31},{1,0},{2,1},{3,2},{4,3},{5,4},{6,5},{7,6},{8,7},{9,8},{10,9... | collective-permute-start | bytes 1179656 | tf_op jit(solution)/shard_map/ppermute | solution.py:186
  66.4 7.0 %collective-permute-start.15 = (bf16[176,128]{1,0:T(8,128)(2,1)S(1)}, bf16[176,128]{1,0:T(8,128)(2,1)S(1)}, u32[]{:S(2)}, u32[]{:S(2)}) collective-permute-start(bf16[176,128]{1,0:T(8,128)(2,1)S(1)} %fusion.7), channel_id=1, source_target_pairs={{0,24},{1,25},{2,26},{3,27},{4,28},{5,29},{6,30},{7,31},{8,16},{9,... | collective-permute-start | bytes 135176 | tf_op jit(solution)/shard_map/ppermute | solution.py:179
  71.3 4.9 %collective-permute-start.14 = (bf16[176,128]{1,0:T(8,128)(2,1)S(1)}, bf16[176,128]{1,0:T(8,128)(2,1)S(1)}, u32[]{:S(2)}, u32[]{:S(2)}) collective-permute-start(bf16[176,128]{1,0:T(8,128)(2,1)S(1)} %fusion.7), channel_id=1, source_target_pairs={{0,16},{1,17},{2,18},{3,19},{4,20},{5,21},{6,22},{7,23},{8,24},{9,... | collective-permute-start | bytes 135176 | tf_op jit(solution)/shard_map/ppermute | solution.py:179
  71.3 4.9 %collective-permute-start.13 = (bf16[176,128]{1,0:T(8,128)(2,1)S(1)}, bf16[176,128]{1,0:T(8,128)(2,1)S(1)}, u32[]{:S(2)}, u32[]{:S(2)}) collective-permute-start(bf16[176,128]{1,0:T(8,128)(2,1)S(1)} %fusion.7), channel_id=1, source_target_pairs={{0,8},{1,9},{2,10},{3,11},{4,12},{5,13},{6,14},{7,15},{8,0},{9,1},... | collective-permute-start | bytes 135176 | tf_op jit(solution)/shard_map/ppermute | solution.py:179
  72.0 17.9 %collective-permute-start.4 = (bf16[1536,128]{1,0:T(8,128)(2,1)S(1)}, bf16[1536,128]{1,0:T(8,128)(2,1)S(1)}, u32[]{:S(2)}, u32[]{:S(2)}) collective-permute-start(bf16[1536,128]{1,0:T(8,128)(2,1)S(1)} %get-tuple-element.21), channel_id=1, source_target_pairs={{0,1},{1,2},{2,3},{3,4},{4,5},{5,6},{6,7},{7,8},{8,9},{9,10},{10,1... | collective-permute-start | bytes 1179656 | tf_op jit(solution)/shard_map/ppermute | solution.py:186
  76.3 10.5 %collective-permute-start.18 = (bf16[704,128]{1,0:T(8,128)(2,1)S(1)}, bf16[704,128]{1,0:T(8,128)(2,1)S(1)}, u32[]{:S(2)}, u32[]{:S(2)}) collective-permute-start(bf16[704,128]{1,0:T(8,128)(2,1)S(1)} %pad_maximum_fusion.refs_0_), channel_id=1, source_target_pairs={{0,6},{1,7},{2,4},{3,5},{4,2},{5,3},{6,0},{7,1},{8,14},{9,15},{10,... | collective-permute-start | bytes 540680 | tf_op jit(solution)/shard_map/ppermute | solution.py:179
  76.4 12.4 %collective-permute-start.17 = (bf16[704,128]{1,0:T(8,128)(2,1)S(1)}, bf16[704,128]{1,0:T(8,128)(2,1)S(1)}, u32[]{:S(2)}, u32[]{:S(2)}) collective-permute-start(bf16[704,128]{1,0:T(8,128)(2,1)S(1)} %pad_maximum_fusion.refs_0_), channel_id=1, source_target_pairs={{0,4},{1,5},{2,6},{3,7},{4,0},{5,1},{6,2},{7,3},{8,12},{9,13},{10,... | collective-permute-start | bytes 540680 | tf_op jit(solution)/shard_map/ppermute | solution.py:179
  76.4 12.3 %collective-permute-start.16 = (bf16[704,128]{1,0:T(8,128)(2,1)S(1)}, bf16[704,128]{1,0:T(8,128)(2,1)S(1)}, u32[]{:S(2)}, u32[]{:S(2)}) collective-permute-start(bf16[704,128]{1,0:T(8,128)(2,1)S(1)} %pad_maximum_fusion.refs_0_), channel_id=1, source_target_pairs={{0,2},{1,3},{2,0},{3,1},{4,6},{5,7},{6,4},{7,5},{8,10},{9,11},{10,... | collective-permute-start | bytes 540680 | tf_op jit(solution)/shard_map/ppermute | solution.py:179
  79.8 11.8 %collective-permute-start.19 = (bf16[704,128]{1,0:T(8,128)(2,1)S(1)}, bf16[704,128]{1,0:T(8,128)(2,1)S(1)}, u32[]{:S(2)}, u32[]{:S(2)}) collective-permute-start(bf16[704,128]{1,0:T(8,128)(2,1)S(1)} %pad_maximum_fusion.refs_0_), channel_id=1, source_target_pairs={{0,1},{1,0},{2,3},{3,2},{4,5},{5,4},{6,7},{7,6},{8,9},{9,8},{10,11... | collective-permute-start | bytes 540680 | tf_op jit(solution)/shard_map/ppermute | solution.py:179
  86.8 4.8 %collective-permute-start.22 = (bf16[704,128]{1,0:T(8,128)(2,1)S(1)}, bf16[704,128]{1,0:T(8,128)(2,1)S(1)}, u32[]{:S(2)}, u32[]{:S(2)}) collective-permute-start(bf16[704,128]{1,0:T(8,128)(2,1)S(1)} %collective-permute-done.18.refs_3_), channel_id=1, source_target_pairs={{0,1},{1,0},{2,3},{3,2},{4,5},{5,4},{6,7},{7,6},{8,9},{9,8},{10,11... | collective-permute-start | bytes 540680 | tf_op jit(solution)/shard_map/ppermute | solution.py:179
  88.7 2.9 %collective-permute-start.21 = (bf16[704,128]{1,0:T(8,128)(2,1)S(1)}, bf16[704,128]{1,0:T(8,128)(2,1)S(1)}, u32[]{:S(2)}, u32[]{:S(2)}) collective-permute-start(bf16[704,128]{1,0:T(8,128)(2,1)S(1)} %collective-permute-done.17.refs_2_), channel_id=1, source_target_pairs={{0,1},{1,0},{2,3},{3,2},{4,5},{5,4},{6,7},{7,6},{8,9},{9,8},{10,11... | collective-permute-start | bytes 540680 | tf_op jit(solution)/shard_map/ppermute | solution.py:179
  88.7 2.9 %collective-permute-start.20 = (bf16[704,128]{1,0:T(8,128)(2,1)S(1)}, bf16[704,128]{1,0:T(8,128)(2,1)S(1)}, u32[]{:S(2)}, u32[]{:S(2)}) collective-permute-start(bf16[704,128]{1,0:T(8,128)(2,1)S(1)} %collective-permute-done.16.refs_1_), channel_id=1, source_target_pairs={{0,1},{1,0},{2,3},{3,2},{4,5},{5,4},{6,7},{7,6},{8,9},{9,8},{10,11... | collective-permute-start | bytes 540680 | tf_op jit(solution)/shard_map/ppermute | solution.py:179

commit v2 on v1

--- a/solution.py
+++ b/solution.py
@@ -195,15 +195,40 @@
     return jnp.stack([north, south])
 
 
+def paired(spread, width):
+    steps, rest = divmod(spread, width)
+    return rest == 0 and lax.axis_size("lon") % (2 * steps) == 0
+
+
+def side_of(spread, width):
+    if not paired(spread, width):
+        return 0
+    return lax.rem(lax.axis_index("lon") // (spread // width), 2)
+
+
+def inner_pairs(steps):
+    return [(i, i + steps if i // steps % 2 == 0 else i - steps) for i in range(lax.axis_size("lon"))]
+
+
+def outer_pairs(steps):
+    count = lax.axis_size("lon")
+    return [(i, (i - steps if i // steps % 2 == 0 else i + steps) % count) for i in range(count)]
+
+
 def beside(field, packed, spread, pack):
     width = field.shape[1]
     steps, rest = divmod(spread, width)
+    if paired(spread, width):
+        return (
+            lax.ppermute(packed, "lon", inner_pairs(steps)),
+            lax.ppermute(packed, "lon", outer_pairs(steps)),
+        )
     if rest == 0:
-        return moved(packed, steps), moved(packed, -steps)
+        return moved(packed, -steps), moved(packed, steps)
     cut = width - rest
     west = jnp.concatenate([moved(field[:, cut:], steps + 1), moved(field[:, :cut], steps)], axis=1)
     east = jnp.concatenate([moved(field[:, rest:], -steps), moved(field[:, :rest], -steps - 1)], axis=1)
-    return pack(west), pack(east)
+    return pack(east), pack(west)
 
 
 def shards(inputs, cotangent, first_weight, second_weight):
@@ -213,29 +238,29 @@
     scale = 1.0 / math.sqrt(rows * lax.axis_size("lat") * count)
     bf16, f32 = jnp.bfloat16, jnp.float32
     pshape = packed_shape(rows, channels)
-    ext_shape = (rows + 2 * width, channels)
-    ext = pltpu.VMEM(ext_shape, bf16)
+    ext_rows = rows + 2 * width
+    ext = pltpu.VMEM((ext_rows, channels), bf16)
+    sides = pltpu.VMEM((3, ext_rows, channels), bf16)
     tap_flops = 2 * rows * channels * channels
     blocks = row_blocks(rows)
 
-    def pack_body(*refs):
-        half = len(refs) // 2
-        for source, target in zip(refs[:half], refs[half:]):
-            pack_into(target, source[...])
-
-    def pack(*fields):
-        flat = [f.reshape(rows, channels) for f in fields]
-        return call(pack_body, [shape_of(pshape, bf16)] * len(flat), flat, name="pack")
+    def pack_body(source, target):
+        pack_into(target, source[...])
 
     def pack_one(field):
-        return pack(field)[0]
+        return call(pack_body, [shape_of(pshape, bf16)], [field.reshape(rows, channels)], name="pack")[0]
 
     def rims_of(field, spread):
         rim = lat_rim(field)
         if rim is None:
             return []
-        west, east = beside(rim, rim, spread, lambda r: r)
-        return [r.reshape(2 * width, channels) for r in (rim, west, east)]
+        inner, outer = beside(rim, rim, spread, lambda r: r)
+        return [r.reshape(2 * width, channels) for r in (rim, inner, outer)]
+
+    def place_sides(scratch, inner_ref, outer_ref, rims, spread):
+        side = side_of(spread, width)
+        extend(scratch.at[2 - 2 * side], unpacked(inner_ref, rows, channels), rims[0], width)
+        extend(scratch.at[2 * side], unpacked(outer_ref, rows, channels), rims[1], width)
 
     x = inputs.reshape(rows, channels)
     g = cotangent.reshape(rows, channels)
@@ -243,9 +268,8 @@
     g_rims = rims_of(cotangent, SECOND_SPREAD)
     rimmed = bool(x_rims)
 
-    x_packed, g_packed = pack(inputs, cotangent)
-    x_west, x_east = beside(inputs, x_packed, FIRST_SPREAD, pack_one)
-    g_west, g_east = beside(cotangent, g_packed, SECOND_SPREAD, pack_one)
+    x_inner, x_outer = beside(inputs, pack_one(inputs), FIRST_SPREAD, pack_one)
+    g_inner, g_outer = beside(cotangent, pack_one(cotangent), SECOND_SPREAD, pack_one)
 
     def own_body(x_ref, g_ref, w1_ref, w2_ref, *rest):
         rims, (part1, part2, xe, ge) = (rest[:2], rest[2:]) if rimmed else ((None, None), rest)
@@ -265,13 +289,12 @@
         name="own_columns",
     )
 
-    def hidden_body(part_ref, west_ref, east_ref, w_ref, *rest):
-        rims, (hidden_t, slope, we, ee, hid) = (rest[:2], rest[2:]) if rimmed else ((None, None), rest)
-        extend(we, unpacked(west_ref, rows, channels), rims[0], width)
-        extend(ee, unpacked(east_ref, rows, channels), rims[1], width)
+    def hidden_body(part_ref, inner_ref, outer_ref, w_ref, *rest):
+        rims, (hidden_t, slope, se, hid) = (rest[:2], rest[2:]) if rimmed else ((None, None), rest)
+        place_sides(se, inner_ref, outer_ref, rims, FIRST_SPREAD)
         for start, size in blocks:
             act = part_ref[start : start + size, :] + conv_block(
-                [(we, w_ref, -1, False), (ee, w_ref, 1, False)], start, size, width
+                [(se.at[0], w_ref, -1, False), (se.at[2], w_ref, 1, False)], start, size, width
             )
             sigma = jax.nn.sigmoid(act)
             slope[start : start + size, :] = sigma * (1.0 + act * (1.0 - sigma))
@@ -281,99 +304,141 @@
     hidden_t, slope = call(
         hidden_body,
         [shape_of((channels, rows), bf16), shape_of((rows, channels), f32)],
-        [part1, x_west, x_east, first_weight] + x_rims[1:],
-        [ext, ext, pltpu.VMEM((rows, channels), f32)],
+        [part1, x_inner, x_outer, first_weight] + x_rims[1:],
+        [sides, pltpu.VMEM((rows, channels), f32)],
         flops=6 * tap_flops,
         name="hidden",
     )
 
-    def grad_body(part_ref, slope_ref, west_ref, east_ref, w_ref, *rest):
-        rims, (pre_grad, packed, we, ee) = (rest[:2], rest[2:]) if rimmed else ((None, None), rest)
-        extend(we, unpacked(west_ref, rows, channels), rims[0], width)
-        extend(ee, unpacked(east_ref, rows, channels), rims[1], width)
+    def grad_body(part_ref, slope_ref, inner_ref, outer_ref, w_ref, *rest):
+        rims, (pre_grad, packed, pre_t, se, pre) = (rest[:2], rest[2:]) if rimmed else ((None, None), rest)
+        place_sides(se, inner_ref, outer_ref, rims, SECOND_SPREAD)
         for start, size in blocks:
             grad = part_ref[start : start + size, :] + conv_block(
-                [(we, w_ref, -1, True), (ee, w_ref, 1, True)], start, size, width
+                [(se.at[0], w_ref, -1, True), (se.at[2], w_ref, 1, True)], start, size, width
             )
-            pre_grad[start : start + size, :] = (grad * slope_ref[start : start + size, :]).astype(bf16)
+            value = (grad * slope_ref[start : start + size, :]).astype(bf16)
+            pre_grad[start : start + size, :] = value
+            pre[start : start + size, :] = value.astype(f32)
         pack_into(packed, pre_grad[...])
-
-    pre_grad, pre_packed = call(
+        pre_t[...] = pre[...].T.astype(bf16)
+
+    pre_grad, pre_packed, pre_t = call(
         grad_body,
-        [shape_of((rows, channels), bf16), shape_of(pshape, bf16)],
-        [part2, slope, g_west, g_east, second_weight] + g_rims[1:],
-        [ext, ext],
+        [shape_of((rows, channels), bf16), shape_of(pshape, bf16), shape_of((channels, rows), bf16)],
+        [part2, slope, g_inner, g_outer, second_weight] + g_rims[1:],
+        [sides, pltpu.VMEM((rows, channels), f32)],
         flops=6 * tap_flops,
         name="pre_grad",
     )
-    pre_field = pre_grad.reshape(height, width, channels)
-    p_west, p_east = beside(pre_field, pre_packed, FIRST_SPREAD, pack_one)
-    p_rims = rims_of(pre_field, FIRST_SPREAD)
 
     stages = radices(count)
-    pieces = count // 2 if stages else 1
+    pieces = count // 2
     flat = flat_rows(channels, pieces)
-
-    def kernels_body(hidden_t, pre_ref, x_ref, xw_ref, xe_ref, g_ref, gw_ref, ge_ref, *rest):
-        rims, rest = (rest[:6], rest[6:]) if rimmed else ((None,) * 6, rest)
-        own, send, both, e0, e1, e2, f0, f1, f2 = rest
-        extend(e0, unpacked(gw_ref, rows, channels), rims[4], width)
-        extend(e1, g_ref[...], rims[3], width)
-        extend(e2, unpacked(ge_ref, rows, channels), rims[5], width)
-        extend(f0, unpacked(xw_ref, rows, channels), rims[1], width)
-        extend(f1, x_ref[...], rims[0], width)
-        extend(f2, unpacked(xe_ref, rows, channels), rims[2], width)
-
-        def window(field, a):
-            return field[(1 + a) * width : (1 + a) * width + rows, :]
-
-        second = []
-        for a in (-1, 0, 1):
-            for b in (-1, 0, 1):
-                tap = window((e0, e1, e2)[1 - b], -a)
-                second.append(jnp.dot(hidden_t[...], tap, preferred_element_type=f32))
-        used = flat_rows(channels, 1) // ROW_TILE * ROW_TILE
-        if used < flat:
-            both[:, used - ROW_TILE :, :] = jnp.zeros((2, flat - used + ROW_TILE, LANES), f32)
-        store_flat(both, 0, second)
-        pre_t = pre_ref[...].astype(f32).T.astype(bf16)
-        first = []
-        for a in (-1, 0, 1):
-            for b in (-1, 0, 1):
-                first.append(jnp.dot(pre_t, window((f0, f1, f2)[1 + b], a), preferred_element_type=f32))
-        store_flat(both, 1, first)
-        mine = lax.rem(lax.axis_index("lon"), 2)
-        own[...] = both[mine]
-        send[...] = both[1 - mine].astype(bf16)
-
-    own, send = call(
-        kernels_body,
-        [shape_of((flat, LANES), f32), shape_of((flat, LANES), bf16)],
-        [hidden_t, pre_grad, x, x_west, x_east, g, g_west, g_east] + x_rims + g_rims,
-        [pltpu.VMEM((2, flat, LANES), f32)] + [ext] * 6,
-        flops=18 * tap_flops,
-        name="kernel_gradients",
-    )
-
+    used = flat_rows(channels, 1)
     index = lax.axis_index("lon")
-    total = own + swapped(send, count, 1, 1).astype(f32)
+
+    def kernel_gradient(which):
+        def body(hid_ref, pre_ref, x_ref, xi_ref, xo_ref, g_ref, gi_ref, go_ref, *rest):
+            rims, (out, flat_ref, se) = (rest[:6], rest[6:]) if rimmed else ((None,) * 6, rest)
+
+            def window(b, a):
+                return se[1 + b, (1 + a) * width : (1 + a) * width + rows, :]
+
+            if used < flat:
+                flat_ref[0, used - ROW_TILE :, :] = jnp.zeros((flat - used + ROW_TILE, LANES), f32)
+            chosen = which(lax.rem(lax.axis_index("lon"), 2))
+
+            @pl.when(chosen == 0)
+            def _():
+                place_sides(se, gi_ref, go_ref, rims[4:6], SECOND_SPREAD)
+                extend(se.at[1], g_ref[...], rims[3], width)
+                store_flat(
+                    flat_ref,
+                    0,
+                    [
+                        jnp.dot(hid_ref[...], window(-b, -a), preferred_element_type=f32)
+                        for a in (-1, 0, 1)
+                        for b in (-1, 0, 1)
+                    ],
+                )
+
+            @pl.when(chosen == 1)
+            def _():
+                place_sides(se, xi_ref, xo_ref, rims[1:3], FIRST_SPREAD)
+                extend(se.at[1], x_ref[...], rims[0], width)
+                store_flat(
+                    flat_ref,
+                    0,
+                    [
+                        jnp.dot(pre_ref[...], window(b, a), preferred_element_type=f32)
+                        for a in (-1, 0, 1)
+                        for b in (-1, 0, 1)
+                    ],
+                )
+
+            out[...] = flat_ref[0].astype(out.dtype)
+
+        return body
+
+    fields = [hidden_t, pre_t, x, x_inner, x_outer, g, g_inner, g_outer] + x_rims + g_rims
+    flat_scratch = pltpu.VMEM((1, flat, LANES), f32)
+    (send,) = call(
+        kernel_gradient(lambda core: 1 - core),
+        [shape_of((flat, LANES), bf16)],
+        fields,
+        [flat_scratch, sides],
+        flops=9 * tap_flops,
+        name="sibling_kernel_gradient",
+    )
+    received = [swapped(send, count, 1, 1)]
+    (own,) = call(
+        kernel_gradient(lambda core: core),
+        [shape_of((flat, LANES), f32)],
+        fields,
+        [flat_scratch, sides],
+        flops=9 * tap_flops,
+        name="own_kernel_gradient",
+    )
+
+    def digit_of(stride, radix):
+        return lax.rem(lax.axis_index("lon") // stride, radix)
+
+    def combine(own, received, stride, radix):
+        m = own.shape[0] // radix
+
+        def body(own_ref, *refs):
+            got, (mine, *sends) = refs[: len(received)], refs[len(received) :]
+            digit = digit_of(stride, radix)
+            for k, target in enumerate([mine] + sends):
+                at = pl.ds(pl.multiple_of((digit ^ k) * m, m), m)
+                value = own_ref[at, :]
+                for ref in got:
+                    value = value + ref[at, :].astype(f32)
+                target[...] = value.astype(target.dtype)
+
+        outs = [shape_of((m, LANES), f32)] + [shape_of((m, LANES), bf16)] * (radix - 1)
+        return call(body, outs, [own] + received, name="combine")
+
     stride = 2
     for radix in stages[1:]:
-        digit = index // stride % radix
-        split = total.reshape(radix, -1, LANES)
-        parts = [
-            swapped(
-                lax.dynamic_index_in_dim(split, digit ^ k, 0, keepdims=False).astype(bf16), count, stride, k
-            )
-            for k in range(1, radix)
-        ]
-        total = lax.dynamic_index_in_dim(split, digit, 0, keepdims=False)
-        for part in parts:
-            total = total + part.astype(f32)
+        own, *sends = combine(own, received, stride, radix)
+        received = [swapped(part, count, stride, k + 1) for k, part in enumerate(sends)]
         stride *= radix
     if lax.axis_size("lat") > 1:
-        total = lax.psum(total, "lat")
-    held = total.astype(bf16)
+        for part in received:
+            own = own + part.astype(f32)
+        held = lax.psum(own, "lat").astype(bf16)
+    else:
+
+        def last_body(own_ref, *refs):
+            value = own_ref[...]
+            for ref in refs[:-1]:
+                value = value + ref[...].astype(f32)
+            refs[-1][...] = value.astype(bf16)
+
+        (held,) = call(last_body, [shape_of(own.shape, bf16)], [own] + received, name="combine_last")
+
     for radix in reversed(stages[2:]):
         stride //= radix
         held = jnp.concatenate([held] + [swapped(held, count, stride, k) for k in range(1, radix)], axis=0)
@@ -381,41 +446,27 @@
     quarter = [held] + [swapped(held, count, 2, k) for k in range(1, group)]
     sibling = [swapped(q, count, 1, 1) for q in quarter]
 
-    def own_grad_body(p_ref, w_ref, *rest):
-        rim, (part, pe) = (rest[0], rest[1:]) if rimmed else (None, rest)
-        extend(pe, p_ref[...], rim, width)
+    pre_field = pre_grad.reshape(height, width, channels)
+    p_rims = rims_of(pre_field, FIRST_SPREAD)
+    p_inner, p_outer = beside(pre_field, pre_packed, FIRST_SPREAD, pack_one)
+
+    def input_body(p_ref, inner_ref, outer_ref, w_ref, *rest):
+        rims, (out, se) = (rest[:3], rest[3:]) if rimmed else ((None,) * 3, rest)
+        place_sides(se, inner_ref, outer_ref, rims[1:], FIRST_SPREAD)
+        extend(se.at[1], p_ref[...], rims[0], width)
         for start, size in blocks:
-            part[start : start + size, :] = conv_block([(pe, w_ref, 0, True)], start, size, width)
-
-    (part3,) = call(
-        own_grad_body,
-        [shape_of((rows, channels), f32)],
-        [pre_grad, first_weight] + p_rims[:1],
-        [ext],
-        flops=3 * tap_flops,
-        name="own_input_gradient",
-    )
-
-    def input_body(part_ref, west_ref, east_ref, w_ref, *rest):
-        rims, (out, we, ee) = (rest[:2], rest[2:]) if rimmed else ((None, None), rest)
-        extend(we, unpacked(west_ref, rows, channels), rims[0], width)
-        extend(ee, unpacked(east_ref, rows, channels), rims[1], width)
-        for start, size in blocks:
-            grad = part_ref[start : start + size, :] + conv_block(
-                [(we, w_ref, -1, True), (ee, w_ref, 1, True)], start, size, width
-            )
+            grad = conv_block([(se.at[1 + b], w_ref, b, True) for b in (-1, 0, 1)], start, size, width)
             out[start : start + size, :] = grad.astype(bf16)
 
     (input_gradient,) = call(
         input_body,
         [shape_of((rows, channels), bf16)],
-        [part3, p_west, p_east, first_weight] + p_rims[1:],
-        [ext, ext],
-        flops=6 * tap_flops,
+        [pre_grad, p_inner, p_outer, first_weight] + p_rims,
+        [sides],
+        flops=9 * tap_flops,
         name="input_gradient",
     )
 
-    rest_radices = stages[2:]
     unit = flat // pieces
 
     def final_body(*refs):
@@ -425,13 +476,10 @@
         for side in range(2):
             lead = mine if side == 0 else 1 - mine
             for k in range(group):
-                begin = (lax.rem(place // 2, group) ^ k) * (pieces // group)
-                parts = [(begin, 0)]
                 stride, span = 2 * group, pieces // group
-                offset_parts = [(begin, 0, span)]
-                walk = [(begin, 0)]
-                for radix in rest_radices:
-                    digit = lax.rem(place // stride, radix)
+                walk = [((digit_of(2, group) ^ k) * span, 0)]
+                for radix in stages[2:]:
+                    digit = digit_of(stride, radix)
                     span //= radix
                     walk = [
                         (at + (digit ^ j) * span, order + j * span) for at, order in walk for j in range(radix)

time: 94.8 us -> 85 us (0.90)
  waiting for transfers between devices: 44.5 us -> 37.8 us
  other arithmetic: 2.32 us -> 0.01 us
    ppermute x17, waiting for transfers between devices: 29.7 us -> 21.9 us  [swapped(): lax.ppermute(value, 'lon', [(i, i ^ k * stride) for i in range(count)])]
    ppermute x17, starting transfers between devices: 20.5 us -> 17.4 us  [swapped(): lax.ppermute(value, 'lon', [(i, i ^ k * stride) for i in range(count)])]
    add x2 -> x0, other arithmetic: 2.28 us -> none  [the longest x1 1.23 us: shards(): total = own + swapped(send, count, 1, 1).astype(f32)]
    ppermute x6, starting transfers between devices: 9.64 us -> 11.9 us  [the longest x3 11.9 us: beside(): lax.ppermute(packed, 'lon', outer_pairs(steps))]
    ppermute x6, waiting for transfers between devices: 14.7 us -> 15.9 us  [the longest x3 9.84 us: beside(): lax.ppermute(packed, 'lon', outer_pairs(steps))]
    pallas_call x8 -> x12, Pallas kernels: 12.2 us -> 12.4 us  [call(): pl.pallas_call(body, out_shape=list(outs), in_specs=[pl.BlockSpec(memory_...]
  transfers between devices with their start and end apart: 23 -> 23, of which waited for: 13 -> 12; matrix products, arithmetic and copies ran while one was open for 0% -> 0% of each run, Pallas kernels for 5% -> 8%
where the time goes in v2:
time: 85 us; the launch traced here: 84.7 us
  waiting for transfers between devices  37.8 us (44%)
  starting transfers between devices  29.3 us (34%)
  Pallas kernels  12.4 us (15%)
  local copies, waits for them, and re-layouts  4.43 us (5%)
    ppermute x17, waiting for transfers between devices, swapped(): lax.ppermute(value, 'lon', [(i, i ^ k * stride) for i in range(count)])  21.9 us
    ppermute x17, starting transfers between devices, swapped(): lax.ppermute(value, 'lon', [(i, i ^ k * stride) for i in range(count)])  17.4 us
    pallas_call x12, Pallas kernels, call(): pl.pallas_call(body, out_shape=list(outs), in_specs=[pl.BlockSpec(memory_...  12.4 us
    ppermute x3, starting transfers between devices, beside(): lax.ppermute(packed, 'lon', outer_pairs(steps))  11.9 us
    ppermute x3, waiting for transfers between devices, beside(): lax.ppermute(packed, 'lon', outer_pairs(steps))  9.84 us
    ppermute x3, waiting for transfers between devices, beside(): lax.ppermute(packed, 'lon', inner_pairs(steps))  6.04 us
    unnamed x16, local copies, waits for them, and re-layouts  4.43 us
  transfers between devices with their start and end apart: 23, of which 12 were waited for; matrix products, arithmetic and copies ran while one was open for 0% of the time, Pallas kernels for 8%

profile of v2, /device:TPU:0, one launch (start us, length us, event | category | flops | bytes accessed | tf_op | source)
XLA Modules:
  0.0 84.7 jit_solution(16273006524465663982)
XLA Ops:
  0.6 1.0 %copy-done = bf16[32,32,192]{2,1,0:T(8,128)(2,1)S(1)} copy-done((bf16[32,32,192]{2,1,0:T(8,128)(2,1)S(1)}, bf16[32,32,192]{2,1,0:T(8,128)(2,1)}, u32[]{:S(2)}) %copy-start) | copy-done | bytes 393240
  1.8 6.4 %collective-permute-start.1 = (bf16[1536,128]{1,0:T(8,128)(2,1)S(1)}, bf16[1536,128]{1,0:T(8,128)(2,1)S(1)}, u32[]{:S(2)}, u32[]{:S(2)}) collective-permute-start(bf16[1536,128]{1,0:T(8,128)(2,1)S(1)} %pack.2), channel_id=1, source_target_pairs={{0,31},{1,2},{2,1},{3,4},{4,3},{5,6},{6,5},{7,8},{8,7},{9,10},{10,... | collective-permute-start | bytes 1179656 | tf_op jit(solution)/shard_map/ppermute | solution.py:224
  8.2 1.0 %copy-done.2 = bf16[32,32,192]{2,1,0:T(8,128)(2,1)S(1)} copy-done((bf16[32,32,192]{2,1,0:T(8,128)(2,1)S(1)}, bf16[32,32,192]{2,1,0:T(8,128)(2,1)}, u32[]{:S(2)}) %copy-start.2) | copy-done | bytes 393240
  9.4 0.7 collective-permute-start.3
  10.1 1.2 %copy-done.4 = bf16[3,3,192,192]{3,2,1,0:T(8,128)(2,1)S(1)} copy-done((bf16[3,3,192,192]{3,2,1,0:T(8,128)(2,1)S(1)}, bf16[3,3,192,192]{3,2,1,0:T(8,128)(2,1)}, u32[]{:S(2)}) %copy-start.4) | copy-done | bytes 663576
  11.3 1.2 %copy-done.6 = bf16[3,3,192,192]{3,2,1,0:T(8,128)(2,1)S(1)} copy-done((bf16[3,3,192,192]{3,2,1,0:T(8,128)(2,1)S(1)}, bf16[3,3,192,192]{3,2,1,0:T(8,128)(2,1)}, u32[]{:S(2)}) %copy-start.6) | copy-done | bytes 663576
  12.5 1.0 %own_columns.1 = (f32[1024,192]{1,0:T(8,128)S(1)}, f32[1024,192]{1,0:T(8,128)S(1)}) custom-call(bf16[1024,192]{1,0:T(8,128)(2,1)S(1)} %bitcast.4, bf16[1024,192]{1,0:T(8,128)(2,1)S(1)} %bitcast.8, bf16[3,3,192,192]{3,2,1,0:T(8,128)(2,1)S(1)} %copy-done.4, bf16[3,3,192,192]{3,2,1,0:T(8,128)(2,1)S(1)} %copy-done.6), custom_call_target="tpu_custom_call" | custom-call | flops 452984832 | bytes 3686400 | tf_op jit(solution)/shard_map/own_columns/pallas_call | solution.py:19
  13.4 2.8 %collective-permute-done.1.outer_ref.xo_ref = bf16[1536,128]{1,0:T(8,128)(2,1)S(1)} collective-permute-done((bf16[1536,128]{1,0:T(8,128)(2,1)S(1)}, bf16[1536,128]{1,0:T(8,128)(2,1)S(1)}, u32[]{:S(2)}, u32[]{:S(2)}) %collective-permute-start.1) | collective-permute-done | bytes 393248 | tf_op jit(solution)/shard_map/ppermute | solution.py:224
  16.3 1.4 %hidden.1 = (bf16[192,1024]{1,0:T(8,128)(2,1)S(1)}, f32[1024,192]{1,0:T(8,128)S(1)}) custom-call(f32[1024,192]{1,0:T(8,128)S(1)} %get-tuple-element.21.part_ref, bf16[1536,128]{1,0:T(8,128)(2,1)S(1)} %collective-permute-done.inner_ref.xi_ref, bf16[1536,128]{1,0:T(8,128)(2,1)S(1)} %collective-permute-done.1.outer_ref.xo_ref, ...), custom_call_target="tpu_custom_call" | custom-call | flops 452984832 | bytes 3416064 | tf_op jit(solution)/shard_map/hidden/pallas_call | solution.py:19
  17.7 7.0 %collective-permute-done.3.outer_ref.go_ref = bf16[1536,128]{1,0:T(8,128)(2,1)S(1)} collective-permute-done((bf16[1536,128]{1,0:T(8,128)(2,1)S(1)}, bf16[1536,128]{1,0:T(8,128)(2,1)S(1)}, u32[]{:S(2)}, u32[]{:S(2)}) %collective-permute-start.3) | collective-permute-done | bytes 393248 | tf_op jit(solution)/shard_map/ppermute | solution.py:224
  24.7 6.0 %collective-permute-done.2.inner_ref.gi_ref = bf16[1536,128]{1,0:T(8,128)(2,1)S(1)} collective-permute-done((bf16[1536,128]{1,0:T(8,128)(2,1)S(1)}, bf16[1536,128]{1,0:T(8,128)(2,1)S(1)}, u32[]{:S(2)}, u32[]{:S(2)}) %collective-permute-start.2) | collective-permute-done | bytes 393248 | tf_op jit(solution)/shard_map/ppermute | solution.py:223
  30.7 1.3 %pre_grad.1 = (bf16[1024,192]{1,0:T(8,128)(2,1)S(1)}, bf16[1536,128]{1,0:T(8,128)(2,1)S(1)}, bf16[192,1024]{1,0:T(8,128)(2,1)S(1)}) custom-call(f32[1024,192]{1,0:T(8,128)S(1)} %get-tuple-element.20.part_ref, f32[1024,192]{1,0:T(8,128)S(1)} %get-tuple-element.22.slope_ref, bf16[1536,128]{1,0:T(8,128)(2,1)S(1)} %collective-permute-done.2.inner_ref.gi_ref, ...), custom_call_target="tpu_custom_call" | custom-call | flops 452984832 | bytes 4202496 | tf_op jit(solution)/shard_map/pre_grad/pallas_call | solution.py:19
  32.1 1.5 %sibling_kernel_gradient.1 = bf16[2816,128]{1,0:T(8,128)(2,1)S(1)} custom-call(bf16[192,1024]{1,0:T(8,128)(2,1)S(1)} %get-tuple-element.25.hid_ref, bf16[192,1024]{1,0:T(8,128)(2,1)S(1)} %get-tuple-element.26.pre_ref, bf16[1024,192]{1,0:T(8,128)(2,1)S(1)} %bitcast.5, bf16[1536,128]{1,0:T(8,128)(2,1)S(1)} %collective-permute-done.inner_ref.xi_ref, ...), custom_call_target="tpu_custom_call" | custom-call | flops 679477248 | bytes 3866624 | tf_op jit(solution)/shard_map/sibling_kernel_gradient/pallas_call | solution.py:19
  33.5 0.8 collective-permute-start.6
  34.3 1.7 %own_kernel_gradient.1.own_ref = f32[2816,128]{1,0:T(8,128)S(1)} custom-call(bf16[192,1024]{1,0:T(8,128)(2,1)S(1)} %get-tuple-element.25.hid_ref, bf16[192,1024]{1,0:T(8,128)(2,1)S(1)} %get-tuple-element.26.pre_ref, bf16[1024,192]{1,0:T(8,128)(2,1)S(1)} %bitcast.6, bf16[1536,128]{1,0:T(8,128)(2,1)S(1)} %collective-permute-done.inner_ref.xi_ref, ...), custom_call_target="tpu_custom_call" | custom-call | flops 679477248 | bytes 4587520 | tf_op jit(solution)/shard_map/own_kernel_gradient/pallas_call | solution.py:19
  36.2 1.5 %collective-permute-start.7 = (bf16[704,128]{1,0:T(8,128)(2,1)S(1)}, bf16[704,128]{1,0:T(8,128)(2,1)S(1)}, u32[]{:S(2)}, u32[]{:S(2)}) collective-permute-start(bf16[704,128]{1,0:T(8,128)(2,1)S(1)} %get-tuple-element.28), channel_id=1, source_target_pairs={{0,2},{1,3},{2,0},{3,1},{4,6},{5,7},{6,4},{7,5},{8,10},{9,11},{10,... | collective-permute-start | bytes 540680 | tf_op jit(solution)/shard_map/ppermute | solution.py:179
  37.8 2.0 %collective-permute-start.8 = (bf16[704,128]{1,0:T(8,128)(2,1)S(1)}, bf16[704,128]{1,0:T(8,128)(2,1)S(1)}, u32[]{:S(2)}, u32[]{:S(2)}) collective-permute-start(bf16[704,128]{1,0:T(8,128)(2,1)S(1)} %get-tuple-element.29), channel_id=1, source_target_pairs={{0,4},{1,5},{2,6},{3,7},{4,0},{5,1},{6,2},{7,3},{8,12},{9,13},{10,... | collective-permute-start | bytes 540680 | tf_op jit(solution)/shard_map/ppermute | solution.py:179
  39.9 4.8 %collective-permute-start.5 = (bf16[1536,128]{1,0:T(8,128)(2,1)S(1)}, bf16[1536,128]{1,0:T(8,128)(2,1)S(1)}, u32[]{:S(2)}, u32[]{:S(2)}) collective-permute-start(bf16[1536,128]{1,0:T(8,128)(2,1)S(1)} %get-tuple-element.24), channel_id=1, source_target_pairs={{0,31},{1,2},{2,1},{3,4},{4,3},{5,6},{6,5},{7,8},{8,7},{9,10},{10,... | collective-permute-start | bytes 1179656 | tf_op jit(solution)/shard_map/ppermute | solution.py:224
  44.6 4.7 %collective-permute-done.8.refs_1_ = bf16[704,128]{1,0:T(8,128)(2,1)S(1)} collective-permute-done((bf16[704,128]{1,0:T(8,128)(2,1)S(1)}, bf16[704,128]{1,0:T(8,128)(2,1)S(1)}, u32[]{:S(2)}, u32[]{:S(2)}) %collective-permute-start.8) | collective-permute-done | bytes 180256 | tf_op jit(solution)/shard_map/ppermute | solution.py:179
  49.3 3.2 %collective-permute-done.9.refs_2_ = bf16[704,128]{1,0:T(8,128)(2,1)S(1)} collective-permute-done((bf16[704,128]{1,0:T(8,128)(2,1)S(1)}, bf16[704,128]{1,0:T(8,128)(2,1)S(1)}, u32[]{:S(2)}, u32[]{:S(2)}) %collective-permute-start.9) | collective-permute-done | bytes 180256 | tf_op jit(solution)/shard_map/ppermute | solution.py:179
  52.6 1.6 %collective-permute-start.10 = (bf16[176,128]{1,0:T(8,128)(2,1)S(1)}, bf16[176,128]{1,0:T(8,128)(2,1)S(1)}, u32[]{:S(2)}, u32[]{:S(2)}) collective-permute-start(bf16[176,128]{1,0:T(8,128)(2,1)S(1)} %get-tuple-element.32), channel_id=1, source_target_pairs={{0,8},{1,9},{2,10},{3,11},{4,12},{5,13},{6,14},{7,15},{8,0},{9,1},... | collective-permute-start | bytes 135176 | tf_op jit(solution)/shard_map/ppermute | solution.py:179
  54.2 2.6 %collective-permute-start.11 = (bf16[176,128]{1,0:T(8,128)(2,1)S(1)}, bf16[176,128]{1,0:T(8,128)(2,1)S(1)}, u32[]{:S(2)}, u32[]{:S(2)}) collective-permute-start(bf16[176,128]{1,0:T(8,128)(2,1)S(1)} %get-tuple-element.33), channel_id=1, source_target_pairs={{0,16},{1,17},{2,18},{3,19},{4,20},{5,21},{6,22},{7,23},{8,24},{9,... | collective-permute-start | bytes 135176 | tf_op jit(solution)/shard_map/ppermute | solution.py:179
  57.1 2.6 %collective-permute-done.11.refs_1_ = bf16[176,128]{1,0:T(8,128)(2,1)S(1)} collective-permute-done((bf16[176,128]{1,0:T(8,128)(2,1)S(1)}, bf16[176,128]{1,0:T(8,128)(2,1)S(1)}, u32[]{:S(2)}, u32[]{:S(2)}) %collective-permute-start.11) | collective-permute-done | bytes 45088 | tf_op jit(solution)/shard_map/ppermute | solution.py:179
  59.7 3.0 %collective-permute-done.12.refs_2_ = bf16[176,128]{1,0:T(8,128)(2,1)S(1)} collective-permute-done((bf16[176,128]{1,0:T(8,128)(2,1)S(1)}, bf16[176,128]{1,0:T(8,128)(2,1)S(1)}, u32[]{:S(2)}, u32[]{:S(2)}) %collective-permute-start.12) | collective-permute-done | bytes 45088 | tf_op jit(solution)/shard_map/ppermute | solution.py:179
  63.3 3.9 %collective-permute-start.13 = (bf16[176,128]{1,0:T(8,128)(2,1)S(1)}, bf16[176,128]{1,0:T(8,128)(2,1)S(1)}, u32[]{:S(2)}, u32[]{:S(2)}) collective-permute-start(bf16[176,128]{1,0:T(8,128)(2,1)S(1)} %combine_last.1), channel_id=1, source_target_pairs={{0,8},{1,9},{2,10},{3,11},{4,12},{5,13},{6,14},{7,15},{8,0},{9,1},... | collective-permute-start | bytes 135176 | tf_op jit(solution)/shard_map/ppermute | solution.py:179
  67.2 1.5 %collective-permute-done.15 = bf16[176,128]{1,0:T(8,128)(2,1)S(1)} collective-permute-done((bf16[176,128]{1,0:T(8,128)(2,1)S(1)}, bf16[176,128]{1,0:T(8,128)(2,1)S(1)}, u32[]{:S(2)}, u32[]{:S(2)}) %collective-permute-start.15) | collective-permute-done | bytes 45088 | tf_op jit(solution)/shard_map/ppermute | solution.py:179
  69.2 1.9 %collective-permute-start.18 = (bf16[704,128]{1,0:T(8,128)(2,1)S(1)}, bf16[704,128]{1,0:T(8,128)(2,1)S(1)}, u32[]{:S(2)}, u32[]{:S(2)}) collective-permute-start(bf16[704,128]{1,0:T(8,128)(2,1)S(1)} %pad_maximum_fusion.refs_0_), channel_id=1, source_target_pairs={{0,6},{1,7},{2,4},{3,5},{4,2},{5,3},{6,0},{7,1},{8,14},{9,15},{10,... | collective-permute-start | bytes 540680 | tf_op jit(solution)/shard_map/ppermute | solution.py:179
  71.1 1.6 %collective-permute-start.16 = (bf16[704,128]{1,0:T(8,128)(2,1)S(1)}, bf16[704,128]{1,0:T(8,128)(2,1)S(1)}, u32[]{:S(2)}, u32[]{:S(2)}) collective-permute-start(bf16[704,128]{1,0:T(8,128)(2,1)S(1)} %pad_maximum_fusion.refs_0_), channel_id=1, source_target_pairs={{0,2},{1,3},{2,0},{3,1},{4,6},{5,7},{6,4},{7,5},{8,10},{9,11},{10,... | collective-permute-start | bytes 540680 | tf_op jit(solution)/shard_map/ppermute | solution.py:179
  72.8 4.4 %collective-permute-done.18.refs_3_ = bf16[704,128]{1,0:T(8,128)(2,1)S(1)} collective-permute-done((bf16[704,128]{1,0:T(8,128)(2,1)S(1)}, bf16[704,128]{1,0:T(8,128)(2,1)S(1)}, u32[]{:S(2)}, u32[]{:S(2)}) %collective-permute-start.18) | collective-permute-done | bytes 180256 | tf_op jit(solution)/shard_map/ppermute | solution.py:179
  77.2 1.8 %collective-permute-done.17.refs_2_ = bf16[704,128]{1,0:T(8,128)(2,1)S(1)} collective-permute-done((bf16[704,128]{1,0:T(8,128)(2,1)S(1)}, bf16[704,128]{1,0:T(8,128)(2,1)S(1)}, u32[]{:S(2)}, u32[]{:S(2)}) %collective-permute-start.17) | collective-permute-done | bytes 180256 | tf_op jit(solution)/shard_map/ppermute | solution.py:179
  79.5 2.3 %input_gradient.1 = bf16[1024,192]{1,0:T(8,128)(2,1)} custom-call(bf16[1024,192]{1,0:T(8,128)(2,1)S(1)} %get-tuple-element.23.p_ref, bf16[1536,128]{1,0:T(8,128)(2,1)S(1)} %collective-permute-done.4.inner_ref, bf16[1536,128]{1,0:T(8,128)(2,1)S(1)} %collective-permute-done.5.outer_ref, bf16[3,3,192,192]{3,2,1,0:T(8,128)(2,1)S(1)} %copy-done.5), custom_call_target="tpu_custom_call" | custom-call | flops 679477248 | bytes 2236416 | tf_op jit(solution)/shard_map/input_gradient/pallas_call | solution.py:19
  81.8 2.9 %unpack_gradients.1 = (f32[3,3,192,192]{3,2,1,0:T(8,128)}, f32[3,3,192,192]{3,2,1,0:T(8,128)}) custom-call(bf16[704,128]{1,0:T(8,128)(2,1)S(1)} %pad_maximum_fusion.refs_0_, bf16[704,128]{1,0:T(8,128)(2,1)S(1)} %collective-permute-done.16.refs_1_, bf16[704,128]{1,0:T(8,128)(2,1)S(1)} %collective-permute-done.17.refs_2_, ...), custom_call_target="tpu_custom_call" | custom-call | bytes 4096000 | tf_op jit(solution)/shard_map/unpack_gradients/pallas_call | solution.py:19
  (43 shorter events, 2.6 us)
Async XLA Ops:
  0.6 1.0 %copy-start = (bf16[32,32,192]{2,1,0:T(8,128)(2,1)S(1)}, bf16[32,32,192]{2,1,0:T(8,128)(2,1)}, u32[]{:S(2)}) copy-start(bf16[32,32,192]{2,1,0:T(8,128)(2,1)} %param.4) | copy-start | bytes 1179652
  1.7 8.4 %copy-start.1 = (bf16[32,32,192]{2,1,0:T(8,128)(2,1)S(1)}, bf16[32,32,192]{2,1,0:T(8,128)(2,1)}, u32[]{:S(2)}) copy-start(bf16[32,32,192]{2,1,0:T(8,128)(2,1)} %param.4) | copy-start | bytes 1179652
  1.8 14.5 %collective-permute-start.1 = (bf16[1536,128]{1,0:T(8,128)(2,1)S(1)}, bf16[1536,128]{1,0:T(8,128)(2,1)S(1)}, u32[]{:S(2)}, u32[]{:S(2)}) collective-permute-start(bf16[1536,128]{1,0:T(8,128)(2,1)S(1)} %pack.2), channel_id=1, source_target_pairs={{0,31},{1,2},{2,1},{3,4},{4,3},{5,6},{6,5},{7,8},{8,7},{9,10},{10,... | collective-permute-start | bytes 1179656 | tf_op jit(solution)/shard_map/ppermute | solution.py:224
  8.2 8.0 %collective-permute-start = (bf16[1536,128]{1,0:T(8,128)(2,1)S(1)}, bf16[1536,128]{1,0:T(8,128)(2,1)S(1)}, u32[]{:S(2)}, u32[]{:S(2)}) collective-permute-start(bf16[1536,128]{1,0:T(8,128)(2,1)S(1)} %pack.2), channel_id=1, source_target_pairs={{0,1},{1,0},{2,3},{3,2},{4,5},{5,4},{6,7},{7,6},{8,9},{9,8},{10,11... | collective-permute-start | bytes 1179656 | tf_op jit(solution)/shard_map/ppermute | solution.py:223
  8.2 1.0 %copy-start.2 = (bf16[32,32,192]{2,1,0:T(8,128)(2,1)S(1)}, bf16[32,32,192]{2,1,0:T(8,128)(2,1)}, u32[]{:S(2)}) copy-start(bf16[32,32,192]{2,1,0:T(8,128)(2,1)} %param.5) | copy-start | bytes 1179652
  9.3 7.0 %copy-start.5 = (bf16[3,3,192,192]{3,2,1,0:T(8,128)(2,1)S(1)}, bf16[3,3,192,192]{3,2,1,0:T(8,128)(2,1)}, u32[]{:S(2)}) copy-start(bf16[3,3,192,192]{3,2,1,0:T(8,128)(2,1)} %w_ref.5) | copy-start | bytes 1990660
  9.4 15.3 %collective-permute-start.3 = (bf16[1536,128]{1,0:T(8,128)(2,1)S(1)}, bf16[1536,128]{1,0:T(8,128)(2,1)S(1)}, u32[]{:S(2)}, u32[]{:S(2)}) collective-permute-start(bf16[1536,128]{1,0:T(8,128)(2,1)S(1)} %pack.3), channel_id=1, source_target_pairs={{0,30},{1,31},{2,4},{3,5},{4,2},{5,3},{6,8},{7,9},{8,6},{9,7},{10,... | collective-permute-start | bytes 1179656 | tf_op jit(solution)/shard_map/ppermute | solution.py:224
  10.1 20.6 %collective-permute-start.2 = (bf16[1536,128]{1,0:T(8,128)(2,1)S(1)}, bf16[1536,128]{1,0:T(8,128)(2,1)S(1)}, u32[]{:S(2)}, u32[]{:S(2)}) collective-permute-start(bf16[1536,128]{1,0:T(8,128)(2,1)S(1)} %pack.3), channel_id=1, source_target_pairs={{0,2},{1,3},{2,0},{3,1},{4,6},{5,7},{6,4},{7,5},{8,10},{9,11},{10,... | collective-permute-start | bytes 1179656 | tf_op jit(solution)/shard_map/ppermute | solution.py:223
  10.1 1.2 %copy-start.4 = (bf16[3,3,192,192]{3,2,1,0:T(8,128)(2,1)S(1)}, bf16[3,3,192,192]{3,2,1,0:T(8,128)(2,1)}, u32[]{:S(2)}) copy-start(bf16[3,3,192,192]{3,2,1,0:T(8,128)(2,1)} %w_ref.5) | copy-start | bytes 1990660
  11.3 1.2 %copy-start.6 = (bf16[3,3,192,192]{3,2,1,0:T(8,128)(2,1)S(1)}, bf16[3,3,192,192]{3,2,1,0:T(8,128)(2,1)}, u32[]{:S(2)}) copy-start(bf16[3,3,192,192]{3,2,1,0:T(8,128)(2,1)} %w_ref.4) | copy-start | bytes 1990660
  13.4 17.3 %copy-start.7 = (bf16[3,3,192,192]{3,2,1,0:T(8,128)(2,1)S(1)}, bf16[3,3,192,192]{3,2,1,0:T(8,128)(2,1)}, u32[]{:S(2)}) copy-start(bf16[3,3,192,192]{3,2,1,0:T(8,128)(2,1)} %w_ref.4) | copy-start | bytes 1990660
  30.7 1.3 %copy-start.3 = (bf16[32,32,192]{2,1,0:T(8,128)(2,1)S(1)}, bf16[32,32,192]{2,1,0:T(8,128)(2,1)}, u32[]{:S(2)}) copy-start(bf16[32,32,192]{2,1,0:T(8,128)(2,1)} %param.5) | copy-start | bytes 1179652
  33.5 2.6 %collective-permute-start.6 = (bf16[2816,128]{1,0:T(8,128)(2,1)S(1)}, bf16[2816,128]{1,0:T(8,128)(2,1)S(1)}, u32[]{:S(2)}, u32[]{:S(2)}) collective-permute-start(bf16[2816,128]{1,0:T(8,128)(2,1)S(1)} %sibling_kernel_gradient.1), channel_id=1, source_target_pairs={{0,1},{1,0},{2,3},{3,2},{4,5},{5,4},{6,7},{7,6},{8,9},{9,8},{10,11... | collective-permute-start | bytes 2162696 | tf_op jit(solution)/shard_map/ppermute | solution.py:179
  36.2 8.4 %collective-permute-start.7 = (bf16[704,128]{1,0:T(8,128)(2,1)S(1)}, bf16[704,128]{1,0:T(8,128)(2,1)S(1)}, u32[]{:S(2)}, u32[]{:S(2)}) collective-permute-start(bf16[704,128]{1,0:T(8,128)(2,1)S(1)} %get-tuple-element.28), channel_id=1, source_target_pairs={{0,2},{1,3},{2,0},{3,1},{4,6},{5,7},{6,4},{7,5},{8,10},{9,11},{10,... | collective-permute-start | bytes 540680 | tf_op jit(solution)/shard_map/ppermute | solution.py:179
  37.8 11.5 %collective-permute-start.8 = (bf16[704,128]{1,0:T(8,128)(2,1)S(1)}, bf16[704,128]{1,0:T(8,128)(2,1)S(1)}, u32[]{:S(2)}, u32[]{:S(2)}) collective-permute-start(bf16[704,128]{1,0:T(8,128)(2,1)S(1)} %get-tuple-element.29), channel_id=1, source_target_pairs={{0,4},{1,5},{2,6},{3,7},{4,0},{5,1},{6,2},{7,3},{8,12},{9,13},{10,... | collective-permute-start | bytes 540680 | tf_op jit(solution)/shard_map/ppermute | solution.py:179
  39.8 12.7 %collective-permute-start.9 = (bf16[704,128]{1,0:T(8,128)(2,1)S(1)}, bf16[704,128]{1,0:T(8,128)(2,1)S(1)}, u32[]{:S(2)}, u32[]{:S(2)}) collective-permute-start(bf16[704,128]{1,0:T(8,128)(2,1)S(1)} %get-tuple-element.30), channel_id=1, source_target_pairs={{0,6},{1,7},{2,4},{3,5},{4,2},{5,3},{6,0},{7,1},{8,14},{9,15},{10,... | collective-permute-start | bytes 540680 | tf_op jit(solution)/shard_map/ppermute | solution.py:179
  39.9 32.9 %collective-permute-start.5 = (bf16[1536,128]{1,0:T(8,128)(2,1)S(1)}, bf16[1536,128]{1,0:T(8,128)(2,1)S(1)}, u32[]{:S(2)}, u32[]{:S(2)}) collective-permute-start(bf16[1536,128]{1,0:T(8,128)(2,1)S(1)} %get-tuple-element.24), channel_id=1, source_target_pairs={{0,31},{1,2},{2,1},{3,4},{4,3},{5,6},{6,5},{7,8},{8,7},{9,10},{10,... | collective-permute-start | bytes 1179656 | tf_op jit(solution)/shard_map/ppermute | solution.py:224
  52.6 4.5 %collective-permute-start.10 = (bf16[176,128]{1,0:T(8,128)(2,1)S(1)}, bf16[176,128]{1,0:T(8,128)(2,1)S(1)}, u32[]{:S(2)}, u32[]{:S(2)}) collective-permute-start(bf16[176,128]{1,0:T(8,128)(2,1)S(1)} %get-tuple-element.32), channel_id=1, source_target_pairs={{0,8},{1,9},{2,10},{3,11},{4,12},{5,13},{6,14},{7,15},{8,0},{9,1},... | collective-permute-start | bytes 135176 | tf_op jit(solution)/shard_map/ppermute | solution.py:179
  54.2 5.4 %collective-permute-start.11 = (bf16[176,128]{1,0:T(8,128)(2,1)S(1)}, bf16[176,128]{1,0:T(8,128)(2,1)S(1)}, u32[]{:S(2)}, u32[]{:S(2)}) collective-permute-start(bf16[176,128]{1,0:T(8,128)(2,1)S(1)} %get-tuple-element.33), channel_id=1, source_target_pairs={{0,16},{1,17},{2,18},{3,19},{4,20},{5,21},{6,22},{7,23},{8,24},{9,... | collective-permute-start | bytes 135176 | tf_op jit(solution)/shard_map/ppermute | solution.py:179
  56.8 5.8 %collective-permute-start.12 = (bf16[176,128]{1,0:T(8,128)(2,1)S(1)}, bf16[176,128]{1,0:T(8,128)(2,1)S(1)}, u32[]{:S(2)}, u32[]{:S(2)}) collective-permute-start(bf16[176,128]{1,0:T(8,128)(2,1)S(1)} %get-tuple-element.34), channel_id=1, source_target_pairs={{0,24},{1,25},{2,26},{3,27},{4,28},{5,29},{6,30},{7,31},{8,16},{9,... | collective-permute-start | bytes 135176 | tf_op jit(solution)/shard_map/ppermute | solution.py:179
  62.7 6.0 %collective-permute-start.15 = (bf16[176,128]{1,0:T(8,128)(2,1)S(1)}, bf16[176,128]{1,0:T(8,128)(2,1)S(1)}, u32[]{:S(2)}, u32[]{:S(2)}) collective-permute-start(bf16[176,128]{1,0:T(8,128)(2,1)S(1)} %combine_last.1), channel_id=1, source_target_pairs={{0,24},{1,25},{2,26},{3,27},{4,28},{5,29},{6,30},{7,31},{8,16},{9,... | collective-permute-start | bytes 135176 | tf_op jit(solution)/shard_map/ppermute | solution.py:179
  63.3 5.4 %collective-permute-start.14 = (bf16[176,128]{1,0:T(8,128)(2,1)S(1)}, bf16[176,128]{1,0:T(8,128)(2,1)S(1)}, u32[]{:S(2)}, u32[]{:S(2)}) collective-permute-start(bf16[176,128]{1,0:T(8,128)(2,1)S(1)} %combine_last.1), channel_id=1, source_target_pairs={{0,16},{1,17},{2,18},{3,19},{4,20},{5,21},{6,22},{7,23},{8,24},{9,... | collective-permute-start | bytes 135176 | tf_op jit(solution)/shard_map/ppermute | solution.py:179
  63.3 5.9 %collective-permute-start.13 = (bf16[176,128]{1,0:T(8,128)(2,1)S(1)}, bf16[176,128]{1,0:T(8,128)(2,1)S(1)}, u32[]{:S(2)}, u32[]{:S(2)}) collective-permute-start(bf16[176,128]{1,0:T(8,128)(2,1)S(1)} %combine_last.1), channel_id=1, source_target_pairs={{0,8},{1,9},{2,10},{3,11},{4,12},{5,13},{6,14},{7,15},{8,0},{9,1},... | collective-permute-start | bytes 135176 | tf_op jit(solution)/shard_map/ppermute | solution.py:179
  67.2 12.3 %collective-permute-start.4 = (bf16[1536,128]{1,0:T(8,128)(2,1)S(1)}, bf16[1536,128]{1,0:T(8,128)(2,1)S(1)}, u32[]{:S(2)}, u32[]{:S(2)}) collective-permute-start(bf16[1536,128]{1,0:T(8,128)(2,1)S(1)} %get-tuple-element.24), channel_id=1, source_target_pairs={{0,1},{1,0},{2,3},{3,2},{4,5},{5,4},{6,7},{7,6},{8,9},{9,8},{10,11... | collective-permute-start | bytes 1179656 | tf_op jit(solution)/shard_map/ppermute | solution.py:223
  69.2 8.0 %collective-permute-start.18 = (bf16[704,128]{1,0:T(8,128)(2,1)S(1)}, bf16[704,128]{1,0:T(8,128)(2,1)S(1)}, u32[]{:S(2)}, u32[]{:S(2)}) collective-permute-start(bf16[704,128]{1,0:T(8,128)(2,1)S(1)} %pad_maximum_fusion.refs_0_), channel_id=1, source_target_pairs={{0,6},{1,7},{2,4},{3,5},{4,2},{5,3},{6,0},{7,1},{8,14},{9,15},{10,... | collective-permute-start | bytes 540680 | tf_op jit(solution)/shard_map/ppermute | solution.py:179
  71.1 7.9 %collective-permute-start.17 = (bf16[704,128]{1,0:T(8,128)(2,1)S(1)}, bf16[704,128]{1,0:T(8,128)(2,1)S(1)}, u32[]{:S(2)}, u32[]{:S(2)}) collective-permute-start(bf16[704,128]{1,0:T(8,128)(2,1)S(1)} %pad_maximum_fusion.refs_0_), channel_id=1, source_target_pairs={{0,4},{1,5},{2,6},{3,7},{4,0},{5,1},{6,2},{7,3},{8,12},{9,13},{10,... | collective-permute-start | bytes 540680 | tf_op jit(solution)/shard_map/ppermute | solution.py:179
  71.1 7.9 %collective-permute-start.16 = (bf16[704,128]{1,0:T(8,128)(2,1)S(1)}, bf16[704,128]{1,0:T(8,128)(2,1)S(1)}, u32[]{:S(2)}, u32[]{:S(2)}) collective-permute-start(bf16[704,128]{1,0:T(8,128)(2,1)S(1)} %pad_maximum_fusion.refs_0_), channel_id=1, source_target_pairs={{0,2},{1,3},{2,0},{3,1},{4,6},{5,7},{6,4},{7,5},{8,10},{9,11},{10,... | collective-permute-start | bytes 540680 | tf_op jit(solution)/shard_map/ppermute | solution.py:179
  72.8 9.1 %collective-permute-start.19 = (bf16[704,128]{1,0:T(8,128)(2,1)S(1)}, bf16[704,128]{1,0:T(8,128)(2,1)S(1)}, u32[]{:S(2)}, u32[]{:S(2)}) collective-permute-start(bf16[704,128]{1,0:T(8,128)(2,1)S(1)} %pad_maximum_fusion.refs_0_), channel_id=1, source_target_pairs={{0,1},{1,0},{2,3},{3,2},{4,5},{5,4},{6,7},{7,6},{8,9},{9,8},{10,11... | collective-permute-start | bytes 540680 | tf_op jit(solution)/shard_map/ppermute | solution.py:179
  77.2 4.7 %collective-permute-start.22 = (bf16[704,128]{1,0:T(8,128)(2,1)S(1)}, bf16[704,128]{1,0:T(8,128)(2,1)S(1)}, u32[]{:S(2)}, u32[]{:S(2)}) collective-permute-start(bf16[704,128]{1,0:T(8,128)(2,1)S(1)} %collective-permute-done.18.refs_3_), channel_id=1, source_target_pairs={{0,1},{1,0},{2,3},{3,2},{4,5},{5,4},{6,7},{7,6},{8,9},{9,8},{10,11... | collective-permute-start | bytes 540680 | tf_op jit(solution)/shard_map/ppermute | solution.py:179
  79.0 2.8 %collective-permute-start.21 = (bf16[704,128]{1,0:T(8,128)(2,1)S(1)}, bf16[704,128]{1,0:T(8,128)(2,1)S(1)}, u32[]{:S(2)}, u32[]{:S(2)}) collective-permute-start(bf16[704,128]{1,0:T(8,128)(2,1)S(1)} %collective-permute-done.17.refs_2_), channel_id=1, source_target_pairs={{0,1},{1,0},{2,3},{3,2},{4,5},{5,4},{6,7},{7,6},{8,9},{9,8},{10,11... | collective-permute-start | bytes 540680 | tf_op jit(solution)/shard_map/ppermute | solution.py:179
  79.0 2.8 %collective-permute-start.20 = (bf16[704,128]{1,0:T(8,128)(2,1)S(1)}, bf16[704,128]{1,0:T(8,128)(2,1)S(1)}, u32[]{:S(2)}, u32[]{:S(2)}) collective-permute-start(bf16[704,128]{1,0:T(8,128)(2,1)S(1)} %collective-permute-done.16.refs_1_), channel_id=1, source_target_pairs={{0,1},{1,0},{2,3},{3,2},{4,5},{5,4},{6,7},{7,6},{8,9},{9,8},{10,11... | collective-permute-start | bytes 540680 | tf_op jit(solution)/shard_map/ppermute | solution.py:179

commit v3 on v2

v3 whole, which is shorter than its diff:
```python
import math

import jax
import jax.numpy as jnp
from jax import lax
from jax.experimental import pallas as pl
from jax.experimental.pallas import tpu as pltpu
from jax.sharding import PartitionSpec as P

FIRST_SPREAD = 32
SECOND_SPREAD = 64
LANES = 128
ROW_TILE = 16
P_PARTS = 1
GROUPS = 1
VMEM_LIMIT = 48 * 1024 * 1024


def call(body, outs, args, scratch=(), flops=0, name=None, far_args=(), far_outs=()):
    moved = sum(a.size * a.dtype.itemsize for a in list(args) + list(outs))
    near, far = pl.BlockSpec(memory_space=pltpu.VMEM), pl.BlockSpec(memory_space=pltpu.HBM)
    return pl.pallas_call(
        body,
        out_shape=list(outs),
        in_specs=[far if i in far_args else near for i in range(len(args))],
        out_specs=[far if i in far_outs else near for i in range(len(outs))],
        scratch_shapes=list(scratch),
        compiler_params=pltpu.CompilerParams(vmem_limit_bytes=VMEM_LIMIT),
        cost_estimate=pl.CostEstimate(flops=flops, bytes_accessed=moved, transcendentals=0),
        name=name,
    )(*args)


def shape_of(shape, dtype):
    return jax.ShapeDtypeStruct(shape, dtype)


def packs(rows, channels):
    return channels % LANES * 2 == LANES and rows % (2 * ROW_TILE) == 0


def packed_shape(rows, channels):
    if not packs(rows, channels):
        return (rows, channels)
    full = channels // LANES
    return (rows * full + rows // 2, LANES)


def pack_into(refs, value):
    rows, channels = value.shape
    if packs(rows, channels):
        full = channels // LANES
        rest = value[:, full * LANES :]
        half = rows // 2
        tiles = [value[:, tile * LANES : (tile + 1) * LANES] for tile in range(full)]
        tiles.append(jnp.concatenate([rest[:half], rest[half:]], axis=1))
        value = jnp.concatenate(tiles, axis=0)
    size = value.shape[0] // len(refs)
    for part, ref in enumerate(refs):
        ref[...] = value[part * size : (part + 1) * size]


def unpacked(refs, rows, channels):
    parts = [ref[...] for ref in refs]
    ref = parts[0] if len(parts) == 1 else jnp.concatenate(parts, axis=0)
    if not packs(rows, channels):
        return ref
    full = channels // LANES
    rest = ref[full * rows :, :]
    width = channels - full * LANES
    tail = jnp.concatenate([rest[:, :width], rest[:, width:]], axis=0)
    return jnp.concatenate([ref[t * rows : (t + 1) * rows, :] for t in range(full)] + [tail], axis=1)


def extend(scratch, value, rim, width):
    rows = value.shape[0]
    scratch[width : width + rows, :] = value
    if rim is None:
        blank = jnp.zeros((width, value.shape[1]), value.dtype)
        scratch[:width, :] = blank
        scratch[width + rows :, :] = blank
    else:
        scratch[:width, :] = rim[:width, :]
        scratch[width + rows :, :] = rim[width:, :]


def row_blocks(rows):
    size = rows
    while size > 256 and size % 2 == 0 and size // 2 % ROW_TILE == 0:
        size //= 2
    return [(start, size) for start in range(0, rows, size)]


NT = (((1,), (1,)), ((), ()))
NN = (((1,), (0,)), ((), ()))


def conv_block(terms, start, size, width):
    total = None
    for ext, weight, b, flipped in terms:
        for a in (-1, 0, 1):
            tap = ext[start + (1 + a) * width : start + (1 + a) * width + size, :]
            kernel = weight[1 - a, 1 - b] if flipped else weight[1 + a, 1 + b]
            part = lax.dot_general(tap, kernel, NT if flipped else NN, preferred_element_type=jnp.float32)
            total = part if total is None else total + part
    return total


def flat_rows(channels, pieces):
    if channels % LANES * 2 != LANES:
        rows = 9 * channels * (-(-channels // LANES))
    else:
        rows = 9 * channels * channels // LANES
    unit = pieces * ROW_TILE
    return -(-rows // unit) * unit


def store_flat(ref, lead, blocks):
    channels = blocks[0].shape[0]
    full = channels // LANES
    row = 0
    for block in blocks:
        for tile in range(full):
            ref[lead, row : row + channels, :] = block[:, tile * LANES : (tile + 1) * LANES]
            row += channels
    width = channels - full * LANES
    if width == 0:
        return
    rests = [block[:, full * LANES :] for block in blocks]
    if width * 2 != LANES:
        for rest in rests:
            ref[lead, row : row + channels, :width] = rest
            row += channels
        return
    for pair in range(0, 8, 2):
        ref[lead, row : row + channels, :] = jnp.concatenate([rests[pair], rests[pair + 1]], axis=1)
        row += channels
    half = channels // 2
    ref[lead, row : row + half, :] = jnp.concatenate([rests[8][:half], rests[8][half:]], axis=1)


def load_flat(ref, lead, channels):
    full = channels // LANES
    row = 0
    parts = []
    for _ in range(9):
        tiles = []
        for _ in range(full):
            tiles.append(ref[lead, row : row + channels, :])
            row += channels
        parts.append(tiles)
    width = channels - full * LANES
    if width == 0:
        pass
    elif width * 2 != LANES:
        for tap in range(9):
            parts[tap].append(ref[lead, row : row + channels, :width])
            row += channels
    else:
        for pair in range(0, 8, 2):
            both = ref[lead, row : row + channels, :]
            parts[pair].append(both[:, :width])
            parts[pair + 1].append(both[:, width:])
            row += channels
        both = ref[lead, row : row + channels // 2, :]
        parts[8].append(jnp.concatenate([both[:, :width], both[:, width:]], axis=0))
    return [jnp.concatenate(p, axis=1) if len(p) > 1 else p[0] for p in parts]


def radices(count):
    found = []
    if count % 2 == 0:
        found.append(2)
        count //= 2
    while count % 4 == 0:
        found.append(4)
        count //= 4
    while count % 2 == 0:
        found.append(2)
        count //= 2
    return found if count == 1 else None


def swapped(value, count, stride, k):
    return lax.ppermute(value, "lon", [(i, i ^ (k * stride)) for i in range(count)])


def moved(value, steps):
    count = lax.axis_size("lon")
    if steps % count == 0:
        return value
    return lax.ppermute(value, "lon", [(i, (i + steps) % count) for i in range(count)])


def lat_rim(field):
    count = lax.axis_size("lat")
    if count == 1:
        return None
    north = lax.ppermute(field[-1], "lat", [(i, i + 1) for i in range(count - 1)])
    south = lax.ppermute(field[0], "lat", [(i + 1, i) for i in range(count - 1)])
    return jnp.stack([north, south])


def paired(spread, width):
    steps, rest = divmod(spread, width)
    return rest == 0 and lax.axis_size("lon") % (2 * steps) == 0


def side_of(spread, width):
    if not paired(spread, width):
        return 0
    return lax.rem(lax.axis_index("lon") // (spread // width), 2)


def inner_pairs(steps):
    return [(i, i + steps if i // steps % 2 == 0 else i - steps) for i in range(lax.axis_size("lon"))]


def outer_pairs(steps):
    count = lax.axis_size("lon")
    return [(i, (i - steps if i // steps % 2 == 0 else i + steps) % count) for i in range(count)]


def after(value, *others):
    return lax.optimization_barrier((value, *others))[0]


def beside(field, packed, spread, pack):
    width = field.shape[1]
    steps, rest = divmod(spread, width)
    if paired(spread, width):
        return (
            [lax.ppermute(packed, "lon", inner_pairs(steps))],
            [lax.ppermute(packed, "lon", outer_pairs(steps))],
        )
    if rest == 0:
        return [moved(packed, -steps)], [moved(packed, steps)]
    cut = width - rest
    west = jnp.concatenate([moved(field[:, cut:], steps + 1), moved(field[:, :cut], steps)], axis=1)
    east = jnp.concatenate([moved(field[:, rest:], -steps), moved(field[:, :rest], -steps - 1)], axis=1)
    return [pack(east)], [pack(west)]


def onward_pairs(steps):
    count = lax.axis_size("lon")
    return [(i, (i + 2 * steps if i // steps % 2 == 0 else i - 2 * steps) % count) for i in range(count)]


def shards(inputs, cotangent, first_weight, second_weight):
    height, width, channels = inputs.shape
    rows = height * width
    count = lax.axis_size("lon")
    scale = 1.0 / math.sqrt(rows * lax.axis_size("lat") * count)
    bf16, f32 = jnp.bfloat16, jnp.float32
    pshape = packed_shape(rows, channels)
    ext_rows = rows + 2 * width
    ext = pltpu.VMEM((ext_rows, channels), bf16)
    sides = pltpu.VMEM((3, ext_rows, channels), bf16)
    tap_flops = 2 * rows * channels * channels
    blocks = row_blocks(rows)

    def pack_body(source, *targets):
        pack_into(targets, source[...])

    def pack_one(field, parts=1):
        shape = (pshape[0] // parts, pshape[1])
        packed = call(
            pack_body, [shape_of(shape, bf16)] * parts, [field.reshape(rows, channels)], name="pack"
        )
        return packed if parts > 1 else packed[0]

    def rims_of(field, spread):
        rim = lat_rim(field)
        if rim is None:
            return []
        inner, outer = beside(rim, rim, spread, lambda r: r)
        return [r.reshape(2 * width, channels) for r in (rim, *inner, *outer)]

    def place_sides(scratch, refs, rims, spread):
        side = side_of(spread, width)
        half = len(refs) // 2
        extend(scratch.at[2 - 2 * side], unpacked(refs[:half], rows, channels), rims[0], width)
        extend(scratch.at[2 * side], unpacked(refs[half:], rows, channels), rims[1], width)

    def near_part(field, weight, inner, rims, spread, flipped, name):
        def body(x_ref, w_ref, *rest):
            refs, rest = rest[: len(inner)], rest[len(inner) :]
            (own_rim, inner_rim), (part, e0, e1) = (rest[:2], rest[2:]) if rimmed else ((None, None), rest)
            extend(e0, x_ref[...], own_rim, width)
            extend(e1, unpacked(refs, rows, channels), inner_rim, width)
            b = 1 - 2 * side_of(spread, width)
            for start, size in blocks:
                part[start : start + size, :] = conv_block(
                    [(e0, w_ref, 0, flipped), (e1, w_ref, b, flipped)], start, size, width
                )

        args = [field, weight] + inner + rims[:2]
        return call(body, [shape_of((rows, channels), f32)], args, [ext, ext], 6 * tap_flops, name)[0]

    def far_part(part_ref, scratch, w_ref, spread, flipped, start, size):
        b = 2 * side_of(spread, width) - 1
        return part_ref[start : start + size, :] + conv_block([(scratch, w_ref, b, flipped)], start, size, width)

    x = inputs.reshape(rows, channels)
    g = cotangent.reshape(rows, channels)
    x_rims = rims_of(inputs, FIRST_SPREAD)
    g_rims = rims_of(cotangent, SECOND_SPREAD)
    rimmed = bool(x_rims)

    if paired(SECOND_SPREAD, width):
        steps = SECOND_SPREAD // width
        g_packed = pack_one(cotangent, 2)
        g_inner = [lax.ppermute(part, "lon", inner_pairs(steps)) for part in g_packed]
        g_outer = [
            lax.ppermute(g_inner[0], "lon", onward_pairs(steps)),
            lax.ppermute(g_packed[1], "lon", outer_pairs(steps)),
        ]
    else:
        g_inner, g_outer = beside(cotangent, pack_one(cotangent), SECOND_SPREAD, pack_one)
    if paired(FIRST_SPREAD, width):
        steps = FIRST_SPREAD // width
        x_packed = pack_one(after(inputs, *g_packed), 2)
        x_inner = [lax.ppermute(part, "lon", inner_pairs(steps)) for part in x_packed]
        x_outer = [lax.ppermute(part, "lon", outer_pairs(steps)) for part in x_packed]
    else:
        x_inner, x_outer = beside(inputs, pack_one(inputs), FIRST_SPREAD, pack_one)
    part1 = near_part(x, first_weight, x_inner, x_rims, FIRST_SPREAD, False, "near_pre_act")
    part2 = near_part(g, second_weight, g_inner, g_rims, SECOND_SPREAD, True, "near_hidden_grad")
    x_sides, g_sides = x_inner + x_outer, g_inner + g_outer
    nx, ng = len(x_sides), len(g_sides)

    def hidden_body(part_ref, w_ref, *rest):
        side_refs, rest = rest[: len(x_outer)], rest[len(x_outer) :]
        (rim,), (hidden_t, slope, se, hid) = (rest[:1], rest[1:]) if rimmed else ((None,), rest)
        extend(se, unpacked(side_refs, rows, channels), rim, width)
        for start, size in blocks:
            act = far_part(part_ref, se, w_ref, FIRST_SPREAD, False, start, size)
            sigma = jax.nn.sigmoid(act)
            slope[start : start + size, :] = sigma * (1.0 + act * (1.0 - sigma))
            hid[start : start + size, :] = (act * sigma).astype(bf16).astype(f32)
        hidden_t[...] = hid[...].T.astype(bf16)

    hidden_t, slope = call(
        hidden_body,
        [shape_of((channels, rows), bf16), shape_of((rows, channels), f32)],
        [part1, first_weight] + x_outer + x_rims[2:],
        [ext, pltpu.VMEM((rows, channels), f32)],
        flops=3 * tap_flops,
        name="hidden",
    )

    def grad_body(part_ref, slope_ref, w_ref, *rest):
        side_refs, rest = rest[: len(g_outer)], rest[len(g_outer) :]
        (rim,), (pre_grad, packed, pre_t, se, pre) = (rest[:1], rest[1:]) if rimmed else ((None,), rest)
        extend(se, unpacked(side_refs, rows, channels), rim, width)
        for start, size in blocks:
            grad = far_part(part_ref, se, w_ref, SECOND_SPREAD, True, start, size)
            value = (grad * slope_ref[start : start + size, :]).astype(bf16)
            pre_grad[start : start + size, :] = value
            pre[start : start + size, :] = value.astype(f32)
        pack_into([packed], pre_grad[...])
        pre_t[...] = pre[...].T.astype(bf16)

    pre_grad, pre_packed, pre_t = call(
        grad_body,
        [shape_of((rows, channels), bf16), shape_of(pshape, bf16), shape_of((channels, rows), bf16)],
        [part2, slope, second_weight] + g_outer + g_rims[2:],
        [ext, pltpu.VMEM((rows, channels), f32)],
        flops=3 * tap_flops,
        name="pre_grad",
    )

    stages = radices(count)
    pieces = count // 2
    flat = flat_rows(channels, pieces)
    used = flat_rows(channels, 1)

    def kernel_gradient(which):
        def body(hid_ref, pre_ref, x_ref, g_ref, *rest):
            x_refs, g_refs, rest = rest[:nx], rest[nx : nx + ng], rest[nx + ng :]
            rims, (out, flat_ref, se) = (rest[:6], rest[6:]) if rimmed else ((None,) * 6, rest)

            def window(b, a):
                return se[1 + b, (1 + a) * width : (1 + a) * width + rows, :]

            if used < flat:
                flat_ref[0, used - ROW_TILE :, :] = jnp.zeros((flat - used + ROW_TILE, LANES), f32)
            chosen = which(lax.rem(lax.axis_index("lon"), 2))

            @pl.when(chosen == 0)
            def _():
                place_sides(se, g_refs, rims[4:6], SECOND_SPREAD)
                extend(se.at[1], g_ref[...], rims[3], width)
                store_flat(
                    flat_ref,
                    0,
                    [
                        jnp.dot(hid_ref[...], window(-b, -a), preferred_element_type=f32)
                        for a in (-1, 0, 1)
                        for b in (-1, 0, 1)
                    ],
                )

            @pl.when(chosen == 1)
            def _():
                place_sides(se, x_refs, rims[1:3], FIRST_SPREAD)
                extend(se.at[1], x_ref[...], rims[0], width)
                store_flat(
                    flat_ref,
                    0,
                    [
                        jnp.dot(pre_ref[...], window(b, a), preferred_element_type=f32)
                        for a in (-1, 0, 1)
                        for b in (-1, 0, 1)
                    ],
                )

            out[...] = flat_ref[0].astype(out.dtype)

        return body

    fields = [hidden_t, pre_t, x, g] + x_sides + g_sides + x_rims + g_rims
    flat_scratch = pltpu.VMEM((1, flat, LANES), f32)
    (send,) = call(
        kernel_gradient(lambda core: 1 - core),
        [shape_of((flat, LANES), bf16)],
        fields,
        [flat_scratch, sides],
        flops=9 * tap_flops,
        name="sibling_kernel_gradient",
    )
    received = [swapped(send, count, 1, 1)]
    (own,) = call(
        kernel_gradient(lambda core: core),
        [shape_of((flat, LANES), f32)],
        fields,
        [flat_scratch, sides],
        flops=9 * tap_flops,
        name="own_kernel_gradient",
    )

    def digit_of(stride, radix):
        return lax.rem(lax.axis_index("lon") // stride, radix)

    def combine(own, received, stride, radix, begin, size):
        m = size // radix

        def body(own_ref, *refs):
            got, (mine, *sends) = refs[: len(received)], refs[len(received) :]
            digit = digit_of(stride, radix)
            for k, target in enumerate([mine] + sends):
                at = pl.ds(pl.multiple_of(begin + (digit ^ k) * m, ROW_TILE), m)
                value = own_ref[at, :]
                for ref in got:
                    value = value + ref[at, :].astype(f32)
                target[...] = value.astype(target.dtype)

        outs = [shape_of((m, LANES), f32)] + [shape_of((m, LANES), bf16)] * (radix - 1)
        return call(body, outs, [own] + received, name="combine")

    unit = flat // pieces
    unit_rows = [unit]
    if GROUPS == 2 and unit > ROW_TILE:
        first_rows = -(-unit // (2 * ROW_TILE)) * ROW_TILE
        unit_rows = [first_rows, unit - first_rows]
    begins = [pieces * sum(unit_rows[:i]) for i in range(len(unit_rows))]
    groups = [(own, received, begin, pieces * rows_) for begin, rows_ in zip(begins, unit_rows)]
    stride = 2
    first_got = None
    for radix in stages[1:]:
        following = []
        for own, received, begin, size in groups:
            own, *sends = combine(own, received, stride, radix, begin, size)
            received = [swapped(part, count, stride, k + 1) for k, part in enumerate(sends)]
            following.append((own, received, 0, size // radix))
            first_got = received[0] if first_got is None else first_got
        groups = following
        stride *= radix
    pre_field = pre_grad.reshape(height, width, channels)
    p_rims = rims_of(pre_field, FIRST_SPREAD)
    if paired(FIRST_SPREAD, width):
        steps = FIRST_SPREAD // width
        p_inner = [lax.ppermute(pre_packed, "lon", inner_pairs(steps))]
        size = pshape[0] // P_PARTS
        pre_packed = after(pre_packed, first_got)
        p_outer = [
            lax.ppermute(pre_packed[i * size : (i + 1) * size], "lon", outer_pairs(steps)) for i in range(P_PARTS)
        ]
    else:
        p_inner, p_outer = beside(pre_field, pre_packed, FIRST_SPREAD, pack_one)
    part3 = near_part(pre_grad, first_weight, p_inner, p_rims, FIRST_SPREAD, True, "near_input_gradient")

    def input_body(part_ref, w_ref, *rest):
        side_refs, rest = rest[: len(p_outer)], rest[len(p_outer) :]
        (rim,), (out, se) = (rest[:1], rest[1:]) if rimmed else ((None,), rest)
        extend(se, unpacked(side_refs, rows, channels), rim, width)
        for start, size in blocks:
            out[start : start + size, :] = far_part(part_ref, se, w_ref, FIRST_SPREAD, True, start, size).astype(bf16)

    (input_gradient,) = call(
        input_body,
        [shape_of((rows, channels), bf16)],
        [part3, first_weight] + p_outer + p_rims[2:],
        [ext],
        flops=3 * tap_flops,
        name="input_gradient",
    )

    def finish(own, received):
        if lax.axis_size("lat") > 1:
            for part in received:
                own = own + part.astype(f32)
            return lax.psum(own, "lat").astype(bf16)

        def body(own_ref, *refs):
            value = own_ref[...]
            for ref in refs[:-1]:
                value = value + ref[...].astype(f32)
            refs[-1][...] = value.astype(bf16)

        return call(body, [shape_of(own.shape, bf16)], [own] + received, name="combine_last")[0]

    group = stages[1]
    arrived = []
    for own, received, _, _ in groups:
        held = finish(own, received)
        stride = count
        for radix in reversed(stages[2:]):
            stride //= radix
            held = jnp.concatenate([held] + [swapped(held, count, stride, k) for k in range(1, radix)], axis=0)
        quarter = [held] + [swapped(held, count, 2, k) for k in range(1, group)]
        sibling = [swapped(held, count, 1, 1)]
        sibling += [swapped(after(q, input_gradient), count, 1, 1) for q in quarter[1:]]
        arrived += quarter + sibling

    def final_body(*refs):
        (first_out, second_out, both, stage, sems) = refs[len(arrived) :]
        place = lax.axis_index("lon")
        mine = lax.rem(place, 2)
        for i, ref in enumerate(refs[: len(arrived)]):
            which, side, k = i // (2 * group), i // group % 2, i % group
            lead = mine if side == 0 else 1 - mine
            m = unit_rows[which]
            stride, span = 2 * group, pieces // group
            walk = [((digit_of(2, group) ^ k) * span, 0)]
            for radix in stages[2:]:
                digit = digit_of(stride, radix)
                span //= radix
                walk = [(at + (digit ^ j) * span, order + j * span) for at, order in walk for j in range(radix)]
                stride *= radix
            for at, order in walk:
                target = pl.ds(pl.multiple_of(begins[which] + at * m, ROW_TILE), m)
                both[lead, target, :] = ref[order * m : (order + 1) * m, :].astype(f32)
        copies = []
        for which, out in enumerate((second_out, first_out)):
            for tap, value in enumerate(load_flat(both, which, channels)):
                stage[which, tap] = (value.T if which else value) * scale
                copies.append(
                    pltpu.make_async_copy(
                        stage.at[which, tap], out.at[tap // 3, tap % 3], sems.at[9 * which + tap]
                    )
                )
                copies[-1].start()
        for copy in copies:
            copy.wait()

    first_gradient, second_gradient = call(
        final_body,
        [shape_of((3, 3, channels, channels), f32)] * 2,
        arrived,
        [
            pltpu.VMEM((2, flat, LANES), f32),
            pltpu.VMEM((2, 9, channels, channels), f32),
            pltpu.SemaphoreType.DMA((18,)),
        ],
        name="unpack_gradients",
        far_outs=(0, 1),
    )
    return (input_gradient.reshape(height, width, channels), first_gradient, second_gradient)


def solution(mesh):
    placed = (P("lat", "lon", None), P("lat", "lon", None), P(), P())
    return jax.shard_map(
        shards,
        mesh=mesh,
        in_specs=placed,
        out_specs=(P("lat", "lon", None), P(), P()),
        check_vma=False,
    )
```

time: 85 us -> 80.3 us (0.945)
  waiting for transfers between devices: 37.8 us -> 27.4 us
  starting transfers between devices: 29.3 us -> 36.5 us
  local copies, waits for them, and re-layouts: 4.43 us -> 3.33 us
    ppermute x6 -> x10, waiting for transfers between devices: 15.9 us -> 10.1 us  [the longest x4 6.6 us: shards(): lax.ppermute(part, 'lon', inner_pairs(steps))]
    ppermute x17, waiting for transfers between devices: 21.9 us -> 17.2 us  [swapped(): lax.ppermute(value, 'lon', [(i, i ^ k * stride) for i in range(count)])]
    ppermute x6 -> x10, starting transfers between devices: 11.9 us -> 15.9 us  [the longest x2 5.34 us: shards(): lax.ppermute(part, 'lon', outer_pairs(steps))]
    ppermute x17, starting transfers between devices: 17.4 us -> 20.6 us  [swapped(): lax.ppermute(value, 'lon', [(i, i ^ k * stride) for i in range(count)])]
    unnamed x16 -> x14, local copies, waits for them, and re-layouts: 4.43 us -> 3.33 us
    pallas_call x12 -> x14, Pallas kernels: 12.4 us -> 11.8 us  [call(): pl.pallas_call(body, out_shape=list(outs), in_specs=[far if i in far_args...]
  transfers between devices with their start and end apart: 23 -> 27, of which waited for: 12 -> 14; matrix products, arithmetic and copies ran while one was open for 0% -> 0% of each run, Pallas kernels for 8% -> 9%
where the time goes in v3:
time: 80.3 us; the launch traced here: 80 us
  starting transfers between devices  36.5 us (45%)
  waiting for transfers between devices  27.4 us (34%)
  Pallas kernels  11.8 us (15%)
  local copies, waits for them, and re-layouts  3.33 us (4%)
  between operations  1 us (1%)
    ppermute x17, starting transfers between devices, swapped(): lax.ppermute(value, 'lon', [(i, i ^ k * stride) for i in range(count)])  20.6 us
    ppermute x17, waiting for transfers between devices, swapped(): lax.ppermute(value, 'lon', [(i, i ^ k * stride) for i in range(count)])  17.2 us
    pallas_call x14, Pallas kernels, call(): pl.pallas_call(body, out_shape=list(outs), in_specs=[far if i in far_args...  11.8 us
    ppermute x4, waiting for transfers between devices, shards(): lax.ppermute(part, 'lon', inner_pairs(steps))  6.6 us
    ppermute x2, starting transfers between devices, shards(): lax.ppermute(part, 'lon', outer_pairs(steps))  5.34 us
    ppermute x1, starting transfers between devices, shards(): lax.ppermute(pre_packed[i * size:(i + 1) * size], 'lon', outer_pairs(steps))  3.74 us
    ppermute x1, waiting for transfers between devices, shards(): lax.ppermute(g_inner[0], 'lon', onward_pairs(steps))  3.53 us
    ppermute x4, starting transfers between devices, shards(): lax.ppermute(part, 'lon', inner_pairs(steps))  3.52 us
  transfers between devices with their start and end apart: 27, of which 14 were waited for; matrix products, arithmetic and copies ran while one was open for 0% of the time, Pallas kernels for 9%

profile of v3, /device:TPU:0, one launch (start us, length us, event | category | flops | bytes accessed | tf_op | source)
XLA Modules:
  0.0 80.0 jit_solution(13856932693963384055)
XLA Ops:
  0.6 1.0 %copy-done.2 = bf16[32,32,192]{2,1,0:T(8,128)(2,1)S(1)} copy-done((bf16[32,32,192]{2,1,0:T(8,128)(2,1)S(1)}, bf16[32,32,192]{2,1,0:T(8,128)(2,1)}, u32[]{:S(2)}) %copy-start.2) | copy-done | bytes 393240
  1.8 1.1 %copy-done.4 = bf16[32,32,192]{2,1,0:T(8,128)(2,1)S(1)} copy-done((bf16[32,32,192]{2,1,0:T(8,128)(2,1)S(1)}, bf16[32,32,192]{2,1,0:T(8,128)(2,1)}, u32[]{:S(2)}) %copy-start.4) | copy-done | bytes 393240
  3.6 2.9 %collective-permute-start = (bf16[768,128]{1,0:T(8,128)(2,1)S(1)}, bf16[768,128]{1,0:T(8,128)(2,1)S(1)}, u32[]{:S(2)}, u32[]{:S(2)}) collective-permute-start(bf16[768,128]{1,0:T(8,128)(2,1)S(1)} %get-tuple-element.27), channel_id=1, source_target_pairs={{0,2},{1,3},{2,0},{3,1},{4,6},{5,7},{6,4},{7,5},{8,10},{9,11},{10,... | collective-permute-start | bytes 589832 | tf_op jit(solution)/shard_map/ppermute | solution.py:313
  6.5 3.9 %collective-permute-start.4 = (bf16[768,128]{1,0:T(8,128)(2,1)S(1)}, bf16[768,128]{1,0:T(8,128)(2,1)S(1)}, u32[]{:S(2)}, u32[]{:S(2)}) collective-permute-start(bf16[768,128]{1,0:T(8,128)(2,1)S(1)} %get-tuple-element.30), channel_id=1, source_target_pairs={{0,31},{1,2},{2,1},{3,4},{4,3},{5,6},{6,5},{7,8},{8,7},{9,10},{10,... | collective-permute-start | bytes 589832 | tf_op jit(solution)/shard_map/ppermute | solution.py:324
  10.5 1.4 %collective-permute-start.5 = (bf16[768,128]{1,0:T(8,128)(2,1)S(1)}, bf16[768,128]{1,0:T(8,128)(2,1)S(1)}, u32[]{:S(2)}, u32[]{:S(2)}) collective-permute-start(bf16[768,128]{1,0:T(8,128)(2,1)S(1)} %get-tuple-element.31), channel_id=1, source_target_pairs={{0,31},{1,2},{2,1},{3,4},{4,3},{5,6},{6,5},{7,8},{8,7},{9,10},{10,... | collective-permute-start | bytes 589832 | tf_op jit(solution)/shard_map/ppermute | solution.py:324
  11.9 3.3 %collective-permute-start.7 = (bf16[768,128]{1,0:T(8,128)(2,1)S(1)}, bf16[768,128]{1,0:T(8,128)(2,1)S(1)}, u32[]{:S(2)}, u32[]{:S(2)}) collective-permute-start(bf16[768,128]{1,0:T(8,128)(2,1)S(1)} %get-tuple-element.28), channel_id=1, source_target_pairs={{0,30},{1,31},{2,4},{3,5},{4,2},{5,3},{6,8},{7,9},{8,6},{9,7},{10,... | collective-permute-start | bytes 589832 | tf_op jit(solution)/shard_map/ppermute | solution.py:316
  15.2 3.4 %collective-permute-done.rest_0_.rest_4_ = bf16[768,128]{1,0:T(8,128)(2,1)S(1)} collective-permute-done((bf16[768,128]{1,0:T(8,128)(2,1)S(1)}, bf16[768,128]{1,0:T(8,128)(2,1)S(1)}, u32[]{:S(2)}, u32[]{:S(2)}) %collective-permute-start) | collective-permute-done | bytes 196640 | tf_op jit(solution)/shard_map/ppermute | solution.py:313
  18.7 1.2 %copy-done = bf16[3,3,192,192]{3,2,1,0:T(8,128)(2,1)S(1)} copy-done((bf16[3,3,192,192]{3,2,1,0:T(8,128)(2,1)S(1)}, bf16[3,3,192,192]{3,2,1,0:T(8,128)(2,1)}, u32[]{:S(2)}) %copy-start) | copy-done | bytes 663576
  19.8 1.0 %near_pre_act.1.part_ref = f32[1024,192]{1,0:T(8,128)S(1)} custom-call(bf16[1024,192]{1,0:T(8,128)(2,1)S(1)} %bitcast.9, bf16[3,3,192,192]{3,2,1,0:T(8,128)(2,1)S(1)} %copy-done, bf16[768,128]{1,0:T(8,128)(2,1)S(1)} %collective-permute-done.2.rest_0_, bf16[768,128]{1,0:T(8,128)(2,1)S(1)} %collective-permute-done.3.rest_1_), custom_call_target="tpu_custom_call" | custom-call | flops 452984832 | bytes 2236416 | tf_op jit(solution)/shard_map/near_pre_act/pallas_call | solution.py:22
  21.7 3.1 %collective-permute-done.1.rest_1_.rest_5_ = bf16[768,128]{1,0:T(8,128)(2,1)S(1)} collective-permute-done((bf16[768,128]{1,0:T(8,128)(2,1)S(1)}, bf16[768,128]{1,0:T(8,128)(2,1)S(1)}, u32[]{:S(2)}, u32[]{:S(2)}) %collective-permute-start.1) | collective-permute-done | bytes 196640 | tf_op jit(solution)/shard_map/ppermute | solution.py:313
  24.9 1.0 %near_hidden_grad.1.part_ref = f32[1024,192]{1,0:T(8,128)S(1)} custom-call(bf16[1024,192]{1,0:T(8,128)(2,1)S(1)} %bitcast.5, bf16[3,3,192,192]{3,2,1,0:T(8,128)(2,1)S(1)} %copy-done.6, bf16[768,128]{1,0:T(8,128)(2,1)S(1)} %collective-permute-done.rest_0_.rest_4_, bf16[768,128]{1,0:T(8,128)(2,1)S(1)} %collective-permute-done.1.rest_1_.rest_5_), custom_call_target="tpu_custom_call" | custom-call | flops 452984832 | bytes 2236416 | tf_op jit(solution)/shard_map/near_hidden_grad/pallas_call | solution.py:22
  25.9 3.5 %collective-permute-done.6.rest_0_.rest_6_ = bf16[768,128]{1,0:T(8,128)(2,1)S(1)} collective-permute-done((bf16[768,128]{1,0:T(8,128)(2,1)S(1)}, bf16[768,128]{1,0:T(8,128)(2,1)S(1)}, u32[]{:S(2)}, u32[]{:S(2)}) %collective-permute-start.6) | collective-permute-done | bytes 196640 | tf_op jit(solution)/shard_map/ppermute | solution.py:315
  30.3 1.5 %sibling_kernel_gradient.1 = bf16[2816,128]{1,0:T(8,128)(2,1)S(1)} custom-call(bf16[192,1024]{1,0:T(8,128)(2,1)S(1)} %get-tuple-element.35.hid_ref, bf16[192,1024]{1,0:T(8,128)(2,1)S(1)} %get-tuple-element.36.pre_ref, bf16[1024,192]{1,0:T(8,128)(2,1)S(1)} %bitcast.10, bf16[1024,192]{1,0:T(8,128)(2,1)S(1)} %bitcast.6, ...), custom_call_target="tpu_custom_call" | custom-call | flops 679477248 | bytes 3866624 | tf_op jit(solution)/shard_map/sibling_kernel_gradient/pallas_call | solution.py:22
  31.8 1.6 %own_kernel_gradient.1.own_ref = f32[2816,128]{1,0:T(8,128)S(1)} custom-call(bf16[192,1024]{1,0:T(8,128)(2,1)S(1)} %get-tuple-element.35.hid_ref, bf16[192,1024]{1,0:T(8,128)(2,1)S(1)} %get-tuple-element.36.pre_ref, bf16[1024,192]{1,0:T(8,128)(2,1)S(1)} %bitcast.11, bf16[1024,192]{1,0:T(8,128)(2,1)S(1)} %bitcast.7, ...), custom_call_target="tpu_custom_call" | custom-call | flops 679477248 | bytes 4587520 | tf_op jit(solution)/shard_map/own_kernel_gradient/pallas_call | solution.py:22
  34.1 2.3 %collective-permute-start.10 = (bf16[704,128]{1,0:T(8,128)(2,1)S(1)}, bf16[704,128]{1,0:T(8,128)(2,1)S(1)}, u32[]{:S(2)}, u32[]{:S(2)}) collective-permute-start(bf16[704,128]{1,0:T(8,128)(2,1)S(1)} %get-tuple-element.37), channel_id=1, source_target_pairs={{0,2},{1,3},{2,0},{3,1},{4,6},{5,7},{6,4},{7,5},{8,10},{9,11},{10,... | collective-permute-start | bytes 540680 | tf_op jit(solution)/shard_map/ppermute | solution.py:185
  36.4 1.5 %collective-permute-start.13 = (bf16[704,128]{1,0:T(8,128)(2,1)S(1)}, bf16[704,128]{1,0:T(8,128)(2,1)S(1)}, u32[]{:S(2)}, u32[]{:S(2)}) collective-permute-start(bf16[704,128]{1,0:T(8,128)(2,1)S(1)} %get-tuple-element.41), channel_id=1, source_target_pairs={{0,6},{1,7},{2,4},{3,5},{4,2},{5,3},{6,0},{7,1},{8,14},{9,15},{10,... | collective-permute-start | bytes 540680 | tf_op jit(solution)/shard_map/ppermute | solution.py:185
  38.0 3.8 %collective-permute-done.10.refs_0_ = bf16[704,128]{1,0:T(8,128)(2,1)S(1)} collective-permute-done((bf16[704,128]{1,0:T(8,128)(2,1)S(1)}, bf16[704,128]{1,0:T(8,128)(2,1)S(1)}, u32[]{:S(2)}, u32[]{:S(2)}) %collective-permute-start.10) | collective-permute-done | bytes 180256 | tf_op jit(solution)/shard_map/ppermute | solution.py:185
  41.7 3.7 %collective-permute-start.11 = (bf16[1536,128]{1,0:T(8,128)(2,1)S(1)}, bf16[1536,128]{1,0:T(8,128)(2,1)S(1)}, u32[]{:S(2)}, u32[]{:S(2)}) collective-permute-start(bf16[1536,128]{1,0:T(8,128)(2,1)S(1)} %get-tuple-element.38), channel_id=1, source_target_pairs={{0,31},{1,2},{2,1},{3,4},{4,3},{5,6},{6,5},{7,8},{8,7},{9,10},{10,... | collective-permute-start | bytes 1179656 | tf_op jit(solution)/shard_map/ppermute | solution.py:487
  45.5 1.1 %collective-permute-done.12.refs_1_ = bf16[704,128]{1,0:T(8,128)(2,1)S(1)} collective-permute-done((bf16[704,128]{1,0:T(8,128)(2,1)S(1)}, bf16[704,128]{1,0:T(8,128)(2,1)S(1)}, u32[]{:S(2)}, u32[]{:S(2)}) %collective-permute-start.12) | collective-permute-done | bytes 180256 | tf_op jit(solution)/shard_map/ppermute | solution.py:185
  46.7 4.9 %collective-permute-start.14 = (bf16[176,128]{1,0:T(8,128)(2,1)S(1)}, bf16[176,128]{1,0:T(8,128)(2,1)S(1)}, u32[]{:S(2)}, u32[]{:S(2)}) collective-permute-start(bf16[176,128]{1,0:T(8,128)(2,1)S(1)} %get-tuple-element.43), channel_id=1, source_target_pairs={{0,8},{1,9},{2,10},{3,11},{4,12},{5,13},{6,14},{7,15},{8,0},{9,1},... | collective-permute-start | bytes 135176 | tf_op jit(solution)/shard_map/ppermute | solution.py:185
  52.0 2.0 %collective-permute-start.16 = (bf16[176,128]{1,0:T(8,128)(2,1)S(1)}, bf16[176,128]{1,0:T(8,128)(2,1)S(1)}, u32[]{:S(2)}, u32[]{:S(2)}) collective-permute-start(bf16[176,128]{1,0:T(8,128)(2,1)S(1)} %get-tuple-element.45), channel_id=1, source_target_pairs={{0,24},{1,25},{2,26},{3,27},{4,28},{5,29},{6,30},{7,31},{8,16},{9,... | collective-permute-start | bytes 135176 | tf_op jit(solution)/shard_map/ppermute | solution.py:185
  54.0 2.5 %collective-permute-done.15.refs_1_ = bf16[176,128]{1,0:T(8,128)(2,1)S(1)} collective-permute-done((bf16[176,128]{1,0:T(8,128)(2,1)S(1)}, bf16[176,128]{1,0:T(8,128)(2,1)S(1)}, u32[]{:S(2)}, u32[]{:S(2)}) %collective-permute-start.15) | collective-permute-done | bytes 45088 | tf_op jit(solution)/shard_map/ppermute | solution.py:185
  56.5 1.5 %collective-permute-done.16.refs_2_ = bf16[176,128]{1,0:T(8,128)(2,1)S(1)} collective-permute-done((bf16[176,128]{1,0:T(8,128)(2,1)S(1)}, bf16[176,128]{1,0:T(8,128)(2,1)S(1)}, u32[]{:S(2)}, u32[]{:S(2)}) %collective-permute-start.16) | collective-permute-done | bytes 45088 | tf_op jit(solution)/shard_map/ppermute | solution.py:185
  58.1 3.0 %collective-permute-start.18 = (bf16[176,128]{1,0:T(8,128)(2,1)S(1)}, bf16[176,128]{1,0:T(8,128)(2,1)S(1)}, u32[]{:S(2)}, u32[]{:S(2)}) collective-permute-start(bf16[176,128]{1,0:T(8,128)(2,1)S(1)} %combine_last.1), channel_id=1, source_target_pairs={{0,16},{1,17},{2,18},{3,19},{4,20},{5,21},{6,22},{7,23},{8,24},{9,... | collective-permute-start | bytes 135176 | tf_op jit(solution)/shard_map/ppermute | solution.py:185
  61.1 1.4 %collective-permute-start.19 = (bf16[176,128]{1,0:T(8,128)(2,1)S(1)}, bf16[176,128]{1,0:T(8,128)(2,1)S(1)}, u32[]{:S(2)}, u32[]{:S(2)}) collective-permute-start(bf16[176,128]{1,0:T(8,128)(2,1)S(1)} %combine_last.1), channel_id=1, source_target_pairs={{0,24},{1,25},{2,26},{3,27},{4,28},{5,29},{6,30},{7,31},{8,16},{9,... | collective-permute-start | bytes 135176 | tf_op jit(solution)/shard_map/ppermute | solution.py:185
  63.1 3.8 %collective-permute-done.19 = bf16[176,128]{1,0:T(8,128)(2,1)S(1)} collective-permute-done((bf16[176,128]{1,0:T(8,128)(2,1)S(1)}, bf16[176,128]{1,0:T(8,128)(2,1)S(1)}, u32[]{:S(2)}, u32[]{:S(2)}) %collective-permute-start.19) | collective-permute-done | bytes 45088 | tf_op jit(solution)/shard_map/ppermute | solution.py:185
  67.0 3.6 %collective-permute-start.22 = (bf16[704,128]{1,0:T(8,128)(2,1)S(1)}, bf16[704,128]{1,0:T(8,128)(2,1)S(1)}, u32[]{:S(2)}, u32[]{:S(2)}) collective-permute-start(bf16[704,128]{1,0:T(8,128)(2,1)S(1)} %pad_maximum_fusion.refs_0_), channel_id=1, source_target_pairs={{0,6},{1,7},{2,4},{3,5},{4,2},{5,3},{6,0},{7,1},{8,14},{9,15},{10,... | collective-permute-start | bytes 540680 | tf_op jit(solution)/shard_map/ppermute | solution.py:185
  71.2 1.0 %near_input_gradient.1.part_ref = f32[1024,192]{1,0:T(8,128)S(1)} custom-call(bf16[1024,192]{1,0:T(8,128)(2,1)S(1)} %get-tuple-element.33.x_ref, bf16[3,3,192,192]{3,2,1,0:T(8,128)(2,1)S(1)} %copy-done.1, bf16[1536,128]{1,0:T(8,128)(2,1)S(1)} %collective-permute-done.8.rest_0_), custom_call_target="tpu_custom_call" | custom-call | flops 452984832 | bytes 2236416 | tf_op jit(solution)/shard_map/near_input_gradient/pallas_call | solution.py:22
  72.3 1.4 %input_gradient.1 = bf16[1024,192]{1,0:T(8,128)(2,1)} custom-call(f32[1024,192]{1,0:T(8,128)S(1)} %near_input_gradient.1.part_ref, bf16[3,3,192,192]{3,2,1,0:T(8,128)(2,1)S(1)} %copy-done.1, bf16[1536,128]{1,0:T(8,128)(2,1)S(1)} %collective-permute-done.11.rest_0_), custom_call_target="tpu_custom_call" | custom-call | flops 226492416 | bytes 2236416 | tf_op jit(solution)/shard_map/input_gradient/pallas_call | solution.py:22
  74.1 1.9 %collective-permute-done.21.refs_2_ = bf16[704,128]{1,0:T(8,128)(2,1)S(1)} collective-permute-done((bf16[704,128]{1,0:T(8,128)(2,1)S(1)}, bf16[704,128]{1,0:T(8,128)(2,1)S(1)}, u32[]{:S(2)}, u32[]{:S(2)}) %collective-permute-start.21) | collective-permute-done | bytes 180256 | tf_op jit(solution)/shard_map/ppermute | solution.py:185
  76.5 0.9 %collective-permute-done.25.refs_6_ = bf16[704,128]{1,0:T(8,128)(2,1)S(1)} collective-permute-done((bf16[704,128]{1,0:T(8,128)(2,1)S(1)}, bf16[704,128]{1,0:T(8,128)(2,1)S(1)}, u32[]{:S(2)}, u32[]{:S(2)}) %collective-permute-start.25) | collective-permute-done | bytes 180256 | tf_op jit(solution)/shard_map/ppermute | solution.py:185
  77.7 2.2 %unpack_gradients.1 = (f32[3,3,192,192]{3,2,1,0:T(8,128)}, f32[3,3,192,192]{3,2,1,0:T(8,128)}) custom-call(bf16[704,128]{1,0:T(8,128)(2,1)S(1)} %pad_maximum_fusion.refs_0_, bf16[704,128]{1,0:T(8,128)(2,1)S(1)} %collective-permute-done.20.refs_1_, bf16[704,128]{1,0:T(8,128)(2,1)S(1)} %collective-permute-done.21.refs_2_, ...), custom_call_target="tpu_custom_call" | custom-call | bytes 4096000 | tf_op jit(solution)/shard_map/unpack_gradients/pallas_call | solution.py:22
  (51 shorter events, 6.6 us)
Async XLA Ops:
  1.7 19.2 %copy-start.1 = (bf16[3,3,192,192]{3,2,1,0:T(8,128)(2,1)S(1)}, bf16[3,3,192,192]{3,2,1,0:T(8,128)(2,1)}, u32[]{:S(2)}) copy-start(bf16[3,3,192,192]{3,2,1,0:T(8,128)(2,1)} %w_ref.11) | copy-start | bytes 1990660
  3.0 8.9 %collective-permute-start.2 = (bf16[768,128]{1,0:T(8,128)(2,1)S(1)}, bf16[768,128]{1,0:T(8,128)(2,1)S(1)}, u32[]{:S(2)}, u32[]{:S(2)}) collective-permute-start(bf16[768,128]{1,0:T(8,128)(2,1)S(1)} %get-tuple-element.30), channel_id=1, source_target_pairs={{0,1},{1,0},{2,3},{3,2},{4,5},{5,4},{6,7},{7,6},{8,9},{9,8},{10,11... | collective-permute-start | bytes 589832 | tf_op jit(solution)/shard_map/ppermute | solution.py:323
  3.5 8.3 %collective-permute-start.3 = (bf16[768,128]{1,0:T(8,128)(2,1)S(1)}, bf16[768,128]{1,0:T(8,128)(2,1)S(1)}, u32[]{:S(2)}, u32[]{:S(2)}) collective-permute-start(bf16[768,128]{1,0:T(8,128)(2,1)S(1)} %get-tuple-element.31), channel_id=1, source_target_pairs={{0,1},{1,0},{2,3},{3,2},{4,5},{5,4},{6,7},{7,6},{8,9},{9,8},{10,11... | collective-permute-start | bytes 589832 | tf_op jit(solution)/shard_map/ppermute | solution.py:323
  3.6 15.0 %collective-permute-start = (bf16[768,128]{1,0:T(8,128)(2,1)S(1)}, bf16[768,128]{1,0:T(8,128)(2,1)S(1)}, u32[]{:S(2)}, u32[]{:S(2)}) collective-permute-start(bf16[768,128]{1,0:T(8,128)(2,1)S(1)} %get-tuple-element.27), channel_id=1, source_target_pairs={{0,2},{1,3},{2,0},{3,1},{4,6},{5,7},{6,4},{7,5},{8,10},{9,11},{10,... | collective-permute-start | bytes 589832 | tf_op jit(solution)/shard_map/ppermute | solution.py:313
  6.5 14.3 %collective-permute-start.4 = (bf16[768,128]{1,0:T(8,128)(2,1)S(1)}, bf16[768,128]{1,0:T(8,128)(2,1)S(1)}, u32[]{:S(2)}, u32[]{:S(2)}) collective-permute-start(bf16[768,128]{1,0:T(8,128)(2,1)S(1)} %get-tuple-element.30), channel_id=1, source_target_pairs={{0,31},{1,2},{2,1},{3,4},{4,3},{5,6},{6,5},{7,8},{8,7},{9,10},{10,... | collective-permute-start | bytes 589832 | tf_op jit(solution)/shard_map/ppermute | solution.py:324
  10.5 10.4 %collective-permute-start.5 = (bf16[768,128]{1,0:T(8,128)(2,1)S(1)}, bf16[768,128]{1,0:T(8,128)(2,1)S(1)}, u32[]{:S(2)}, u32[]{:S(2)}) collective-permute-start(bf16[768,128]{1,0:T(8,128)(2,1)S(1)} %get-tuple-element.31), channel_id=1, source_target_pairs={{0,31},{1,2},{2,1},{3,4},{4,3},{5,6},{6,5},{7,8},{8,7},{9,10},{10,... | collective-permute-start | bytes 589832 | tf_op jit(solution)/shard_map/ppermute | solution.py:324
  11.9 13.0 %collective-permute-start.1 = (bf16[768,128]{1,0:T(8,128)(2,1)S(1)}, bf16[768,128]{1,0:T(8,128)(2,1)S(1)}, u32[]{:S(2)}, u32[]{:S(2)}) collective-permute-start(bf16[768,128]{1,0:T(8,128)(2,1)S(1)} %get-tuple-element.28), channel_id=1, source_target_pairs={{0,2},{1,3},{2,0},{3,1},{4,6},{5,7},{6,4},{7,5},{8,10},{9,11},{10,... | collective-permute-start | bytes 589832 | tf_op jit(solution)/shard_map/ppermute | solution.py:313
  11.9 14.0 %collective-permute-start.7 = (bf16[768,128]{1,0:T(8,128)(2,1)S(1)}, bf16[768,128]{1,0:T(8,128)(2,1)S(1)}, u32[]{:S(2)}, u32[]{:S(2)}) collective-permute-start(bf16[768,128]{1,0:T(8,128)(2,1)S(1)} %get-tuple-element.28), channel_id=1, source_target_pairs={{0,30},{1,31},{2,4},{3,5},{4,2},{5,3},{6,8},{7,9},{8,6},{9,7},{10,... | collective-permute-start | bytes 589832 | tf_op jit(solution)/shard_map/ppermute | solution.py:316
  18.7 10.8 %collective-permute-start.6 = (bf16[768,128]{1,0:T(8,128)(2,1)S(1)}, bf16[768,128]{1,0:T(8,128)(2,1)S(1)}, u32[]{:S(2)}, u32[]{:S(2)}) collective-permute-start(bf16[768,128]{1,0:T(8,128)(2,1)S(1)} %collective-permute-done.rest_0_.rest_4_), channel_id=1, source_target_pairs={{0,4},{1,5},{2,30},{3,31},{4,8},{5,9},{6,2},{7,3},{8,12},{9,13},{1... | collective-permute-start | bytes 589832 | tf_op jit(solution)/shard_map/ppermute | solution.py:315
  18.7 1.2 %copy-start = (bf16[3,3,192,192]{3,2,1,0:T(8,128)(2,1)S(1)}, bf16[3,3,192,192]{3,2,1,0:T(8,128)(2,1)}, u32[]{:S(2)}) copy-start(bf16[3,3,192,192]{3,2,1,0:T(8,128)(2,1)} %w_ref.11) | copy-start | bytes 1990660
  20.8 4.1 %copy-start.3 = (bf16[32,32,192]{2,1,0:T(8,128)(2,1)S(1)}, bf16[32,32,192]{2,1,0:T(8,128)(2,1)}, u32[]{:S(2)}) copy-start(bf16[32,32,192]{2,1,0:T(8,128)(2,1)} %param.5) | copy-start | bytes 1179652
  20.8 4.1 %copy-start.6 = (bf16[3,3,192,192]{3,2,1,0:T(8,128)(2,1)S(1)}, bf16[3,3,192,192]{3,2,1,0:T(8,128)(2,1)}, u32[]{:S(2)}) copy-start(bf16[3,3,192,192]{3,2,1,0:T(8,128)(2,1)} %w_ref.9) | copy-start | bytes 1990660
  25.9 4.4 %copy-start.5 = (bf16[32,32,192]{2,1,0:T(8,128)(2,1)S(1)}, bf16[32,32,192]{2,1,0:T(8,128)(2,1)}, u32[]{:S(2)}) copy-start(bf16[32,32,192]{2,1,0:T(8,128)(2,1)} %param.4) | copy-start | bytes 1179652
  31.8 2.3 %collective-permute-start.9 = (bf16[2816,128]{1,0:T(8,128)(2,1)S(1)}, bf16[2816,128]{1,0:T(8,128)(2,1)S(1)}, u32[]{:S(2)}, u32[]{:S(2)}) collective-permute-start(bf16[2816,128]{1,0:T(8,128)(2,1)S(1)} %sibling_kernel_gradient.1), channel_id=1, source_target_pairs={{0,1},{1,0},{2,3},{3,2},{4,5},{5,4},{6,7},{7,6},{8,9},{9,8},{10,11... | collective-permute-start | bytes 2162696 | tf_op jit(solution)/shard_map/ppermute | solution.py:185
  34.1 7.6 %collective-permute-start.10 = (bf16[704,128]{1,0:T(8,128)(2,1)S(1)}, bf16[704,128]{1,0:T(8,128)(2,1)S(1)}, u32[]{:S(2)}, u32[]{:S(2)}) collective-permute-start(bf16[704,128]{1,0:T(8,128)(2,1)S(1)} %get-tuple-element.37), channel_id=1, source_target_pairs={{0,2},{1,3},{2,0},{3,1},{4,6},{5,7},{6,4},{7,5},{8,10},{9,11},{10,... | collective-permute-start | bytes 540680 | tf_op jit(solution)/shard_map/ppermute | solution.py:185
  36.4 10.2 %collective-permute-start.12 = (bf16[704,128]{1,0:T(8,128)(2,1)S(1)}, bf16[704,128]{1,0:T(8,128)(2,1)S(1)}, u32[]{:S(2)}, u32[]{:S(2)}) collective-permute-start(bf16[704,128]{1,0:T(8,128)(2,1)S(1)} %get-tuple-element.40), channel_id=1, source_target_pairs={{0,4},{1,5},{2,6},{3,7},{4,0},{5,1},{6,2},{7,3},{8,12},{9,13},{10,... | collective-permute-start | bytes 540680 | tf_op jit(solution)/shard_map/ppermute | solution.py:185
  36.4 10.2 %collective-permute-start.13 = (bf16[704,128]{1,0:T(8,128)(2,1)S(1)}, bf16[704,128]{1,0:T(8,128)(2,1)S(1)}, u32[]{:S(2)}, u32[]{:S(2)}) collective-permute-start(bf16[704,128]{1,0:T(8,128)(2,1)S(1)} %get-tuple-element.41), channel_id=1, source_target_pairs={{0,6},{1,7},{2,4},{3,5},{4,2},{5,3},{6,0},{7,1},{8,14},{9,15},{10,... | collective-permute-start | bytes 540680 | tf_op jit(solution)/shard_map/ppermute | solution.py:185
  38.0 33.2 %collective-permute-start.8 = (bf16[1536,128]{1,0:T(8,128)(2,1)S(1)}, bf16[1536,128]{1,0:T(8,128)(2,1)S(1)}, u32[]{:S(2)}, u32[]{:S(2)}) collective-permute-start(bf16[1536,128]{1,0:T(8,128)(2,1)S(1)} %get-tuple-element.38), channel_id=1, source_target_pairs={{0,1},{1,0},{2,3},{3,2},{4,5},{5,4},{6,7},{7,6},{8,9},{9,8},{10,11... | collective-permute-start | bytes 1179656 | tf_op jit(solution)/shard_map/ppermute | solution.py:483
  41.7 30.5 %collective-permute-start.11 = (bf16[1536,128]{1,0:T(8,128)(2,1)S(1)}, bf16[1536,128]{1,0:T(8,128)(2,1)S(1)}, u32[]{:S(2)}, u32[]{:S(2)}) collective-permute-start(bf16[1536,128]{1,0:T(8,128)(2,1)S(1)} %get-tuple-element.38), channel_id=1, source_target_pairs={{0,31},{1,2},{2,1},{3,4},{4,3},{5,6},{6,5},{7,8},{8,7},{9,10},{10,... | collective-permute-start | bytes 1179656 | tf_op jit(solution)/shard_map/ppermute | solution.py:487
  46.7 7.4 %collective-permute-start.14 = (bf16[176,128]{1,0:T(8,128)(2,1)S(1)}, bf16[176,128]{1,0:T(8,128)(2,1)S(1)}, u32[]{:S(2)}, u32[]{:S(2)}) collective-permute-start(bf16[176,128]{1,0:T(8,128)(2,1)S(1)} %get-tuple-element.43), channel_id=1, source_target_pairs={{0,8},{1,9},{2,10},{3,11},{4,12},{5,13},{6,14},{7,15},{8,0},{9,1},... | collective-permute-start | bytes 135176 | tf_op jit(solution)/shard_map/ppermute | solution.py:185
  51.6 4.9 %collective-permute-start.15 = (bf16[176,128]{1,0:T(8,128)(2,1)S(1)}, bf16[176,128]{1,0:T(8,128)(2,1)S(1)}, u32[]{:S(2)}, u32[]{:S(2)}) collective-permute-start(bf16[176,128]{1,0:T(8,128)(2,1)S(1)} %get-tuple-element.44), channel_id=1, source_target_pairs={{0,16},{1,17},{2,18},{3,19},{4,20},{5,21},{6,22},{7,23},{8,24},{9,... | collective-permute-start | bytes 135176 | tf_op jit(solution)/shard_map/ppermute | solution.py:185
  52.0 6.0 %collective-permute-start.16 = (bf16[176,128]{1,0:T(8,128)(2,1)S(1)}, bf16[176,128]{1,0:T(8,128)(2,1)S(1)}, u32[]{:S(2)}, u32[]{:S(2)}) collective-permute-start(bf16[176,128]{1,0:T(8,128)(2,1)S(1)} %get-tuple-element.45), channel_id=1, source_target_pairs={{0,24},{1,25},{2,26},{3,27},{4,28},{5,29},{6,30},{7,31},{8,16},{9,... | collective-permute-start | bytes 135176 | tf_op jit(solution)/shard_map/ppermute | solution.py:185
  58.0 4.5 %collective-permute-start.17 = (bf16[176,128]{1,0:T(8,128)(2,1)S(1)}, bf16[176,128]{1,0:T(8,128)(2,1)S(1)}, u32[]{:S(2)}, u32[]{:S(2)}) collective-permute-start(bf16[176,128]{1,0:T(8,128)(2,1)S(1)} %combine_last.1), channel_id=1, source_target_pairs={{0,8},{1,9},{2,10},{3,11},{4,12},{5,13},{6,14},{7,15},{8,0},{9,1},... | collective-permute-start | bytes 135176 | tf_op jit(solution)/shard_map/ppermute | solution.py:185
  58.1 5.0 %collective-permute-start.18 = (bf16[176,128]{1,0:T(8,128)(2,1)S(1)}, bf16[176,128]{1,0:T(8,128)(2,1)S(1)}, u32[]{:S(2)}, u32[]{:S(2)}) collective-permute-start(bf16[176,128]{1,0:T(8,128)(2,1)S(1)} %combine_last.1), channel_id=1, source_target_pairs={{0,16},{1,17},{2,18},{3,19},{4,20},{5,21},{6,22},{7,23},{8,24},{9,... | collective-permute-start | bytes 135176 | tf_op jit(solution)/shard_map/ppermute | solution.py:185
  61.1 5.8 %collective-permute-start.19 = (bf16[176,128]{1,0:T(8,128)(2,1)S(1)}, bf16[176,128]{1,0:T(8,128)(2,1)S(1)}, u32[]{:S(2)}, u32[]{:S(2)}) collective-permute-start(bf16[176,128]{1,0:T(8,128)(2,1)S(1)} %combine_last.1), channel_id=1, source_target_pairs={{0,24},{1,25},{2,26},{3,27},{4,28},{5,29},{6,30},{7,31},{8,16},{9,... | collective-permute-start | bytes 135176 | tf_op jit(solution)/shard_map/ppermute | solution.py:185
  67.0 7.0 %collective-permute-start.22 = (bf16[704,128]{1,0:T(8,128)(2,1)S(1)}, bf16[704,128]{1,0:T(8,128)(2,1)S(1)}, u32[]{:S(2)}, u32[]{:S(2)}) collective-permute-start(bf16[704,128]{1,0:T(8,128)(2,1)S(1)} %pad_maximum_fusion.refs_0_), channel_id=1, source_target_pairs={{0,6},{1,7},{2,4},{3,5},{4,2},{5,3},{6,0},{7,1},{8,14},{9,15},{10,... | collective-permute-start | bytes 540680 | tf_op jit(solution)/shard_map/ppermute | solution.py:185
  70.5 5.5 %collective-permute-start.21 = (bf16[704,128]{1,0:T(8,128)(2,1)S(1)}, bf16[704,128]{1,0:T(8,128)(2,1)S(1)}, u32[]{:S(2)}, u32[]{:S(2)}) collective-permute-start(bf16[704,128]{1,0:T(8,128)(2,1)S(1)} %pad_maximum_fusion.refs_0_), channel_id=1, source_target_pairs={{0,4},{1,5},{2,6},{3,7},{4,0},{5,1},{6,2},{7,3},{8,12},{9,13},{10,... | collective-permute-start | bytes 540680 | tf_op jit(solution)/shard_map/ppermute | solution.py:185
  70.5 5.5 %collective-permute-start.20 = (bf16[704,128]{1,0:T(8,128)(2,1)S(1)}, bf16[704,128]{1,0:T(8,128)(2,1)S(1)}, u32[]{:S(2)}, u32[]{:S(2)}) collective-permute-start(bf16[704,128]{1,0:T(8,128)(2,1)S(1)} %pad_maximum_fusion.refs_0_), channel_id=1, source_target_pairs={{0,2},{1,3},{2,0},{3,1},{4,6},{5,7},{6,4},{7,5},{8,10},{9,11},{10,... | collective-permute-start | bytes 540680 | tf_op jit(solution)/shard_map/ppermute | solution.py:185
  72.2 4.4 %collective-permute-start.23 = (bf16[704,128]{1,0:T(8,128)(2,1)S(1)}, bf16[704,128]{1,0:T(8,128)(2,1)S(1)}, u32[]{:S(2)}, u32[]{:S(2)}) collective-permute-start(bf16[704,128]{1,0:T(8,128)(2,1)S(1)} %pad_maximum_fusion.refs_0_), channel_id=1, source_target_pairs={{0,1},{1,0},{2,3},{3,2},{4,5},{5,4},{6,7},{7,6},{8,9},{9,8},{10,11... | collective-permute-start | bytes 540680 | tf_op jit(solution)/shard_map/ppermute | solution.py:185
  74.0 2.5 %collective-permute-start.26 = (bf16[704,128]{1,0:T(8,128)(2,1)S(1)}, bf16[704,128]{1,0:T(8,128)(2,1)S(1)}, u32[]{:S(2)}, u32[]{:S(2)}) collective-permute-start(bf16[704,128]{1,0:T(8,128)(2,1)S(1)} %collective-permute-done.22.refs_3_), channel_id=1, source_target_pairs={{0,1},{1,0},{2,3},{3,2},{4,5},{5,4},{6,7},{7,6},{8,9},{9,8},{10,11... | collective-permute-start | bytes 540680 | tf_op jit(solution)/shard_map/ppermute | solution.py:185
  76.0 1.4 %collective-permute-start.25 = (bf16[704,128]{1,0:T(8,128)(2,1)S(1)}, bf16[704,128]{1,0:T(8,128)(2,1)S(1)}, u32[]{:S(2)}, u32[]{:S(2)}) collective-permute-start(bf16[704,128]{1,0:T(8,128)(2,1)S(1)} %collective-permute-done.21.refs_2_), channel_id=1, source_target_pairs={{0,1},{1,0},{2,3},{3,2},{4,5},{5,4},{6,7},{7,6},{8,9},{9,8},{10,11... | collective-permute-start | bytes 540680 | tf_op jit(solution)/shard_map/ppermute | solution.py:185
  76.0 1.7 %collective-permute-start.24 = (bf16[704,128]{1,0:T(8,128)(2,1)S(1)}, bf16[704,128]{1,0:T(8,128)(2,1)S(1)}, u32[]{:S(2)}, u32[]{:S(2)}) collective-permute-start(bf16[704,128]{1,0:T(8,128)(2,1)S(1)} %collective-permute-done.20.refs_1_), channel_id=1, source_target_pairs={{0,1},{1,0},{2,3},{3,2},{4,5},{5,4},{6,7},{7,6},{8,9},{9,8},{10,11... | collective-permute-start | bytes 540680 | tf_op jit(solution)/shard_map/ppermute | solution.py:185
  (2 other events, 2.2 us)

commit v4 on v3

--- a/solution.py
+++ b/solution.py
@@ -11,12 +11,12 @@
 SECOND_SPREAD = 64
 LANES = 128
 ROW_TILE = 16
-P_PARTS = 1
-GROUPS = 1
+G_SHARE = 13 / 24
+X_SHARE = 5 / 12
 VMEM_LIMIT = 48 * 1024 * 1024
 
 
-def call(body, outs, args, scratch=(), flops=0, name=None, far_args=(), far_outs=()):
+def call(body, outs, args, scratch=(), flops=0, name=None, far_args=(), far_outs=(), aliases={}):
     moved = sum(a.size * a.dtype.itemsize for a in list(args) + list(outs))
     near, far = pl.BlockSpec(memory_space=pltpu.VMEM), pl.BlockSpec(memory_space=pltpu.HBM)
     return pl.pallas_call(
@@ -25,6 +25,7 @@
         in_specs=[far if i in far_args else near for i in range(len(args))],
         out_specs=[far if i in far_outs else near for i in range(len(outs))],
         scratch_shapes=list(scratch),
+        input_output_aliases=aliases,
         compiler_params=pltpu.CompilerParams(vmem_limit_bytes=VMEM_LIMIT),
         cost_estimate=pl.CostEstimate(flops=flops, bytes_accessed=moved, transcendentals=0),
         name=name,
@@ -55,9 +56,10 @@
         tiles = [value[:, tile * LANES : (tile + 1) * LANES] for tile in range(full)]
         tiles.append(jnp.concatenate([rest[:half], rest[half:]], axis=1))
         value = jnp.concatenate(tiles, axis=0)
-    size = value.shape[0] // len(refs)
-    for part, ref in enumerate(refs):
-        ref[...] = value[part * size : (part + 1) * size]
+    begin = 0
+    for ref in refs:
+        ref[...] = value[begin : begin + ref.shape[0]]
+        begin += ref.shape[0]
 
 
 def unpacked(refs, rows, channels):
@@ -262,12 +264,14 @@
     def pack_body(source, *targets):
         pack_into(targets, source[...])
 
-    def pack_one(field, parts=1):
-        shape = (pshape[0] // parts, pshape[1])
-        packed = call(
-            pack_body, [shape_of(shape, bf16)] * parts, [field.reshape(rows, channels)], name="pack"
-        )
-        return packed if parts > 1 else packed[0]
+    def pack_one(field, share=None):
+        sizes = [pshape[0]]
+        if share is not None:
+            first = max(int(pshape[0] * share) // ROW_TILE, 1) * ROW_TILE
+            sizes = [first, pshape[0] - first]
+        shapes = [shape_of((size, pshape[1]), bf16) for size in sizes]
+        packed = call(pack_body, shapes, [field.reshape(rows, channels)], name="pack")
+        return packed[0] if share is None else packed
 
     def rims_of(field, spread):
         rim = lat_rim(field)
@@ -309,7 +313,7 @@
 
     if paired(SECOND_SPREAD, width):
         steps = SECOND_SPREAD // width
-        g_packed = pack_one(cotangent, 2)
+        g_packed = pack_one(cotangent, G_SHARE)
         g_inner = [lax.ppermute(part, "lon", inner_pairs(steps)) for part in g_packed]
         g_outer = [
             lax.ppermute(g_inner[0], "lon", onward_pairs(steps)),
@@ -319,7 +323,7 @@
         g_inner, g_outer = beside(cotangent, pack_one(cotangent), SECOND_SPREAD, pack_one)
     if paired(FIRST_SPREAD, width):
         steps = FIRST_SPREAD // width
-        x_packed = pack_one(after(inputs, *g_packed), 2)
+        x_packed = pack_one(after(inputs, *g_packed), X_SHARE)
         x_inner = [lax.ppermute(part, "lon", inner_pairs(steps)) for part in x_packed]
         x_outer = [lax.ppermute(part, "lon", outer_pairs(steps)) for part in x_packed]
     else:
@@ -442,14 +446,14 @@
     def digit_of(stride, radix):
         return lax.rem(lax.axis_index("lon") // stride, radix)
 
-    def combine(own, received, stride, radix, begin, size):
-        m = size // radix
+    def combine(own, received, stride, radix):
+        m = own.shape[0] // radix
 
         def body(own_ref, *refs):
             got, (mine, *sends) = refs[: len(received)], refs[len(received) :]
             digit = digit_of(stride, radix)
             for k, target in enumerate([mine] + sends):
-                at = pl.ds(pl.multiple_of(begin + (digit ^ k) * m, ROW_TILE), m)
+                at = pl.ds(pl.multiple_of((digit ^ k) * m, ROW_TILE), m)
                 value = own_ref[at, :]
                 for ref in got:
                     value = value + ref[at, :].astype(f32)
@@ -458,34 +462,19 @@
         outs = [shape_of((m, LANES), f32)] + [shape_of((m, LANES), bf16)] * (radix - 1)
         return call(body, outs, [own] + received, name="combine")
 
-    unit = flat // pieces
-    unit_rows = [unit]
-    if GROUPS == 2 and unit > ROW_TILE:
-        first_rows = -(-unit // (2 * ROW_TILE)) * ROW_TILE
-        unit_rows = [first_rows, unit - first_rows]
-    begins = [pieces * sum(unit_rows[:i]) for i in range(len(unit_rows))]
-    groups = [(own, received, begin, pieces * rows_) for begin, rows_ in zip(begins, unit_rows)]
     stride = 2
     first_got = None
     for radix in stages[1:]:
-        following = []
-        for own, received, begin, size in groups:
-            own, *sends = combine(own, received, stride, radix, begin, size)
-            received = [swapped(part, count, stride, k + 1) for k, part in enumerate(sends)]
-            following.append((own, received, 0, size // radix))
-            first_got = received[0] if first_got is None else first_got
-        groups = following
+        own, *sends = combine(own, received, stride, radix)
+        received = [swapped(part, count, stride, k + 1) for k, part in enumerate(sends)]
+        first_got = received[0] if first_got is None else first_got
         stride *= radix
     pre_field = pre_grad.reshape(height, width, channels)
     p_rims = rims_of(pre_field, FIRST_SPREAD)
     if paired(FIRST_SPREAD, width):
         steps = FIRST_SPREAD // width
         p_inner = [lax.ppermute(pre_packed, "lon", inner_pairs(steps))]
-        size = pshape[0] // P_PARTS
-        pre_packed = after(pre_packed, first_got)
-        p_outer = [
-            lax.ppermute(pre_packed[i * size : (i + 1) * size], "lon", outer_pairs(steps)) for i in range(P_PARTS)
-        ]
+        p_outer = [lax.ppermute(after(pre_packed, first_got), "lon", outer_pairs(steps))]
     else:
         p_inner, p_outer = beside(pre_field, pre_packed, FIRST_SPREAD, pack_one)
     part3 = near_part(pre_grad, first_weight, p_inner, p_rims, FIRST_SPREAD, True, "near_input_gradient")
@@ -521,61 +510,64 @@
         return call(body, [shape_of(own.shape, bf16)], [own] + received, name="combine_last")[0]
 
     group = stages[1]
-    arrived = []
-    for own, received, _, _ in groups:
-        held = finish(own, received)
-        stride = count
-        for radix in reversed(stages[2:]):
-            stride //= radix
-            held = jnp.concatenate([held] + [swapped(held, count, stride, k) for k in range(1, radix)], axis=0)
-        quarter = [held] + [swapped(held, count, 2, k) for k in range(1, group)]
-        sibling = [swapped(held, count, 1, 1)]
-        sibling += [swapped(after(q, input_gradient), count, 1, 1) for q in quarter[1:]]
-        arrived += quarter + sibling
-
-    def final_body(*refs):
-        (first_out, second_out, both, stage, sems) = refs[len(arrived) :]
-        place = lax.axis_index("lon")
-        mine = lax.rem(place, 2)
-        for i, ref in enumerate(refs[: len(arrived)]):
-            which, side, k = i // (2 * group), i // group % 2, i % group
-            lead = mine if side == 0 else 1 - mine
-            m = unit_rows[which]
-            stride, span = 2 * group, pieces // group
-            walk = [((digit_of(2, group) ^ k) * span, 0)]
-            for radix in stages[2:]:
-                digit = digit_of(stride, radix)
-                span //= radix
-                walk = [(at + (digit ^ j) * span, order + j * span) for at, order in walk for j in range(radix)]
-                stride *= radix
-            for at, order in walk:
-                target = pl.ds(pl.multiple_of(begins[which] + at * m, ROW_TILE), m)
-                both[lead, target, :] = ref[order * m : (order + 1) * m, :].astype(f32)
-        copies = []
-        for which, out in enumerate((second_out, first_out)):
-            for tap, value in enumerate(load_flat(both, which, channels)):
-                stage[which, tap] = (value.T if which else value) * scale
-                copies.append(
-                    pltpu.make_async_copy(
-                        stage.at[which, tap], out.at[tap // 3, tap % 3], sems.at[9 * which + tap]
-                    )
-                )
-                copies[-1].start()
-        for copy in copies:
-            copy.wait()
-
-    first_gradient, second_gradient = call(
-        final_body,
-        [shape_of((3, 3, channels, channels), f32)] * 2,
-        arrived,
-        [
-            pltpu.VMEM((2, flat, LANES), f32),
-            pltpu.VMEM((2, 9, channels, channels), f32),
-            pltpu.SemaphoreType.DMA((18,)),
-        ],
-        name="unpack_gradients",
-        far_outs=(0, 1),
-    )
+    held = finish(own, received)
+    stride = count
+    for radix in reversed(stages[2:]):
+        stride //= radix
+        held = jnp.concatenate([held] + [swapped(held, count, stride, k) for k in range(1, radix)], axis=0)
+    quarter = [held] + [swapped(held, count, 2, k) for k in range(1, group)]
+    sibling = [swapped(held, count, 1, 1)]
+    sibling += [swapped(after(q, input_gradient), count, 1, 1) for q in quarter[1:]]
+    unit = flat // pieces
+
+    def unpack(parts, which, previous):
+        def body(*refs):
+            second_out, first_out, flat_ref, stage, sems = refs[group + len(previous) :]
+            for k, ref in enumerate(refs[:group]):
+                stride, span = 2 * group, pieces // group
+                walk = [((digit_of(2, group) ^ k) * span, 0)]
+                for radix in stages[2:]:
+                    digit = digit_of(stride, radix)
+                    span //= radix
+                    walk = [
+                        (at + (digit ^ j) * span, order + j * span) for at, order in walk for j in range(radix)
+                    ]
+                    stride *= radix
+                for at, order in walk:
+                    target = pl.ds(pl.multiple_of(at * unit, ROW_TILE), unit)
+                    flat_ref[0, target, :] = ref[order * unit : (order + 1) * unit, :].astype(f32)
+            chosen = which(lax.rem(lax.axis_index("lon"), 2))
+
+            def write(out, transposed):
+                copies = []
+                for tap, value in enumerate(load_flat(flat_ref, 0, channels)):
+                    stage[tap] = (value.T if transposed else value) * scale
+                    copies.append(pltpu.make_async_copy(stage.at[tap], out.at[tap // 3, tap % 3], sems.at[tap]))
+                    copies[-1].start()
+                for copy in copies:
+                    copy.wait()
+
+            @pl.when(chosen == 0)
+            def _():
+                write(second_out, False)
+
+            @pl.when(chosen == 1)
+            def _():
+                write(first_out, True)
+
+        return call(
+            body,
+            [shape_of((3, 3, channels, channels), f32)] * 2,
+            parts + previous,
+            [flat_scratch, pltpu.VMEM((9, channels, channels), f32), pltpu.SemaphoreType.DMA((9,))],
+            name="unpack_gradient",
+            far_args=tuple(range(group, group + len(previous))),
+            far_outs=(0, 1),
+            aliases={group + i: i for i in range(len(previous))},
+        )
+
+    own_written = unpack(quarter, lambda core: core, [])
+    second_gradient, first_gradient = unpack(sibling, lambda core: 1 - core, list(own_written))
     return (input_gradient.reshape(height, width, channels), first_gradient, second_gradient)
 
 

time: 80.3 us -> 75.7 us (0.943)
  waiting for transfers between devices: 27.4 us -> 21.2 us
  local copies, waits for them, and re-layouts: 3.33 us -> 4.3 us
    ppermute x4, waiting for transfers between devices: 6.6 us -> 2.2 us  [shards(): lax.ppermute(part, 'lon', inner_pairs(steps))]
    ppermute x1, waiting for transfers between devices: 3.53 us -> 0.01 us  [shards(): lax.ppermute(g_inner[0], 'lon', onward_pairs(steps))]
    ppermute x17, starting transfers between devices: 20.6 us -> 18.3 us  [swapped(): lax.ppermute(value, 'lon', [(i, i ^ k * stride) for i in range(count)])]
    ppermute x2, starting transfers between devices: 5.34 us -> 7.24 us  [shards(): lax.ppermute(part, 'lon', outer_pairs(steps))]
    ppermute x1, waiting for transfers between devices: 0.01 us -> 1.77 us  [shards(): lax.ppermute(g_packed[1], 'lon', outer_pairs(steps))]
    ppermute x1, starting transfers between devices: 3.74 us -> 2.58 us  [shards(): lax.ppermute(after(pre_packed, first_got), 'lon', outer_pairs(steps))]
    unnamed x14, local copies, waits for them, and re-layouts: 3.33 us -> 4.3 us
    pallas_call x14 -> x15, Pallas kernels: 11.8 us -> 12.5 us  [call(): pl.pallas_call(body, out_shape=list(outs), in_specs=[far if i in far_args...]
  transfers between devices with their start and end apart: 27 -> 27, of which waited for: 14 -> 12; matrix products, arithmetic and copies ran while one was open for 0% -> 0% of each run, Pallas kernels for 9% -> 11%
where the time goes in v4:
time: 75.7 us; the launch traced here: 75.4 us
  starting transfers between devices  36.5 us (48%)
  waiting for transfers between devices  21.2 us (28%)
  Pallas kernels  12.5 us (17%)
  local copies, waits for them, and re-layouts  4.3 us (6%)
  between operations  0.87 us (1%)
    ppermute x17, starting transfers between devices, swapped(): lax.ppermute(value, 'lon', [(i, i ^ k * stride) for i in range(count)])  18.3 us
    ppermute x17, waiting for transfers between devices, swapped(): lax.ppermute(value, 'lon', [(i, i ^ k * stride) for i in range(count)])  17.2 us
    pallas_call x15, Pallas kernels, call(): pl.pallas_call(body, out_shape=list(outs), in_specs=[far if i in far_args...  12.5 us
    ppermute x2, starting transfers between devices, shards(): lax.ppermute(part, 'lon', outer_pairs(steps))  7.24 us
    unnamed x14, local copies, waits for them, and re-layouts  4.3 us
    ppermute x1, starting transfers between devices, shards(): lax.ppermute(g_packed[1], 'lon', outer_pairs(steps))  4.02 us
    ppermute x4, starting transfers between devices, shards(): lax.ppermute(part, 'lon', inner_pairs(steps))  3.65 us
    ppermute x1, starting transfers between devices, shards(): lax.ppermute(after(pre_packed, first_got), 'lon', outer_pairs(steps))  2.58 us
  transfers between devices with their start and end apart: 27, of which 12 were waited for; matrix products, arithmetic and copies ran while one was open for 0% of the time, Pallas kernels for 11%

profile of v4, /device:TPU:0, one launch (start us, length us, event | category | flops | bytes accessed | tf_op | source)
XLA Modules:
  0.0 75.4 jit_solution(16635297494515865421)
XLA Ops:
  0.6 1.0 %copy-done.1 = bf16[32,32,192]{2,1,0:T(8,128)(2,1)S(1)} copy-done((bf16[32,32,192]{2,1,0:T(8,128)(2,1)S(1)}, bf16[32,32,192]{2,1,0:T(8,128)(2,1)}, u32[]{:S(2)}) %copy-start.1) | copy-done | bytes 393240
  1.8 3.0 %collective-permute-start = (bf16[832,128]{1,0:T(8,128)(2,1)S(1)}, bf16[832,128]{1,0:T(8,128)(2,1)S(1)}, u32[]{:S(2)}, u32[]{:S(2)}) collective-permute-start(bf16[832,128]{1,0:T(8,128)(2,1)S(1)} %get-tuple-element.29), channel_id=1, source_target_pairs={{0,2},{1,3},{2,0},{3,1},{4,6},{5,7},{6,4},{7,5},{8,10},{9,11},{10,... | collective-permute-start | bytes 638984 | tf_op jit(solution)/shard_map/ppermute | solution.py:317
  4.9 1.0 %copy-done.4 = bf16[32,32,192]{2,1,0:T(8,128)(2,1)S(1)} copy-done((bf16[32,32,192]{2,1,0:T(8,128)(2,1)S(1)}, bf16[32,32,192]{2,1,0:T(8,128)(2,1)}, u32[]{:S(2)}) %copy-start.4) | copy-done | bytes 393240
  6.6 5.6 %collective-permute-start.5 = (bf16[896,128]{1,0:T(8,128)(2,1)S(1)}, bf16[896,128]{1,0:T(8,128)(2,1)S(1)}, u32[]{:S(2)}, u32[]{:S(2)}) collective-permute-start(bf16[896,128]{1,0:T(8,128)(2,1)S(1)} %get-tuple-element.33), channel_id=1, source_target_pairs={{0,31},{1,2},{2,1},{3,4},{4,3},{5,6},{6,5},{7,8},{8,7},{9,10},{10,... | collective-permute-start | bytes 688136 | tf_op jit(solution)/shard_map/ppermute | solution.py:328
  13.0 1.6 %collective-permute-start.4 = (bf16[640,128]{1,0:T(8,128)(2,1)S(1)}, bf16[640,128]{1,0:T(8,128)(2,1)S(1)}, u32[]{:S(2)}, u32[]{:S(2)}) collective-permute-start(bf16[640,128]{1,0:T(8,128)(2,1)S(1)} %get-tuple-element.32), channel_id=1, source_target_pairs={{0,31},{1,2},{2,1},{3,4},{4,3},{5,6},{6,5},{7,8},{8,7},{9,10},{10,... | collective-permute-start | bytes 491528 | tf_op jit(solution)/shard_map/ppermute | solution.py:328
  14.6 2.2 %collective-permute-done.1.rest_1_.rest_5_ = bf16[704,128]{1,0:T(8,128)(2,1)S(1)} collective-permute-done((bf16[704,128]{1,0:T(8,128)(2,1)S(1)}, bf16[704,128]{1,0:T(8,128)(2,1)S(1)}, u32[]{:S(2)}, u32[]{:S(2)}) %collective-permute-start.1) | collective-permute-done | bytes 180256 | tf_op jit(solution)/shard_map/ppermute | solution.py:317
  16.8 4.0 %collective-permute-start.7 = (bf16[704,128]{1,0:T(8,128)(2,1)S(1)}, bf16[704,128]{1,0:T(8,128)(2,1)S(1)}, u32[]{:S(2)}, u32[]{:S(2)}) collective-permute-start(bf16[704,128]{1,0:T(8,128)(2,1)S(1)} %get-tuple-element.30), channel_id=1, source_target_pairs={{0,30},{1,31},{2,4},{3,5},{4,2},{5,3},{6,8},{7,9},{8,6},{9,7},{10,... | collective-permute-start | bytes 540680 | tf_op jit(solution)/shard_map/ppermute | solution.py:320
  20.8 1.0 %copy-done.2 = bf16[32,32,192]{2,1,0:T(8,128)(2,1)S(1)} copy-done((bf16[32,32,192]{2,1,0:T(8,128)(2,1)S(1)}, bf16[32,32,192]{2,1,0:T(8,128)(2,1)}, u32[]{:S(2)}) %copy-start.2) | copy-done | bytes 393240
  21.9 1.2 %copy-done.6 = bf16[3,3,192,192]{3,2,1,0:T(8,128)(2,1)S(1)} copy-done((bf16[3,3,192,192]{3,2,1,0:T(8,128)(2,1)S(1)}, bf16[3,3,192,192]{3,2,1,0:T(8,128)(2,1)}, u32[]{:S(2)}) %copy-start.6) | copy-done | bytes 663576
  23.0 1.0 %near_hidden_grad.1.part_ref = f32[1024,192]{1,0:T(8,128)S(1)} custom-call(bf16[1024,192]{1,0:T(8,128)(2,1)S(1)} %bitcast.5, bf16[3,3,192,192]{3,2,1,0:T(8,128)(2,1)S(1)} %copy-done.6, bf16[832,128]{1,0:T(8,128)(2,1)S(1)} %collective-permute-done.rest_0_.rest_4_, bf16[704,128]{1,0:T(8,128)(2,1)S(1)} %collective-permute-done.1.rest_1_.rest_5_), custom_call_target="tpu_custom_call" | custom-call | flops 452984832 | bytes 2236416 | tf_op jit(solution)/shard_map/near_hidden_grad/pallas_call | solution.py:22
  25.9 1.8 %collective-permute-done.7.rest_1_.rest_7_ = bf16[704,128]{1,0:T(8,128)(2,1)S(1)} collective-permute-done((bf16[704,128]{1,0:T(8,128)(2,1)S(1)}, bf16[704,128]{1,0:T(8,128)(2,1)S(1)}, u32[]{:S(2)}, u32[]{:S(2)}) %collective-permute-start.7) | collective-permute-done | bytes 180256 | tf_op jit(solution)/shard_map/ppermute | solution.py:320
  28.5 1.5 %sibling_kernel_gradient.1 = bf16[2816,128]{1,0:T(8,128)(2,1)S(1)} custom-call(bf16[192,1024]{1,0:T(8,128)(2,1)S(1)} %get-tuple-element.37.hid_ref, bf16[192,1024]{1,0:T(8,128)(2,1)S(1)} %get-tuple-element.38.pre_ref, bf16[1024,192]{1,0:T(8,128)(2,1)S(1)} %bitcast.10, bf16[1024,192]{1,0:T(8,128)(2,1)S(1)} %bitcast.6, ...), custom_call_target="tpu_custom_call" | custom-call | flops 679477248 | bytes 3866624 | tf_op jit(solution)/shard_map/sibling_kernel_gradient/pallas_call | solution.py:22
  30.1 1.5 %own_kernel_gradient.1.own_ref = f32[2816,128]{1,0:T(8,128)S(1)} custom-call(bf16[192,1024]{1,0:T(8,128)(2,1)S(1)} %get-tuple-element.37.hid_ref, bf16[192,1024]{1,0:T(8,128)(2,1)S(1)} %get-tuple-element.38.pre_ref, bf16[1024,192]{1,0:T(8,128)(2,1)S(1)} %bitcast.11, bf16[1024,192]{1,0:T(8,128)(2,1)S(1)} %bitcast.7, ...), custom_call_target="tpu_custom_call" | custom-call | flops 679477248 | bytes 4587520 | tf_op jit(solution)/shard_map/own_kernel_gradient/pallas_call | solution.py:22
  32.4 1.4 %collective-permute-start.10 = (bf16[704,128]{1,0:T(8,128)(2,1)S(1)}, bf16[704,128]{1,0:T(8,128)(2,1)S(1)}, u32[]{:S(2)}, u32[]{:S(2)}) collective-permute-start(bf16[704,128]{1,0:T(8,128)(2,1)S(1)} %get-tuple-element.39), channel_id=1, source_target_pairs={{0,2},{1,3},{2,0},{3,1},{4,6},{5,7},{6,4},{7,5},{8,10},{9,11},{10,... | collective-permute-start | bytes 540680 | tf_op jit(solution)/shard_map/ppermute | solution.py:187
  33.8 2.2 %collective-permute-start.13 = (bf16[704,128]{1,0:T(8,128)(2,1)S(1)}, bf16[704,128]{1,0:T(8,128)(2,1)S(1)}, u32[]{:S(2)}, u32[]{:S(2)}) collective-permute-start(bf16[704,128]{1,0:T(8,128)(2,1)S(1)} %get-tuple-element.43), channel_id=1, source_target_pairs={{0,6},{1,7},{2,4},{3,5},{4,2},{5,3},{6,0},{7,1},{8,14},{9,15},{10,... | collective-permute-start | bytes 540680 | tf_op jit(solution)/shard_map/ppermute | solution.py:187
  35.9 3.9 %collective-permute-done.10.refs_0_ = bf16[704,128]{1,0:T(8,128)(2,1)S(1)} collective-permute-done((bf16[704,128]{1,0:T(8,128)(2,1)S(1)}, bf16[704,128]{1,0:T(8,128)(2,1)S(1)}, u32[]{:S(2)}, u32[]{:S(2)}) %collective-permute-start.10) | collective-permute-done | bytes 180256 | tf_op jit(solution)/shard_map/ppermute | solution.py:187
  39.8 2.6 %collective-permute-start.11 = (bf16[1536,128]{1,0:T(8,128)(2,1)S(1)}, bf16[1536,128]{1,0:T(8,128)(2,1)S(1)}, u32[]{:S(2)}, u32[]{:S(2)}) collective-permute-start(bf16[1536,128]{1,0:T(8,128)(2,1)S(1)} %get-tuple-element.40), channel_id=1, source_target_pairs={{0,31},{1,2},{2,1},{3,4},{4,3},{5,6},{6,5},{7,8},{8,7},{9,10},{10,... | collective-permute-start | bytes 1179656 | tf_op jit(solution)/shard_map/ppermute | solution.py:477
  42.4 1.5 %collective-permute-done.12.refs_1_ = bf16[704,128]{1,0:T(8,128)(2,1)S(1)} collective-permute-done((bf16[704,128]{1,0:T(8,128)(2,1)S(1)}, bf16[704,128]{1,0:T(8,128)(2,1)S(1)}, u32[]{:S(2)}, u32[]{:S(2)}) %collective-permute-start.12) | collective-permute-done | bytes 180256 | tf_op jit(solution)/shard_map/ppermute | solution.py:187
  44.0 2.2 %collective-permute-done.13.refs_2_ = bf16[704,128]{1,0:T(8,128)(2,1)S(1)} collective-permute-done((bf16[704,128]{1,0:T(8,128)(2,1)S(1)}, bf16[704,128]{1,0:T(8,128)(2,1)S(1)}, u32[]{:S(2)}, u32[]{:S(2)}) %collective-permute-start.13) | collective-permute-done | bytes 180256 | tf_op jit(solution)/shard_map/ppermute | solution.py:187
  46.3 1.5 %collective-permute-start.14 = (bf16[176,128]{1,0:T(8,128)(2,1)S(1)}, bf16[176,128]{1,0:T(8,128)(2,1)S(1)}, u32[]{:S(2)}, u32[]{:S(2)}) collective-permute-start(bf16[176,128]{1,0:T(8,128)(2,1)S(1)} %get-tuple-element.45), channel_id=1, source_target_pairs={{0,8},{1,9},{2,10},{3,11},{4,12},{5,13},{6,14},{7,15},{8,0},{9,1},... | collective-permute-start | bytes 135176 | tf_op jit(solution)/shard_map/ppermute | solution.py:187
  48.5 2.3 %collective-permute-start.16 = (bf16[176,128]{1,0:T(8,128)(2,1)S(1)}, bf16[176,128]{1,0:T(8,128)(2,1)S(1)}, u32[]{:S(2)}, u32[]{:S(2)}) collective-permute-start(bf16[176,128]{1,0:T(8,128)(2,1)S(1)} %get-tuple-element.47), channel_id=1, source_target_pairs={{0,24},{1,25},{2,26},{3,27},{4,28},{5,29},{6,30},{7,31},{8,16},{9,... | collective-permute-start | bytes 135176 | tf_op jit(solution)/shard_map/ppermute | solution.py:187
  50.8 2.5 %collective-permute-done.15.refs_1_ = bf16[176,128]{1,0:T(8,128)(2,1)S(1)} collective-permute-done((bf16[176,128]{1,0:T(8,128)(2,1)S(1)}, bf16[176,128]{1,0:T(8,128)(2,1)S(1)}, u32[]{:S(2)}, u32[]{:S(2)}) %collective-permute-start.15) | collective-permute-done | bytes 45088 | tf_op jit(solution)/shard_map/ppermute | solution.py:187
  53.3 1.1 %collective-permute-done.16.refs_2_ = bf16[176,128]{1,0:T(8,128)(2,1)S(1)} collective-permute-done((bf16[176,128]{1,0:T(8,128)(2,1)S(1)}, bf16[176,128]{1,0:T(8,128)(2,1)S(1)}, u32[]{:S(2)}, u32[]{:S(2)}) %collective-permute-start.16) | collective-permute-done | bytes 45088 | tf_op jit(solution)/shard_map/ppermute | solution.py:187
  54.4 2.3 %collective-permute-start.19 = (bf16[176,128]{1,0:T(8,128)(2,1)S(1)}, bf16[176,128]{1,0:T(8,128)(2,1)S(1)}, u32[]{:S(2)}, u32[]{:S(2)}) collective-permute-start(bf16[176,128]{1,0:T(8,128)(2,1)S(1)} %combine_last.1), channel_id=1, source_target_pairs={{0,24},{1,25},{2,26},{3,27},{4,28},{5,29},{6,30},{7,31},{8,16},{9,... | collective-permute-start | bytes 135176 | tf_op jit(solution)/shard_map/ppermute | solution.py:187
  56.7 2.2 %collective-permute-start.17 = (bf16[176,128]{1,0:T(8,128)(2,1)S(1)}, bf16[176,128]{1,0:T(8,128)(2,1)S(1)}, u32[]{:S(2)}, u32[]{:S(2)}) collective-permute-start(bf16[176,128]{1,0:T(8,128)(2,1)S(1)} %combine_last.1), channel_id=1, source_target_pairs={{0,8},{1,9},{2,10},{3,11},{4,12},{5,13},{6,14},{7,15},{8,0},{9,1},... | collective-permute-start | bytes 135176 | tf_op jit(solution)/shard_map/ppermute | solution.py:187
  58.8 1.5 %collective-permute-done.19 = bf16[176,128]{1,0:T(8,128)(2,1)S(1)} collective-permute-done((bf16[176,128]{1,0:T(8,128)(2,1)S(1)}, bf16[176,128]{1,0:T(8,128)(2,1)S(1)}, u32[]{:S(2)}, u32[]{:S(2)}) %collective-permute-start.19) | collective-permute-done | bytes 45088 | tf_op jit(solution)/shard_map/ppermute | solution.py:187
  60.3 1.3 %collective-permute-done.18 = bf16[176,128]{1,0:T(8,128)(2,1)S(1)} collective-permute-done((bf16[176,128]{1,0:T(8,128)(2,1)S(1)}, bf16[176,128]{1,0:T(8,128)(2,1)S(1)}, u32[]{:S(2)}, u32[]{:S(2)}) %collective-permute-start.18) | collective-permute-done | bytes 45088 | tf_op jit(solution)/shard_map/ppermute | solution.py:187
  61.7 4.6 %collective-permute-start.25 = (bf16[704,128]{1,0:T(8,128)(2,1)S(1)}, bf16[704,128]{1,0:T(8,128)(2,1)S(1)}, u32[]{:S(2)}, u32[]{:S(2)}) collective-permute-start(bf16[704,128]{1,0:T(8,128)(2,1)S(1)} %pad_maximum_fusion.refs_0_), channel_id=1, source_target_pairs={{0,6},{1,7},{2,4},{3,5},{4,2},{5,3},{6,0},{7,1},{8,14},{9,15},{10,... | collective-permute-start | bytes 540680 | tf_op jit(solution)/shard_map/ppermute | solution.py:187
  67.9 1.4 %input_gradient.1 = bf16[1024,192]{1,0:T(8,128)(2,1)} custom-call(f32[1024,192]{1,0:T(8,128)S(1)} %near_input_gradient.1.part_ref, bf16[3,3,192,192]{3,2,1,0:T(8,128)(2,1)S(1)} %copy-done, bf16[1536,128]{1,0:T(8,128)(2,1)S(1)} %collective-permute-done.11.rest_0_), custom_call_target="tpu_custom_call" | custom-call | flops 226492416 | bytes 2236416 | tf_op jit(solution)/shard_map/input_gradient/pallas_call | solution.py:22
  69.7 2.0 %collective-permute-done.23.refs_2_ = bf16[704,128]{1,0:T(8,128)(2,1)S(1)} collective-permute-done((bf16[704,128]{1,0:T(8,128)(2,1)S(1)}, bf16[704,128]{1,0:T(8,128)(2,1)S(1)}, u32[]{:S(2)}, u32[]{:S(2)}) %collective-permute-start.23) | collective-permute-done | bytes 180256 | tf_op jit(solution)/shard_map/ppermute | solution.py:187
  72.2 1.4 %unpack_gradient.2 = (f32[3,3,192,192]{3,2,1,0:T(8,128)}, f32[3,3,192,192]{3,2,1,0:T(8,128)}) custom-call(bf16[704,128]{1,0:T(8,128)(2,1)S(1)} %pad_maximum_fusion.refs_0_, bf16[704,128]{1,0:T(8,128)(2,1)S(1)} %collective-permute-done.21.refs_1_, bf16[704,128]{1,0:T(8,128)(2,1)S(1)} %collective-permute-done.23.refs_2_, ...), custom_call_target="tpu_custom_call" | custom-call | bytes 3375104 | tf_op jit(solution)/shard_map/unpack_gradient/pallas_call | solution.py:22
  73.7 1.7 %unpack_gradient.3 = (f32[3,3,192,192]{3,2,1,0:T(8,128)}, f32[3,3,192,192]{3,2,1,0:T(8,128)}) custom-call(bf16[704,128]{1,0:T(8,128)(2,1)S(1)} %collective-permute-done.20.refs_0_, bf16[704,128]{1,0:T(8,128)(2,1)S(1)} %collective-permute-done.22.refs_1_, ...), custom_call_target="tpu_custom_call", output_to_operand_aliasing={{0}: (4, {}), {1}: (5, {})} | custom-call | bytes 6029312 | tf_op jit(solution)/shard_map/unpack_gradient/pallas_call | solution.py:22
  (52 shorter events, 8.6 us)
Async XLA Ops:
  0.6 1.0 %copy-start.1 = (bf16[32,32,192]{2,1,0:T(8,128)(2,1)S(1)}, bf16[32,32,192]{2,1,0:T(8,128)(2,1)}, u32[]{:S(2)}) copy-start(bf16[32,32,192]{2,1,0:T(8,128)(2,1)} %param.5) | copy-start | bytes 1179652
  1.7 22.4 %copy-start.5 = (bf16[32,32,192]{2,1,0:T(8,128)(2,1)S(1)}, bf16[32,32,192]{2,1,0:T(8,128)(2,1)}, u32[]{:S(2)}) copy-start(bf16[32,32,192]{2,1,0:T(8,128)(2,1)} %param.4) | copy-start | bytes 1179652
  1.8 22.2 %copy-start = (bf16[3,3,192,192]{3,2,1,0:T(8,128)(2,1)S(1)}, bf16[3,3,192,192]{3,2,1,0:T(8,128)(2,1)}, u32[]{:S(2)}) copy-start(bf16[3,3,192,192]{3,2,1,0:T(8,128)(2,1)} %w_ref.11) | copy-start | bytes 1990660
  1.8 10.4 %collective-permute-start = (bf16[832,128]{1,0:T(8,128)(2,1)S(1)}, bf16[832,128]{1,0:T(8,128)(2,1)S(1)}, u32[]{:S(2)}, u32[]{:S(2)}) collective-permute-start(bf16[832,128]{1,0:T(8,128)(2,1)S(1)} %get-tuple-element.29), channel_id=1, source_target_pairs={{0,2},{1,3},{2,0},{3,1},{4,6},{5,7},{6,4},{7,5},{8,10},{9,11},{10,... | collective-permute-start | bytes 638984 | tf_op jit(solution)/shard_map/ppermute | solution.py:317
  4.8 12.0 %collective-permute-start.1 = (bf16[704,128]{1,0:T(8,128)(2,1)S(1)}, bf16[704,128]{1,0:T(8,128)(2,1)S(1)}, u32[]{:S(2)}, u32[]{:S(2)}) collective-permute-start(bf16[704,128]{1,0:T(8,128)(2,1)S(1)} %get-tuple-element.30), channel_id=1, source_target_pairs={{0,2},{1,3},{2,0},{3,1},{4,6},{5,7},{6,4},{7,5},{8,10},{9,11},{10,... | collective-permute-start | bytes 540680 | tf_op jit(solution)/shard_map/ppermute | solution.py:317
  6.1 6.9 %collective-permute-start.2 = (bf16[640,128]{1,0:T(8,128)(2,1)S(1)}, bf16[640,128]{1,0:T(8,128)(2,1)S(1)}, u32[]{:S(2)}, u32[]{:S(2)}) collective-permute-start(bf16[640,128]{1,0:T(8,128)(2,1)S(1)} %get-tuple-element.32), channel_id=1, source_target_pairs={{0,1},{1,0},{2,3},{3,2},{4,5},{5,4},{6,7},{7,6},{8,9},{9,8},{10,11... | collective-permute-start | bytes 491528 | tf_op jit(solution)/shard_map/ppermute | solution.py:327
  6.1 17.9 %collective-permute-start.3 = (bf16[896,128]{1,0:T(8,128)(2,1)S(1)}, bf16[896,128]{1,0:T(8,128)(2,1)S(1)}, u32[]{:S(2)}, u32[]{:S(2)}) collective-permute-start(bf16[896,128]{1,0:T(8,128)(2,1)S(1)} %get-tuple-element.33), channel_id=1, source_target_pairs={{0,1},{1,0},{2,3},{3,2},{4,5},{5,4},{6,7},{7,6},{8,9},{9,8},{10,11... | collective-permute-start | bytes 688136 | tf_op jit(solution)/shard_map/ppermute | solution.py:327
  6.6 18.4 %collective-permute-start.5 = (bf16[896,128]{1,0:T(8,128)(2,1)S(1)}, bf16[896,128]{1,0:T(8,128)(2,1)S(1)}, u32[]{:S(2)}, u32[]{:S(2)}) collective-permute-start(bf16[896,128]{1,0:T(8,128)(2,1)S(1)} %get-tuple-element.33), channel_id=1, source_target_pairs={{0,31},{1,2},{2,1},{3,4},{4,3},{5,6},{6,5},{7,8},{8,7},{9,10},{10,... | collective-permute-start | bytes 688136 | tf_op jit(solution)/shard_map/ppermute | solution.py:328
  12.3 15.4 %collective-permute-start.6 = (bf16[832,128]{1,0:T(8,128)(2,1)S(1)}, bf16[832,128]{1,0:T(8,128)(2,1)S(1)}, u32[]{:S(2)}, u32[]{:S(2)}) collective-permute-start(bf16[832,128]{1,0:T(8,128)(2,1)S(1)} %collective-permute-done.rest_0_.rest_4_), channel_id=1, source_target_pairs={{0,4},{1,5},{2,30},{3,31},{4,8},{5,9},{6,2},{7,3},{8,12},{9,13},{1... | collective-permute-start | bytes 638984 | tf_op jit(solution)/shard_map/ppermute | solution.py:319
  13.0 12.0 %collective-permute-start.4 = (bf16[640,128]{1,0:T(8,128)(2,1)S(1)}, bf16[640,128]{1,0:T(8,128)(2,1)S(1)}, u32[]{:S(2)}, u32[]{:S(2)}) collective-permute-start(bf16[640,128]{1,0:T(8,128)(2,1)S(1)} %get-tuple-element.32), channel_id=1, source_target_pairs={{0,31},{1,2},{2,1},{3,4},{4,3},{5,6},{6,5},{7,8},{8,7},{9,10},{10,... | collective-permute-start | bytes 491528 | tf_op jit(solution)/shard_map/ppermute | solution.py:328
  16.8 10.9 %collective-permute-start.7 = (bf16[704,128]{1,0:T(8,128)(2,1)S(1)}, bf16[704,128]{1,0:T(8,128)(2,1)S(1)}, u32[]{:S(2)}, u32[]{:S(2)}) collective-permute-start(bf16[704,128]{1,0:T(8,128)(2,1)S(1)} %get-tuple-element.30), channel_id=1, source_target_pairs={{0,30},{1,31},{2,4},{3,5},{4,2},{5,3},{6,8},{7,9},{8,6},{9,7},{10,... | collective-permute-start | bytes 540680 | tf_op jit(solution)/shard_map/ppermute | solution.py:320
  21.9 1.2 %copy-start.6 = (bf16[3,3,192,192]{3,2,1,0:T(8,128)(2,1)S(1)}, bf16[3,3,192,192]{3,2,1,0:T(8,128)(2,1)}, u32[]{:S(2)}) copy-start(bf16[3,3,192,192]{3,2,1,0:T(8,128)(2,1)} %w_ref.9) | copy-start | bytes 1990660
  25.9 2.6 %copy-start.3 = (bf16[32,32,192]{2,1,0:T(8,128)(2,1)S(1)}, bf16[32,32,192]{2,1,0:T(8,128)(2,1)}, u32[]{:S(2)}) copy-start(bf16[32,32,192]{2,1,0:T(8,128)(2,1)} %param.5) | copy-start | bytes 1179652
  30.0 2.3 %collective-permute-start.9 = (bf16[2816,128]{1,0:T(8,128)(2,1)S(1)}, bf16[2816,128]{1,0:T(8,128)(2,1)S(1)}, u32[]{:S(2)}, u32[]{:S(2)}) collective-permute-start(bf16[2816,128]{1,0:T(8,128)(2,1)S(1)} %sibling_kernel_gradient.1), channel_id=1, source_target_pairs={{0,1},{1,0},{2,3},{3,2},{4,5},{5,4},{6,7},{7,6},{8,9},{9,8},{10,11... | collective-permute-start | bytes 2162696 | tf_op jit(solution)/shard_map/ppermute | solution.py:187
  32.4 7.5 %collective-permute-start.10 = (bf16[704,128]{1,0:T(8,128)(2,1)S(1)}, bf16[704,128]{1,0:T(8,128)(2,1)S(1)}, u32[]{:S(2)}, u32[]{:S(2)}) collective-permute-start(bf16[704,128]{1,0:T(8,128)(2,1)S(1)} %get-tuple-element.39), channel_id=1, source_target_pairs={{0,2},{1,3},{2,0},{3,1},{4,6},{5,7},{6,4},{7,5},{8,10},{9,11},{10,... | collective-permute-start | bytes 540680 | tf_op jit(solution)/shard_map/ppermute | solution.py:187
  33.8 10.2 %collective-permute-start.12 = (bf16[704,128]{1,0:T(8,128)(2,1)S(1)}, bf16[704,128]{1,0:T(8,128)(2,1)S(1)}, u32[]{:S(2)}, u32[]{:S(2)}) collective-permute-start(bf16[704,128]{1,0:T(8,128)(2,1)S(1)} %get-tuple-element.42), channel_id=1, source_target_pairs={{0,4},{1,5},{2,6},{3,7},{4,0},{5,1},{6,2},{7,3},{8,12},{9,13},{10,... | collective-permute-start | bytes 540680 | tf_op jit(solution)/shard_map/ppermute | solution.py:187
  33.8 12.4 %collective-permute-start.13 = (bf16[704,128]{1,0:T(8,128)(2,1)S(1)}, bf16[704,128]{1,0:T(8,128)(2,1)S(1)}, u32[]{:S(2)}, u32[]{:S(2)}) collective-permute-start(bf16[704,128]{1,0:T(8,128)(2,1)S(1)} %get-tuple-element.43), channel_id=1, source_target_pairs={{0,6},{1,7},{2,4},{3,5},{4,2},{5,3},{6,0},{7,1},{8,14},{9,15},{10,... | collective-permute-start | bytes 540680 | tf_op jit(solution)/shard_map/ppermute | solution.py:187
  35.9 30.9 %collective-permute-start.8 = (bf16[1536,128]{1,0:T(8,128)(2,1)S(1)}, bf16[1536,128]{1,0:T(8,128)(2,1)S(1)}, u32[]{:S(2)}, u32[]{:S(2)}) collective-permute-start(bf16[1536,128]{1,0:T(8,128)(2,1)S(1)} %get-tuple-element.40), channel_id=1, source_target_pairs={{0,1},{1,0},{2,3},{3,2},{4,5},{5,4},{6,7},{7,6},{8,9},{9,8},{10,11... | collective-permute-start | bytes 1179656 | tf_op jit(solution)/shard_map/ppermute | solution.py:476
  39.8 28.1 %collective-permute-start.11 = (bf16[1536,128]{1,0:T(8,128)(2,1)S(1)}, bf16[1536,128]{1,0:T(8,128)(2,1)S(1)}, u32[]{:S(2)}, u32[]{:S(2)}) collective-permute-start(bf16[1536,128]{1,0:T(8,128)(2,1)S(1)} %get-tuple-element.40), channel_id=1, source_target_pairs={{0,31},{1,2},{2,1},{3,4},{4,3},{5,6},{6,5},{7,8},{8,7},{9,10},{10,... | collective-permute-start | bytes 1179656 | tf_op jit(solution)/shard_map/ppermute | solution.py:477
  46.3 4.5 %collective-permute-start.14 = (bf16[176,128]{1,0:T(8,128)(2,1)S(1)}, bf16[176,128]{1,0:T(8,128)(2,1)S(1)}, u32[]{:S(2)}, u32[]{:S(2)}) collective-permute-start(bf16[176,128]{1,0:T(8,128)(2,1)S(1)} %get-tuple-element.45), channel_id=1, source_target_pairs={{0,8},{1,9},{2,10},{3,11},{4,12},{5,13},{6,14},{7,15},{8,0},{9,1},... | collective-permute-start | bytes 135176 | tf_op jit(solution)/shard_map/ppermute | solution.py:187
  47.8 5.5 %collective-permute-start.15 = (bf16[176,128]{1,0:T(8,128)(2,1)S(1)}, bf16[176,128]{1,0:T(8,128)(2,1)S(1)}, u32[]{:S(2)}, u32[]{:S(2)}) collective-permute-start(bf16[176,128]{1,0:T(8,128)(2,1)S(1)} %get-tuple-element.46), channel_id=1, source_target_pairs={{0,16},{1,17},{2,18},{3,19},{4,20},{5,21},{6,22},{7,23},{8,24},{9,... | collective-permute-start | bytes 135176 | tf_op jit(solution)/shard_map/ppermute | solution.py:187
  48.5 5.9 %collective-permute-start.16 = (bf16[176,128]{1,0:T(8,128)(2,1)S(1)}, bf16[176,128]{1,0:T(8,128)(2,1)S(1)}, u32[]{:S(2)}, u32[]{:S(2)}) collective-permute-start(bf16[176,128]{1,0:T(8,128)(2,1)S(1)} %get-tuple-element.47), channel_id=1, source_target_pairs={{0,24},{1,25},{2,26},{3,27},{4,28},{5,29},{6,30},{7,31},{8,16},{9,... | collective-permute-start | bytes 135176 | tf_op jit(solution)/shard_map/ppermute | solution.py:187
  54.4 5.9 %collective-permute-start.19 = (bf16[176,128]{1,0:T(8,128)(2,1)S(1)}, bf16[176,128]{1,0:T(8,128)(2,1)S(1)}, u32[]{:S(2)}, u32[]{:S(2)}) collective-permute-start(bf16[176,128]{1,0:T(8,128)(2,1)S(1)} %combine_last.1), channel_id=1, source_target_pairs={{0,24},{1,25},{2,26},{3,27},{4,28},{5,29},{6,30},{7,31},{8,16},{9,... | collective-permute-start | bytes 135176 | tf_op jit(solution)/shard_map/ppermute | solution.py:187
  56.7 4.9 %collective-permute-start.18 = (bf16[176,128]{1,0:T(8,128)(2,1)S(1)}, bf16[176,128]{1,0:T(8,128)(2,1)S(1)}, u32[]{:S(2)}, u32[]{:S(2)}) collective-permute-start(bf16[176,128]{1,0:T(8,128)(2,1)S(1)} %combine_last.1), channel_id=1, source_target_pairs={{0,16},{1,17},{2,18},{3,19},{4,20},{5,21},{6,22},{7,23},{8,24},{9,... | collective-permute-start | bytes 135176 | tf_op jit(solution)/shard_map/ppermute | solution.py:187
  56.7 4.9 %collective-permute-start.17 = (bf16[176,128]{1,0:T(8,128)(2,1)S(1)}, bf16[176,128]{1,0:T(8,128)(2,1)S(1)}, u32[]{:S(2)}, u32[]{:S(2)}) collective-permute-start(bf16[176,128]{1,0:T(8,128)(2,1)S(1)} %combine_last.1), channel_id=1, source_target_pairs={{0,8},{1,9},{2,10},{3,11},{4,12},{5,13},{6,14},{7,15},{8,0},{9,1},... | collective-permute-start | bytes 135176 | tf_op jit(solution)/shard_map/ppermute | solution.py:187
  61.7 8.0 %collective-permute-start.25 = (bf16[704,128]{1,0:T(8,128)(2,1)S(1)}, bf16[704,128]{1,0:T(8,128)(2,1)S(1)}, u32[]{:S(2)}, u32[]{:S(2)}) collective-permute-start(bf16[704,128]{1,0:T(8,128)(2,1)S(1)} %pad_maximum_fusion.refs_0_), channel_id=1, source_target_pairs={{0,6},{1,7},{2,4},{3,5},{4,2},{5,3},{6,0},{7,1},{8,14},{9,15},{10,... | collective-permute-start | bytes 540680 | tf_op jit(solution)/shard_map/ppermute | solution.py:187
  66.2 5.5 %collective-permute-start.23 = (bf16[704,128]{1,0:T(8,128)(2,1)S(1)}, bf16[704,128]{1,0:T(8,128)(2,1)S(1)}, u32[]{:S(2)}, u32[]{:S(2)}) collective-permute-start(bf16[704,128]{1,0:T(8,128)(2,1)S(1)} %pad_maximum_fusion.refs_0_), channel_id=1, source_target_pairs={{0,4},{1,5},{2,6},{3,7},{4,0},{5,1},{6,2},{7,3},{8,12},{9,13},{10,... | collective-permute-start | bytes 540680 | tf_op jit(solution)/shard_map/ppermute | solution.py:187
  66.2 5.5 %collective-permute-start.21 = (bf16[704,128]{1,0:T(8,128)(2,1)S(1)}, bf16[704,128]{1,0:T(8,128)(2,1)S(1)}, u32[]{:S(2)}, u32[]{:S(2)}) collective-permute-start(bf16[704,128]{1,0:T(8,128)(2,1)S(1)} %pad_maximum_fusion.refs_0_), channel_id=1, source_target_pairs={{0,2},{1,3},{2,0},{3,1},{4,6},{5,7},{6,4},{7,5},{8,10},{9,11},{10,... | collective-permute-start | bytes 540680 | tf_op jit(solution)/shard_map/ppermute | solution.py:187
  67.9 5.8 %collective-permute-start.20 = (bf16[704,128]{1,0:T(8,128)(2,1)S(1)}, bf16[704,128]{1,0:T(8,128)(2,1)S(1)}, u32[]{:S(2)}, u32[]{:S(2)}) collective-permute-start(bf16[704,128]{1,0:T(8,128)(2,1)S(1)} %pad_maximum_fusion.refs_0_), channel_id=1, source_target_pairs={{0,1},{1,0},{2,3},{3,2},{4,5},{5,4},{6,7},{7,6},{8,9},{9,8},{10,11... | collective-permute-start | bytes 540680 | tf_op jit(solution)/shard_map/ppermute | solution.py:187
  71.7 2.0 %collective-permute-start.22 = (bf16[704,128]{1,0:T(8,128)(2,1)S(1)}, bf16[704,128]{1,0:T(8,128)(2,1)S(1)}, u32[]{:S(2)}, u32[]{:S(2)}) collective-permute-start(bf16[704,128]{1,0:T(8,128)(2,1)S(1)} %collective-permute-done.21.refs_1_), channel_id=1, source_target_pairs={{0,1},{1,0},{2,3},{3,2},{4,5},{5,4},{6,7},{7,6},{8,9},{9,8},{10,11... | collective-permute-start | bytes 540680 | tf_op jit(solution)/shard_map/ppermute | solution.py:187
  71.7 2.0 %collective-permute-start.24 = (bf16[704,128]{1,0:T(8,128)(2,1)S(1)}, bf16[704,128]{1,0:T(8,128)(2,1)S(1)}, u32[]{:S(2)}, u32[]{:S(2)}) collective-permute-start(bf16[704,128]{1,0:T(8,128)(2,1)S(1)} %collective-permute-done.23.refs_2_), channel_id=1, source_target_pairs={{0,1},{1,0},{2,3},{3,2},{4,5},{5,4},{6,7},{7,6},{8,9},{9,8},{10,11... | collective-permute-start | bytes 540680 | tf_op jit(solution)/shard_map/ppermute | solution.py:187
  72.2 1.5 %collective-permute-start.26 = (bf16[704,128]{1,0:T(8,128)(2,1)S(1)}, bf16[704,128]{1,0:T(8,128)(2,1)S(1)}, u32[]{:S(2)}, u32[]{:S(2)}) collective-permute-start(bf16[704,128]{1,0:T(8,128)(2,1)S(1)} %collective-permute-done.25.refs_3_), channel_id=1, source_target_pairs={{0,1},{1,0},{2,3},{3,2},{4,5},{5,4},{6,7},{7,6},{8,9},{9,8},{10,11... | collective-permute-start | bytes 540680 | tf_op jit(solution)/shard_map/ppermute | solution.py:187
  (2 other events, 2.1 us)

commit v5 on v4

--- a/solution.py
+++ b/solution.py
@@ -11,9 +11,9 @@
 SECOND_SPREAD = 64
 LANES = 128
 ROW_TILE = 16
-G_SHARE = 13 / 24
-X_SHARE = 5 / 12
-VMEM_LIMIT = 48 * 1024 * 1024
+G_SHARE = 5 / 8
+X_SHARE = 1 / 2
+VMEM_LIMIT = 20 * 1024 * 1024
 
 
 def call(body, outs, args, scratch=(), flops=0, name=None, far_args=(), far_outs=(), aliases={}):
@@ -108,63 +108,56 @@
     return total
 
 
-def flat_rows(channels, pieces):
-    if channels % LANES * 2 != LANES:
-        rows = 9 * channels * (-(-channels // LANES))
-    else:
-        rows = 9 * channels * channels // LANES
-    unit = pieces * ROW_TILE
-    return -(-rows // unit) * unit
-
-
-def store_flat(ref, lead, blocks):
-    channels = blocks[0].shape[0]
-    full = channels // LANES
-    row = 0
+def part_rows(height, channels):
+    full, width = divmod(channels, LANES)
+    rows = 9 * height * full
+    if width:
+        rows += 9 * height // 2 if width * 2 == LANES else 9 * height
+    return -(-rows // ROW_TILE) * ROW_TILE
+
+
+def store_part(ref, start, end, blocks):
+    height, channels = blocks[0].shape
+    full, width = divmod(channels, LANES)
+    row = start
     for block in blocks:
         for tile in range(full):
-            ref[lead, row : row + channels, :] = block[:, tile * LANES : (tile + 1) * LANES]
-            row += channels
-    width = channels - full * LANES
-    if width == 0:
-        return
+            ref[row : row + height, :] = block[:, tile * LANES : (tile + 1) * LANES]
+            row += height
     rests = [block[:, full * LANES :] for block in blocks]
-    if width * 2 != LANES:
+    if width and width * 2 != LANES:
         for rest in rests:
-            ref[lead, row : row + channels, :width] = rest
-            row += channels
-        return
-    for pair in range(0, 8, 2):
-        ref[lead, row : row + channels, :] = jnp.concatenate([rests[pair], rests[pair + 1]], axis=1)
-        row += channels
-    half = channels // 2
-    ref[lead, row : row + half, :] = jnp.concatenate([rests[8][:half], rests[8][half:]], axis=1)
-
-
-def load_flat(ref, lead, channels):
-    full = channels // LANES
-    row = 0
+            ref[row : row + height, :width] = rest
+            row += height
+    elif width:
+        for pair in range(0, 8, 2):
+            ref[row : row + height, :] = jnp.concatenate([rests[pair], rests[pair + 1]], axis=1)
+            row += height
+        half = height // 2
+        ref[row : row + half, :] = jnp.concatenate([rests[8][:half], rests[8][half:]], axis=1)
+        row += half
+    if row < end:
+        ref[row:end, :] = jnp.zeros((end - row, LANES), ref.dtype)
+
+
+def load_part(rows, height, channels):
+    full, width = divmod(channels, LANES)
     parts = []
-    for _ in range(9):
-        tiles = []
-        for _ in range(full):
-            tiles.append(ref[lead, row : row + channels, :])
-            row += channels
-        parts.append(tiles)
-    width = channels - full * LANES
-    if width == 0:
-        pass
-    elif width * 2 != LANES:
+    for tap in range(9):
+        at = tap * full * height
+        parts.append([rows[at + t * height : at + (t + 1) * height] for t in range(full)])
+    row = 9 * full * height
+    if width and width * 2 != LANES:
         for tap in range(9):
-            parts[tap].append(ref[lead, row : row + channels, :width])
-            row += channels
-    else:
+            parts[tap].append(rows[row : row + height, :width])
+            row += height
+    elif width:
         for pair in range(0, 8, 2):
-            both = ref[lead, row : row + channels, :]
+            both = rows[row : row + height]
             parts[pair].append(both[:, :width])
             parts[pair + 1].append(both[:, width:])
-            row += channels
-        both = ref[lead, row : row + channels // 2, :]
+            row += height
+        both = rows[row : row + height // 2]
         parts[8].append(jnp.concatenate([both[:, :width], both[:, width:]], axis=0))
     return [jnp.concatenate(p, axis=1) if len(p) > 1 else p[0] for p in parts]
 
@@ -256,8 +249,8 @@
     bf16, f32 = jnp.bfloat16, jnp.float32
     pshape = packed_shape(rows, channels)
     ext_rows = rows + 2 * width
-    ext = pltpu.VMEM((ext_rows, channels), bf16)
-    sides = pltpu.VMEM((3, ext_rows, channels), bf16)
+    ext_shape, turned_shape = (ext_rows, channels), (3 * channels, rows)
+    ext = pltpu.VMEM(ext_shape, bf16)
     tap_flops = 2 * rows * channels * channels
     blocks = row_blocks(rows)
 
@@ -280,16 +273,16 @@
         inner, outer = beside(rim, rim, spread, lambda r: r)
         return [r.reshape(2 * width, channels) for r in (rim, *inner, *outer)]
 
-    def place_sides(scratch, refs, rims, spread):
-        side = side_of(spread, width)
-        half = len(refs) // 2
-        extend(scratch.at[2 - 2 * side], unpacked(refs[:half], rows, channels), rims[0], width)
-        extend(scratch.at[2 * side], unpacked(refs[half:], rows, channels), rims[1], width)
-
-    def near_part(field, weight, inner, rims, spread, flipped, name):
+    def turn(target, source):
+        for a in range(3):
+            value = source[a * width : a * width + rows, :].astype(f32).T
+            target[a * channels : (a + 1) * channels, :] = value.astype(bf16)
+
+    def near_part(field, weight, inner, rims, spread, flipped, name, keep=None):
         def body(x_ref, w_ref, *rest):
             refs, rest = rest[: len(inner)], rest[len(inner) :]
-            (own_rim, inner_rim), (part, e0, e1) = (rest[:2], rest[2:]) if rimmed else ((None, None), rest)
+            (own_rim, inner_rim), (part, *rest) = (rest[:2], rest[2:]) if rimmed else ((None, None), rest)
+            e0, e1 = rest[:2] if keep == "rims" else rest[-2:]
             extend(e0, x_ref[...], own_rim, width)
             extend(e1, unpacked(refs, rows, channels), inner_rim, width)
             b = 1 - 2 * side_of(spread, width)
@@ -297,9 +290,14 @@
                 part[start : start + size, :] = conv_block(
                     [(e0, w_ref, 0, flipped), (e1, w_ref, b, flipped)], start, size, width
                 )
+            if keep == "turned":
+                turn(rest[0], e0)
+                turn(rest[1], e1)
 
         args = [field, weight] + inner + rims[:2]
-        return call(body, [shape_of((rows, channels), f32)], args, [ext, ext], 6 * tap_flops, name)[0]
+        kept = {"rims": ext_shape, "turned": turned_shape}
+        outs = [shape_of((rows, channels), f32)] + ([shape_of(kept[keep], bf16)] * 2 if keep else [])
+        return call(body, outs, args, [] if keep == "rims" else [ext, ext], 6 * tap_flops, name)
 
     def far_part(part_ref, scratch, w_ref, spread, flipped, start, size):
         b = 2 * side_of(spread, width) - 1
@@ -328,14 +326,16 @@
         x_outer = [lax.ppermute(part, "lon", outer_pairs(steps)) for part in x_packed]
     else:
         x_inner, x_outer = beside(inputs, pack_one(inputs), FIRST_SPREAD, pack_one)
-    part1 = near_part(x, first_weight, x_inner, x_rims, FIRST_SPREAD, False, "near_pre_act")
-    part2 = near_part(g, second_weight, g_inner, g_rims, SECOND_SPREAD, True, "near_hidden_grad")
-    x_sides, g_sides = x_inner + x_outer, g_inner + g_outer
-    nx, ng = len(x_sides), len(g_sides)
+    part1, x_own, x_near = near_part(
+        x, first_weight, x_inner, x_rims, FIRST_SPREAD, False, "near_pre_act", "turned"
+    )
+    part2, g_own, g_near = near_part(
+        g, second_weight, g_inner, g_rims, SECOND_SPREAD, True, "near_hidden_grad", "rims"
+    )
 
     def hidden_body(part_ref, w_ref, *rest):
         side_refs, rest = rest[: len(x_outer)], rest[len(x_outer) :]
-        (rim,), (hidden_t, slope, se, hid) = (rest[:1], rest[1:]) if rimmed else ((None,), rest)
+        (rim,), (hidden_t, slope, turned, se, hid) = (rest[:1], rest[1:]) if rimmed else ((None,), rest)
         extend(se, unpacked(side_refs, rows, channels), rim, width)
         for start, size in blocks:
             act = far_part(part_ref, se, w_ref, FIRST_SPREAD, False, start, size)
@@ -343,93 +343,95 @@
             slope[start : start + size, :] = sigma * (1.0 + act * (1.0 - sigma))
             hid[start : start + size, :] = (act * sigma).astype(bf16).astype(f32)
         hidden_t[...] = hid[...].T.astype(bf16)
-
-    hidden_t, slope = call(
+        turn(turned, se)
+
+    hidden_t, slope, x_far = call(
         hidden_body,
-        [shape_of((channels, rows), bf16), shape_of((rows, channels), f32)],
+        [shape_of((channels, rows), bf16), shape_of((rows, channels), f32), shape_of(turned_shape, bf16)],
         [part1, first_weight] + x_outer + x_rims[2:],
         [ext, pltpu.VMEM((rows, channels), f32)],
         flops=3 * tap_flops,
         name="hidden",
     )
 
+    def second_sums(hid_ref, field):
+        return [
+            jnp.dot(hid_ref[...], field[(1 - a) * width : (1 - a) * width + rows, :], preferred_element_type=f32)
+            for a in (-1, 0, 1)
+        ]
+
     def grad_body(part_ref, slope_ref, w_ref, *rest):
         side_refs, rest = rest[: len(g_outer)], rest[len(g_outer) :]
-        (rim,), (pre_grad, packed, pre_t, se, pre) = (rest[:1], rest[1:]) if rimmed else ((None,), rest)
+        (rim,), (pre_grad, packed, se) = (rest[:1], rest[1:]) if rimmed else ((None,), rest)
         extend(se, unpacked(side_refs, rows, channels), rim, width)
         for start, size in blocks:
             grad = far_part(part_ref, se, w_ref, SECOND_SPREAD, True, start, size)
-            value = (grad * slope_ref[start : start + size, :]).astype(bf16)
-            pre_grad[start : start + size, :] = value
-            pre[start : start + size, :] = value.astype(f32)
+            pre_grad[start : start + size, :] = (grad * slope_ref[start : start + size, :]).astype(bf16)
         pack_into([packed], pre_grad[...])
-        pre_t[...] = pre[...].T.astype(bf16)
-
-    pre_grad, pre_packed, pre_t = call(
+
+    pre_grad, pre_packed, g_far = call(
         grad_body,
-        [shape_of((rows, channels), bf16), shape_of(pshape, bf16), shape_of((channels, rows), bf16)],
+        [shape_of((rows, channels), bf16), shape_of(pshape, bf16), shape_of(ext_shape, bf16)],
         [part2, slope, second_weight] + g_outer + g_rims[2:],
-        [ext, pltpu.VMEM((rows, channels), f32)],
         flops=3 * tap_flops,
         name="pre_grad",
     )
 
     stages = radices(count)
-    pieces = count // 2
-    flat = flat_rows(channels, pieces)
-    used = flat_rows(channels, 1)
+    group = stages[1]
+    later = stages[2:]
+    height_of_part = channels // group
+    part_size = part_rows(height_of_part, channels)
+    sizes = []
+    for radix in later:
+        size = -(-part_size // (radix * ROW_TILE)) * ROW_TILE
+        step = (part_size - size) // (radix - 1)
+        if len(later) > 1 or step % ROW_TILE or step * (radix - 1) + size != part_size:
+            part_size = -(-part_size // (math.prod(later) * ROW_TILE)) * math.prod(later) * ROW_TILE
+            break
+        sizes = [(size, step)]
+    if len(sizes) < len(later):
+        sizes, size = [], part_size
+        for radix in later:
+            size //= radix
+            sizes.append((size, size))
+    flat = group * part_size
 
     def kernel_gradient(which):
-        def body(hid_ref, pre_ref, x_ref, g_ref, *rest):
-            x_refs, g_refs, rest = rest[:nx], rest[nx : nx + ng], rest[nx + ng :]
-            rims, (out, flat_ref, se) = (rest[:6], rest[6:]) if rimmed else ((None,) * 6, rest)
-
-            def window(b, a):
-                return se[1 + b, (1 + a) * width : (1 + a) * width + rows, :]
-
-            if used < flat:
-                flat_ref[0, used - ROW_TILE :, :] = jnp.zeros((flat - used + ROW_TILE, LANES), f32)
+        def body(hid_ref, g0, g1, g2, pre_ref, x0, x1, x2, out, flat_ref):
             chosen = which(lax.rem(lax.axis_index("lon"), 2))
+
+            def put(mid, inner, outer, spread, sign):
+                east_first = side_of(spread, width) == 0
+                nine = []
+                for at in range(3):
+                    east = jnp.where(east_first, inner[at], outer[at])
+                    west = jnp.where(east_first, outer[at], inner[at])
+                    nine += [west, mid[at], east][::sign]
+                for c in range(group):
+                    rows_of = slice(c * height_of_part, (c + 1) * height_of_part)
+                    store_part(flat_ref, c * part_size, (c + 1) * part_size, [block[rows_of] for block in nine])
 
             @pl.when(chosen == 0)
             def _():
-                place_sides(se, g_refs, rims[4:6], SECOND_SPREAD)
-                extend(se.at[1], g_ref[...], rims[3], width)
-                store_flat(
-                    flat_ref,
-                    0,
-                    [
-                        jnp.dot(hid_ref[...], window(-b, -a), preferred_element_type=f32)
-                        for a in (-1, 0, 1)
-                        for b in (-1, 0, 1)
-                    ],
-                )
+                put(*(second_sums(hid_ref, ref) for ref in (g0, g1, g2)), SECOND_SPREAD, -1)
 
             @pl.when(chosen == 1)
             def _():
-                place_sides(se, x_refs, rims[1:3], FIRST_SPREAD)
-                extend(se.at[1], x_ref[...], rims[0], width)
-                store_flat(
-                    flat_ref,
-                    0,
-                    [
-                        jnp.dot(pre_ref[...], window(b, a), preferred_element_type=f32)
-                        for a in (-1, 0, 1)
-                        for b in (-1, 0, 1)
-                    ],
-                )
-
-            out[...] = flat_ref[0].astype(out.dtype)
+                sums = [jnp.dot(ref[...], pre_ref[...], preferred_element_type=f32) for ref in (x0, x1, x2)]
+                put(*([t[a * channels : (a + 1) * channels] for a in range(3)] for t in sums), FIRST_SPREAD, 1)
+
+            out[...] = flat_ref[...].astype(out.dtype)
 
         return body
 
-    fields = [hidden_t, pre_t, x, g] + x_sides + g_sides + x_rims + g_rims
-    flat_scratch = pltpu.VMEM((1, flat, LANES), f32)
+    fields = [hidden_t, g_own, g_near, g_far, pre_grad, x_own, x_near, x_far]
+    flat_scratch = pltpu.VMEM((flat, LANES), f32)
     (send,) = call(
         kernel_gradient(lambda core: 1 - core),
         [shape_of((flat, LANES), bf16)],
         fields,
-        [flat_scratch, sides],
+        [flat_scratch],
         flops=9 * tap_flops,
         name="sibling_kernel_gradient",
     )
@@ -438,7 +440,7 @@
         kernel_gradient(lambda core: core),
         [shape_of((flat, LANES), f32)],
         fields,
-        [flat_scratch, sides],
+        [flat_scratch],
         flops=9 * tap_flops,
         name="own_kernel_gradient",
     )
@@ -446,38 +448,36 @@
     def digit_of(stride, radix):
         return lax.rem(lax.axis_index("lon") // stride, radix)
 
-    def combine(own, received, stride, radix):
-        m = own.shape[0] // radix
-
+    def combine(own, received, stride, radix, size, step):
         def body(own_ref, *refs):
             got, (mine, *sends) = refs[: len(received)], refs[len(received) :]
             digit = digit_of(stride, radix)
             for k, target in enumerate([mine] + sends):
-                at = pl.ds(pl.multiple_of((digit ^ k) * m, ROW_TILE), m)
+                at = pl.ds(pl.multiple_of((digit ^ k) * step, ROW_TILE), size)
                 value = own_ref[at, :]
                 for ref in got:
                     value = value + ref[at, :].astype(f32)
                 target[...] = value.astype(target.dtype)
 
-        outs = [shape_of((m, LANES), f32)] + [shape_of((m, LANES), bf16)] * (radix - 1)
+        outs = [shape_of((size, LANES), f32)] + [shape_of((size, LANES), bf16)] * (radix - 1)
         return call(body, outs, [own] + received, name="combine")
 
     stride = 2
-    first_got = None
-    for radix in stages[1:]:
-        own, *sends = combine(own, received, stride, radix)
+    plane_got = None
+    for radix, (size, step) in zip(stages[1:], [(part_size, part_size)] + sizes):
+        own, *sends = combine(own, received, stride, radix, size, step)
         received = [swapped(part, count, stride, k + 1) for k, part in enumerate(sends)]
-        first_got = received[0] if first_got is None else first_got
+        plane_got = received[-1] if plane_got is None else plane_got
         stride *= radix
     pre_field = pre_grad.reshape(height, width, channels)
     p_rims = rims_of(pre_field, FIRST_SPREAD)
     if paired(FIRST_SPREAD, width):
         steps = FIRST_SPREAD // width
         p_inner = [lax.ppermute(pre_packed, "lon", inner_pairs(steps))]
-        p_outer = [lax.ppermute(after(pre_packed, first_got), "lon", outer_pairs(steps))]
+        p_outer = [lax.ppermute(after(pre_packed, plane_got), "lon", outer_pairs(steps))]
     else:
         p_inner, p_outer = beside(pre_field, pre_packed, FIRST_SPREAD, pack_one)
-    part3 = near_part(pre_grad, first_weight, p_inner, p_rims, FIRST_SPREAD, True, "near_input_gradient")
+    (part3,) = near_part(pre_grad, first_weight, p_inner, p_rims, FIRST_SPREAD, True, "near_input_gradient")
 
     def input_body(part_ref, w_ref, *rest):
         side_refs, rest = rest[: len(p_outer)], rest[len(p_outer) :]
@@ -509,65 +509,71 @@
 
         return call(body, [shape_of(own.shape, bf16)], [own] + received, name="combine_last")[0]
 
-    group = stages[1]
+    def assemble(pieces, stride, radix, size, step):
+        def body(*refs):
+            digit = digit_of(stride, radix)
+            for k, ref in enumerate(refs[:-1]):
+                place = digit ^ k
+                refs[-1][pl.ds(pl.multiple_of(place * step, ROW_TILE), step), :] = ref[:step, :]
+                if step < size:
+
+                    @pl.when(place == radix - 1)
+                    def _():
+                        refs[-1][radix * step :, :] = ref[step:, :]
+
+        total = step * (radix - 1) + size
+        return call(body, [shape_of((total, LANES), bf16)], pieces, name="assemble")[0]
+
     held = finish(own, received)
     stride = count
-    for radix in reversed(stages[2:]):
+    for radix, (size, step) in reversed(list(zip(later, sizes))):
         stride //= radix
-        held = jnp.concatenate([held] + [swapped(held, count, stride, k) for k in range(1, radix)], axis=0)
+        pieces = [held] + [swapped(held, count, stride, k) for k in range(1, radix)]
+        held = assemble(pieces, stride, radix, size, step)
+    def unpack(parts, previous):
+        def body(*refs):
+            second_out, first_out, stage, sems = refs[len(parts) + len(previous) :]
+            core = lax.rem(lax.axis_index("lon"), 2)
+            for i, (_, k, side) in enumerate(parts):
+                for tap, value in enumerate(load_part(refs[i][...].astype(f32), height_of_part, channels)):
+                    stage[i, tap] = value * scale
+                start = pl.multiple_of((digit_of(2, group) ^ k) * height_of_part, height_of_part)
+                for which, out in enumerate((second_out, first_out)):
+
+                    @pl.when((core + side) % 2 == which)
+                    def _():
+                        for tap in range(9):
+                            target = out.at[tap // 3, tap % 3, pl.ds(start, height_of_part)]
+                            pltpu.make_async_copy(stage.at[i, tap], target, sems.at[9 * i + tap]).start()
+
+            for i in range(len(parts)):
+                for tap in range(9):
+                    target = second_out.at[tap // 3, tap % 3, pl.ds(0, height_of_part)]
+                    pltpu.make_async_copy(stage.at[i, tap], target, sems.at[9 * i + tap]).wait()
+
+        count_in = len(parts)
+        return list(
+            call(
+                body,
+                [shape_of((3, 3, channels, channels), f32)] * 2,
+                [array for array, _, _ in parts] + previous,
+                [
+                    pltpu.VMEM((count_in, 9, height_of_part, channels), f32),
+                    pltpu.SemaphoreType.DMA((9 * count_in,)),
+                ],
+                name="unpack_gradients",
+                far_args=tuple(range(count_in, count_in + len(previous))),
+                far_outs=(0, 1),
+                aliases={count_in + i: i for i in range(len(previous))},
+            )
+        )
+
     quarter = [held] + [swapped(held, count, 2, k) for k in range(1, group)]
     sibling = [swapped(held, count, 1, 1)]
     sibling += [swapped(after(q, input_gradient), count, 1, 1) for q in quarter[1:]]
-    unit = flat // pieces
-
-    def unpack(parts, which, previous):
-        def body(*refs):
-            second_out, first_out, flat_ref, stage, sems = refs[group + len(previous) :]
-            for k, ref in enumerate(refs[:group]):
-                stride, span = 2 * group, pieces // group
-                walk = [((digit_of(2, group) ^ k) * span, 0)]
-                for radix in stages[2:]:
-                    digit = digit_of(stride, radix)
-                    span //= radix
-                    walk = [
-                        (at + (digit ^ j) * span, order + j * span) for at, order in walk for j in range(radix)
-                    ]
-                    stride *= radix
-                for at, order in walk:
-                    target = pl.ds(pl.multiple_of(at * unit, ROW_TILE), unit)
-                    flat_ref[0, target, :] = ref[order * unit : (order + 1) * unit, :].astype(f32)
-            chosen = which(lax.rem(lax.axis_index("lon"), 2))
-
-            def write(out, transposed):
-                copies = []
-                for tap, value in enumerate(load_flat(flat_ref, 0, channels)):
-                    stage[tap] = (value.T if transposed else value) * scale
-                    copies.append(pltpu.make_async_copy(stage.at[tap], out.at[tap // 3, tap % 3], sems.at[tap]))
-                    copies[-1].start()
-                for copy in copies:
-                    copy.wait()
-
-            @pl.when(chosen == 0)
-            def _():
-                write(second_out, False)
-
-            @pl.when(chosen == 1)
-            def _():
-                write(first_out, True)
-
-        return call(
-            body,
-            [shape_of((3, 3, channels, channels), f32)] * 2,
-            parts + previous,
-            [flat_scratch, pltpu.VMEM((9, channels, channels), f32), pltpu.SemaphoreType.DMA((9,))],
-            name="unpack_gradient",
-            far_args=tuple(range(group, group + len(previous))),
-            far_outs=(0, 1),
-            aliases={group + i: i for i in range(len(previous))},
-        )
-
-    own_written = unpack(quarter, lambda core: core, [])
-    second_gradient, first_gradient = unpack(sibling, lambda core: 1 - core, list(own_written))
+    written = unpack([(part, k, 0) for k, part in enumerate(quarter)], [])
+    written = unpack([(part, k, 1) for k, part in enumerate(sibling)], written)
+    second_gradient, first_gradient = written
     return (input_gradient.reshape(height, width, channels), first_gradient, second_gradient)
 
 

time: 75.7 us -> 73.9 us (0.976)
  starting transfers between devices: 36.5 us -> 32.8 us
  waiting for transfers between devices: 21.2 us -> 24.3 us
  local copies, waits for them, and re-layouts: 4.3 us -> 3.34 us
    ppermute x4, starting transfers between devices: 3.65 us -> 7.56 us  [shards(): lax.ppermute(part, 'lon', inner_pairs(steps))]
    ppermute x2, starting transfers between devices: 7.24 us -> 5.34 us  [shards(): lax.ppermute(part, 'lon', outer_pairs(steps))]
    ppermute x17, starting transfers between devices: 18.3 us -> 16.5 us  [swapped(): lax.ppermute(value, 'lon', [(i, i ^ k * stride) for i in range(count)])]
    ppermute x17, waiting for transfers between devices: 17.2 us -> 19 us  [swapped(): lax.ppermute(value, 'lon', [(i, i ^ k * stride) for i in range(count)])]
    ppermute x1, starting transfers between devices: 2.58 us -> 0.8 us  [shards(): lax.ppermute(after(pre_packed, plane_got), 'lon', outer_pairs(steps))]
    ppermute x1, starting transfers between devices: 4.02 us -> 2.45 us  [shards(): lax.ppermute(g_packed[1], 'lon', outer_pairs(steps))]
    ppermute x4, waiting for transfers between devices: 2.2 us -> 3.28 us  [shards(): lax.ppermute(part, 'lon', inner_pairs(steps))]
    unnamed x14 -> x12, local copies, waits for them, and re-layouts: 4.3 us -> 3.34 us
  transfers between devices with their start and end apart: 27 -> 27, of which waited for: 12 -> 12; matrix products, arithmetic and copies ran while one was open for 0% -> 0% of each run, Pallas kernels for 11% -> 12%
where the time goes in v5:
time: 73.9 us; the launch traced here: 73.7 us
  starting transfers between devices  32.8 us (44%)
  waiting for transfers between devices  24.3 us (33%)
  Pallas kernels  12.3 us (17%)
  local copies, waits for them, and re-layouts  3.34 us (5%)
  between operations  0.87 us (1%)
    ppermute x17, waiting for transfers between devices, swapped(): lax.ppermute(value, 'lon', [(i, i ^ k * stride) for i in range(count)])  19 us
    ppermute x17, starting transfers between devices, swapped(): lax.ppermute(value, 'lon', [(i, i ^ k * stride) for i in range(count)])  16.5 us
    pallas_call x16, Pallas kernels, call(): pl.pallas_call(body, out_shape=list(outs), in_specs=[far if i in far_args...  12.3 us
    ppermute x4, starting transfers between devices, shards(): lax.ppermute(part, 'lon', inner_pairs(steps))  7.56 us
    ppermute x2, starting transfers between devices, shards(): lax.ppermute(part, 'lon', outer_pairs(steps))  5.34 us
    unnamed x12, local copies, waits for them, and re-layouts  3.34 us
    ppermute x4, waiting for transfers between devices, shards(): lax.ppermute(part, 'lon', inner_pairs(steps))  3.28 us
    ppermute x1, starting transfers between devices, shards(): lax.ppermute(g_packed[1], 'lon', outer_pairs(steps))  2.45 us
  transfers between devices with their start and end apart: 27, of which 12 were waited for; matrix products, arithmetic and copies ran while one was open for 0% of the time, Pallas kernels for 12%

profile of v5, /device:TPU:0, one launch (start us, length us, event | category | flops | bytes accessed | tf_op | source)
XLA Modules:
  0.0 73.7 jit_solution(13346138067514173545)
XLA Ops:
  0.7 1.1 %copy-done.4 = bf16[32,32,192]{2,1,0:T(8,128)(2,1)S(1)} copy-done((bf16[32,32,192]{2,1,0:T(8,128)(2,1)S(1)}, bf16[32,32,192]{2,1,0:T(8,128)(2,1)}, u32[]{:S(2)}) %copy-start.4) | copy-done | bytes 393240
  1.9 3.0 %collective-permute-start = (bf16[960,128]{1,0:T(8,128)(2,1)S(1)}, bf16[960,128]{1,0:T(8,128)(2,1)S(1)}, u32[]{:S(2)}, u32[]{:S(2)}) collective-permute-start(bf16[960,128]{1,0:T(8,128)(2,1)S(1)} %get-tuple-element.36), channel_id=1, source_target_pairs={{0,2},{1,3},{2,0},{3,1},{4,6},{5,7},{6,4},{7,5},{8,10},{9,11},{10,... | collective-permute-start | bytes 737288 | tf_op jit(solution)/shard_map/ppermute | solution.py:315
  4.9 1.0 %copy-done.3 = bf16[32,32,192]{2,1,0:T(8,128)(2,1)S(1)} copy-done((bf16[32,32,192]{2,1,0:T(8,128)(2,1)S(1)}, bf16[32,32,192]{2,1,0:T(8,128)(2,1)}, u32[]{:S(2)}) %copy-start.3) | copy-done | bytes 393240
  6.6 4.2 %collective-permute-start.4 = (bf16[768,128]{1,0:T(8,128)(2,1)S(1)}, bf16[768,128]{1,0:T(8,128)(2,1)S(1)}, u32[]{:S(2)}, u32[]{:S(2)}) collective-permute-start(bf16[768,128]{1,0:T(8,128)(2,1)S(1)} %get-tuple-element.40), channel_id=1, source_target_pairs={{0,31},{1,2},{2,1},{3,4},{4,3},{5,6},{6,5},{7,8},{8,7},{9,10},{10,... | collective-permute-start | bytes 589832 | tf_op jit(solution)/shard_map/ppermute | solution.py:326
  10.8 1.1 %collective-permute-start.5 = (bf16[768,128]{1,0:T(8,128)(2,1)S(1)}, bf16[768,128]{1,0:T(8,128)(2,1)S(1)}, u32[]{:S(2)}, u32[]{:S(2)}) collective-permute-start(bf16[768,128]{1,0:T(8,128)(2,1)S(1)} %get-tuple-element.41), channel_id=1, source_target_pairs={{0,31},{1,2},{2,1},{3,4},{4,3},{5,6},{6,5},{7,8},{8,7},{9,10},{10,... | collective-permute-start | bytes 589832 | tf_op jit(solution)/shard_map/ppermute | solution.py:326
  12.0 3.3 %collective-permute-done.rest_0_ = bf16[960,128]{1,0:T(8,128)(2,1)S(1)} collective-permute-done((bf16[960,128]{1,0:T(8,128)(2,1)S(1)}, bf16[960,128]{1,0:T(8,128)(2,1)S(1)}, u32[]{:S(2)}, u32[]{:S(2)}) %collective-permute-start) | collective-permute-done | bytes 245792 | tf_op jit(solution)/shard_map/ppermute | solution.py:315
  15.2 4.0 %collective-permute-start.1 = (bf16[576,128]{1,0:T(8,128)(2,1)S(1)}, bf16[576,128]{1,0:T(8,128)(2,1)S(1)}, u32[]{:S(2)}, u32[]{:S(2)}) collective-permute-start(bf16[576,128]{1,0:T(8,128)(2,1)S(1)} %get-tuple-element.37), channel_id=1, source_target_pairs={{0,2},{1,3},{2,0},{3,1},{4,6},{5,7},{6,4},{7,5},{8,10},{9,11},{10,... | collective-permute-start | bytes 442376 | tf_op jit(solution)/shard_map/ppermute | solution.py:315
  19.2 2.4 %collective-permute-start.7 = (bf16[576,128]{1,0:T(8,128)(2,1)S(1)}, bf16[576,128]{1,0:T(8,128)(2,1)S(1)}, u32[]{:S(2)}, u32[]{:S(2)}) collective-permute-start(bf16[576,128]{1,0:T(8,128)(2,1)S(1)} %get-tuple-element.37), channel_id=1, source_target_pairs={{0,30},{1,31},{2,4},{3,5},{4,2},{5,3},{6,8},{7,9},{8,6},{9,7},{10,... | collective-permute-start | bytes 442376 | tf_op jit(solution)/shard_map/ppermute | solution.py:318
  21.7 1.2 %copy-done = bf16[3,3,192,192]{3,2,1,0:T(8,128)(2,1)S(1)} copy-done((bf16[3,3,192,192]{3,2,1,0:T(8,128)(2,1)S(1)}, bf16[3,3,192,192]{3,2,1,0:T(8,128)(2,1)}, u32[]{:S(2)}) %copy-start) | copy-done | bytes 663576
  22.9 1.0 %near_pre_act.1 = (f32[1024,192]{1,0:T(8,128)S(1)}, bf16[576,1024]{1,0:T(8,128)(2,1)S(1)}, bf16[576,1024]{1,0:T(8,128)(2,1)S(1)}) custom-call(bf16[1024,192]{1,0:T(8,128)(2,1)S(1)} %bitcast.5, bf16[3,3,192,192]{3,2,1,0:T(8,128)(2,1)S(1)} %copy-done, bf16[768,128]{1,0:T(8,128)(2,1)S(1)} %collective-permute-done.2.rest_0_, ...), custom_call_target="tpu_custom_call" | custom-call | flops 452984832 | bytes 4595712 | tf_op jit(solution)/shard_map/near_pre_act/pallas_call | solution.py:22
  23.9 1.0 %hidden.1 = (bf16[192,1024]{1,0:T(8,128)(2,1)S(1)}, f32[1024,192]{1,0:T(8,128)S(1)}, bf16[576,1024]{1,0:T(8,128)(2,1)S(1)}) custom-call(f32[1024,192]{1,0:T(8,128)S(1)} %get-tuple-element.42.part_ref, bf16[3,3,192,192]{3,2,1,0:T(8,128)(2,1)S(1)} %copy-done.1, bf16[768,128]{1,0:T(8,128)(2,1)S(1)} %collective-permute-done.4.rest_0_, ...), custom_call_target="tpu_custom_call" | custom-call | flops 226492416 | bytes 4202496 | tf_op jit(solution)/shard_map/hidden/pallas_call | solution.py:22
  24.9 1.0 %near_hidden_grad.1 = (f32[1024,192]{1,0:T(8,128)S(1)}, bf16[1088,192]{1,0:T(8,128)(2,1)S(1)}, bf16[1088,192]{1,0:T(8,128)(2,1)S(1)}) custom-call(bf16[1024,192]{1,0:T(8,128)(2,1)S(1)} %bitcast.7, bf16[3,3,192,192]{3,2,1,0:T(8,128)(2,1)S(1)} %copy-done.2, bf16[960,128]{1,0:T(8,128)(2,1)S(1)} %collective-permute-done.rest_0_, ...), custom_call_target="tpu_custom_call" | custom-call | flops 452984832 | bytes 3072000 | tf_op jit(solution)/shard_map/near_hidden_grad/pallas_call | solution.py:22
  25.9 2.1 %collective-permute-done.7.rest_1_ = bf16[576,128]{1,0:T(8,128)(2,1)S(1)} collective-permute-done((bf16[576,128]{1,0:T(8,128)(2,1)S(1)}, bf16[576,128]{1,0:T(8,128)(2,1)S(1)}, u32[]{:S(2)}, u32[]{:S(2)}) %collective-permute-start.7) | collective-permute-done | bytes 147488 | tf_op jit(solution)/shard_map/ppermute | solution.py:318
  28.7 1.2 %sibling_kernel_gradient.1 = bf16[2624,128]{1,0:T(8,128)(2,1)S(1)} custom-call(bf16[192,1024]{1,0:T(8,128)(2,1)S(1)} %get-tuple-element.46.hid_ref, bf16[1088,192]{1,0:T(8,128)(2,1)S(1)} %get-tuple-element.47.g0, bf16[1088,192]{1,0:T(8,128)(2,1)S(1)} %get-tuple-element.48.g1, bf16[1088,192]{1,0:T(8,128)(2,1)S(1)} %get-tuple-element.49.g2, ...), custom_call_target="tpu_custom_call" | custom-call | flops 679477248 | bytes 6250496 | tf_op jit(solution)/shard_map/sibling_kernel_gradient/pallas_call | solution.py:22
  30.1 1.3 %own_kernel_gradient.1.own_ref = f32[2624,128]{1,0:T(8,128)S(1)} custom-call(bf16[192,1024]{1,0:T(8,128)(2,1)S(1)} %get-tuple-element.46.hid_ref, bf16[1088,192]{1,0:T(8,128)(2,1)S(1)} %get-tuple-element.47.g0, bf16[1088,192]{1,0:T(8,128)(2,1)S(1)} %get-tuple-element.48.g1, bf16[1088,192]{1,0:T(8,128)(2,1)S(1)} %get-tuple-element.49.g2, ...), custom_call_target="tpu_custom_call" | custom-call | flops 679477248 | bytes 6922240 | tf_op jit(solution)/shard_map/own_kernel_gradient/pallas_call | solution.py:22
  33.0 2.9 %collective-permute-start.13 = (bf16[656,128]{1,0:T(8,128)(2,1)S(1)}, bf16[656,128]{1,0:T(8,128)(2,1)S(1)}, u32[]{:S(2)}, u32[]{:S(2)}) collective-permute-start(bf16[656,128]{1,0:T(8,128)(2,1)S(1)} %get-tuple-element.57), channel_id=1, source_target_pairs={{0,4},{1,5},{2,6},{3,7},{4,0},{5,1},{6,2},{7,3},{8,12},{9,13},{10,... | collective-permute-start | bytes 503816 | tf_op jit(solution)/shard_map/ppermute | solution.py:180
  35.9 4.6 %collective-permute-done.10.refs_2_ = bf16[656,128]{1,0:T(8,128)(2,1)S(1)} collective-permute-done((bf16[656,128]{1,0:T(8,128)(2,1)S(1)}, bf16[656,128]{1,0:T(8,128)(2,1)S(1)}, u32[]{:S(2)}, u32[]{:S(2)}) %collective-permute-start.10) | collective-permute-done | bytes 167968 | tf_op jit(solution)/shard_map/ppermute | solution.py:180
  41.3 2.0 %collective-permute-done.13.refs_1_ = bf16[656,128]{1,0:T(8,128)(2,1)S(1)} collective-permute-done((bf16[656,128]{1,0:T(8,128)(2,1)S(1)}, bf16[656,128]{1,0:T(8,128)(2,1)S(1)}, u32[]{:S(2)}, u32[]{:S(2)}) %collective-permute-start.13) | collective-permute-done | bytes 167968 | tf_op jit(solution)/shard_map/ppermute | solution.py:180
  43.9 2.6 %collective-permute-start.15 = (bf16[176,128]{1,0:T(8,128)(2,1)S(1)}, bf16[176,128]{1,0:T(8,128)(2,1)S(1)}, u32[]{:S(2)}, u32[]{:S(2)}) collective-permute-start(bf16[176,128]{1,0:T(8,128)(2,1)S(1)} %get-tuple-element.60), channel_id=1, source_target_pairs={{0,16},{1,17},{2,18},{3,19},{4,20},{5,21},{6,22},{7,23},{8,24},{9,... | collective-permute-start | bytes 135176 | tf_op jit(solution)/shard_map/ppermute | solution.py:180
  46.5 1.3 %collective-permute-start.16 = (bf16[176,128]{1,0:T(8,128)(2,1)S(1)}, bf16[176,128]{1,0:T(8,128)(2,1)S(1)}, u32[]{:S(2)}, u32[]{:S(2)}) collective-permute-start(bf16[176,128]{1,0:T(8,128)(2,1)S(1)} %get-tuple-element.61), channel_id=1, source_target_pairs={{0,24},{1,25},{2,26},{3,27},{4,28},{5,29},{6,30},{7,31},{8,16},{9,... | collective-permute-start | bytes 135176 | tf_op jit(solution)/shard_map/ppermute | solution.py:180
  49.2 3.1 %collective-permute-done.16.refs_2_ = bf16[176,128]{1,0:T(8,128)(2,1)S(1)} collective-permute-done((bf16[176,128]{1,0:T(8,128)(2,1)S(1)}, bf16[176,128]{1,0:T(8,128)(2,1)S(1)}, u32[]{:S(2)}, u32[]{:S(2)}) %collective-permute-start.16) | collective-permute-done | bytes 45088 | tf_op jit(solution)/shard_map/ppermute | solution.py:180
  52.4 2.5 %collective-permute-start.18 = (bf16[176,128]{1,0:T(8,128)(2,1)S(1)}, bf16[176,128]{1,0:T(8,128)(2,1)S(1)}, u32[]{:S(2)}, u32[]{:S(2)}) collective-permute-start(bf16[176,128]{1,0:T(8,128)(2,1)S(1)} %combine_last.1.refs_0_), channel_id=1, source_target_pairs={{0,16},{1,17},{2,18},{3,19},{4,20},{5,21},{6,22},{7,23},{8,24},{9,... | collective-permute-start | bytes 135176 | tf_op jit(solution)/shard_map/ppermute | solution.py:180
  55.0 1.8 %collective-permute-start.19 = (bf16[176,128]{1,0:T(8,128)(2,1)S(1)}, bf16[176,128]{1,0:T(8,128)(2,1)S(1)}, u32[]{:S(2)}, u32[]{:S(2)}) collective-permute-start(bf16[176,128]{1,0:T(8,128)(2,1)S(1)} %combine_last.1.refs_0_), channel_id=1, source_target_pairs={{0,24},{1,25},{2,26},{3,27},{4,28},{5,29},{6,30},{7,31},{8,16},{9,... | collective-permute-start | bytes 135176 | tf_op jit(solution)/shard_map/ppermute | solution.py:180
  57.6 3.2 %collective-permute-done.19.refs_3_ = bf16[176,128]{1,0:T(8,128)(2,1)S(1)} collective-permute-done((bf16[176,128]{1,0:T(8,128)(2,1)S(1)}, bf16[176,128]{1,0:T(8,128)(2,1)S(1)}, u32[]{:S(2)}, u32[]{:S(2)}) %collective-permute-start.19) | collective-permute-done | bytes 45088 | tf_op jit(solution)/shard_map/ppermute | solution.py:180
  60.8 2.1 %collective-permute-start.25 = (bf16[656,128]{1,0:T(8,128)(2,1)S(1)}, bf16[656,128]{1,0:T(8,128)(2,1)S(1)}, u32[]{:S(2)}, u32[]{:S(2)}) collective-permute-start(bf16[656,128]{1,0:T(8,128)(2,1)S(1)} %assemble.1.refs_0_), channel_id=1, source_target_pairs={{0,6},{1,7},{2,4},{3,5},{4,2},{5,3},{6,0},{7,1},{8,14},{9,15},{10,... | collective-permute-start | bytes 503816 | tf_op jit(solution)/shard_map/ppermute | solution.py:180
  63.0 1.5 %collective-permute-start.21 = (bf16[656,128]{1,0:T(8,128)(2,1)S(1)}, bf16[656,128]{1,0:T(8,128)(2,1)S(1)}, u32[]{:S(2)}, u32[]{:S(2)}) collective-permute-start(bf16[656,128]{1,0:T(8,128)(2,1)S(1)} %assemble.1.refs_0_), channel_id=1, source_target_pairs={{0,2},{1,3},{2,0},{3,1},{4,6},{5,7},{6,4},{7,5},{8,10},{9,11},{10,... | collective-permute-start | bytes 503816 | tf_op jit(solution)/shard_map/ppermute | solution.py:180
  64.4 1.0 %near_input_gradient.1.part_ref = f32[1024,192]{1,0:T(8,128)S(1)} custom-call(bf16[1024,192]{1,0:T(8,128)(2,1)S(1)} %get-tuple-element.44.x_ref.pre_ref, bf16[3,3,192,192]{3,2,1,0:T(8,128)(2,1)S(1)} %copy-done.1, bf16[1536,128]{1,0:T(8,128)(2,1)S(1)} %collective-permute-done.8.rest_0_), custom_call_target="tpu_custom_call" | custom-call | flops 452984832 | bytes 2236416 | tf_op jit(solution)/shard_map/near_input_gradient/pallas_call | solution.py:22
  65.5 1.4 %input_gradient.1 = bf16[1024,192]{1,0:T(8,128)(2,1)} custom-call(f32[1024,192]{1,0:T(8,128)S(1)} %near_input_gradient.1.part_ref, bf16[3,3,192,192]{3,2,1,0:T(8,128)(2,1)S(1)} %copy-done.1, bf16[1536,128]{1,0:T(8,128)(2,1)S(1)} %collective-permute-done.11.rest_0_), custom_call_target="tpu_custom_call" | custom-call | flops 226492416 | bytes 2236416 | tf_op jit(solution)/shard_map/input_gradient/pallas_call | solution.py:22
  66.9 1.4 %collective-permute-done.25.refs_3_ = bf16[656,128]{1,0:T(8,128)(2,1)S(1)} collective-permute-done((bf16[656,128]{1,0:T(8,128)(2,1)S(1)}, bf16[656,128]{1,0:T(8,128)(2,1)S(1)}, u32[]{:S(2)}, u32[]{:S(2)}) %collective-permute-start.25) | collective-permute-done | bytes 167968 | tf_op jit(solution)/shard_map/ppermute | solution.py:180
  68.3 1.6 %collective-permute-done.23.refs_2_ = bf16[656,128]{1,0:T(8,128)(2,1)S(1)} collective-permute-done((bf16[656,128]{1,0:T(8,128)(2,1)S(1)}, bf16[656,128]{1,0:T(8,128)(2,1)S(1)}, u32[]{:S(2)}, u32[]{:S(2)}) %collective-permute-start.23) | collective-permute-done | bytes 167968 | tf_op jit(solution)/shard_map/ppermute | solution.py:180
  70.4 1.6 %unpack_gradients.2 = (f32[3,3,192,192]{3,2,1,0:T(8,128)}, f32[3,3,192,192]{3,2,1,0:T(8,128)}) custom-call(bf16[656,128]{1,0:T(8,128)(2,1)S(1)} %assemble.1.refs_0_, bf16[656,128]{1,0:T(8,128)(2,1)S(1)} %collective-permute-done.21.refs_1_, bf16[656,128]{1,0:T(8,128)(2,1)S(1)} %collective-permute-done.23.refs_2_, ...), custom_call_target="tpu_custom_call" | custom-call | bytes 3325952 | tf_op jit(solution)/shard_map/unpack_gradients/pallas_call | solution.py:22
  72.1 1.6 %unpack_gradients.3 = (f32[3,3,192,192]{3,2,1,0:T(8,128)}, f32[3,3,192,192]{3,2,1,0:T(8,128)}) custom-call(bf16[656,128]{1,0:T(8,128)(2,1)S(1)} %collective-permute-done.20.refs_0_, bf16[656,128]{1,0:T(8,128)(2,1)S(1)} %collective-permute-done.22.refs_1_, ...), custom_call_target="tpu_custom_call", output_to_operand_aliasing={{0}: (4, {}), {1}: (5, {})} | custom-call | bytes 5980160 | tf_op jit(solution)/shard_map/unpack_gradients/pallas_call | solution.py:22
  (50 shorter events, 7.7 us)
Async XLA Ops:
  0.6 23.3 %copy-start.1 = (bf16[3,3,192,192]{3,2,1,0:T(8,128)(2,1)S(1)}, bf16[3,3,192,192]{3,2,1,0:T(8,128)(2,1)}, u32[]{:S(2)}) copy-start(bf16[3,3,192,192]{3,2,1,0:T(8,128)(2,1)} %w_ref.11) | copy-start | bytes 1990660
  0.6 1.1 %copy-start.4 = (bf16[32,32,192]{2,1,0:T(8,128)(2,1)S(1)}, bf16[32,32,192]{2,1,0:T(8,128)(2,1)}, u32[]{:S(2)}) copy-start(bf16[32,32,192]{2,1,0:T(8,128)(2,1)} %param.5) | copy-start | bytes 1179652
  1.9 13.4 %collective-permute-start = (bf16[960,128]{1,0:T(8,128)(2,1)S(1)}, bf16[960,128]{1,0:T(8,128)(2,1)S(1)}, u32[]{:S(2)}, u32[]{:S(2)}) collective-permute-start(bf16[960,128]{1,0:T(8,128)(2,1)S(1)} %get-tuple-element.36), channel_id=1, source_target_pairs={{0,2},{1,3},{2,0},{3,1},{4,6},{5,7},{6,4},{7,5},{8,10},{9,11},{10,... | collective-permute-start | bytes 737288 | tf_op jit(solution)/shard_map/ppermute | solution.py:315
  6.0 9.2 %collective-permute-start.2 = (bf16[768,128]{1,0:T(8,128)(2,1)S(1)}, bf16[768,128]{1,0:T(8,128)(2,1)S(1)}, u32[]{:S(2)}, u32[]{:S(2)}) collective-permute-start(bf16[768,128]{1,0:T(8,128)(2,1)S(1)} %get-tuple-element.40), channel_id=1, source_target_pairs={{0,1},{1,0},{2,3},{3,2},{4,5},{5,4},{6,7},{7,6},{8,9},{9,8},{10,11... | collective-permute-start | bytes 589832 | tf_op jit(solution)/shard_map/ppermute | solution.py:325
  6.1 13.1 %collective-permute-start.3 = (bf16[768,128]{1,0:T(8,128)(2,1)S(1)}, bf16[768,128]{1,0:T(8,128)(2,1)S(1)}, u32[]{:S(2)}, u32[]{:S(2)}) collective-permute-start(bf16[768,128]{1,0:T(8,128)(2,1)S(1)} %get-tuple-element.41), channel_id=1, source_target_pairs={{0,1},{1,0},{2,3},{3,2},{4,5},{5,4},{6,7},{7,6},{8,9},{9,8},{10,11... | collective-permute-start | bytes 589832 | tf_op jit(solution)/shard_map/ppermute | solution.py:325
  6.6 17.2 %collective-permute-start.4 = (bf16[768,128]{1,0:T(8,128)(2,1)S(1)}, bf16[768,128]{1,0:T(8,128)(2,1)S(1)}, u32[]{:S(2)}, u32[]{:S(2)}) collective-permute-start(bf16[768,128]{1,0:T(8,128)(2,1)S(1)} %get-tuple-element.40), channel_id=1, source_target_pairs={{0,31},{1,2},{2,1},{3,4},{4,3},{5,6},{6,5},{7,8},{8,7},{9,10},{10,... | collective-permute-start | bytes 589832 | tf_op jit(solution)/shard_map/ppermute | solution.py:326
  10.8 13.0 %collective-permute-start.5 = (bf16[768,128]{1,0:T(8,128)(2,1)S(1)}, bf16[768,128]{1,0:T(8,128)(2,1)S(1)}, u32[]{:S(2)}, u32[]{:S(2)}) collective-permute-start(bf16[768,128]{1,0:T(8,128)(2,1)S(1)} %get-tuple-element.41), channel_id=1, source_target_pairs={{0,31},{1,2},{2,1},{3,4},{4,3},{5,6},{6,5},{7,8},{8,7},{9,10},{10,... | collective-permute-start | bytes 589832 | tf_op jit(solution)/shard_map/ppermute | solution.py:326
  15.2 12.7 %collective-permute-start.6 = (bf16[960,128]{1,0:T(8,128)(2,1)S(1)}, bf16[960,128]{1,0:T(8,128)(2,1)S(1)}, u32[]{:S(2)}, u32[]{:S(2)}) collective-permute-start(bf16[960,128]{1,0:T(8,128)(2,1)S(1)} %collective-permute-done.rest_0_), channel_id=1, source_target_pairs={{0,4},{1,5},{2,30},{3,31},{4,8},{5,9},{6,2},{7,3},{8,12},{9,13},{1... | collective-permute-start | bytes 737288 | tf_op jit(solution)/shard_map/ppermute | solution.py:317
  15.2 9.6 %collective-permute-start.1 = (bf16[576,128]{1,0:T(8,128)(2,1)S(1)}, bf16[576,128]{1,0:T(8,128)(2,1)S(1)}, u32[]{:S(2)}, u32[]{:S(2)}) collective-permute-start(bf16[576,128]{1,0:T(8,128)(2,1)S(1)} %get-tuple-element.37), channel_id=1, source_target_pairs={{0,2},{1,3},{2,0},{3,1},{4,6},{5,7},{6,4},{7,5},{8,10},{9,11},{10,... | collective-permute-start | bytes 442376 | tf_op jit(solution)/shard_map/ppermute | solution.py:315
  19.2 8.7 %collective-permute-start.7 = (bf16[576,128]{1,0:T(8,128)(2,1)S(1)}, bf16[576,128]{1,0:T(8,128)(2,1)S(1)}, u32[]{:S(2)}, u32[]{:S(2)}) collective-permute-start(bf16[576,128]{1,0:T(8,128)(2,1)S(1)} %get-tuple-element.37), channel_id=1, source_target_pairs={{0,30},{1,31},{2,4},{3,5},{4,2},{5,3},{6,8},{7,9},{8,6},{9,7},{10,... | collective-permute-start | bytes 442376 | tf_op jit(solution)/shard_map/ppermute | solution.py:318
  21.7 1.2 %copy-start = (bf16[3,3,192,192]{3,2,1,0:T(8,128)(2,1)S(1)}, bf16[3,3,192,192]{3,2,1,0:T(8,128)(2,1)}, u32[]{:S(2)}) copy-start(bf16[3,3,192,192]{3,2,1,0:T(8,128)(2,1)} %w_ref.11) | copy-start | bytes 1990660
  22.9 2.0 %copy-start.2 = (bf16[3,3,192,192]{3,2,1,0:T(8,128)(2,1)S(1)}, bf16[3,3,192,192]{3,2,1,0:T(8,128)(2,1)}, u32[]{:S(2)}) copy-start(bf16[3,3,192,192]{3,2,1,0:T(8,128)(2,1)} %w_ref.9) | copy-start | bytes 1990660
  22.9 2.0 %copy-start.5 = (bf16[32,32,192]{2,1,0:T(8,128)(2,1)S(1)}, bf16[32,32,192]{2,1,0:T(8,128)(2,1)}, u32[]{:S(2)}) copy-start(bf16[32,32,192]{2,1,0:T(8,128)(2,1)} %param.5) | copy-start | bytes 1179652
  30.0 2.2 %collective-permute-start.9 = (bf16[2624,128]{1,0:T(8,128)(2,1)S(1)}, bf16[2624,128]{1,0:T(8,128)(2,1)S(1)}, u32[]{:S(2)}, u32[]{:S(2)}) collective-permute-start(bf16[2624,128]{1,0:T(8,128)(2,1)S(1)} %sibling_kernel_gradient.1), channel_id=1, source_target_pairs={{0,1},{1,0},{2,3},{3,2},{4,5},{5,4},{6,7},{7,6},{8,9},{9,8},{10,11... | collective-permute-start | bytes 2015240 | tf_op jit(solution)/shard_map/ppermute | solution.py:180
  32.3 8.1 %collective-permute-start.10 = (bf16[656,128]{1,0:T(8,128)(2,1)S(1)}, bf16[656,128]{1,0:T(8,128)(2,1)S(1)}, u32[]{:S(2)}, u32[]{:S(2)}) collective-permute-start(bf16[656,128]{1,0:T(8,128)(2,1)S(1)} %get-tuple-element.53), channel_id=1, source_target_pairs={{0,6},{1,7},{2,4},{3,5},{4,2},{5,3},{6,0},{7,1},{8,14},{9,15},{10,... | collective-permute-start | bytes 503816 | tf_op jit(solution)/shard_map/ppermute | solution.py:180
  32.4 32.0 %collective-permute-start.8 = (bf16[1536,128]{1,0:T(8,128)(2,1)S(1)}, bf16[1536,128]{1,0:T(8,128)(2,1)S(1)}, u32[]{:S(2)}, u32[]{:S(2)}) collective-permute-start(bf16[1536,128]{1,0:T(8,128)(2,1)S(1)} %get-tuple-element.54), channel_id=1, source_target_pairs={{0,1},{1,0},{2,3},{3,2},{4,5},{5,4},{6,7},{7,6},{8,9},{9,8},{10,11... | collective-permute-start | bytes 1179656 | tf_op jit(solution)/shard_map/ppermute | solution.py:476
  32.6 8.7 %collective-permute-start.12 = (bf16[656,128]{1,0:T(8,128)(2,1)S(1)}, bf16[656,128]{1,0:T(8,128)(2,1)S(1)}, u32[]{:S(2)}, u32[]{:S(2)}) collective-permute-start(bf16[656,128]{1,0:T(8,128)(2,1)S(1)} %get-tuple-element.56), channel_id=1, source_target_pairs={{0,2},{1,3},{2,0},{3,1},{4,6},{5,7},{6,4},{7,5},{8,10},{9,11},{10,... | collective-permute-start | bytes 503816 | tf_op jit(solution)/shard_map/ppermute | solution.py:180
  33.0 10.3 %collective-permute-start.13 = (bf16[656,128]{1,0:T(8,128)(2,1)S(1)}, bf16[656,128]{1,0:T(8,128)(2,1)S(1)}, u32[]{:S(2)}, u32[]{:S(2)}) collective-permute-start(bf16[656,128]{1,0:T(8,128)(2,1)S(1)} %get-tuple-element.57), channel_id=1, source_target_pairs={{0,4},{1,5},{2,6},{3,7},{4,0},{5,1},{6,2},{7,3},{8,12},{9,13},{10,... | collective-permute-start | bytes 503816 | tf_op jit(solution)/shard_map/ppermute | solution.py:180
  40.5 25.0 %collective-permute-start.11 = (bf16[1536,128]{1,0:T(8,128)(2,1)S(1)}, bf16[1536,128]{1,0:T(8,128)(2,1)S(1)}, u32[]{:S(2)}, u32[]{:S(2)}) collective-permute-start(bf16[1536,128]{1,0:T(8,128)(2,1)S(1)} %get-tuple-element.54), channel_id=1, source_target_pairs={{0,31},{1,2},{2,1},{3,4},{4,3},{5,6},{6,5},{7,8},{8,7},{9,10},{10,... | collective-permute-start | bytes 1179656 | tf_op jit(solution)/shard_map/ppermute | solution.py:477
  43.3 5.2 %collective-permute-start.14 = (bf16[176,128]{1,0:T(8,128)(2,1)S(1)}, bf16[176,128]{1,0:T(8,128)(2,1)S(1)}, u32[]{:S(2)}, u32[]{:S(2)}) collective-permute-start(bf16[176,128]{1,0:T(8,128)(2,1)S(1)} %get-tuple-element.59), channel_id=1, source_target_pairs={{0,8},{1,9},{2,10},{3,11},{4,12},{5,13},{6,14},{7,15},{8,0},{9,1},... | collective-permute-start | bytes 135176 | tf_op jit(solution)/shard_map/ppermute | solution.py:180
  43.9 5.3 %collective-permute-start.15 = (bf16[176,128]{1,0:T(8,128)(2,1)S(1)}, bf16[176,128]{1,0:T(8,128)(2,1)S(1)}, u32[]{:S(2)}, u32[]{:S(2)}) collective-permute-start(bf16[176,128]{1,0:T(8,128)(2,1)S(1)} %get-tuple-element.60), channel_id=1, source_target_pairs={{0,16},{1,17},{2,18},{3,19},{4,20},{5,21},{6,22},{7,23},{8,24},{9,... | collective-permute-start | bytes 135176 | tf_op jit(solution)/shard_map/ppermute | solution.py:180
  46.5 5.8 %collective-permute-start.16 = (bf16[176,128]{1,0:T(8,128)(2,1)S(1)}, bf16[176,128]{1,0:T(8,128)(2,1)S(1)}, u32[]{:S(2)}, u32[]{:S(2)}) collective-permute-start(bf16[176,128]{1,0:T(8,128)(2,1)S(1)} %get-tuple-element.61), channel_id=1, source_target_pairs={{0,24},{1,25},{2,26},{3,27},{4,28},{5,29},{6,30},{7,31},{8,16},{9,... | collective-permute-start | bytes 135176 | tf_op jit(solution)/shard_map/ppermute | solution.py:180
  52.4 4.5 %collective-permute-start.17 = (bf16[176,128]{1,0:T(8,128)(2,1)S(1)}, bf16[176,128]{1,0:T(8,128)(2,1)S(1)}, u32[]{:S(2)}, u32[]{:S(2)}) collective-permute-start(bf16[176,128]{1,0:T(8,128)(2,1)S(1)} %combine_last.1.refs_0_), channel_id=1, source_target_pairs={{0,8},{1,9},{2,10},{3,11},{4,12},{5,13},{6,14},{7,15},{8,0},{9,1},... | collective-permute-start | bytes 135176 | tf_op jit(solution)/shard_map/ppermute | solution.py:180
  52.4 5.2 %collective-permute-start.18 = (bf16[176,128]{1,0:T(8,128)(2,1)S(1)}, bf16[176,128]{1,0:T(8,128)(2,1)S(1)}, u32[]{:S(2)}, u32[]{:S(2)}) collective-permute-start(bf16[176,128]{1,0:T(8,128)(2,1)S(1)} %combine_last.1.refs_0_), channel_id=1, source_target_pairs={{0,16},{1,17},{2,18},{3,19},{4,20},{5,21},{6,22},{7,23},{8,24},{9,... | collective-permute-start | bytes 135176 | tf_op jit(solution)/shard_map/ppermute | solution.py:180
  55.0 5.8 %collective-permute-start.19 = (bf16[176,128]{1,0:T(8,128)(2,1)S(1)}, bf16[176,128]{1,0:T(8,128)(2,1)S(1)}, u32[]{:S(2)}, u32[]{:S(2)}) collective-permute-start(bf16[176,128]{1,0:T(8,128)(2,1)S(1)} %combine_last.1.refs_0_), channel_id=1, source_target_pairs={{0,24},{1,25},{2,26},{3,27},{4,28},{5,29},{6,30},{7,31},{8,16},{9,... | collective-permute-start | bytes 135176 | tf_op jit(solution)/shard_map/ppermute | solution.py:180
  60.8 7.5 %collective-permute-start.25 = (bf16[656,128]{1,0:T(8,128)(2,1)S(1)}, bf16[656,128]{1,0:T(8,128)(2,1)S(1)}, u32[]{:S(2)}, u32[]{:S(2)}) collective-permute-start(bf16[656,128]{1,0:T(8,128)(2,1)S(1)} %assemble.1.refs_0_), channel_id=1, source_target_pairs={{0,6},{1,7},{2,4},{3,5},{4,2},{5,3},{6,0},{7,1},{8,14},{9,15},{10,... | collective-permute-start | bytes 503816 | tf_op jit(solution)/shard_map/ppermute | solution.py:180
  62.9 7.0 %collective-permute-start.23 = (bf16[656,128]{1,0:T(8,128)(2,1)S(1)}, bf16[656,128]{1,0:T(8,128)(2,1)S(1)}, u32[]{:S(2)}, u32[]{:S(2)}) collective-permute-start(bf16[656,128]{1,0:T(8,128)(2,1)S(1)} %assemble.1.refs_0_), channel_id=1, source_target_pairs={{0,4},{1,5},{2,6},{3,7},{4,0},{5,1},{6,2},{7,3},{8,12},{9,13},{10,... | collective-permute-start | bytes 503816 | tf_op jit(solution)/shard_map/ppermute | solution.py:180
  63.0 7.0 %collective-permute-start.21 = (bf16[656,128]{1,0:T(8,128)(2,1)S(1)}, bf16[656,128]{1,0:T(8,128)(2,1)S(1)}, u32[]{:S(2)}, u32[]{:S(2)}) collective-permute-start(bf16[656,128]{1,0:T(8,128)(2,1)S(1)} %assemble.1.refs_0_), channel_id=1, source_target_pairs={{0,2},{1,3},{2,0},{3,1},{4,6},{5,7},{6,4},{7,5},{8,10},{9,11},{10,... | collective-permute-start | bytes 503816 | tf_op jit(solution)/shard_map/ppermute | solution.py:180
  65.4 6.6 %collective-permute-start.20 = (bf16[656,128]{1,0:T(8,128)(2,1)S(1)}, bf16[656,128]{1,0:T(8,128)(2,1)S(1)}, u32[]{:S(2)}, u32[]{:S(2)}) collective-permute-start(bf16[656,128]{1,0:T(8,128)(2,1)S(1)} %assemble.1.refs_0_), channel_id=1, source_target_pairs={{0,1},{1,0},{2,3},{3,2},{4,5},{5,4},{6,7},{7,6},{8,9},{9,8},{10,11... | collective-permute-start | bytes 503816 | tf_op jit(solution)/shard_map/ppermute | solution.py:180
  68.3 3.7 %collective-permute-start.26 = (bf16[656,128]{1,0:T(8,128)(2,1)S(1)}, bf16[656,128]{1,0:T(8,128)(2,1)S(1)}, u32[]{:S(2)}, u32[]{:S(2)}) collective-permute-start(bf16[656,128]{1,0:T(8,128)(2,1)S(1)} %collective-permute-done.25.refs_3_), channel_id=1, source_target_pairs={{0,1},{1,0},{2,3},{3,2},{4,5},{5,4},{6,7},{7,6},{8,9},{9,8},{10,11... | collective-permute-start | bytes 503816 | tf_op jit(solution)/shard_map/ppermute | solution.py:180
  69.9 2.1 %collective-permute-start.24 = (bf16[656,128]{1,0:T(8,128)(2,1)S(1)}, bf16[656,128]{1,0:T(8,128)(2,1)S(1)}, u32[]{:S(2)}, u32[]{:S(2)}) collective-permute-start(bf16[656,128]{1,0:T(8,128)(2,1)S(1)} %collective-permute-done.23.refs_2_), channel_id=1, source_target_pairs={{0,1},{1,0},{2,3},{3,2},{4,5},{5,4},{6,7},{7,6},{8,9},{9,8},{10,11... | collective-permute-start | bytes 503816 | tf_op jit(solution)/shard_map/ppermute | solution.py:180
  69.9 2.1 %collective-permute-start.22 = (bf16[656,128]{1,0:T(8,128)(2,1)S(1)}, bf16[656,128]{1,0:T(8,128)(2,1)S(1)}, u32[]{:S(2)}, u32[]{:S(2)}) collective-permute-start(bf16[656,128]{1,0:T(8,128)(2,1)S(1)} %collective-permute-done.21.refs_1_), channel_id=1, source_target_pairs={{0,1},{1,0},{2,3},{3,2},{4,5},{5,4},{6,7},{7,6},{8,9},{9,8},{10,11... | collective-permute-start | bytes 503816 | tf_op jit(solution)/shard_map/ppermute | solution.py:180
  (1 other events, 1.0 us)

commit v6 on v5

--- a/solution.py
+++ b/solution.py
@@ -11,8 +11,8 @@
 SECOND_SPREAD = 64
 LANES = 128
 ROW_TILE = 16
-G_SHARE = 5 / 8
-X_SHARE = 1 / 2
+G_SHARE = (7, 12)
+X_SHARE = (49, 96)
 VMEM_LIMIT = 20 * 1024 * 1024
 
 
@@ -260,7 +260,7 @@
     def pack_one(field, share=None):
         sizes = [pshape[0]]
         if share is not None:
-            first = max(int(pshape[0] * share) // ROW_TILE, 1) * ROW_TILE
+            first = max(pshape[0] * share[0] // share[1] // ROW_TILE, 1) * ROW_TILE
             sizes = [first, pshape[0] - first]
         shapes = [shape_of((size, pshape[1]), bf16) for size in sizes]
         packed = call(pack_body, shapes, [field.reshape(rows, channels)], name="pack")

time: 73.9 us -> 73.5 us (level)
  waiting for transfers between devices: 24.3 us -> 23.1 us
  starting transfers between devices: 32.8 us -> 33.7 us
    ppermute x1, starting transfers between devices: 0.8 us -> 1.92 us  [shards(): lax.ppermute(after(pre_packed, plane_got), 'lon', outer_pairs(steps))]
  transfers between devices with their start and end apart: 27 -> 27, of which waited for: 12 -> 13; matrix products, arithmetic and copies ran while one was open for 0% -> 0% of each run, Pallas kernels for 12% -> 12%
where the time goes in v6:
time: 73.5 us; the launch traced here: 73.2 us
  starting transfers between devices  33.7 us (46%)
  waiting for transfers between devices  23.1 us (31%)
  Pallas kernels  12.3 us (17%)
  local copies, waits for them, and re-layouts  3.34 us (5%)
  between operations  0.84 us (1%)
    ppermute x17, waiting for transfers between devices, swapped(): lax.ppermute(value, 'lon', [(i, i ^ k * stride) for i in range(count)])  18.5 us
    ppermute x17, starting transfers between devices, swapped(): lax.ppermute(value, 'lon', [(i, i ^ k * stride) for i in range(count)])  16.7 us
    pallas_call x16, Pallas kernels, call(): pl.pallas_call(body, out_shape=list(outs), in_specs=[far if i in far_args...  12.3 us
    ppermute x4, starting transfers between devices, shards(): lax.ppermute(part, 'lon', inner_pairs(steps))  7.19 us
    ppermute x2, starting transfers between devices, shards(): lax.ppermute(part, 'lon', outer_pairs(steps))  5.34 us
    unnamed x12, local copies, waits for them, and re-layouts  3.34 us
    ppermute x4, waiting for transfers between devices, shards(): lax.ppermute(part, 'lon', inner_pairs(steps))  3.02 us
    ppermute x1, starting transfers between devices, shards(): lax.ppermute(g_packed[1], 'lon', outer_pairs(steps))  2.56 us
  transfers between devices with their start and end apart: 27, of which 13 were waited for; matrix products, arithmetic and copies ran while one was open for 0% of the time, Pallas kernels for 12%

profile of v6, /device:TPU:0, one launch (start us, length us, event | category | flops | bytes accessed | tf_op | source)
XLA Modules:
  0.0 73.2 jit_solution(12888941798079727459)
XLA Ops:
  0.7 1.1 %copy-done.4 = bf16[32,32,192]{2,1,0:T(8,128)(2,1)S(1)} copy-done((bf16[32,32,192]{2,1,0:T(8,128)(2,1)S(1)}, bf16[32,32,192]{2,1,0:T(8,128)(2,1)}, u32[]{:S(2)}) %copy-start.4) | copy-done | bytes 393240
  1.9 3.0 %collective-permute-start = (bf16[896,128]{1,0:T(8,128)(2,1)S(1)}, bf16[896,128]{1,0:T(8,128)(2,1)S(1)}, u32[]{:S(2)}, u32[]{:S(2)}) collective-permute-start(bf16[896,128]{1,0:T(8,128)(2,1)S(1)} %get-tuple-element.36), channel_id=1, source_target_pairs={{0,2},{1,3},{2,0},{3,1},{4,6},{5,7},{6,4},{7,5},{8,10},{9,11},{10,... | collective-permute-start | bytes 688136 | tf_op jit(solution)/shard_map/ppermute | solution.py:315
  4.9 1.0 %copy-done.3 = bf16[32,32,192]{2,1,0:T(8,128)(2,1)S(1)} copy-done((bf16[32,32,192]{2,1,0:T(8,128)(2,1)S(1)}, bf16[32,32,192]{2,1,0:T(8,128)(2,1)}, u32[]{:S(2)}) %copy-start.3) | copy-done | bytes 393240
  6.6 4.2 %collective-permute-start.4 = (bf16[784,128]{1,0:T(8,128)(2,1)S(1)}, bf16[784,128]{1,0:T(8,128)(2,1)S(1)}, u32[]{:S(2)}, u32[]{:S(2)}) collective-permute-start(bf16[784,128]{1,0:T(8,128)(2,1)S(1)} %get-tuple-element.40), channel_id=1, source_target_pairs={{0,31},{1,2},{2,1},{3,4},{4,3},{5,6},{6,5},{7,8},{8,7},{9,10},{10,... | collective-permute-start | bytes 602120 | tf_op jit(solution)/shard_map/ppermute | solution.py:326
  10.8 1.1 %collective-permute-start.5 = (bf16[752,128]{1,0:T(8,128)(2,1)S(1)}, bf16[752,128]{1,0:T(8,128)(2,1)S(1)}, u32[]{:S(2)}, u32[]{:S(2)}) collective-permute-start(bf16[752,128]{1,0:T(8,128)(2,1)S(1)} %get-tuple-element.41), channel_id=1, source_target_pairs={{0,31},{1,2},{2,1},{3,4},{4,3},{5,6},{6,5},{7,8},{8,7},{9,10},{10,... | collective-permute-start | bytes 577544 | tf_op jit(solution)/shard_map/ppermute | solution.py:326
  12.0 2.3 %collective-permute-done.rest_0_ = bf16[896,128]{1,0:T(8,128)(2,1)S(1)} collective-permute-done((bf16[896,128]{1,0:T(8,128)(2,1)S(1)}, bf16[896,128]{1,0:T(8,128)(2,1)S(1)}, u32[]{:S(2)}, u32[]{:S(2)}) %collective-permute-start) | collective-permute-done | bytes 229408 | tf_op jit(solution)/shard_map/ppermute | solution.py:315
  14.3 3.6 %collective-permute-start.1 = (bf16[640,128]{1,0:T(8,128)(2,1)S(1)}, bf16[640,128]{1,0:T(8,128)(2,1)S(1)}, u32[]{:S(2)}, u32[]{:S(2)}) collective-permute-start(bf16[640,128]{1,0:T(8,128)(2,1)S(1)} %get-tuple-element.37), channel_id=1, source_target_pairs={{0,2},{1,3},{2,0},{3,1},{4,6},{5,7},{6,4},{7,5},{8,10},{9,11},{10,... | collective-permute-start | bytes 491528 | tf_op jit(solution)/shard_map/ppermute | solution.py:315
  17.9 2.6 %collective-permute-start.7 = (bf16[640,128]{1,0:T(8,128)(2,1)S(1)}, bf16[640,128]{1,0:T(8,128)(2,1)S(1)}, u32[]{:S(2)}, u32[]{:S(2)}) collective-permute-start(bf16[640,128]{1,0:T(8,128)(2,1)S(1)} %get-tuple-element.37), channel_id=1, source_target_pairs={{0,30},{1,31},{2,4},{3,5},{4,2},{5,3},{6,8},{7,9},{8,6},{9,7},{10,... | collective-permute-start | bytes 491528 | tf_op jit(solution)/shard_map/ppermute | solution.py:318
  20.5 1.2 %copy-done = bf16[3,3,192,192]{3,2,1,0:T(8,128)(2,1)S(1)} copy-done((bf16[3,3,192,192]{3,2,1,0:T(8,128)(2,1)S(1)}, bf16[3,3,192,192]{3,2,1,0:T(8,128)(2,1)}, u32[]{:S(2)}) %copy-start) | copy-done | bytes 663576
  21.7 1.0 %near_pre_act.1 = (f32[1024,192]{1,0:T(8,128)S(1)}, bf16[576,1024]{1,0:T(8,128)(2,1)S(1)}, bf16[576,1024]{1,0:T(8,128)(2,1)S(1)}) custom-call(bf16[1024,192]{1,0:T(8,128)(2,1)S(1)} %bitcast.5, bf16[3,3,192,192]{3,2,1,0:T(8,128)(2,1)S(1)} %copy-done, bf16[784,128]{1,0:T(8,128)(2,1)S(1)} %collective-permute-done.2.rest_0_, ...), custom_call_target="tpu_custom_call" | custom-call | flops 452984832 | bytes 4595712 | tf_op jit(solution)/shard_map/near_pre_act/pallas_call | solution.py:22
  22.7 1.0 %hidden.1 = (bf16[192,1024]{1,0:T(8,128)(2,1)S(1)}, f32[1024,192]{1,0:T(8,128)S(1)}, bf16[576,1024]{1,0:T(8,128)(2,1)S(1)}) custom-call(f32[1024,192]{1,0:T(8,128)S(1)} %get-tuple-element.42.part_ref, bf16[3,3,192,192]{3,2,1,0:T(8,128)(2,1)S(1)} %copy-done.1, bf16[784,128]{1,0:T(8,128)(2,1)S(1)} %collective-permute-done.4.rest_0_, ...), custom_call_target="tpu_custom_call" | custom-call | flops 226492416 | bytes 4202496 | tf_op jit(solution)/shard_map/hidden/pallas_call | solution.py:22
  24.4 1.0 %near_hidden_grad.1 = (f32[1024,192]{1,0:T(8,128)S(1)}, bf16[1088,192]{1,0:T(8,128)(2,1)S(1)}, bf16[1088,192]{1,0:T(8,128)(2,1)S(1)}) custom-call(bf16[1024,192]{1,0:T(8,128)(2,1)S(1)} %bitcast.7, bf16[3,3,192,192]{3,2,1,0:T(8,128)(2,1)S(1)} %copy-done.2, bf16[896,128]{1,0:T(8,128)(2,1)S(1)} %collective-permute-done.rest_0_, ...), custom_call_target="tpu_custom_call" | custom-call | flops 452984832 | bytes 3072000 | tf_op jit(solution)/shard_map/near_hidden_grad/pallas_call | solution.py:22
  25.4 1.6 %collective-permute-done.7.rest_1_ = bf16[640,128]{1,0:T(8,128)(2,1)S(1)} collective-permute-done((bf16[640,128]{1,0:T(8,128)(2,1)S(1)}, bf16[640,128]{1,0:T(8,128)(2,1)S(1)}, u32[]{:S(2)}, u32[]{:S(2)}) %collective-permute-start.7) | collective-permute-done | bytes 163872 | tf_op jit(solution)/shard_map/ppermute | solution.py:318
  27.7 1.2 %sibling_kernel_gradient.1 = bf16[2624,128]{1,0:T(8,128)(2,1)S(1)} custom-call(bf16[192,1024]{1,0:T(8,128)(2,1)S(1)} %get-tuple-element.46.hid_ref, bf16[1088,192]{1,0:T(8,128)(2,1)S(1)} %get-tuple-element.47.g0, bf16[1088,192]{1,0:T(8,128)(2,1)S(1)} %get-tuple-element.48.g1, bf16[1088,192]{1,0:T(8,128)(2,1)S(1)} %get-tuple-element.49.g2, ...), custom_call_target="tpu_custom_call" | custom-call | flops 679477248 | bytes 6250496 | tf_op jit(solution)/shard_map/sibling_kernel_gradient/pallas_call | solution.py:22
  29.0 1.3 %own_kernel_gradient.1.own_ref = f32[2624,128]{1,0:T(8,128)S(1)} custom-call(bf16[192,1024]{1,0:T(8,128)(2,1)S(1)} %get-tuple-element.46.hid_ref, bf16[1088,192]{1,0:T(8,128)(2,1)S(1)} %get-tuple-element.47.g0, bf16[1088,192]{1,0:T(8,128)(2,1)S(1)} %get-tuple-element.48.g1, bf16[1088,192]{1,0:T(8,128)(2,1)S(1)} %get-tuple-element.49.g2, ...), custom_call_target="tpu_custom_call" | custom-call | flops 679477248 | bytes 6922240 | tf_op jit(solution)/shard_map/own_kernel_gradient/pallas_call | solution.py:22
  32.1 2.4 %collective-permute-start.12 = (bf16[656,128]{1,0:T(8,128)(2,1)S(1)}, bf16[656,128]{1,0:T(8,128)(2,1)S(1)}, u32[]{:S(2)}, u32[]{:S(2)}) collective-permute-start(bf16[656,128]{1,0:T(8,128)(2,1)S(1)} %get-tuple-element.56), channel_id=1, source_target_pairs={{0,2},{1,3},{2,0},{3,1},{4,6},{5,7},{6,4},{7,5},{8,10},{9,11},{10,... | collective-permute-start | bytes 503816 | tf_op jit(solution)/shard_map/ppermute | solution.py:180
  34.8 4.5 %collective-permute-done.10.refs_2_ = bf16[656,128]{1,0:T(8,128)(2,1)S(1)} collective-permute-done((bf16[656,128]{1,0:T(8,128)(2,1)S(1)}, bf16[656,128]{1,0:T(8,128)(2,1)S(1)}, u32[]{:S(2)}, u32[]{:S(2)}) %collective-permute-start.10) | collective-permute-done | bytes 167968 | tf_op jit(solution)/shard_map/ppermute | solution.py:180
  39.4 1.9 %collective-permute-start.11 = (bf16[1536,128]{1,0:T(8,128)(2,1)S(1)}, bf16[1536,128]{1,0:T(8,128)(2,1)S(1)}, u32[]{:S(2)}, u32[]{:S(2)}) collective-permute-start(bf16[1536,128]{1,0:T(8,128)(2,1)S(1)} %get-tuple-element.54), channel_id=1, source_target_pairs={{0,31},{1,2},{2,1},{3,4},{4,3},{5,6},{6,5},{7,8},{8,7},{9,10},{10,... | collective-permute-start | bytes 1179656 | tf_op jit(solution)/shard_map/ppermute | solution.py:477
  41.3 1.2 %collective-permute-done.12.refs_0_ = bf16[656,128]{1,0:T(8,128)(2,1)S(1)} collective-permute-done((bf16[656,128]{1,0:T(8,128)(2,1)S(1)}, bf16[656,128]{1,0:T(8,128)(2,1)S(1)}, u32[]{:S(2)}, u32[]{:S(2)}) %collective-permute-start.12) | collective-permute-done | bytes 167968 | tf_op jit(solution)/shard_map/ppermute | solution.py:180
  42.6 1.6 %collective-permute-start.14 = (bf16[176,128]{1,0:T(8,128)(2,1)S(1)}, bf16[176,128]{1,0:T(8,128)(2,1)S(1)}, u32[]{:S(2)}, u32[]{:S(2)}) collective-permute-start(bf16[176,128]{1,0:T(8,128)(2,1)S(1)} %get-tuple-element.59), channel_id=1, source_target_pairs={{0,8},{1,9},{2,10},{3,11},{4,12},{5,13},{6,14},{7,15},{8,0},{9,1},... | collective-permute-start | bytes 135176 | tf_op jit(solution)/shard_map/ppermute | solution.py:180
  44.3 2.6 %collective-permute-start.15 = (bf16[176,128]{1,0:T(8,128)(2,1)S(1)}, bf16[176,128]{1,0:T(8,128)(2,1)S(1)}, u32[]{:S(2)}, u32[]{:S(2)}) collective-permute-start(bf16[176,128]{1,0:T(8,128)(2,1)S(1)} %get-tuple-element.60), channel_id=1, source_target_pairs={{0,16},{1,17},{2,18},{3,19},{4,20},{5,21},{6,22},{7,23},{8,24},{9,... | collective-permute-start | bytes 135176 | tf_op jit(solution)/shard_map/ppermute | solution.py:180
  47.1 1.5 %collective-permute-done.14.refs_0_ = bf16[176,128]{1,0:T(8,128)(2,1)S(1)} collective-permute-done((bf16[176,128]{1,0:T(8,128)(2,1)S(1)}, bf16[176,128]{1,0:T(8,128)(2,1)S(1)}, u32[]{:S(2)}, u32[]{:S(2)}) %collective-permute-start.14) | collective-permute-done | bytes 45088 | tf_op jit(solution)/shard_map/ppermute | solution.py:180
  49.3 3.4 %collective-permute-done.16.refs_2_ = bf16[176,128]{1,0:T(8,128)(2,1)S(1)} collective-permute-done((bf16[176,128]{1,0:T(8,128)(2,1)S(1)}, bf16[176,128]{1,0:T(8,128)(2,1)S(1)}, u32[]{:S(2)}, u32[]{:S(2)}) %collective-permute-start.16) | collective-permute-done | bytes 45088 | tf_op jit(solution)/shard_map/ppermute | solution.py:180
  52.8 2.2 %collective-permute-start.18 = (bf16[176,128]{1,0:T(8,128)(2,1)S(1)}, bf16[176,128]{1,0:T(8,128)(2,1)S(1)}, u32[]{:S(2)}, u32[]{:S(2)}) collective-permute-start(bf16[176,128]{1,0:T(8,128)(2,1)S(1)} %combine_last.1.refs_0_), channel_id=1, source_target_pairs={{0,16},{1,17},{2,18},{3,19},{4,20},{5,21},{6,22},{7,23},{8,24},{9,... | collective-permute-start | bytes 135176 | tf_op jit(solution)/shard_map/ppermute | solution.py:180
  55.0 2.1 %collective-permute-start.19 = (bf16[176,128]{1,0:T(8,128)(2,1)S(1)}, bf16[176,128]{1,0:T(8,128)(2,1)S(1)}, u32[]{:S(2)}, u32[]{:S(2)}) collective-permute-start(bf16[176,128]{1,0:T(8,128)(2,1)S(1)} %combine_last.1.refs_0_), channel_id=1, source_target_pairs={{0,24},{1,25},{2,26},{3,27},{4,28},{5,29},{6,30},{7,31},{8,16},{9,... | collective-permute-start | bytes 135176 | tf_op jit(solution)/shard_map/ppermute | solution.py:180
  57.9 2.9 %collective-permute-done.19.refs_3_ = bf16[176,128]{1,0:T(8,128)(2,1)S(1)} collective-permute-done((bf16[176,128]{1,0:T(8,128)(2,1)S(1)}, bf16[176,128]{1,0:T(8,128)(2,1)S(1)}, u32[]{:S(2)}, u32[]{:S(2)}) %collective-permute-start.19) | collective-permute-done | bytes 45088 | tf_op jit(solution)/shard_map/ppermute | solution.py:180
  60.9 1.1 %collective-permute-start.25 = (bf16[656,128]{1,0:T(8,128)(2,1)S(1)}, bf16[656,128]{1,0:T(8,128)(2,1)S(1)}, u32[]{:S(2)}, u32[]{:S(2)}) collective-permute-start(bf16[656,128]{1,0:T(8,128)(2,1)S(1)} %assemble.1.refs_0_), channel_id=1, source_target_pairs={{0,6},{1,7},{2,4},{3,5},{4,2},{5,3},{6,0},{7,1},{8,14},{9,15},{10,... | collective-permute-start | bytes 503816 | tf_op jit(solution)/shard_map/ppermute | solution.py:180
  62.9 1.5 %collective-permute-start.21 = (bf16[656,128]{1,0:T(8,128)(2,1)S(1)}, bf16[656,128]{1,0:T(8,128)(2,1)S(1)}, u32[]{:S(2)}, u32[]{:S(2)}) collective-permute-start(bf16[656,128]{1,0:T(8,128)(2,1)S(1)} %assemble.1.refs_0_), channel_id=1, source_target_pairs={{0,2},{1,3},{2,0},{3,1},{4,6},{5,7},{6,4},{7,5},{8,10},{9,11},{10,... | collective-permute-start | bytes 503816 | tf_op jit(solution)/shard_map/ppermute | solution.py:180
  65.5 1.4 %input_gradient.1 = bf16[1024,192]{1,0:T(8,128)(2,1)} custom-call(f32[1024,192]{1,0:T(8,128)S(1)} %near_input_gradient.1.part_ref, bf16[3,3,192,192]{3,2,1,0:T(8,128)(2,1)S(1)} %copy-done.1, bf16[1536,128]{1,0:T(8,128)(2,1)S(1)} %collective-permute-done.11.rest_0_), custom_call_target="tpu_custom_call" | custom-call | flops 226492416 | bytes 2236416 | tf_op jit(solution)/shard_map/input_gradient/pallas_call | solution.py:22
  66.9 1.7 %collective-permute-done.25.refs_3_ = bf16[656,128]{1,0:T(8,128)(2,1)S(1)} collective-permute-done((bf16[656,128]{1,0:T(8,128)(2,1)S(1)}, bf16[656,128]{1,0:T(8,128)(2,1)S(1)}, u32[]{:S(2)}, u32[]{:S(2)}) %collective-permute-start.25) | collective-permute-done | bytes 167968 | tf_op jit(solution)/shard_map/ppermute | solution.py:180
  70.0 1.6 %unpack_gradients.2 = (f32[3,3,192,192]{3,2,1,0:T(8,128)}, f32[3,3,192,192]{3,2,1,0:T(8,128)}) custom-call(bf16[656,128]{1,0:T(8,128)(2,1)S(1)} %assemble.1.refs_0_, bf16[656,128]{1,0:T(8,128)(2,1)S(1)} %collective-permute-done.21.refs_1_, bf16[656,128]{1,0:T(8,128)(2,1)S(1)} %collective-permute-done.23.refs_2_, ...), custom_call_target="tpu_custom_call" | custom-call | bytes 3325952 | tf_op jit(solution)/shard_map/unpack_gradients/pallas_call | solution.py:22
  71.6 1.6 %unpack_gradients.3 = (f32[3,3,192,192]{3,2,1,0:T(8,128)}, f32[3,3,192,192]{3,2,1,0:T(8,128)}) custom-call(bf16[656,128]{1,0:T(8,128)(2,1)S(1)} %collective-permute-done.20.refs_0_, bf16[656,128]{1,0:T(8,128)(2,1)S(1)} %collective-permute-done.22.refs_1_, ...), custom_call_target="tpu_custom_call", output_to_operand_aliasing={{0}: (4, {}), {1}: (5, {})} | custom-call | bytes 5980160 | tf_op jit(solution)/shard_map/unpack_gradients/pallas_call | solution.py:22
  (50 shorter events, 9.7 us)
Async XLA Ops:
  0.6 22.1 %copy-start.1 = (bf16[3,3,192,192]{3,2,1,0:T(8,128)(2,1)S(1)}, bf16[3,3,192,192]{3,2,1,0:T(8,128)(2,1)}, u32[]{:S(2)}) copy-start(bf16[3,3,192,192]{3,2,1,0:T(8,128)(2,1)} %w_ref.11) | copy-start | bytes 1990660
  0.6 1.1 %copy-start.4 = (bf16[32,32,192]{2,1,0:T(8,128)(2,1)S(1)}, bf16[32,32,192]{2,1,0:T(8,128)(2,1)}, u32[]{:S(2)}) copy-start(bf16[32,32,192]{2,1,0:T(8,128)(2,1)} %param.5) | copy-start | bytes 1179652
  1.9 12.4 %collective-permute-start = (bf16[896,128]{1,0:T(8,128)(2,1)S(1)}, bf16[896,128]{1,0:T(8,128)(2,1)S(1)}, u32[]{:S(2)}, u32[]{:S(2)}) collective-permute-start(bf16[896,128]{1,0:T(8,128)(2,1)S(1)} %get-tuple-element.36), channel_id=1, source_target_pairs={{0,2},{1,3},{2,0},{3,1},{4,6},{5,7},{6,4},{7,5},{8,10},{9,11},{10,... | collective-permute-start | bytes 688136 | tf_op jit(solution)/shard_map/ppermute | solution.py:315
  6.0 8.3 %collective-permute-start.3 = (bf16[752,128]{1,0:T(8,128)(2,1)S(1)}, bf16[752,128]{1,0:T(8,128)(2,1)S(1)}, u32[]{:S(2)}, u32[]{:S(2)}) collective-permute-start(bf16[752,128]{1,0:T(8,128)(2,1)S(1)} %get-tuple-element.41), channel_id=1, source_target_pairs={{0,1},{1,0},{2,3},{3,2},{4,5},{5,4},{6,7},{7,6},{8,9},{9,8},{10,11... | collective-permute-start | bytes 577544 | tf_op jit(solution)/shard_map/ppermute | solution.py:325
  6.1 11.8 %collective-permute-start.2 = (bf16[784,128]{1,0:T(8,128)(2,1)S(1)}, bf16[784,128]{1,0:T(8,128)(2,1)S(1)}, u32[]{:S(2)}, u32[]{:S(2)}) collective-permute-start(bf16[784,128]{1,0:T(8,128)(2,1)S(1)} %get-tuple-element.40), channel_id=1, source_target_pairs={{0,1},{1,0},{2,3},{3,2},{4,5},{5,4},{6,7},{7,6},{8,9},{9,8},{10,11... | collective-permute-start | bytes 602120 | tf_op jit(solution)/shard_map/ppermute | solution.py:325
  6.6 16.1 %collective-permute-start.4 = (bf16[784,128]{1,0:T(8,128)(2,1)S(1)}, bf16[784,128]{1,0:T(8,128)(2,1)S(1)}, u32[]{:S(2)}, u32[]{:S(2)}) collective-permute-start(bf16[784,128]{1,0:T(8,128)(2,1)S(1)} %get-tuple-element.40), channel_id=1, source_target_pairs={{0,31},{1,2},{2,1},{3,4},{4,3},{5,6},{6,5},{7,8},{8,7},{9,10},{10,... | collective-permute-start | bytes 602120 | tf_op jit(solution)/shard_map/ppermute | solution.py:326
  10.8 11.8 %collective-permute-start.5 = (bf16[752,128]{1,0:T(8,128)(2,1)S(1)}, bf16[752,128]{1,0:T(8,128)(2,1)S(1)}, u32[]{:S(2)}, u32[]{:S(2)}) collective-permute-start(bf16[752,128]{1,0:T(8,128)(2,1)S(1)} %get-tuple-element.41), channel_id=1, source_target_pairs={{0,31},{1,2},{2,1},{3,4},{4,3},{5,6},{6,5},{7,8},{8,7},{9,10},{10,... | collective-permute-start | bytes 577544 | tf_op jit(solution)/shard_map/ppermute | solution.py:326
  14.3 12.6 %collective-permute-start.6 = (bf16[896,128]{1,0:T(8,128)(2,1)S(1)}, bf16[896,128]{1,0:T(8,128)(2,1)S(1)}, u32[]{:S(2)}, u32[]{:S(2)}) collective-permute-start(bf16[896,128]{1,0:T(8,128)(2,1)S(1)} %collective-permute-done.rest_0_), channel_id=1, source_target_pairs={{0,4},{1,5},{2,30},{3,31},{4,8},{5,9},{6,2},{7,3},{8,12},{9,13},{1... | collective-permute-start | bytes 688136 | tf_op jit(solution)/shard_map/ppermute | solution.py:317
  14.3 10.0 %collective-permute-start.1 = (bf16[640,128]{1,0:T(8,128)(2,1)S(1)}, bf16[640,128]{1,0:T(8,128)(2,1)S(1)}, u32[]{:S(2)}, u32[]{:S(2)}) collective-permute-start(bf16[640,128]{1,0:T(8,128)(2,1)S(1)} %get-tuple-element.37), channel_id=1, source_target_pairs={{0,2},{1,3},{2,0},{3,1},{4,6},{5,7},{6,4},{7,5},{8,10},{9,11},{10,... | collective-permute-start | bytes 491528 | tf_op jit(solution)/shard_map/ppermute | solution.py:315
  17.9 9.0 %collective-permute-start.7 = (bf16[640,128]{1,0:T(8,128)(2,1)S(1)}, bf16[640,128]{1,0:T(8,128)(2,1)S(1)}, u32[]{:S(2)}, u32[]{:S(2)}) collective-permute-start(bf16[640,128]{1,0:T(8,128)(2,1)S(1)} %get-tuple-element.37), channel_id=1, source_target_pairs={{0,30},{1,31},{2,4},{3,5},{4,2},{5,3},{6,8},{7,9},{8,6},{9,7},{10,... | collective-permute-start | bytes 491528 | tf_op jit(solution)/shard_map/ppermute | solution.py:318
  20.5 1.2 %copy-start = (bf16[3,3,192,192]{3,2,1,0:T(8,128)(2,1)S(1)}, bf16[3,3,192,192]{3,2,1,0:T(8,128)(2,1)}, u32[]{:S(2)}) copy-start(bf16[3,3,192,192]{3,2,1,0:T(8,128)(2,1)} %w_ref.11) | copy-start | bytes 1990660
  21.7 2.7 %copy-start.2 = (bf16[3,3,192,192]{3,2,1,0:T(8,128)(2,1)S(1)}, bf16[3,3,192,192]{3,2,1,0:T(8,128)(2,1)}, u32[]{:S(2)}) copy-start(bf16[3,3,192,192]{3,2,1,0:T(8,128)(2,1)} %w_ref.9) | copy-start | bytes 1990660
  21.7 2.7 %copy-start.5 = (bf16[32,32,192]{2,1,0:T(8,128)(2,1)S(1)}, bf16[32,32,192]{2,1,0:T(8,128)(2,1)}, u32[]{:S(2)}) copy-start(bf16[32,32,192]{2,1,0:T(8,128)(2,1)} %param.5) | copy-start | bytes 1179652
  28.9 2.2 %collective-permute-start.9 = (bf16[2624,128]{1,0:T(8,128)(2,1)S(1)}, bf16[2624,128]{1,0:T(8,128)(2,1)S(1)}, u32[]{:S(2)}, u32[]{:S(2)}) collective-permute-start(bf16[2624,128]{1,0:T(8,128)(2,1)S(1)} %sibling_kernel_gradient.1), channel_id=1, source_target_pairs={{0,1},{1,0},{2,3},{3,2},{4,5},{5,4},{6,7},{7,6},{8,9},{9,8},{10,11... | collective-permute-start | bytes 2015240 | tf_op jit(solution)/shard_map/ppermute | solution.py:180
  31.3 8.1 %collective-permute-start.10 = (bf16[656,128]{1,0:T(8,128)(2,1)S(1)}, bf16[656,128]{1,0:T(8,128)(2,1)S(1)}, u32[]{:S(2)}, u32[]{:S(2)}) collective-permute-start(bf16[656,128]{1,0:T(8,128)(2,1)S(1)} %get-tuple-element.53), channel_id=1, source_target_pairs={{0,6},{1,7},{2,4},{3,5},{4,2},{5,3},{6,0},{7,1},{8,14},{9,15},{10,... | collective-permute-start | bytes 503816 | tf_op jit(solution)/shard_map/ppermute | solution.py:180
  32.1 32.3 %collective-permute-start.8 = (bf16[1536,128]{1,0:T(8,128)(2,1)S(1)}, bf16[1536,128]{1,0:T(8,128)(2,1)S(1)}, u32[]{:S(2)}, u32[]{:S(2)}) collective-permute-start(bf16[1536,128]{1,0:T(8,128)(2,1)S(1)} %get-tuple-element.54), channel_id=1, source_target_pairs={{0,1},{1,0},{2,3},{3,2},{4,5},{5,4},{6,7},{7,6},{8,9},{9,8},{10,11... | collective-permute-start | bytes 1179656 | tf_op jit(solution)/shard_map/ppermute | solution.py:476
  32.1 10.4 %collective-permute-start.12 = (bf16[656,128]{1,0:T(8,128)(2,1)S(1)}, bf16[656,128]{1,0:T(8,128)(2,1)S(1)}, u32[]{:S(2)}, u32[]{:S(2)}) collective-permute-start(bf16[656,128]{1,0:T(8,128)(2,1)S(1)} %get-tuple-element.56), channel_id=1, source_target_pairs={{0,2},{1,3},{2,0},{3,1},{4,6},{5,7},{6,4},{7,5},{8,10},{9,11},{10,... | collective-permute-start | bytes 503816 | tf_op jit(solution)/shard_map/ppermute | solution.py:180
  34.6 7.9 %collective-permute-start.13 = (bf16[656,128]{1,0:T(8,128)(2,1)S(1)}, bf16[656,128]{1,0:T(8,128)(2,1)S(1)}, u32[]{:S(2)}, u32[]{:S(2)}) collective-permute-start(bf16[656,128]{1,0:T(8,128)(2,1)S(1)} %get-tuple-element.57), channel_id=1, source_target_pairs={{0,4},{1,5},{2,6},{3,7},{4,0},{5,1},{6,2},{7,3},{8,12},{9,13},{10,... | collective-permute-start | bytes 503816 | tf_op jit(solution)/shard_map/ppermute | solution.py:180
  39.4 26.2 %collective-permute-start.11 = (bf16[1536,128]{1,0:T(8,128)(2,1)S(1)}, bf16[1536,128]{1,0:T(8,128)(2,1)S(1)}, u32[]{:S(2)}, u32[]{:S(2)}) collective-permute-start(bf16[1536,128]{1,0:T(8,128)(2,1)S(1)} %get-tuple-element.54), channel_id=1, source_target_pairs={{0,31},{1,2},{2,1},{3,4},{4,3},{5,6},{6,5},{7,8},{8,7},{9,10},{10,... | collective-permute-start | bytes 1179656 | tf_op jit(solution)/shard_map/ppermute | solution.py:477
  42.6 6.0 %collective-permute-start.14 = (bf16[176,128]{1,0:T(8,128)(2,1)S(1)}, bf16[176,128]{1,0:T(8,128)(2,1)S(1)}, u32[]{:S(2)}, u32[]{:S(2)}) collective-permute-start(bf16[176,128]{1,0:T(8,128)(2,1)S(1)} %get-tuple-element.59), channel_id=1, source_target_pairs={{0,8},{1,9},{2,10},{3,11},{4,12},{5,13},{6,14},{7,15},{8,0},{9,1},... | collective-permute-start | bytes 135176 | tf_op jit(solution)/shard_map/ppermute | solution.py:180
  44.3 5.1 %collective-permute-start.15 = (bf16[176,128]{1,0:T(8,128)(2,1)S(1)}, bf16[176,128]{1,0:T(8,128)(2,1)S(1)}, u32[]{:S(2)}, u32[]{:S(2)}) collective-permute-start(bf16[176,128]{1,0:T(8,128)(2,1)S(1)} %get-tuple-element.60), channel_id=1, source_target_pairs={{0,16},{1,17},{2,18},{3,19},{4,20},{5,21},{6,22},{7,23},{8,24},{9,... | collective-permute-start | bytes 135176 | tf_op jit(solution)/shard_map/ppermute | solution.py:180
  46.8 5.8 %collective-permute-start.16 = (bf16[176,128]{1,0:T(8,128)(2,1)S(1)}, bf16[176,128]{1,0:T(8,128)(2,1)S(1)}, u32[]{:S(2)}, u32[]{:S(2)}) collective-permute-start(bf16[176,128]{1,0:T(8,128)(2,1)S(1)} %get-tuple-element.61), channel_id=1, source_target_pairs={{0,24},{1,25},{2,26},{3,27},{4,28},{5,29},{6,30},{7,31},{8,16},{9,... | collective-permute-start | bytes 135176 | tf_op jit(solution)/shard_map/ppermute | solution.py:180
  52.7 4.5 %collective-permute-start.17 = (bf16[176,128]{1,0:T(8,128)(2,1)S(1)}, bf16[176,128]{1,0:T(8,128)(2,1)S(1)}, u32[]{:S(2)}, u32[]{:S(2)}) collective-permute-start(bf16[176,128]{1,0:T(8,128)(2,1)S(1)} %combine_last.1.refs_0_), channel_id=1, source_target_pairs={{0,8},{1,9},{2,10},{3,11},{4,12},{5,13},{6,14},{7,15},{8,0},{9,1},... | collective-permute-start | bytes 135176 | tf_op jit(solution)/shard_map/ppermute | solution.py:180
  52.8 5.1 %collective-permute-start.18 = (bf16[176,128]{1,0:T(8,128)(2,1)S(1)}, bf16[176,128]{1,0:T(8,128)(2,1)S(1)}, u32[]{:S(2)}, u32[]{:S(2)}) collective-permute-start(bf16[176,128]{1,0:T(8,128)(2,1)S(1)} %combine_last.1.refs_0_), channel_id=1, source_target_pairs={{0,16},{1,17},{2,18},{3,19},{4,20},{5,21},{6,22},{7,23},{8,24},{9,... | collective-permute-start | bytes 135176 | tf_op jit(solution)/shard_map/ppermute | solution.py:180
  55.0 5.8 %collective-permute-start.19 = (bf16[176,128]{1,0:T(8,128)(2,1)S(1)}, bf16[176,128]{1,0:T(8,128)(2,1)S(1)}, u32[]{:S(2)}, u32[]{:S(2)}) collective-permute-start(bf16[176,128]{1,0:T(8,128)(2,1)S(1)} %combine_last.1.refs_0_), channel_id=1, source_target_pairs={{0,24},{1,25},{2,26},{3,27},{4,28},{5,29},{6,30},{7,31},{8,16},{9,... | collective-permute-start | bytes 135176 | tf_op jit(solution)/shard_map/ppermute | solution.py:180
  60.9 7.8 %collective-permute-start.25 = (bf16[656,128]{1,0:T(8,128)(2,1)S(1)}, bf16[656,128]{1,0:T(8,128)(2,1)S(1)}, u32[]{:S(2)}, u32[]{:S(2)}) collective-permute-start(bf16[656,128]{1,0:T(8,128)(2,1)S(1)} %assemble.1.refs_0_), channel_id=1, source_target_pairs={{0,6},{1,7},{2,4},{3,5},{4,2},{5,3},{6,0},{7,1},{8,14},{9,15},{10,... | collective-permute-start | bytes 503816 | tf_op jit(solution)/shard_map/ppermute | solution.py:180
  62.0 7.5 %collective-permute-start.23 = (bf16[656,128]{1,0:T(8,128)(2,1)S(1)}, bf16[656,128]{1,0:T(8,128)(2,1)S(1)}, u32[]{:S(2)}, u32[]{:S(2)}) collective-permute-start(bf16[656,128]{1,0:T(8,128)(2,1)S(1)} %assemble.1.refs_0_), channel_id=1, source_target_pairs={{0,4},{1,5},{2,6},{3,7},{4,0},{5,1},{6,2},{7,3},{8,12},{9,13},{10,... | collective-permute-start | bytes 503816 | tf_op jit(solution)/shard_map/ppermute | solution.py:180
  62.9 6.6 %collective-permute-start.21 = (bf16[656,128]{1,0:T(8,128)(2,1)S(1)}, bf16[656,128]{1,0:T(8,128)(2,1)S(1)}, u32[]{:S(2)}, u32[]{:S(2)}) collective-permute-start(bf16[656,128]{1,0:T(8,128)(2,1)S(1)} %assemble.1.refs_0_), channel_id=1, source_target_pairs={{0,2},{1,3},{2,0},{3,1},{4,6},{5,7},{6,4},{7,5},{8,10},{9,11},{10,... | collective-permute-start | bytes 503816 | tf_op jit(solution)/shard_map/ppermute | solution.py:180
  65.4 6.2 %collective-permute-start.20 = (bf16[656,128]{1,0:T(8,128)(2,1)S(1)}, bf16[656,128]{1,0:T(8,128)(2,1)S(1)}, u32[]{:S(2)}, u32[]{:S(2)}) collective-permute-start(bf16[656,128]{1,0:T(8,128)(2,1)S(1)} %assemble.1.refs_0_), channel_id=1, source_target_pairs={{0,1},{1,0},{2,3},{3,2},{4,5},{5,4},{6,7},{7,6},{8,9},{9,8},{10,11... | collective-permute-start | bytes 503816 | tf_op jit(solution)/shard_map/ppermute | solution.py:180
  68.6 3.0 %collective-permute-start.26 = (bf16[656,128]{1,0:T(8,128)(2,1)S(1)}, bf16[656,128]{1,0:T(8,128)(2,1)S(1)}, u32[]{:S(2)}, u32[]{:S(2)}) collective-permute-start(bf16[656,128]{1,0:T(8,128)(2,1)S(1)} %collective-permute-done.25.refs_3_), channel_id=1, source_target_pairs={{0,1},{1,0},{2,3},{3,2},{4,5},{5,4},{6,7},{7,6},{8,9},{9,8},{10,11... | collective-permute-start | bytes 503816 | tf_op jit(solution)/shard_map/ppermute | solution.py:180
  69.5 2.1 %collective-permute-start.24 = (bf16[656,128]{1,0:T(8,128)(2,1)S(1)}, bf16[656,128]{1,0:T(8,128)(2,1)S(1)}, u32[]{:S(2)}, u32[]{:S(2)}) collective-permute-start(bf16[656,128]{1,0:T(8,128)(2,1)S(1)} %collective-permute-done.23.refs_2_), channel_id=1, source_target_pairs={{0,1},{1,0},{2,3},{3,2},{4,5},{5,4},{6,7},{7,6},{8,9},{9,8},{10,11... | collective-permute-start | bytes 503816 | tf_op jit(solution)/shard_map/ppermute | solution.py:180
  69.5 2.1 %collective-permute-start.22 = (bf16[656,128]{1,0:T(8,128)(2,1)S(1)}, bf16[656,128]{1,0:T(8,128)(2,1)S(1)}, u32[]{:S(2)}, u32[]{:S(2)}) collective-permute-start(bf16[656,128]{1,0:T(8,128)(2,1)S(1)} %collective-permute-done.21.refs_1_), channel_id=1, source_target_pairs={{0,1},{1,0},{2,3},{3,2},{4,5},{5,4},{6,7},{7,6},{8,9},{9,8},{10,11... | collective-permute-start | bytes 503816 | tf_op jit(solution)/shard_map/ppermute | solution.py:180
  (1 other events, 1.0 us)

commit v7 on v6

--- a/solution.py
+++ b/solution.py
@@ -398,7 +398,8 @@
     flat = group * part_size
 
     def kernel_gradient(which):
-        def body(hid_ref, g0, g1, g2, pre_ref, x0, x1, x2, out, flat_ref):
+        def body(hid_ref, g0, g1, g2, pre_ref, x0, x1, x2, out, *scratch):
+            flat_ref = scratch[0] if scratch else out
             chosen = which(lax.rem(lax.axis_index("lon"), 2))
 
             def put(mid, inner, outer, spread, sign):
@@ -421,7 +422,8 @@
                 sums = [jnp.dot(ref[...], pre_ref[...], preferred_element_type=f32) for ref in (x0, x1, x2)]
                 put(*([t[a * channels : (a + 1) * channels] for a in range(3)] for t in sums), FIRST_SPREAD, 1)
 
-            out[...] = flat_ref[...].astype(out.dtype)
+            if scratch:
+                out[...] = flat_ref[...].astype(out.dtype)
 
         return body
 
@@ -440,7 +442,6 @@
         kernel_gradient(lambda core: core),
         [shape_of((flat, LANES), f32)],
         fields,
-        [flat_scratch],
         flops=9 * tap_flops,
         name="own_kernel_gradient",
     )
@@ -536,20 +537,18 @@
             core = lax.rem(lax.axis_index("lon"), 2)
             for i, (_, k, side) in enumerate(parts):
                 for tap, value in enumerate(load_part(refs[i][...].astype(f32), height_of_part, channels)):
-                    stage[i, tap] = value * scale
+                    stage[i, tap // 3, tap % 3] = value * scale
                 start = pl.multiple_of((digit_of(2, group) ^ k) * height_of_part, height_of_part)
                 for which, out in enumerate((second_out, first_out)):
 
                     @pl.when((core + side) % 2 == which)
                     def _():
-                        for tap in range(9):
-                            target = out.at[tap // 3, tap % 3, pl.ds(start, height_of_part)]
-                            pltpu.make_async_copy(stage.at[i, tap], target, sems.at[9 * i + tap]).start()
+                        target = out.at[:, :, pl.ds(start, height_of_part)]
+                        pltpu.make_async_copy(stage.at[i], target, sems.at[i]).start()
 
             for i in range(len(parts)):
-                for tap in range(9):
-                    target = second_out.at[tap // 3, tap % 3, pl.ds(0, height_of_part)]
-                    pltpu.make_async_copy(stage.at[i, tap], target, sems.at[9 * i + tap]).wait()
+                target = second_out.at[:, :, pl.ds(0, height_of_part)]
+                pltpu.make_async_copy(stage.at[i], target, sems.at[i]).wait()
 
         count_in = len(parts)
         return list(
@@ -558,8 +557,8 @@
                 [shape_of((3, 3, channels, channels), f32)] * 2,
                 [array for array, _, _ in parts] + previous,
                 [
-                    pltpu.VMEM((count_in, 9, height_of_part, channels), f32),
-                    pltpu.SemaphoreType.DMA((9 * count_in,)),
+                    pltpu.VMEM((count_in, 3, 3, height_of_part, channels), f32),
+                    pltpu.SemaphoreType.DMA((count_in,)),
                 ],
                 name="unpack_gradients",
                 far_args=tuple(range(count_in, count_in + len(previous))),

time: 73.5 us -> 72.9 us (level)
  transfers between devices with their start and end apart: 27 -> 27, of which waited for: 13 -> 13; matrix products, arithmetic and copies ran while one was open for 0% -> 0% of each run, Pallas kernels for 12% -> 11%
where the time goes in v7:
time: 72.9 us; the launch traced here: 72.7 us
  starting transfers between devices  33.7 us (46%)
  waiting for transfers between devices  23.1 us (32%)
  Pallas kernels  11.7 us (16%)
  local copies, waits for them, and re-layouts  3.34 us (5%)
  between operations  0.84 us (1%)
    ppermute x17, waiting for transfers between devices, swapped(): lax.ppermute(value, 'lon', [(i, i ^ k * stride) for i in range(count)])  18.6 us
    ppermute x17, starting transfers between devices, swapped(): lax.ppermute(value, 'lon', [(i, i ^ k * stride) for i in range(count)])  16.7 us
    pallas_call x16, Pallas kernels, call(): pl.pallas_call(body, out_shape=list(outs), in_specs=[far if i in far_args...  11.7 us
    ppermute x4, starting transfers between devices, shards(): lax.ppermute(part, 'lon', inner_pairs(steps))  7.19 us
    ppermute x2, starting transfers between devices, shards(): lax.ppermute(part, 'lon', outer_pairs(steps))  5.34 us
    unnamed x12, local copies, waits for them, and re-layouts  3.34 us
    ppermute x4, waiting for transfers between devices, shards(): lax.ppermute(part, 'lon', inner_pairs(steps))  3.02 us
    ppermute x1, starting transfers between devices, shards(): lax.ppermute(g_packed[1], 'lon', outer_pairs(steps))  2.56 us
  transfers between devices with their start and end apart: 27, of which 13 were waited for; matrix products, arithmetic and copies ran while one was open for 0% of the time, Pallas kernels for 11%

profile of v7, /device:TPU:0, one launch (start us, length us, event | category | flops | bytes accessed | tf_op | source)
XLA Modules:
  0.0 72.7 jit_solution(12407194753122525915)
XLA Ops:
  0.7 1.1 %copy-done.4 = bf16[32,32,192]{2,1,0:T(8,128)(2,1)S(1)} copy-done((bf16[32,32,192]{2,1,0:T(8,128)(2,1)S(1)}, bf16[32,32,192]{2,1,0:T(8,128)(2,1)}, u32[]{:S(2)}) %copy-start.4) | copy-done | bytes 393240
  1.9 3.0 %collective-permute-start = (bf16[896,128]{1,0:T(8,128)(2,1)S(1)}, bf16[896,128]{1,0:T(8,128)(2,1)S(1)}, u32[]{:S(2)}, u32[]{:S(2)}) collective-permute-start(bf16[896,128]{1,0:T(8,128)(2,1)S(1)} %get-tuple-element.36), channel_id=1, source_target_pairs={{0,2},{1,3},{2,0},{3,1},{4,6},{5,7},{6,4},{7,5},{8,10},{9,11},{10,... | collective-permute-start | bytes 688136 | tf_op jit(solution)/shard_map/ppermute | solution.py:315
  4.9 1.0 %copy-done.3 = bf16[32,32,192]{2,1,0:T(8,128)(2,1)S(1)} copy-done((bf16[32,32,192]{2,1,0:T(8,128)(2,1)S(1)}, bf16[32,32,192]{2,1,0:T(8,128)(2,1)}, u32[]{:S(2)}) %copy-start.3) | copy-done | bytes 393240
  6.6 4.2 %collective-permute-start.4 = (bf16[784,128]{1,0:T(8,128)(2,1)S(1)}, bf16[784,128]{1,0:T(8,128)(2,1)S(1)}, u32[]{:S(2)}, u32[]{:S(2)}) collective-permute-start(bf16[784,128]{1,0:T(8,128)(2,1)S(1)} %get-tuple-element.40), channel_id=1, source_target_pairs={{0,31},{1,2},{2,1},{3,4},{4,3},{5,6},{6,5},{7,8},{8,7},{9,10},{10,... | collective-permute-start | bytes 602120 | tf_op jit(solution)/shard_map/ppermute | solution.py:326
  10.8 1.1 %collective-permute-start.5 = (bf16[752,128]{1,0:T(8,128)(2,1)S(1)}, bf16[752,128]{1,0:T(8,128)(2,1)S(1)}, u32[]{:S(2)}, u32[]{:S(2)}) collective-permute-start(bf16[752,128]{1,0:T(8,128)(2,1)S(1)} %get-tuple-element.41), channel_id=1, source_target_pairs={{0,31},{1,2},{2,1},{3,4},{4,3},{5,6},{6,5},{7,8},{8,7},{9,10},{10,... | collective-permute-start | bytes 577544 | tf_op jit(solution)/shard_map/ppermute | solution.py:326
  12.0 2.3 %collective-permute-done.rest_0_ = bf16[896,128]{1,0:T(8,128)(2,1)S(1)} collective-permute-done((bf16[896,128]{1,0:T(8,128)(2,1)S(1)}, bf16[896,128]{1,0:T(8,128)(2,1)S(1)}, u32[]{:S(2)}, u32[]{:S(2)}) %collective-permute-start) | collective-permute-done | bytes 229408 | tf_op jit(solution)/shard_map/ppermute | solution.py:315
  14.3 3.6 %collective-permute-start.1 = (bf16[640,128]{1,0:T(8,128)(2,1)S(1)}, bf16[640,128]{1,0:T(8,128)(2,1)S(1)}, u32[]{:S(2)}, u32[]{:S(2)}) collective-permute-start(bf16[640,128]{1,0:T(8,128)(2,1)S(1)} %get-tuple-element.37), channel_id=1, source_target_pairs={{0,2},{1,3},{2,0},{3,1},{4,6},{5,7},{6,4},{7,5},{8,10},{9,11},{10,... | collective-permute-start | bytes 491528 | tf_op jit(solution)/shard_map/ppermute | solution.py:315
  17.9 2.6 %collective-permute-start.7 = (bf16[640,128]{1,0:T(8,128)(2,1)S(1)}, bf16[640,128]{1,0:T(8,128)(2,1)S(1)}, u32[]{:S(2)}, u32[]{:S(2)}) collective-permute-start(bf16[640,128]{1,0:T(8,128)(2,1)S(1)} %get-tuple-element.37), channel_id=1, source_target_pairs={{0,30},{1,31},{2,4},{3,5},{4,2},{5,3},{6,8},{7,9},{8,6},{9,7},{10,... | collective-permute-start | bytes 491528 | tf_op jit(solution)/shard_map/ppermute | solution.py:318
  20.5 1.2 %copy-done = bf16[3,3,192,192]{3,2,1,0:T(8,128)(2,1)S(1)} copy-done((bf16[3,3,192,192]{3,2,1,0:T(8,128)(2,1)S(1)}, bf16[3,3,192,192]{3,2,1,0:T(8,128)(2,1)}, u32[]{:S(2)}) %copy-start) | copy-done | bytes 663576
  21.7 1.0 %near_pre_act.1 = (f32[1024,192]{1,0:T(8,128)S(1)}, bf16[576,1024]{1,0:T(8,128)(2,1)S(1)}, bf16[576,1024]{1,0:T(8,128)(2,1)S(1)}) custom-call(bf16[1024,192]{1,0:T(8,128)(2,1)S(1)} %bitcast.5, bf16[3,3,192,192]{3,2,1,0:T(8,128)(2,1)S(1)} %copy-done, bf16[784,128]{1,0:T(8,128)(2,1)S(1)} %collective-permute-done.2.rest_0_, ...), custom_call_target="tpu_custom_call" | custom-call | flops 452984832 | bytes 4595712 | tf_op jit(solution)/shard_map/near_pre_act/pallas_call | solution.py:22
  22.7 1.0 %hidden.1 = (bf16[192,1024]{1,0:T(8,128)(2,1)S(1)}, f32[1024,192]{1,0:T(8,128)S(1)}, bf16[576,1024]{1,0:T(8,128)(2,1)S(1)}) custom-call(f32[1024,192]{1,0:T(8,128)S(1)} %get-tuple-element.42.part_ref, bf16[3,3,192,192]{3,2,1,0:T(8,128)(2,1)S(1)} %copy-done.1, bf16[784,128]{1,0:T(8,128)(2,1)S(1)} %collective-permute-done.4.rest_0_, ...), custom_call_target="tpu_custom_call" | custom-call | flops 226492416 | bytes 4202496 | tf_op jit(solution)/shard_map/hidden/pallas_call | solution.py:22
  24.4 1.0 %near_hidden_grad.1 = (f32[1024,192]{1,0:T(8,128)S(1)}, bf16[1088,192]{1,0:T(8,128)(2,1)S(1)}, bf16[1088,192]{1,0:T(8,128)(2,1)S(1)}) custom-call(bf16[1024,192]{1,0:T(8,128)(2,1)S(1)} %bitcast.7, bf16[3,3,192,192]{3,2,1,0:T(8,128)(2,1)S(1)} %copy-done.2, bf16[896,128]{1,0:T(8,128)(2,1)S(1)} %collective-permute-done.rest_0_, ...), custom_call_target="tpu_custom_call" | custom-call | flops 452984832 | bytes 3072000 | tf_op jit(solution)/shard_map/near_hidden_grad/pallas_call | solution.py:22
  25.4 1.6 %collective-permute-done.7.rest_1_ = bf16[640,128]{1,0:T(8,128)(2,1)S(1)} collective-permute-done((bf16[640,128]{1,0:T(8,128)(2,1)S(1)}, bf16[640,128]{1,0:T(8,128)(2,1)S(1)}, u32[]{:S(2)}, u32[]{:S(2)}) %collective-permute-start.7) | collective-permute-done | bytes 163872 | tf_op jit(solution)/shard_map/ppermute | solution.py:318
  27.7 1.2 %sibling_kernel_gradient.1 = bf16[2624,128]{1,0:T(8,128)(2,1)S(1)} custom-call(bf16[192,1024]{1,0:T(8,128)(2,1)S(1)} %get-tuple-element.46.hid_ref, bf16[1088,192]{1,0:T(8,128)(2,1)S(1)} %get-tuple-element.47.g0, bf16[1088,192]{1,0:T(8,128)(2,1)S(1)} %get-tuple-element.48.g1, bf16[1088,192]{1,0:T(8,128)(2,1)S(1)} %get-tuple-element.49.g2, ...), custom_call_target="tpu_custom_call" | custom-call | flops 679477248 | bytes 6250496 | tf_op jit(solution)/shard_map/sibling_kernel_gradient/pallas_call | solution.py:22
  29.0 1.2 %own_kernel_gradient.1.own_ref = f32[2624,128]{1,0:T(8,128)S(1)} custom-call(bf16[192,1024]{1,0:T(8,128)(2,1)S(1)} %get-tuple-element.46.hid_ref, bf16[1088,192]{1,0:T(8,128)(2,1)S(1)} %get-tuple-element.47.g0, bf16[1088,192]{1,0:T(8,128)(2,1)S(1)} %get-tuple-element.48.g1, bf16[1088,192]{1,0:T(8,128)(2,1)S(1)} %get-tuple-element.49.g2, ...), custom_call_target="tpu_custom_call" | custom-call | flops 679477248 | bytes 6922240 | tf_op jit(solution)/shard_map/own_kernel_gradient/pallas_call | solution.py:22
  32.1 2.4 %collective-permute-start.12 = (bf16[656,128]{1,0:T(8,128)(2,1)S(1)}, bf16[656,128]{1,0:T(8,128)(2,1)S(1)}, u32[]{:S(2)}, u32[]{:S(2)}) collective-permute-start(bf16[656,128]{1,0:T(8,128)(2,1)S(1)} %get-tuple-element.56), channel_id=1, source_target_pairs={{0,2},{1,3},{2,0},{3,1},{4,6},{5,7},{6,4},{7,5},{8,10},{9,11},{10,... | collective-permute-start | bytes 503816 | tf_op jit(solution)/shard_map/ppermute | solution.py:180
  34.8 4.5 %collective-permute-done.10.refs_2_ = bf16[656,128]{1,0:T(8,128)(2,1)S(1)} collective-permute-done((bf16[656,128]{1,0:T(8,128)(2,1)S(1)}, bf16[656,128]{1,0:T(8,128)(2,1)S(1)}, u32[]{:S(2)}, u32[]{:S(2)}) %collective-permute-start.10) | collective-permute-done | bytes 167968 | tf_op jit(solution)/shard_map/ppermute | solution.py:180
  39.4 1.9 %collective-permute-start.11 = (bf16[1536,128]{1,0:T(8,128)(2,1)S(1)}, bf16[1536,128]{1,0:T(8,128)(2,1)S(1)}, u32[]{:S(2)}, u32[]{:S(2)}) collective-permute-start(bf16[1536,128]{1,0:T(8,128)(2,1)S(1)} %get-tuple-element.54), channel_id=1, source_target_pairs={{0,31},{1,2},{2,1},{3,4},{4,3},{5,6},{6,5},{7,8},{8,7},{9,10},{10,... | collective-permute-start | bytes 1179656 | tf_op jit(solution)/shard_map/ppermute | solution.py:478
  41.3 1.2 %collective-permute-done.12.refs_0_ = bf16[656,128]{1,0:T(8,128)(2,1)S(1)} collective-permute-done((bf16[656,128]{1,0:T(8,128)(2,1)S(1)}, bf16[656,128]{1,0:T(8,128)(2,1)S(1)}, u32[]{:S(2)}, u32[]{:S(2)}) %collective-permute-start.12) | collective-permute-done | bytes 167968 | tf_op jit(solution)/shard_map/ppermute | solution.py:180
  42.6 1.6 %collective-permute-start.14 = (bf16[176,128]{1,0:T(8,128)(2,1)S(1)}, bf16[176,128]{1,0:T(8,128)(2,1)S(1)}, u32[]{:S(2)}, u32[]{:S(2)}) collective-permute-start(bf16[176,128]{1,0:T(8,128)(2,1)S(1)} %get-tuple-element.59), channel_id=1, source_target_pairs={{0,8},{1,9},{2,10},{3,11},{4,12},{5,13},{6,14},{7,15},{8,0},{9,1},... | collective-permute-start | bytes 135176 | tf_op jit(solution)/shard_map/ppermute | solution.py:180
  44.3 2.6 %collective-permute-start.15 = (bf16[176,128]{1,0:T(8,128)(2,1)S(1)}, bf16[176,128]{1,0:T(8,128)(2,1)S(1)}, u32[]{:S(2)}, u32[]{:S(2)}) collective-permute-start(bf16[176,128]{1,0:T(8,128)(2,1)S(1)} %get-tuple-element.60), channel_id=1, source_target_pairs={{0,16},{1,17},{2,18},{3,19},{4,20},{5,21},{6,22},{7,23},{8,24},{9,... | collective-permute-start | bytes 135176 | tf_op jit(solution)/shard_map/ppermute | solution.py:180
  47.1 1.5 %collective-permute-done.14.refs_0_ = bf16[176,128]{1,0:T(8,128)(2,1)S(1)} collective-permute-done((bf16[176,128]{1,0:T(8,128)(2,1)S(1)}, bf16[176,128]{1,0:T(8,128)(2,1)S(1)}, u32[]{:S(2)}, u32[]{:S(2)}) %collective-permute-start.14) | collective-permute-done | bytes 45088 | tf_op jit(solution)/shard_map/ppermute | solution.py:180
  49.3 3.4 %collective-permute-done.16.refs_2_ = bf16[176,128]{1,0:T(8,128)(2,1)S(1)} collective-permute-done((bf16[176,128]{1,0:T(8,128)(2,1)S(1)}, bf16[176,128]{1,0:T(8,128)(2,1)S(1)}, u32[]{:S(2)}, u32[]{:S(2)}) %collective-permute-start.16) | collective-permute-done | bytes 45088 | tf_op jit(solution)/shard_map/ppermute | solution.py:180
  52.8 2.2 %collective-permute-start.18 = (bf16[176,128]{1,0:T(8,128)(2,1)S(1)}, bf16[176,128]{1,0:T(8,128)(2,1)S(1)}, u32[]{:S(2)}, u32[]{:S(2)}) collective-permute-start(bf16[176,128]{1,0:T(8,128)(2,1)S(1)} %combine_last.1.refs_0_), channel_id=1, source_target_pairs={{0,16},{1,17},{2,18},{3,19},{4,20},{5,21},{6,22},{7,23},{8,24},{9,... | collective-permute-start | bytes 135176 | tf_op jit(solution)/shard_map/ppermute | solution.py:180
  55.0 2.1 %collective-permute-start.19 = (bf16[176,128]{1,0:T(8,128)(2,1)S(1)}, bf16[176,128]{1,0:T(8,128)(2,1)S(1)}, u32[]{:S(2)}, u32[]{:S(2)}) collective-permute-start(bf16[176,128]{1,0:T(8,128)(2,1)S(1)} %combine_last.1.refs_0_), channel_id=1, source_target_pairs={{0,24},{1,25},{2,26},{3,27},{4,28},{5,29},{6,30},{7,31},{8,16},{9,... | collective-permute-start | bytes 135176 | tf_op jit(solution)/shard_map/ppermute | solution.py:180
  57.9 2.9 %collective-permute-done.19.refs_3_ = bf16[176,128]{1,0:T(8,128)(2,1)S(1)} collective-permute-done((bf16[176,128]{1,0:T(8,128)(2,1)S(1)}, bf16[176,128]{1,0:T(8,128)(2,1)S(1)}, u32[]{:S(2)}, u32[]{:S(2)}) %collective-permute-start.19) | collective-permute-done | bytes 45088 | tf_op jit(solution)/shard_map/ppermute | solution.py:180
  60.9 1.1 %collective-permute-start.25 = (bf16[656,128]{1,0:T(8,128)(2,1)S(1)}, bf16[656,128]{1,0:T(8,128)(2,1)S(1)}, u32[]{:S(2)}, u32[]{:S(2)}) collective-permute-start(bf16[656,128]{1,0:T(8,128)(2,1)S(1)} %assemble.1.refs_0_), channel_id=1, source_target_pairs={{0,6},{1,7},{2,4},{3,5},{4,2},{5,3},{6,0},{7,1},{8,14},{9,15},{10,... | collective-permute-start | bytes 503816 | tf_op jit(solution)/shard_map/ppermute | solution.py:180
  62.9 1.5 %collective-permute-start.21 = (bf16[656,128]{1,0:T(8,128)(2,1)S(1)}, bf16[656,128]{1,0:T(8,128)(2,1)S(1)}, u32[]{:S(2)}, u32[]{:S(2)}) collective-permute-start(bf16[656,128]{1,0:T(8,128)(2,1)S(1)} %assemble.1.refs_0_), channel_id=1, source_target_pairs={{0,2},{1,3},{2,0},{3,1},{4,6},{5,7},{6,4},{7,5},{8,10},{9,11},{10,... | collective-permute-start | bytes 503816 | tf_op jit(solution)/shard_map/ppermute | solution.py:180
  65.5 1.4 %input_gradient.1 = bf16[1024,192]{1,0:T(8,128)(2,1)} custom-call(f32[1024,192]{1,0:T(8,128)S(1)} %near_input_gradient.1.part_ref, bf16[3,3,192,192]{3,2,1,0:T(8,128)(2,1)S(1)} %copy-done.1, bf16[1536,128]{1,0:T(8,128)(2,1)S(1)} %collective-permute-done.11.rest_0_), custom_call_target="tpu_custom_call" | custom-call | flops 226492416 | bytes 2236416 | tf_op jit(solution)/shard_map/input_gradient/pallas_call | solution.py:22
  66.9 1.7 %collective-permute-done.25.refs_3_ = bf16[656,128]{1,0:T(8,128)(2,1)S(1)} collective-permute-done((bf16[656,128]{1,0:T(8,128)(2,1)S(1)}, bf16[656,128]{1,0:T(8,128)(2,1)S(1)}, u32[]{:S(2)}, u32[]{:S(2)}) %collective-permute-start.25) | collective-permute-done | bytes 167968 | tf_op jit(solution)/shard_map/ppermute | solution.py:180
  70.0 1.3 %unpack_gradients.2 = (f32[3,3,192,192]{3,2,1,0:T(8,128)}, f32[3,3,192,192]{3,2,1,0:T(8,128)}) custom-call(bf16[656,128]{1,0:T(8,128)(2,1)S(1)} %assemble.1.refs_0_, bf16[656,128]{1,0:T(8,128)(2,1)S(1)} %collective-permute-done.21.refs_1_, bf16[656,128]{1,0:T(8,128)(2,1)S(1)} %collective-permute-done.23.refs_2_, ...), custom_call_target="tpu_custom_call" | custom-call | bytes 3325952 | tf_op jit(solution)/shard_map/unpack_gradients/pallas_call | solution.py:22
  71.4 1.3 %unpack_gradients.3 = (f32[3,3,192,192]{3,2,1,0:T(8,128)}, f32[3,3,192,192]{3,2,1,0:T(8,128)}) custom-call(bf16[656,128]{1,0:T(8,128)(2,1)S(1)} %collective-permute-done.20.refs_0_, bf16[656,128]{1,0:T(8,128)(2,1)S(1)} %collective-permute-done.22.refs_1_, ...), custom_call_target="tpu_custom_call", output_to_operand_aliasing={{0}: (4, {}), {1}: (5, {})} | custom-call | bytes 5980160 | tf_op jit(solution)/shard_map/unpack_gradients/pallas_call | solution.py:22
  (50 shorter events, 9.8 us)
Async XLA Ops:
  0.6 22.1 %copy-start.1 = (bf16[3,3,192,192]{3,2,1,0:T(8,128)(2,1)S(1)}, bf16[3,3,192,192]{3,2,1,0:T(8,128)(2,1)}, u32[]{:S(2)}) copy-start(bf16[3,3,192,192]{3,2,1,0:T(8,128)(2,1)} %w_ref.11) | copy-start | bytes 1990660
  0.6 1.1 %copy-start.4 = (bf16[32,32,192]{2,1,0:T(8,128)(2,1)S(1)}, bf16[32,32,192]{2,1,0:T(8,128)(2,1)}, u32[]{:S(2)}) copy-start(bf16[32,32,192]{2,1,0:T(8,128)(2,1)} %param.5) | copy-start | bytes 1179652
  1.9 12.4 %collective-permute-start = (bf16[896,128]{1,0:T(8,128)(2,1)S(1)}, bf16[896,128]{1,0:T(8,128)(2,1)S(1)}, u32[]{:S(2)}, u32[]{:S(2)}) collective-permute-start(bf16[896,128]{1,0:T(8,128)(2,1)S(1)} %get-tuple-element.36), channel_id=1, source_target_pairs={{0,2},{1,3},{2,0},{3,1},{4,6},{5,7},{6,4},{7,5},{8,10},{9,11},{10,... | collective-permute-start | bytes 688136 | tf_op jit(solution)/shard_map/ppermute | solution.py:315
  6.0 8.3 %collective-permute-start.3 = (bf16[752,128]{1,0:T(8,128)(2,1)S(1)}, bf16[752,128]{1,0:T(8,128)(2,1)S(1)}, u32[]{:S(2)}, u32[]{:S(2)}) collective-permute-start(bf16[752,128]{1,0:T(8,128)(2,1)S(1)} %get-tuple-element.41), channel_id=1, source_target_pairs={{0,1},{1,0},{2,3},{3,2},{4,5},{5,4},{6,7},{7,6},{8,9},{9,8},{10,11... | collective-permute-start | bytes 577544 | tf_op jit(solution)/shard_map/ppermute | solution.py:325
  6.1 11.8 %collective-permute-start.2 = (bf16[784,128]{1,0:T(8,128)(2,1)S(1)}, bf16[784,128]{1,0:T(8,128)(2,1)S(1)}, u32[]{:S(2)}, u32[]{:S(2)}) collective-permute-start(bf16[784,128]{1,0:T(8,128)(2,1)S(1)} %get-tuple-element.40), channel_id=1, source_target_pairs={{0,1},{1,0},{2,3},{3,2},{4,5},{5,4},{6,7},{7,6},{8,9},{9,8},{10,11... | collective-permute-start | bytes 602120 | tf_op jit(solution)/shard_map/ppermute | solution.py:325
  6.6 16.1 %collective-permute-start.4 = (bf16[784,128]{1,0:T(8,128)(2,1)S(1)}, bf16[784,128]{1,0:T(8,128)(2,1)S(1)}, u32[]{:S(2)}, u32[]{:S(2)}) collective-permute-start(bf16[784,128]{1,0:T(8,128)(2,1)S(1)} %get-tuple-element.40), channel_id=1, source_target_pairs={{0,31},{1,2},{2,1},{3,4},{4,3},{5,6},{6,5},{7,8},{8,7},{9,10},{10,... | collective-permute-start | bytes 602120 | tf_op jit(solution)/shard_map/ppermute | solution.py:326
  10.8 11.8 %collective-permute-start.5 = (bf16[752,128]{1,0:T(8,128)(2,1)S(1)}, bf16[752,128]{1,0:T(8,128)(2,1)S(1)}, u32[]{:S(2)}, u32[]{:S(2)}) collective-permute-start(bf16[752,128]{1,0:T(8,128)(2,1)S(1)} %get-tuple-element.41), channel_id=1, source_target_pairs={{0,31},{1,2},{2,1},{3,4},{4,3},{5,6},{6,5},{7,8},{8,7},{9,10},{10,... | collective-permute-start | bytes 577544 | tf_op jit(solution)/shard_map/ppermute | solution.py:326
  14.3 12.6 %collective-permute-start.6 = (bf16[896,128]{1,0:T(8,128)(2,1)S(1)}, bf16[896,128]{1,0:T(8,128)(2,1)S(1)}, u32[]{:S(2)}, u32[]{:S(2)}) collective-permute-start(bf16[896,128]{1,0:T(8,128)(2,1)S(1)} %collective-permute-done.rest_0_), channel_id=1, source_target_pairs={{0,4},{1,5},{2,30},{3,31},{4,8},{5,9},{6,2},{7,3},{8,12},{9,13},{1... | collective-permute-start | bytes 688136 | tf_op jit(solution)/shard_map/ppermute | solution.py:317
  14.3 10.0 %collective-permute-start.1 = (bf16[640,128]{1,0:T(8,128)(2,1)S(1)}, bf16[640,128]{1,0:T(8,128)(2,1)S(1)}, u32[]{:S(2)}, u32[]{:S(2)}) collective-permute-start(bf16[640,128]{1,0:T(8,128)(2,1)S(1)} %get-tuple-element.37), channel_id=1, source_target_pairs={{0,2},{1,3},{2,0},{3,1},{4,6},{5,7},{6,4},{7,5},{8,10},{9,11},{10,... | collective-permute-start | bytes 491528 | tf_op jit(solution)/shard_map/ppermute | solution.py:315
  17.9 9.0 %collective-permute-start.7 = (bf16[640,128]{1,0:T(8,128)(2,1)S(1)}, bf16[640,128]{1,0:T(8,128)(2,1)S(1)}, u32[]{:S(2)}, u32[]{:S(2)}) collective-permute-start(bf16[640,128]{1,0:T(8,128)(2,1)S(1)} %get-tuple-element.37), channel_id=1, source_target_pairs={{0,30},{1,31},{2,4},{3,5},{4,2},{5,3},{6,8},{7,9},{8,6},{9,7},{10,... | collective-permute-start | bytes 491528 | tf_op jit(solution)/shard_map/ppermute | solution.py:318
  20.5 1.2 %copy-start = (bf16[3,3,192,192]{3,2,1,0:T(8,128)(2,1)S(1)}, bf16[3,3,192,192]{3,2,1,0:T(8,128)(2,1)}, u32[]{:S(2)}) copy-start(bf16[3,3,192,192]{3,2,1,0:T(8,128)(2,1)} %w_ref.11) | copy-start | bytes 1990660
  21.7 2.7 %copy-start.2 = (bf16[3,3,192,192]{3,2,1,0:T(8,128)(2,1)S(1)}, bf16[3,3,192,192]{3,2,1,0:T(8,128)(2,1)}, u32[]{:S(2)}) copy-start(bf16[3,3,192,192]{3,2,1,0:T(8,128)(2,1)} %w_ref.9) | copy-start | bytes 1990660
  21.7 2.7 %copy-start.5 = (bf16[32,32,192]{2,1,0:T(8,128)(2,1)S(1)}, bf16[32,32,192]{2,1,0:T(8,128)(2,1)}, u32[]{:S(2)}) copy-start(bf16[32,32,192]{2,1,0:T(8,128)(2,1)} %param.5) | copy-start | bytes 1179652
  28.9 2.2 %collective-permute-start.9 = (bf16[2624,128]{1,0:T(8,128)(2,1)S(1)}, bf16[2624,128]{1,0:T(8,128)(2,1)S(1)}, u32[]{:S(2)}, u32[]{:S(2)}) collective-permute-start(bf16[2624,128]{1,0:T(8,128)(2,1)S(1)} %sibling_kernel_gradient.1), channel_id=1, source_target_pairs={{0,1},{1,0},{2,3},{3,2},{4,5},{5,4},{6,7},{7,6},{8,9},{9,8},{10,11... | collective-permute-start | bytes 2015240 | tf_op jit(solution)/shard_map/ppermute | solution.py:180
  31.3 8.1 %collective-permute-start.10 = (bf16[656,128]{1,0:T(8,128)(2,1)S(1)}, bf16[656,128]{1,0:T(8,128)(2,1)S(1)}, u32[]{:S(2)}, u32[]{:S(2)}) collective-permute-start(bf16[656,128]{1,0:T(8,128)(2,1)S(1)} %get-tuple-element.53), channel_id=1, source_target_pairs={{0,6},{1,7},{2,4},{3,5},{4,2},{5,3},{6,0},{7,1},{8,14},{9,15},{10,... | collective-permute-start | bytes 503816 | tf_op jit(solution)/shard_map/ppermute | solution.py:180
  32.1 32.3 %collective-permute-start.8 = (bf16[1536,128]{1,0:T(8,128)(2,1)S(1)}, bf16[1536,128]{1,0:T(8,128)(2,1)S(1)}, u32[]{:S(2)}, u32[]{:S(2)}) collective-permute-start(bf16[1536,128]{1,0:T(8,128)(2,1)S(1)} %get-tuple-element.54), channel_id=1, source_target_pairs={{0,1},{1,0},{2,3},{3,2},{4,5},{5,4},{6,7},{7,6},{8,9},{9,8},{10,11... | collective-permute-start | bytes 1179656 | tf_op jit(solution)/shard_map/ppermute | solution.py:477
  32.1 10.4 %collective-permute-start.12 = (bf16[656,128]{1,0:T(8,128)(2,1)S(1)}, bf16[656,128]{1,0:T(8,128)(2,1)S(1)}, u32[]{:S(2)}, u32[]{:S(2)}) collective-permute-start(bf16[656,128]{1,0:T(8,128)(2,1)S(1)} %get-tuple-element.56), channel_id=1, source_target_pairs={{0,2},{1,3},{2,0},{3,1},{4,6},{5,7},{6,4},{7,5},{8,10},{9,11},{10,... | collective-permute-start | bytes 503816 | tf_op jit(solution)/shard_map/ppermute | solution.py:180
  34.6 7.9 %collective-permute-start.13 = (bf16[656,128]{1,0:T(8,128)(2,1)S(1)}, bf16[656,128]{1,0:T(8,128)(2,1)S(1)}, u32[]{:S(2)}, u32[]{:S(2)}) collective-permute-start(bf16[656,128]{1,0:T(8,128)(2,1)S(1)} %get-tuple-element.57), channel_id=1, source_target_pairs={{0,4},{1,5},{2,6},{3,7},{4,0},{5,1},{6,2},{7,3},{8,12},{9,13},{10,... | collective-permute-start | bytes 503816 | tf_op jit(solution)/shard_map/ppermute | solution.py:180
  39.4 26.2 %collective-permute-start.11 = (bf16[1536,128]{1,0:T(8,128)(2,1)S(1)}, bf16[1536,128]{1,0:T(8,128)(2,1)S(1)}, u32[]{:S(2)}, u32[]{:S(2)}) collective-permute-start(bf16[1536,128]{1,0:T(8,128)(2,1)S(1)} %get-tuple-element.54), channel_id=1, source_target_pairs={{0,31},{1,2},{2,1},{3,4},{4,3},{5,6},{6,5},{7,8},{8,7},{9,10},{10,... | collective-permute-start | bytes 1179656 | tf_op jit(solution)/shard_map/ppermute | solution.py:478
  42.6 6.0 %collective-permute-start.14 = (bf16[176,128]{1,0:T(8,128)(2,1)S(1)}, bf16[176,128]{1,0:T(8,128)(2,1)S(1)}, u32[]{:S(2)}, u32[]{:S(2)}) collective-permute-start(bf16[176,128]{1,0:T(8,128)(2,1)S(1)} %get-tuple-element.59), channel_id=1, source_target_pairs={{0,8},{1,9},{2,10},{3,11},{4,12},{5,13},{6,14},{7,15},{8,0},{9,1},... | collective-permute-start | bytes 135176 | tf_op jit(solution)/shard_map/ppermute | solution.py:180
  44.3 5.1 %collective-permute-start.15 = (bf16[176,128]{1,0:T(8,128)(2,1)S(1)}, bf16[176,128]{1,0:T(8,128)(2,1)S(1)}, u32[]{:S(2)}, u32[]{:S(2)}) collective-permute-start(bf16[176,128]{1,0:T(8,128)(2,1)S(1)} %get-tuple-element.60), channel_id=1, source_target_pairs={{0,16},{1,17},{2,18},{3,19},{4,20},{5,21},{6,22},{7,23},{8,24},{9,... | collective-permute-start | bytes 135176 | tf_op jit(solution)/shard_map/ppermute | solution.py:180
  46.8 5.8 %collective-permute-start.16 = (bf16[176,128]{1,0:T(8,128)(2,1)S(1)}, bf16[176,128]{1,0:T(8,128)(2,1)S(1)}, u32[]{:S(2)}, u32[]{:S(2)}) collective-permute-start(bf16[176,128]{1,0:T(8,128)(2,1)S(1)} %get-tuple-element.61), channel_id=1, source_target_pairs={{0,24},{1,25},{2,26},{3,27},{4,28},{5,29},{6,30},{7,31},{8,16},{9,... | collective-permute-start | bytes 135176 | tf_op jit(solution)/shard_map/ppermute | solution.py:180
  52.7 4.5 %collective-permute-start.17 = (bf16[176,128]{1,0:T(8,128)(2,1)S(1)}, bf16[176,128]{1,0:T(8,128)(2,1)S(1)}, u32[]{:S(2)}, u32[]{:S(2)}) collective-permute-start(bf16[176,128]{1,0:T(8,128)(2,1)S(1)} %combine_last.1.refs_0_), channel_id=1, source_target_pairs={{0,8},{1,9},{2,10},{3,11},{4,12},{5,13},{6,14},{7,15},{8,0},{9,1},... | collective-permute-start | bytes 135176 | tf_op jit(solution)/shard_map/ppermute | solution.py:180
  52.8 5.1 %collective-permute-start.18 = (bf16[176,128]{1,0:T(8,128)(2,1)S(1)}, bf16[176,128]{1,0:T(8,128)(2,1)S(1)}, u32[]{:S(2)}, u32[]{:S(2)}) collective-permute-start(bf16[176,128]{1,0:T(8,128)(2,1)S(1)} %combine_last.1.refs_0_), channel_id=1, source_target_pairs={{0,16},{1,17},{2,18},{3,19},{4,20},{5,21},{6,22},{7,23},{8,24},{9,... | collective-permute-start | bytes 135176 | tf_op jit(solution)/shard_map/ppermute | solution.py:180
  55.0 5.8 %collective-permute-start.19 = (bf16[176,128]{1,0:T(8,128)(2,1)S(1)}, bf16[176,128]{1,0:T(8,128)(2,1)S(1)}, u32[]{:S(2)}, u32[]{:S(2)}) collective-permute-start(bf16[176,128]{1,0:T(8,128)(2,1)S(1)} %combine_last.1.refs_0_), channel_id=1, source_target_pairs={{0,24},{1,25},{2,26},{3,27},{4,28},{5,29},{6,30},{7,31},{8,16},{9,... | collective-permute-start | bytes 135176 | tf_op jit(solution)/shard_map/ppermute | solution.py:180
  60.9 7.8 %collective-permute-start.25 = (bf16[656,128]{1,0:T(8,128)(2,1)S(1)}, bf16[656,128]{1,0:T(8,128)(2,1)S(1)}, u32[]{:S(2)}, u32[]{:S(2)}) collective-permute-start(bf16[656,128]{1,0:T(8,128)(2,1)S(1)} %assemble.1.refs_0_), channel_id=1, source_target_pairs={{0,6},{1,7},{2,4},{3,5},{4,2},{5,3},{6,0},{7,1},{8,14},{9,15},{10,... | collective-permute-start | bytes 503816 | tf_op jit(solution)/shard_map/ppermute | solution.py:180
  62.0 7.5 %collective-permute-start.23 = (bf16[656,128]{1,0:T(8,128)(2,1)S(1)}, bf16[656,128]{1,0:T(8,128)(2,1)S(1)}, u32[]{:S(2)}, u32[]{:S(2)}) collective-permute-start(bf16[656,128]{1,0:T(8,128)(2,1)S(1)} %assemble.1.refs_0_), channel_id=1, source_target_pairs={{0,4},{1,5},{2,6},{3,7},{4,0},{5,1},{6,2},{7,3},{8,12},{9,13},{10,... | collective-permute-start | bytes 503816 | tf_op jit(solution)/shard_map/ppermute | solution.py:180
  62.9 6.6 %collective-permute-start.21 = (bf16[656,128]{1,0:T(8,128)(2,1)S(1)}, bf16[656,128]{1,0:T(8,128)(2,1)S(1)}, u32[]{:S(2)}, u32[]{:S(2)}) collective-permute-start(bf16[656,128]{1,0:T(8,128)(2,1)S(1)} %assemble.1.refs_0_), channel_id=1, source_target_pairs={{0,2},{1,3},{2,0},{3,1},{4,6},{5,7},{6,4},{7,5},{8,10},{9,11},{10,... | collective-permute-start | bytes 503816 | tf_op jit(solution)/shard_map/ppermute | solution.py:180
  65.4 5.9 %collective-permute-start.20 = (bf16[656,128]{1,0:T(8,128)(2,1)S(1)}, bf16[656,128]{1,0:T(8,128)(2,1)S(1)}, u32[]{:S(2)}, u32[]{:S(2)}) collective-permute-start(bf16[656,128]{1,0:T(8,128)(2,1)S(1)} %assemble.1.refs_0_), channel_id=1, source_target_pairs={{0,1},{1,0},{2,3},{3,2},{4,5},{5,4},{6,7},{7,6},{8,9},{9,8},{10,11... | collective-permute-start | bytes 503816 | tf_op jit(solution)/shard_map/ppermute | solution.py:180
  68.6 2.7 %collective-permute-start.26 = (bf16[656,128]{1,0:T(8,128)(2,1)S(1)}, bf16[656,128]{1,0:T(8,128)(2,1)S(1)}, u32[]{:S(2)}, u32[]{:S(2)}) collective-permute-start(bf16[656,128]{1,0:T(8,128)(2,1)S(1)} %collective-permute-done.25.refs_3_), channel_id=1, source_target_pairs={{0,1},{1,0},{2,3},{3,2},{4,5},{5,4},{6,7},{7,6},{8,9},{9,8},{10,11... | collective-permute-start | bytes 503816 | tf_op jit(solution)/shard_map/ppermute | solution.py:180
  69.5 1.9 %collective-permute-start.24 = (bf16[656,128]{1,0:T(8,128)(2,1)S(1)}, bf16[656,128]{1,0:T(8,128)(2,1)S(1)}, u32[]{:S(2)}, u32[]{:S(2)}) collective-permute-start(bf16[656,128]{1,0:T(8,128)(2,1)S(1)} %collective-permute-done.23.refs_2_), channel_id=1, source_target_pairs={{0,1},{1,0},{2,3},{3,2},{4,5},{5,4},{6,7},{7,6},{8,9},{9,8},{10,11... | collective-permute-start | bytes 503816 | tf_op jit(solution)/shard_map/ppermute | solution.py:180
  69.5 1.9 %collective-permute-start.22 = (bf16[656,128]{1,0:T(8,128)(2,1)S(1)}, bf16[656,128]{1,0:T(8,128)(2,1)S(1)}, u32[]{:S(2)}, u32[]{:S(2)}) collective-permute-start(bf16[656,128]{1,0:T(8,128)(2,1)S(1)} %collective-permute-done.21.refs_1_), channel_id=1, source_target_pairs={{0,1},{1,0},{2,3},{3,2},{4,5},{5,4},{6,7},{7,6},{8,9},{9,8},{10,11... | collective-permute-start | bytes 503816 | tf_op jit(solution)/shard_map/ppermute | solution.py:180
  (1 other events, 1.0 us)

commit v8 on v7

--- a/solution.py
+++ b/solution.py
@@ -362,16 +362,15 @@
 
     def grad_body(part_ref, slope_ref, w_ref, *rest):
         side_refs, rest = rest[: len(g_outer)], rest[len(g_outer) :]
-        (rim,), (pre_grad, packed, se) = (rest[:1], rest[1:]) if rimmed else ((None,), rest)
+        (rim,), (pre_grad, se) = (rest[:1], rest[1:]) if rimmed else ((None,), rest)
         extend(se, unpacked(side_refs, rows, channels), rim, width)
         for start, size in blocks:
             grad = far_part(part_ref, se, w_ref, SECOND_SPREAD, True, start, size)
             pre_grad[start : start + size, :] = (grad * slope_ref[start : start + size, :]).astype(bf16)
-        pack_into([packed], pre_grad[...])
-
-    pre_grad, pre_packed, g_far = call(
+
+    pre_grad, g_far = call(
         grad_body,
-        [shape_of((rows, channels), bf16), shape_of(pshape, bf16), shape_of(ext_shape, bf16)],
+        [shape_of((rows, channels), bf16), shape_of(ext_shape, bf16)],
         [part2, slope, second_weight] + g_outer + g_rims[2:],
         flops=3 * tap_flops,
         name="pre_grad",
@@ -471,6 +470,7 @@
         plane_got = received[-1] if plane_got is None else plane_got
         stride *= radix
     pre_field = pre_grad.reshape(height, width, channels)
+    pre_packed = pack_one(pre_field)
     p_rims = rims_of(pre_field, FIRST_SPREAD)
     if paired(FIRST_SPREAD, width):
         steps = FIRST_SPREAD // width

time: 72.9 us -> 72.8 us (level)
    pallas_call x16 -> x17, Pallas kernels: 11.7 us -> 11.6 us  [call(): pl.pallas_call(body, out_shape=list(outs), in_specs=[far if i in far_args...]
where the time goes in v8:
time: 72.8 us; the launch traced here: 72.5 us
  starting transfers between devices  33.9 us (47%)
  waiting for transfers between devices  22.8 us (31%)
  Pallas kernels  11.6 us (16%)
  local copies, waits for them, and re-layouts  3.34 us (5%)
  between operations  0.86 us (1%)
    ppermute x17, waiting for transfers between devices, swapped(): lax.ppermute(value, 'lon', [(i, i ^ k * stride) for i in range(count)])  18.3 us
    ppermute x17, starting transfers between devices, swapped(): lax.ppermute(value, 'lon', [(i, i ^ k * stride) for i in range(count)])  16.7 us
    pallas_call x17, Pallas kernels, call(): pl.pallas_call(body, out_shape=list(outs), in_specs=[far if i in far_args...  11.6 us
    ppermute x4, starting transfers between devices, shards(): lax.ppermute(part, 'lon', inner_pairs(steps))  7.19 us
    ppermute x2, starting transfers between devices, shards(): lax.ppermute(part, 'lon', outer_pairs(steps))  5.34 us
    unnamed x12, local copies, waits for them, and re-layouts  3.34 us
    ppermute x4, waiting for transfers between devices, shards(): lax.ppermute(part, 'lon', inner_pairs(steps))  3.01 us
    ppermute x1, starting transfers between devices, shards(): lax.ppermute(g_packed[1], 'lon', outer_pairs(steps))  2.56 us
  transfers between devices with their start and end apart: 27, of which 13 were waited for; matrix products, arithmetic and copies ran while one was open for 0% of the time, Pallas kernels for 11%

profile of v8, /device:TPU:0, one launch (start us, length us, event | category | flops | bytes accessed | tf_op | source)
XLA Modules:
  0.0 72.5 jit_solution(17148359503142688657)
XLA Ops:
  0.7 1.1 %copy-done.4 = bf16[32,32,192]{2,1,0:T(8,128)(2,1)S(1)} copy-done((bf16[32,32,192]{2,1,0:T(8,128)(2,1)S(1)}, bf16[32,32,192]{2,1,0:T(8,128)(2,1)}, u32[]{:S(2)}) %copy-start.4) | copy-done | bytes 393240
  1.9 3.0 %collective-permute-start = (bf16[896,128]{1,0:T(8,128)(2,1)S(1)}, bf16[896,128]{1,0:T(8,128)(2,1)S(1)}, u32[]{:S(2)}, u32[]{:S(2)}) collective-permute-start(bf16[896,128]{1,0:T(8,128)(2,1)S(1)} %get-tuple-element.35), channel_id=1, source_target_pairs={{0,2},{1,3},{2,0},{3,1},{4,6},{5,7},{6,4},{7,5},{8,10},{9,11},{10,... | collective-permute-start | bytes 688136 | tf_op jit(solution)/shard_map/ppermute | solution.py:315
  4.9 1.0 %copy-done.3 = bf16[32,32,192]{2,1,0:T(8,128)(2,1)S(1)} copy-done((bf16[32,32,192]{2,1,0:T(8,128)(2,1)S(1)}, bf16[32,32,192]{2,1,0:T(8,128)(2,1)}, u32[]{:S(2)}) %copy-start.3) | copy-done | bytes 393240
  6.6 4.2 %collective-permute-start.4 = (bf16[784,128]{1,0:T(8,128)(2,1)S(1)}, bf16[784,128]{1,0:T(8,128)(2,1)S(1)}, u32[]{:S(2)}, u32[]{:S(2)}) collective-permute-start(bf16[784,128]{1,0:T(8,128)(2,1)S(1)} %get-tuple-element.39), channel_id=1, source_target_pairs={{0,31},{1,2},{2,1},{3,4},{4,3},{5,6},{6,5},{7,8},{8,7},{9,10},{10,... | collective-permute-start | bytes 602120 | tf_op jit(solution)/shard_map/ppermute | solution.py:326
  10.8 1.1 %collective-permute-start.5 = (bf16[752,128]{1,0:T(8,128)(2,1)S(1)}, bf16[752,128]{1,0:T(8,128)(2,1)S(1)}, u32[]{:S(2)}, u32[]{:S(2)}) collective-permute-start(bf16[752,128]{1,0:T(8,128)(2,1)S(1)} %get-tuple-element.40), channel_id=1, source_target_pairs={{0,31},{1,2},{2,1},{3,4},{4,3},{5,6},{6,5},{7,8},{8,7},{9,10},{10,... | collective-permute-start | bytes 577544 | tf_op jit(solution)/shard_map/ppermute | solution.py:326
  12.0 2.3 %collective-permute-done.rest_0_ = bf16[896,128]{1,0:T(8,128)(2,1)S(1)} collective-permute-done((bf16[896,128]{1,0:T(8,128)(2,1)S(1)}, bf16[896,128]{1,0:T(8,128)(2,1)S(1)}, u32[]{:S(2)}, u32[]{:S(2)}) %collective-permute-start) | collective-permute-done | bytes 229408 | tf_op jit(solution)/shard_map/ppermute | solution.py:315
  14.3 3.6 %collective-permute-start.1 = (bf16[640,128]{1,0:T(8,128)(2,1)S(1)}, bf16[640,128]{1,0:T(8,128)(2,1)S(1)}, u32[]{:S(2)}, u32[]{:S(2)}) collective-permute-start(bf16[640,128]{1,0:T(8,128)(2,1)S(1)} %get-tuple-element.36), channel_id=1, source_target_pairs={{0,2},{1,3},{2,0},{3,1},{4,6},{5,7},{6,4},{7,5},{8,10},{9,11},{10,... | collective-permute-start | bytes 491528 | tf_op jit(solution)/shard_map/ppermute | solution.py:315
  17.9 2.6 %collective-permute-start.7 = (bf16[640,128]{1,0:T(8,128)(2,1)S(1)}, bf16[640,128]{1,0:T(8,128)(2,1)S(1)}, u32[]{:S(2)}, u32[]{:S(2)}) collective-permute-start(bf16[640,128]{1,0:T(8,128)(2,1)S(1)} %get-tuple-element.36), channel_id=1, source_target_pairs={{0,30},{1,31},{2,4},{3,5},{4,2},{5,3},{6,8},{7,9},{8,6},{9,7},{10,... | collective-permute-start | bytes 491528 | tf_op jit(solution)/shard_map/ppermute | solution.py:318
  20.5 1.2 %copy-done = bf16[3,3,192,192]{3,2,1,0:T(8,128)(2,1)S(1)} copy-done((bf16[3,3,192,192]{3,2,1,0:T(8,128)(2,1)S(1)}, bf16[3,3,192,192]{3,2,1,0:T(8,128)(2,1)}, u32[]{:S(2)}) %copy-start) | copy-done | bytes 663576
  21.7 1.0 %near_pre_act.1 = (f32[1024,192]{1,0:T(8,128)S(1)}, bf16[576,1024]{1,0:T(8,128)(2,1)S(1)}, bf16[576,1024]{1,0:T(8,128)(2,1)S(1)}) custom-call(bf16[1024,192]{1,0:T(8,128)(2,1)S(1)} %bitcast.5, bf16[3,3,192,192]{3,2,1,0:T(8,128)(2,1)S(1)} %copy-done, bf16[784,128]{1,0:T(8,128)(2,1)S(1)} %collective-permute-done.2.rest_0_, ...), custom_call_target="tpu_custom_call" | custom-call | flops 452984832 | bytes 4595712 | tf_op jit(solution)/shard_map/near_pre_act/pallas_call | solution.py:22
  22.7 1.0 %hidden.1 = (bf16[192,1024]{1,0:T(8,128)(2,1)S(1)}, f32[1024,192]{1,0:T(8,128)S(1)}, bf16[576,1024]{1,0:T(8,128)(2,1)S(1)}) custom-call(f32[1024,192]{1,0:T(8,128)S(1)} %get-tuple-element.41.part_ref, bf16[3,3,192,192]{3,2,1,0:T(8,128)(2,1)S(1)} %copy-done.1, bf16[784,128]{1,0:T(8,128)(2,1)S(1)} %collective-permute-done.4.rest_0_, ...), custom_call_target="tpu_custom_call" | custom-call | flops 226492416 | bytes 4202496 | tf_op jit(solution)/shard_map/hidden/pallas_call | solution.py:22
  24.4 1.0 %near_hidden_grad.1 = (f32[1024,192]{1,0:T(8,128)S(1)}, bf16[1088,192]{1,0:T(8,128)(2,1)S(1)}, bf16[1088,192]{1,0:T(8,128)(2,1)S(1)}) custom-call(bf16[1024,192]{1,0:T(8,128)(2,1)S(1)} %bitcast.7, bf16[3,3,192,192]{3,2,1,0:T(8,128)(2,1)S(1)} %copy-done.2, bf16[896,128]{1,0:T(8,128)(2,1)S(1)} %collective-permute-done.rest_0_, ...), custom_call_target="tpu_custom_call" | custom-call | flops 452984832 | bytes 3072000 | tf_op jit(solution)/shard_map/near_hidden_grad/pallas_call | solution.py:22
  25.4 1.6 %collective-permute-done.7.rest_1_ = bf16[640,128]{1,0:T(8,128)(2,1)S(1)} collective-permute-done((bf16[640,128]{1,0:T(8,128)(2,1)S(1)}, bf16[640,128]{1,0:T(8,128)(2,1)S(1)}, u32[]{:S(2)}, u32[]{:S(2)}) %collective-permute-start.7) | collective-permute-done | bytes 163872 | tf_op jit(solution)/shard_map/ppermute | solution.py:318
  27.5 1.2 %sibling_kernel_gradient.1 = bf16[2624,128]{1,0:T(8,128)(2,1)S(1)} custom-call(bf16[192,1024]{1,0:T(8,128)(2,1)S(1)} %get-tuple-element.44.hid_ref, bf16[1088,192]{1,0:T(8,128)(2,1)S(1)} %get-tuple-element.45.g0, bf16[1088,192]{1,0:T(8,128)(2,1)S(1)} %get-tuple-element.46.g1, bf16[1088,192]{1,0:T(8,128)(2,1)S(1)} %get-tuple-element.47.g2, ...), custom_call_target="tpu_custom_call" | custom-call | flops 679477248 | bytes 6250496 | tf_op jit(solution)/shard_map/sibling_kernel_gradient/pallas_call | solution.py:22
  28.8 1.2 %own_kernel_gradient.1.own_ref = f32[2624,128]{1,0:T(8,128)S(1)} custom-call(bf16[192,1024]{1,0:T(8,128)(2,1)S(1)} %get-tuple-element.44.hid_ref, bf16[1088,192]{1,0:T(8,128)(2,1)S(1)} %get-tuple-element.45.g0, bf16[1088,192]{1,0:T(8,128)(2,1)S(1)} %get-tuple-element.46.g1, bf16[1088,192]{1,0:T(8,128)(2,1)S(1)} %get-tuple-element.47.g2, ...), custom_call_target="tpu_custom_call" | custom-call | flops 679477248 | bytes 6922240 | tf_op jit(solution)/shard_map/own_kernel_gradient/pallas_call | solution.py:22
  32.2 2.5 %collective-permute-start.12 = (bf16[656,128]{1,0:T(8,128)(2,1)S(1)}, bf16[656,128]{1,0:T(8,128)(2,1)S(1)}, u32[]{:S(2)}, u32[]{:S(2)}) collective-permute-start(bf16[656,128]{1,0:T(8,128)(2,1)S(1)} %get-tuple-element.54), channel_id=1, source_target_pairs={{0,2},{1,3},{2,0},{3,1},{4,6},{5,7},{6,4},{7,5},{8,10},{9,11},{10,... | collective-permute-start | bytes 503816 | tf_op jit(solution)/shard_map/ppermute | solution.py:180
  34.9 4.3 %collective-permute-done.10.refs_2_ = bf16[656,128]{1,0:T(8,128)(2,1)S(1)} collective-permute-done((bf16[656,128]{1,0:T(8,128)(2,1)S(1)}, bf16[656,128]{1,0:T(8,128)(2,1)S(1)}, u32[]{:S(2)}, u32[]{:S(2)}) %collective-permute-start.10) | collective-permute-done | bytes 167968 | tf_op jit(solution)/shard_map/ppermute | solution.py:180
  39.2 2.0 %collective-permute-start.11 = (bf16[1536,128]{1,0:T(8,128)(2,1)S(1)}, bf16[1536,128]{1,0:T(8,128)(2,1)S(1)}, u32[]{:S(2)}, u32[]{:S(2)}) collective-permute-start(bf16[1536,128]{1,0:T(8,128)(2,1)S(1)} %pack.5), channel_id=1, source_target_pairs={{0,31},{1,2},{2,1},{3,4},{4,3},{5,6},{6,5},{7,8},{8,7},{9,10},{10,... | collective-permute-start | bytes 1179656 | tf_op jit(solution)/shard_map/ppermute | solution.py:478
  41.1 1.2 %collective-permute-done.12.refs_0_ = bf16[656,128]{1,0:T(8,128)(2,1)S(1)} collective-permute-done((bf16[656,128]{1,0:T(8,128)(2,1)S(1)}, bf16[656,128]{1,0:T(8,128)(2,1)S(1)}, u32[]{:S(2)}, u32[]{:S(2)}) %collective-permute-start.12) | collective-permute-done | bytes 167968 | tf_op jit(solution)/shard_map/ppermute | solution.py:180
  42.5 1.6 %collective-permute-start.14 = (bf16[176,128]{1,0:T(8,128)(2,1)S(1)}, bf16[176,128]{1,0:T(8,128)(2,1)S(1)}, u32[]{:S(2)}, u32[]{:S(2)}) collective-permute-start(bf16[176,128]{1,0:T(8,128)(2,1)S(1)} %get-tuple-element.57), channel_id=1, source_target_pairs={{0,8},{1,9},{2,10},{3,11},{4,12},{5,13},{6,14},{7,15},{8,0},{9,1},... | collective-permute-start | bytes 135176 | tf_op jit(solution)/shard_map/ppermute | solution.py:180
  44.1 2.6 %collective-permute-start.15 = (bf16[176,128]{1,0:T(8,128)(2,1)S(1)}, bf16[176,128]{1,0:T(8,128)(2,1)S(1)}, u32[]{:S(2)}, u32[]{:S(2)}) collective-permute-start(bf16[176,128]{1,0:T(8,128)(2,1)S(1)} %get-tuple-element.58), channel_id=1, source_target_pairs={{0,16},{1,17},{2,18},{3,19},{4,20},{5,21},{6,22},{7,23},{8,24},{9,... | collective-permute-start | bytes 135176 | tf_op jit(solution)/shard_map/ppermute | solution.py:180
  46.9 1.5 %collective-permute-done.14.refs_0_ = bf16[176,128]{1,0:T(8,128)(2,1)S(1)} collective-permute-done((bf16[176,128]{1,0:T(8,128)(2,1)S(1)}, bf16[176,128]{1,0:T(8,128)(2,1)S(1)}, u32[]{:S(2)}, u32[]{:S(2)}) %collective-permute-start.14) | collective-permute-done | bytes 45088 | tf_op jit(solution)/shard_map/ppermute | solution.py:180
  49.2 3.4 %collective-permute-done.16.refs_2_ = bf16[176,128]{1,0:T(8,128)(2,1)S(1)} collective-permute-done((bf16[176,128]{1,0:T(8,128)(2,1)S(1)}, bf16[176,128]{1,0:T(8,128)(2,1)S(1)}, u32[]{:S(2)}, u32[]{:S(2)}) %collective-permute-start.16) | collective-permute-done | bytes 45088 | tf_op jit(solution)/shard_map/ppermute | solution.py:180
  52.6 2.2 %collective-permute-start.18 = (bf16[176,128]{1,0:T(8,128)(2,1)S(1)}, bf16[176,128]{1,0:T(8,128)(2,1)S(1)}, u32[]{:S(2)}, u32[]{:S(2)}) collective-permute-start(bf16[176,128]{1,0:T(8,128)(2,1)S(1)} %combine_last.1.refs_0_), channel_id=1, source_target_pairs={{0,16},{1,17},{2,18},{3,19},{4,20},{5,21},{6,22},{7,23},{8,24},{9,... | collective-permute-start | bytes 135176 | tf_op jit(solution)/shard_map/ppermute | solution.py:180
  54.9 2.1 %collective-permute-start.19 = (bf16[176,128]{1,0:T(8,128)(2,1)S(1)}, bf16[176,128]{1,0:T(8,128)(2,1)S(1)}, u32[]{:S(2)}, u32[]{:S(2)}) collective-permute-start(bf16[176,128]{1,0:T(8,128)(2,1)S(1)} %combine_last.1.refs_0_), channel_id=1, source_target_pairs={{0,24},{1,25},{2,26},{3,27},{4,28},{5,29},{6,30},{7,31},{8,16},{9,... | collective-permute-start | bytes 135176 | tf_op jit(solution)/shard_map/ppermute | solution.py:180
  57.8 2.9 %collective-permute-done.19.refs_3_ = bf16[176,128]{1,0:T(8,128)(2,1)S(1)} collective-permute-done((bf16[176,128]{1,0:T(8,128)(2,1)S(1)}, bf16[176,128]{1,0:T(8,128)(2,1)S(1)}, u32[]{:S(2)}, u32[]{:S(2)}) %collective-permute-start.19) | collective-permute-done | bytes 45088 | tf_op jit(solution)/shard_map/ppermute | solution.py:180
  60.8 1.0 %collective-permute-start.25 = (bf16[656,128]{1,0:T(8,128)(2,1)S(1)}, bf16[656,128]{1,0:T(8,128)(2,1)S(1)}, u32[]{:S(2)}, u32[]{:S(2)}) collective-permute-start(bf16[656,128]{1,0:T(8,128)(2,1)S(1)} %assemble.1.refs_0_), channel_id=1, source_target_pairs={{0,6},{1,7},{2,4},{3,5},{4,2},{5,3},{6,0},{7,1},{8,14},{9,15},{10,... | collective-permute-start | bytes 503816 | tf_op jit(solution)/shard_map/ppermute | solution.py:180
  62.8 1.6 %collective-permute-start.21 = (bf16[656,128]{1,0:T(8,128)(2,1)S(1)}, bf16[656,128]{1,0:T(8,128)(2,1)S(1)}, u32[]{:S(2)}, u32[]{:S(2)}) collective-permute-start(bf16[656,128]{1,0:T(8,128)(2,1)S(1)} %assemble.1.refs_0_), channel_id=1, source_target_pairs={{0,2},{1,3},{2,0},{3,1},{4,6},{5,7},{6,4},{7,5},{8,10},{9,11},{10,... | collective-permute-start | bytes 503816 | tf_op jit(solution)/shard_map/ppermute | solution.py:180
  65.4 1.4 %input_gradient.1 = bf16[1024,192]{1,0:T(8,128)(2,1)} custom-call(f32[1024,192]{1,0:T(8,128)S(1)} %near_input_gradient.1.part_ref, bf16[3,3,192,192]{3,2,1,0:T(8,128)(2,1)S(1)} %copy-done.1, bf16[1536,128]{1,0:T(8,128)(2,1)S(1)} %collective-permute-done.11.rest_0_), custom_call_target="tpu_custom_call" | custom-call | flops 226492416 | bytes 2236416 | tf_op jit(solution)/shard_map/input_gradient/pallas_call | solution.py:22
  66.8 1.7 %collective-permute-done.25.refs_3_ = bf16[656,128]{1,0:T(8,128)(2,1)S(1)} collective-permute-done((bf16[656,128]{1,0:T(8,128)(2,1)S(1)}, bf16[656,128]{1,0:T(8,128)(2,1)S(1)}, u32[]{:S(2)}, u32[]{:S(2)}) %collective-permute-start.25) | collective-permute-done | bytes 167968 | tf_op jit(solution)/shard_map/ppermute | solution.py:180
  69.8 1.3 %unpack_gradients.2 = (f32[3,3,192,192]{3,2,1,0:T(8,128)}, f32[3,3,192,192]{3,2,1,0:T(8,128)}) custom-call(bf16[656,128]{1,0:T(8,128)(2,1)S(1)} %assemble.1.refs_0_, bf16[656,128]{1,0:T(8,128)(2,1)S(1)} %collective-permute-done.21.refs_1_, bf16[656,128]{1,0:T(8,128)(2,1)S(1)} %collective-permute-done.23.refs_2_, ...), custom_call_target="tpu_custom_call" | custom-call | bytes 3325952 | tf_op jit(solution)/shard_map/unpack_gradients/pallas_call | solution.py:22
  71.2 1.3 %unpack_gradients.3 = (f32[3,3,192,192]{3,2,1,0:T(8,128)}, f32[3,3,192,192]{3,2,1,0:T(8,128)}) custom-call(bf16[656,128]{1,0:T(8,128)(2,1)S(1)} %collective-permute-done.20.refs_0_, bf16[656,128]{1,0:T(8,128)(2,1)S(1)} %collective-permute-done.22.refs_1_, ...), custom_call_target="tpu_custom_call", output_to_operand_aliasing={{0}: (4, {}), {1}: (5, {})} | custom-call | bytes 5980160 | tf_op jit(solution)/shard_map/unpack_gradients/pallas_call | solution.py:22
  (51 shorter events, 9.8 us)
Async XLA Ops:
  0.6 22.1 %copy-start.1 = (bf16[3,3,192,192]{3,2,1,0:T(8,128)(2,1)S(1)}, bf16[3,3,192,192]{3,2,1,0:T(8,128)(2,1)}, u32[]{:S(2)}) copy-start(bf16[3,3,192,192]{3,2,1,0:T(8,128)(2,1)} %w_ref.11) | copy-start | bytes 1990660
  0.6 1.1 %copy-start.4 = (bf16[32,32,192]{2,1,0:T(8,128)(2,1)S(1)}, bf16[32,32,192]{2,1,0:T(8,128)(2,1)}, u32[]{:S(2)}) copy-start(bf16[32,32,192]{2,1,0:T(8,128)(2,1)} %param.5) | copy-start | bytes 1179652
  1.9 12.4 %collective-permute-start = (bf16[896,128]{1,0:T(8,128)(2,1)S(1)}, bf16[896,128]{1,0:T(8,128)(2,1)S(1)}, u32[]{:S(2)}, u32[]{:S(2)}) collective-permute-start(bf16[896,128]{1,0:T(8,128)(2,1)S(1)} %get-tuple-element.35), channel_id=1, source_target_pairs={{0,2},{1,3},{2,0},{3,1},{4,6},{5,7},{6,4},{7,5},{8,10},{9,11},{10,... | collective-permute-start | bytes 688136 | tf_op jit(solution)/shard_map/ppermute | solution.py:315
  6.0 8.3 %collective-permute-start.3 = (bf16[752,128]{1,0:T(8,128)(2,1)S(1)}, bf16[752,128]{1,0:T(8,128)(2,1)S(1)}, u32[]{:S(2)}, u32[]{:S(2)}) collective-permute-start(bf16[752,128]{1,0:T(8,128)(2,1)S(1)} %get-tuple-element.40), channel_id=1, source_target_pairs={{0,1},{1,0},{2,3},{3,2},{4,5},{5,4},{6,7},{7,6},{8,9},{9,8},{10,11... | collective-permute-start | bytes 577544 | tf_op jit(solution)/shard_map/ppermute | solution.py:325
  6.1 11.8 %collective-permute-start.2 = (bf16[784,128]{1,0:T(8,128)(2,1)S(1)}, bf16[784,128]{1,0:T(8,128)(2,1)S(1)}, u32[]{:S(2)}, u32[]{:S(2)}) collective-permute-start(bf16[784,128]{1,0:T(8,128)(2,1)S(1)} %get-tuple-element.39), channel_id=1, source_target_pairs={{0,1},{1,0},{2,3},{3,2},{4,5},{5,4},{6,7},{7,6},{8,9},{9,8},{10,11... | collective-permute-start | bytes 602120 | tf_op jit(solution)/shard_map/ppermute | solution.py:325
  6.6 16.1 %collective-permute-start.4 = (bf16[784,128]{1,0:T(8,128)(2,1)S(1)}, bf16[784,128]{1,0:T(8,128)(2,1)S(1)}, u32[]{:S(2)}, u32[]{:S(2)}) collective-permute-start(bf16[784,128]{1,0:T(8,128)(2,1)S(1)} %get-tuple-element.39), channel_id=1, source_target_pairs={{0,31},{1,2},{2,1},{3,4},{4,3},{5,6},{6,5},{7,8},{8,7},{9,10},{10,... | collective-permute-start | bytes 602120 | tf_op jit(solution)/shard_map/ppermute | solution.py:326
  10.8 11.8 %collective-permute-start.5 = (bf16[752,128]{1,0:T(8,128)(2,1)S(1)}, bf16[752,128]{1,0:T(8,128)(2,1)S(1)}, u32[]{:S(2)}, u32[]{:S(2)}) collective-permute-start(bf16[752,128]{1,0:T(8,128)(2,1)S(1)} %get-tuple-element.40), channel_id=1, source_target_pairs={{0,31},{1,2},{2,1},{3,4},{4,3},{5,6},{6,5},{7,8},{8,7},{9,10},{10,... | collective-permute-start | bytes 577544 | tf_op jit(solution)/shard_map/ppermute | solution.py:326
  14.3 12.6 %collective-permute-start.6 = (bf16[896,128]{1,0:T(8,128)(2,1)S(1)}, bf16[896,128]{1,0:T(8,128)(2,1)S(1)}, u32[]{:S(2)}, u32[]{:S(2)}) collective-permute-start(bf16[896,128]{1,0:T(8,128)(2,1)S(1)} %collective-permute-done.rest_0_), channel_id=1, source_target_pairs={{0,4},{1,5},{2,30},{3,31},{4,8},{5,9},{6,2},{7,3},{8,12},{9,13},{1... | collective-permute-start | bytes 688136 | tf_op jit(solution)/shard_map/ppermute | solution.py:317
  14.3 10.0 %collective-permute-start.1 = (bf16[640,128]{1,0:T(8,128)(2,1)S(1)}, bf16[640,128]{1,0:T(8,128)(2,1)S(1)}, u32[]{:S(2)}, u32[]{:S(2)}) collective-permute-start(bf16[640,128]{1,0:T(8,128)(2,1)S(1)} %get-tuple-element.36), channel_id=1, source_target_pairs={{0,2},{1,3},{2,0},{3,1},{4,6},{5,7},{6,4},{7,5},{8,10},{9,11},{10,... | collective-permute-start | bytes 491528 | tf_op jit(solution)/shard_map/ppermute | solution.py:315
  17.9 9.0 %collective-permute-start.7 = (bf16[640,128]{1,0:T(8,128)(2,1)S(1)}, bf16[640,128]{1,0:T(8,128)(2,1)S(1)}, u32[]{:S(2)}, u32[]{:S(2)}) collective-permute-start(bf16[640,128]{1,0:T(8,128)(2,1)S(1)} %get-tuple-element.36), channel_id=1, source_target_pairs={{0,30},{1,31},{2,4},{3,5},{4,2},{5,3},{6,8},{7,9},{8,6},{9,7},{10,... | collective-permute-start | bytes 491528 | tf_op jit(solution)/shard_map/ppermute | solution.py:318
  20.5 1.2 %copy-start = (bf16[3,3,192,192]{3,2,1,0:T(8,128)(2,1)S(1)}, bf16[3,3,192,192]{3,2,1,0:T(8,128)(2,1)}, u32[]{:S(2)}) copy-start(bf16[3,3,192,192]{3,2,1,0:T(8,128)(2,1)} %w_ref.11) | copy-start | bytes 1990660
  21.7 2.7 %copy-start.2 = (bf16[3,3,192,192]{3,2,1,0:T(8,128)(2,1)S(1)}, bf16[3,3,192,192]{3,2,1,0:T(8,128)(2,1)}, u32[]{:S(2)}) copy-start(bf16[3,3,192,192]{3,2,1,0:T(8,128)(2,1)} %w_ref.9) | copy-start | bytes 1990660
  21.7 2.7 %copy-start.5 = (bf16[32,32,192]{2,1,0:T(8,128)(2,1)S(1)}, bf16[32,32,192]{2,1,0:T(8,128)(2,1)}, u32[]{:S(2)}) copy-start(bf16[32,32,192]{2,1,0:T(8,128)(2,1)} %param.5) | copy-start | bytes 1179652
  28.8 2.2 %collective-permute-start.9 = (bf16[2624,128]{1,0:T(8,128)(2,1)S(1)}, bf16[2624,128]{1,0:T(8,128)(2,1)S(1)}, u32[]{:S(2)}, u32[]{:S(2)}) collective-permute-start(bf16[2624,128]{1,0:T(8,128)(2,1)S(1)} %sibling_kernel_gradient.1), channel_id=1, source_target_pairs={{0,1},{1,0},{2,3},{3,2},{4,5},{5,4},{6,7},{7,6},{8,9},{9,8},{10,11... | collective-permute-start | bytes 2015240 | tf_op jit(solution)/shard_map/ppermute | solution.py:180
  31.1 8.1 %collective-permute-start.10 = (bf16[656,128]{1,0:T(8,128)(2,1)S(1)}, bf16[656,128]{1,0:T(8,128)(2,1)S(1)}, u32[]{:S(2)}, u32[]{:S(2)}) collective-permute-start(bf16[656,128]{1,0:T(8,128)(2,1)S(1)} %get-tuple-element.51), channel_id=1, source_target_pairs={{0,6},{1,7},{2,4},{3,5},{4,2},{5,3},{6,0},{7,1},{8,14},{9,15},{10,... | collective-permute-start | bytes 503816 | tf_op jit(solution)/shard_map/ppermute | solution.py:180
  32.1 32.2 %collective-permute-start.8 = (bf16[1536,128]{1,0:T(8,128)(2,1)S(1)}, bf16[1536,128]{1,0:T(8,128)(2,1)S(1)}, u32[]{:S(2)}, u32[]{:S(2)}) collective-permute-start(bf16[1536,128]{1,0:T(8,128)(2,1)S(1)} %pack.5), channel_id=1, source_target_pairs={{0,1},{1,0},{2,3},{3,2},{4,5},{5,4},{6,7},{7,6},{8,9},{9,8},{10,11... | collective-permute-start | bytes 1179656 | tf_op jit(solution)/shard_map/ppermute | solution.py:477
  32.2 10.2 %collective-permute-start.12 = (bf16[656,128]{1,0:T(8,128)(2,1)S(1)}, bf16[656,128]{1,0:T(8,128)(2,1)S(1)}, u32[]{:S(2)}, u32[]{:S(2)}) collective-permute-start(bf16[656,128]{1,0:T(8,128)(2,1)S(1)} %get-tuple-element.54), channel_id=1, source_target_pairs={{0,2},{1,3},{2,0},{3,1},{4,6},{5,7},{6,4},{7,5},{8,10},{9,11},{10,... | collective-permute-start | bytes 503816 | tf_op jit(solution)/shard_map/ppermute | solution.py:180
  34.7 7.7 %collective-permute-start.13 = (bf16[656,128]{1,0:T(8,128)(2,1)S(1)}, bf16[656,128]{1,0:T(8,128)(2,1)S(1)}, u32[]{:S(2)}, u32[]{:S(2)}) collective-permute-start(bf16[656,128]{1,0:T(8,128)(2,1)S(1)} %get-tuple-element.55), channel_id=1, source_target_pairs={{0,4},{1,5},{2,6},{3,7},{4,0},{5,1},{6,2},{7,3},{8,12},{9,13},{10,... | collective-permute-start | bytes 503816 | tf_op jit(solution)/shard_map/ppermute | solution.py:180
  39.2 26.2 %collective-permute-start.11 = (bf16[1536,128]{1,0:T(8,128)(2,1)S(1)}, bf16[1536,128]{1,0:T(8,128)(2,1)S(1)}, u32[]{:S(2)}, u32[]{:S(2)}) collective-permute-start(bf16[1536,128]{1,0:T(8,128)(2,1)S(1)} %pack.5), channel_id=1, source_target_pairs={{0,31},{1,2},{2,1},{3,4},{4,3},{5,6},{6,5},{7,8},{8,7},{9,10},{10,... | collective-permute-start | bytes 1179656 | tf_op jit(solution)/shard_map/ppermute | solution.py:478
  42.5 6.0 %collective-permute-start.14 = (bf16[176,128]{1,0:T(8,128)(2,1)S(1)}, bf16[176,128]{1,0:T(8,128)(2,1)S(1)}, u32[]{:S(2)}, u32[]{:S(2)}) collective-permute-start(bf16[176,128]{1,0:T(8,128)(2,1)S(1)} %get-tuple-element.57), channel_id=1, source_target_pairs={{0,8},{1,9},{2,10},{3,11},{4,12},{5,13},{6,14},{7,15},{8,0},{9,1},... | collective-permute-start | bytes 135176 | tf_op jit(solution)/shard_map/ppermute | solution.py:180
  44.1 5.1 %collective-permute-start.15 = (bf16[176,128]{1,0:T(8,128)(2,1)S(1)}, bf16[176,128]{1,0:T(8,128)(2,1)S(1)}, u32[]{:S(2)}, u32[]{:S(2)}) collective-permute-start(bf16[176,128]{1,0:T(8,128)(2,1)S(1)} %get-tuple-element.58), channel_id=1, source_target_pairs={{0,16},{1,17},{2,18},{3,19},{4,20},{5,21},{6,22},{7,23},{8,24},{9,... | collective-permute-start | bytes 135176 | tf_op jit(solution)/shard_map/ppermute | solution.py:180
  46.7 5.8 %collective-permute-start.16 = (bf16[176,128]{1,0:T(8,128)(2,1)S(1)}, bf16[176,128]{1,0:T(8,128)(2,1)S(1)}, u32[]{:S(2)}, u32[]{:S(2)}) collective-permute-start(bf16[176,128]{1,0:T(8,128)(2,1)S(1)} %get-tuple-element.59), channel_id=1, source_target_pairs={{0,24},{1,25},{2,26},{3,27},{4,28},{5,29},{6,30},{7,31},{8,16},{9,... | collective-permute-start | bytes 135176 | tf_op jit(solution)/shard_map/ppermute | solution.py:180
  52.6 4.5 %collective-permute-start.17 = (bf16[176,128]{1,0:T(8,128)(2,1)S(1)}, bf16[176,128]{1,0:T(8,128)(2,1)S(1)}, u32[]{:S(2)}, u32[]{:S(2)}) collective-permute-start(bf16[176,128]{1,0:T(8,128)(2,1)S(1)} %combine_last.1.refs_0_), channel_id=1, source_target_pairs={{0,8},{1,9},{2,10},{3,11},{4,12},{5,13},{6,14},{7,15},{8,0},{9,1},... | collective-permute-start | bytes 135176 | tf_op jit(solution)/shard_map/ppermute | solution.py:180
  52.6 5.1 %collective-permute-start.18 = (bf16[176,128]{1,0:T(8,128)(2,1)S(1)}, bf16[176,128]{1,0:T(8,128)(2,1)S(1)}, u32[]{:S(2)}, u32[]{:S(2)}) collective-permute-start(bf16[176,128]{1,0:T(8,128)(2,1)S(1)} %combine_last.1.refs_0_), channel_id=1, source_target_pairs={{0,16},{1,17},{2,18},{3,19},{4,20},{5,21},{6,22},{7,23},{8,24},{9,... | collective-permute-start | bytes 135176 | tf_op jit(solution)/shard_map/ppermute | solution.py:180
  54.9 5.8 %collective-permute-start.19 = (bf16[176,128]{1,0:T(8,128)(2,1)S(1)}, bf16[176,128]{1,0:T(8,128)(2,1)S(1)}, u32[]{:S(2)}, u32[]{:S(2)}) collective-permute-start(bf16[176,128]{1,0:T(8,128)(2,1)S(1)} %combine_last.1.refs_0_), channel_id=1, source_target_pairs={{0,24},{1,25},{2,26},{3,27},{4,28},{5,29},{6,30},{7,31},{8,16},{9,... | collective-permute-start | bytes 135176 | tf_op jit(solution)/shard_map/ppermute | solution.py:180
  60.8 7.7 %collective-permute-start.25 = (bf16[656,128]{1,0:T(8,128)(2,1)S(1)}, bf16[656,128]{1,0:T(8,128)(2,1)S(1)}, u32[]{:S(2)}, u32[]{:S(2)}) collective-permute-start(bf16[656,128]{1,0:T(8,128)(2,1)S(1)} %assemble.1.refs_0_), channel_id=1, source_target_pairs={{0,6},{1,7},{2,4},{3,5},{4,2},{5,3},{6,0},{7,1},{8,14},{9,15},{10,... | collective-permute-start | bytes 503816 | tf_op jit(solution)/shard_map/ppermute | solution.py:180
  61.8 7.5 %collective-permute-start.23 = (bf16[656,128]{1,0:T(8,128)(2,1)S(1)}, bf16[656,128]{1,0:T(8,128)(2,1)S(1)}, u32[]{:S(2)}, u32[]{:S(2)}) collective-permute-start(bf16[656,128]{1,0:T(8,128)(2,1)S(1)} %assemble.1.refs_0_), channel_id=1, source_target_pairs={{0,4},{1,5},{2,6},{3,7},{4,0},{5,1},{6,2},{7,3},{8,12},{9,13},{10,... | collective-permute-start | bytes 503816 | tf_op jit(solution)/shard_map/ppermute | solution.py:180
  62.8 6.6 %collective-permute-start.21 = (bf16[656,128]{1,0:T(8,128)(2,1)S(1)}, bf16[656,128]{1,0:T(8,128)(2,1)S(1)}, u32[]{:S(2)}, u32[]{:S(2)}) collective-permute-start(bf16[656,128]{1,0:T(8,128)(2,1)S(1)} %assemble.1.refs_0_), channel_id=1, source_target_pairs={{0,2},{1,3},{2,0},{3,1},{4,6},{5,7},{6,4},{7,5},{8,10},{9,11},{10,... | collective-permute-start | bytes 503816 | tf_op jit(solution)/shard_map/ppermute | solution.py:180
  65.3 5.9 %collective-permute-start.20 = (bf16[656,128]{1,0:T(8,128)(2,1)S(1)}, bf16[656,128]{1,0:T(8,128)(2,1)S(1)}, u32[]{:S(2)}, u32[]{:S(2)}) collective-permute-start(bf16[656,128]{1,0:T(8,128)(2,1)S(1)} %assemble.1.refs_0_), channel_id=1, source_target_pairs={{0,1},{1,0},{2,3},{3,2},{4,5},{5,4},{6,7},{7,6},{8,9},{9,8},{10,11... | collective-permute-start | bytes 503816 | tf_op jit(solution)/shard_map/ppermute | solution.py:180
  68.5 2.7 %collective-permute-start.26 = (bf16[656,128]{1,0:T(8,128)(2,1)S(1)}, bf16[656,128]{1,0:T(8,128)(2,1)S(1)}, u32[]{:S(2)}, u32[]{:S(2)}) collective-permute-start(bf16[656,128]{1,0:T(8,128)(2,1)S(1)} %collective-permute-done.25.refs_3_), channel_id=1, source_target_pairs={{0,1},{1,0},{2,3},{3,2},{4,5},{5,4},{6,7},{7,6},{8,9},{9,8},{10,11... | collective-permute-start | bytes 503816 | tf_op jit(solution)/shard_map/ppermute | solution.py:180
  69.3 1.9 %collective-permute-start.24 = (bf16[656,128]{1,0:T(8,128)(2,1)S(1)}, bf16[656,128]{1,0:T(8,128)(2,1)S(1)}, u32[]{:S(2)}, u32[]{:S(2)}) collective-permute-start(bf16[656,128]{1,0:T(8,128)(2,1)S(1)} %collective-permute-done.23.refs_2_), channel_id=1, source_target_pairs={{0,1},{1,0},{2,3},{3,2},{4,5},{5,4},{6,7},{7,6},{8,9},{9,8},{10,11... | collective-permute-start | bytes 503816 | tf_op jit(solution)/shard_map/ppermute | solution.py:180
  69.3 1.9 %collective-permute-start.22 = (bf16[656,128]{1,0:T(8,128)(2,1)S(1)}, bf16[656,128]{1,0:T(8,128)(2,1)S(1)}, u32[]{:S(2)}, u32[]{:S(2)}) collective-permute-start(bf16[656,128]{1,0:T(8,128)(2,1)S(1)} %collective-permute-done.21.refs_1_), channel_id=1, source_target_pairs={{0,1},{1,0},{2,3},{3,2},{4,5},{5,4},{6,7},{7,6},{8,9},{9,8},{10,11... | collective-permute-start | bytes 503816 | tf_op jit(solution)/shard_map/ppermute | solution.py:180
  (1 other events, 1.0 us)

commit v9 on v8

--- a/solution.py
+++ b/solution.py
@@ -88,7 +88,7 @@
 
 def row_blocks(rows):
     size = rows
-    while size > 256 and size % 2 == 0 and size // 2 % ROW_TILE == 0:
+    while size > 512 and size % 2 == 0 and size // 2 % ROW_TILE == 0:
         size //= 2
     return [(start, size) for start in range(0, rows, size)]
 

time: 72.8 us -> 72.8 us (level)
  no operation moved by 1% of the time
where the time goes in v9:
time: 72.8 us; the launch traced here: 72.6 us
  starting transfers between devices  33.9 us (47%)
  waiting for transfers between devices  22.8 us (31%)
  Pallas kernels  11.7 us (16%)
  local copies, waits for them, and re-layouts  3.34 us (5%)
  between operations  0.85 us (1%)
    ppermute x17, waiting for transfers between devices, swapped(): lax.ppermute(value, 'lon', [(i, i ^ k * stride) for i in range(count)])  18.2 us
    ppermute x17, starting transfers between devices, swapped(): lax.ppermute(value, 'lon', [(i, i ^ k * stride) for i in range(count)])  16.7 us
    pallas_call x17, Pallas kernels, call(): pl.pallas_call(body, out_shape=list(outs), in_specs=[far if i in far_args...  11.7 us
    ppermute x4, starting transfers between devices, shards(): lax.ppermute(part, 'lon', inner_pairs(steps))  7.19 us
    ppermute x2, starting transfers between devices, shards(): lax.ppermute(part, 'lon', outer_pairs(steps))  5.34 us
    unnamed x12, local copies, waits for them, and re-layouts  3.34 us
    ppermute x4, waiting for transfers between devices, shards(): lax.ppermute(part, 'lon', inner_pairs(steps))  3.03 us
    ppermute x1, starting transfers between devices, shards(): lax.ppermute(g_packed[1], 'lon', outer_pairs(steps))  2.56 us
  transfers between devices with their start and end apart: 27, of which 13 were waited for; matrix products, arithmetic and copies ran while one was open for 0% of the time, Pallas kernels for 11%

profile of v9, /device:TPU:0, one launch (start us, length us, event | category | flops | bytes accessed | tf_op | source)
XLA Modules:
  0.0 72.6 jit_solution(10579895592775639101)
XLA Ops:
  0.7 1.1 %copy-done.4 = bf16[32,32,192]{2,1,0:T(8,128)(2,1)S(1)} copy-done((bf16[32,32,192]{2,1,0:T(8,128)(2,1)S(1)}, bf16[32,32,192]{2,1,0:T(8,128)(2,1)}, u32[]{:S(2)}) %copy-start.4) | copy-done | bytes 393240
  1.9 3.0 %collective-permute-start = (bf16[896,128]{1,0:T(8,128)(2,1)S(1)}, bf16[896,128]{1,0:T(8,128)(2,1)S(1)}, u32[]{:S(2)}, u32[]{:S(2)}) collective-permute-start(bf16[896,128]{1,0:T(8,128)(2,1)S(1)} %get-tuple-element.35), channel_id=1, source_target_pairs={{0,2},{1,3},{2,0},{3,1},{4,6},{5,7},{6,4},{7,5},{8,10},{9,11},{10,... | collective-permute-start | bytes 688136 | tf_op jit(solution)/shard_map/ppermute | solution.py:315
  4.9 1.0 %copy-done.3 = bf16[32,32,192]{2,1,0:T(8,128)(2,1)S(1)} copy-done((bf16[32,32,192]{2,1,0:T(8,128)(2,1)S(1)}, bf16[32,32,192]{2,1,0:T(8,128)(2,1)}, u32[]{:S(2)}) %copy-start.3) | copy-done | bytes 393240
  6.6 4.2 %collective-permute-start.4 = (bf16[784,128]{1,0:T(8,128)(2,1)S(1)}, bf16[784,128]{1,0:T(8,128)(2,1)S(1)}, u32[]{:S(2)}, u32[]{:S(2)}) collective-permute-start(bf16[784,128]{1,0:T(8,128)(2,1)S(1)} %get-tuple-element.39), channel_id=1, source_target_pairs={{0,31},{1,2},{2,1},{3,4},{4,3},{5,6},{6,5},{7,8},{8,7},{9,10},{10,... | collective-permute-start | bytes 602120 | tf_op jit(solution)/shard_map/ppermute | solution.py:326
  10.8 1.1 %collective-permute-start.5 = (bf16[752,128]{1,0:T(8,128)(2,1)S(1)}, bf16[752,128]{1,0:T(8,128)(2,1)S(1)}, u32[]{:S(2)}, u32[]{:S(2)}) collective-permute-start(bf16[752,128]{1,0:T(8,128)(2,1)S(1)} %get-tuple-element.40), channel_id=1, source_target_pairs={{0,31},{1,2},{2,1},{3,4},{4,3},{5,6},{6,5},{7,8},{8,7},{9,10},{10,... | collective-permute-start | bytes 577544 | tf_op jit(solution)/shard_map/ppermute | solution.py:326
  12.0 2.3 %collective-permute-done.rest_0_ = bf16[896,128]{1,0:T(8,128)(2,1)S(1)} collective-permute-done((bf16[896,128]{1,0:T(8,128)(2,1)S(1)}, bf16[896,128]{1,0:T(8,128)(2,1)S(1)}, u32[]{:S(2)}, u32[]{:S(2)}) %collective-permute-start) | collective-permute-done | bytes 229408 | tf_op jit(solution)/shard_map/ppermute | solution.py:315
  14.3 3.6 %collective-permute-start.1 = (bf16[640,128]{1,0:T(8,128)(2,1)S(1)}, bf16[640,128]{1,0:T(8,128)(2,1)S(1)}, u32[]{:S(2)}, u32[]{:S(2)}) collective-permute-start(bf16[640,128]{1,0:T(8,128)(2,1)S(1)} %get-tuple-element.36), channel_id=1, source_target_pairs={{0,2},{1,3},{2,0},{3,1},{4,6},{5,7},{6,4},{7,5},{8,10},{9,11},{10,... | collective-permute-start | bytes 491528 | tf_op jit(solution)/shard_map/ppermute | solution.py:315
  17.9 2.6 %collective-permute-start.7 = (bf16[640,128]{1,0:T(8,128)(2,1)S(1)}, bf16[640,128]{1,0:T(8,128)(2,1)S(1)}, u32[]{:S(2)}, u32[]{:S(2)}) collective-permute-start(bf16[640,128]{1,0:T(8,128)(2,1)S(1)} %get-tuple-element.36), channel_id=1, source_target_pairs={{0,30},{1,31},{2,4},{3,5},{4,2},{5,3},{6,8},{7,9},{8,6},{9,7},{10,... | collective-permute-start | bytes 491528 | tf_op jit(solution)/shard_map/ppermute | solution.py:318
  20.5 1.2 %copy-done = bf16[3,3,192,192]{3,2,1,0:T(8,128)(2,1)S(1)} copy-done((bf16[3,3,192,192]{3,2,1,0:T(8,128)(2,1)S(1)}, bf16[3,3,192,192]{3,2,1,0:T(8,128)(2,1)}, u32[]{:S(2)}) %copy-start) | copy-done | bytes 663576
  21.7 1.0 %near_pre_act.1 = (f32[1024,192]{1,0:T(8,128)S(1)}, bf16[576,1024]{1,0:T(8,128)(2,1)S(1)}, bf16[576,1024]{1,0:T(8,128)(2,1)S(1)}) custom-call(bf16[1024,192]{1,0:T(8,128)(2,1)S(1)} %bitcast.5, bf16[3,3,192,192]{3,2,1,0:T(8,128)(2,1)S(1)} %copy-done, bf16[784,128]{1,0:T(8,128)(2,1)S(1)} %collective-permute-done.2.rest_0_, ...), custom_call_target="tpu_custom_call" | custom-call | flops 452984832 | bytes 4595712 | tf_op jit(solution)/shard_map/near_pre_act/pallas_call | solution.py:22
  24.4 1.0 %near_hidden_grad.1 = (f32[1024,192]{1,0:T(8,128)S(1)}, bf16[1088,192]{1,0:T(8,128)(2,1)S(1)}, bf16[1088,192]{1,0:T(8,128)(2,1)S(1)}) custom-call(bf16[1024,192]{1,0:T(8,128)(2,1)S(1)} %bitcast.7, bf16[3,3,192,192]{3,2,1,0:T(8,128)(2,1)S(1)} %copy-done.2, bf16[896,128]{1,0:T(8,128)(2,1)S(1)} %collective-permute-done.rest_0_, ...), custom_call_target="tpu_custom_call" | custom-call | flops 452984832 | bytes 3072000 | tf_op jit(solution)/shard_map/near_hidden_grad/pallas_call | solution.py:22
  25.4 1.5 %collective-permute-done.7.rest_1_ = bf16[640,128]{1,0:T(8,128)(2,1)S(1)} collective-permute-done((bf16[640,128]{1,0:T(8,128)(2,1)S(1)}, bf16[640,128]{1,0:T(8,128)(2,1)S(1)}, u32[]{:S(2)}, u32[]{:S(2)}) %collective-permute-start.7) | collective-permute-done | bytes 163872 | tf_op jit(solution)/shard_map/ppermute | solution.py:318
  27.5 1.2 %sibling_kernel_gradient.1 = bf16[2624,128]{1,0:T(8,128)(2,1)S(1)} custom-call(bf16[192,1024]{1,0:T(8,128)(2,1)S(1)} %get-tuple-element.44.hid_ref, bf16[1088,192]{1,0:T(8,128)(2,1)S(1)} %get-tuple-element.45.g0, bf16[1088,192]{1,0:T(8,128)(2,1)S(1)} %get-tuple-element.46.g1, bf16[1088,192]{1,0:T(8,128)(2,1)S(1)} %get-tuple-element.47.g2, ...), custom_call_target="tpu_custom_call" | custom-call | flops 679477248 | bytes 6250496 | tf_op jit(solution)/shard_map/sibling_kernel_gradient/pallas_call | solution.py:22
  28.9 1.2 %own_kernel_gradient.1.own_ref = f32[2624,128]{1,0:T(8,128)S(1)} custom-call(bf16[192,1024]{1,0:T(8,128)(2,1)S(1)} %get-tuple-element.44.hid_ref, bf16[1088,192]{1,0:T(8,128)(2,1)S(1)} %get-tuple-element.45.g0, bf16[1088,192]{1,0:T(8,128)(2,1)S(1)} %get-tuple-element.46.g1, bf16[1088,192]{1,0:T(8,128)(2,1)S(1)} %get-tuple-element.47.g2, ...), custom_call_target="tpu_custom_call" | custom-call | flops 679477248 | bytes 6922240 | tf_op jit(solution)/shard_map/own_kernel_gradient/pallas_call | solution.py:22
  32.2 2.5 %collective-permute-start.12 = (bf16[656,128]{1,0:T(8,128)(2,1)S(1)}, bf16[656,128]{1,0:T(8,128)(2,1)S(1)}, u32[]{:S(2)}, u32[]{:S(2)}) collective-permute-start(bf16[656,128]{1,0:T(8,128)(2,1)S(1)} %get-tuple-element.54), channel_id=1, source_target_pairs={{0,2},{1,3},{2,0},{3,1},{4,6},{5,7},{6,4},{7,5},{8,10},{9,11},{10,... | collective-permute-start | bytes 503816 | tf_op jit(solution)/shard_map/ppermute | solution.py:180
  34.9 4.3 %collective-permute-done.10.refs_2_ = bf16[656,128]{1,0:T(8,128)(2,1)S(1)} collective-permute-done((bf16[656,128]{1,0:T(8,128)(2,1)S(1)}, bf16[656,128]{1,0:T(8,128)(2,1)S(1)}, u32[]{:S(2)}, u32[]{:S(2)}) %collective-permute-start.10) | collective-permute-done | bytes 167968 | tf_op jit(solution)/shard_map/ppermute | solution.py:180
  39.2 2.0 %collective-permute-start.11 = (bf16[1536,128]{1,0:T(8,128)(2,1)S(1)}, bf16[1536,128]{1,0:T(8,128)(2,1)S(1)}, u32[]{:S(2)}, u32[]{:S(2)}) collective-permute-start(bf16[1536,128]{1,0:T(8,128)(2,1)S(1)} %pack.5), channel_id=1, source_target_pairs={{0,31},{1,2},{2,1},{3,4},{4,3},{5,6},{6,5},{7,8},{8,7},{9,10},{10,... | collective-permute-start | bytes 1179656 | tf_op jit(solution)/shard_map/ppermute | solution.py:478
  41.2 1.2 %collective-permute-done.12.refs_0_ = bf16[656,128]{1,0:T(8,128)(2,1)S(1)} collective-permute-done((bf16[656,128]{1,0:T(8,128)(2,1)S(1)}, bf16[656,128]{1,0:T(8,128)(2,1)S(1)}, u32[]{:S(2)}, u32[]{:S(2)}) %collective-permute-start.12) | collective-permute-done | bytes 167968 | tf_op jit(solution)/shard_map/ppermute | solution.py:180
  42.5 1.6 %collective-permute-start.14 = (bf16[176,128]{1,0:T(8,128)(2,1)S(1)}, bf16[176,128]{1,0:T(8,128)(2,1)S(1)}, u32[]{:S(2)}, u32[]{:S(2)}) collective-permute-start(bf16[176,128]{1,0:T(8,128)(2,1)S(1)} %get-tuple-element.57), channel_id=1, source_target_pairs={{0,8},{1,9},{2,10},{3,11},{4,12},{5,13},{6,14},{7,15},{8,0},{9,1},... | collective-permute-start | bytes 135176 | tf_op jit(solution)/shard_map/ppermute | solution.py:180
  44.1 2.6 %collective-permute-start.15 = (bf16[176,128]{1,0:T(8,128)(2,1)S(1)}, bf16[176,128]{1,0:T(8,128)(2,1)S(1)}, u32[]{:S(2)}, u32[]{:S(2)}) collective-permute-start(bf16[176,128]{1,0:T(8,128)(2,1)S(1)} %get-tuple-element.58), channel_id=1, source_target_pairs={{0,16},{1,17},{2,18},{3,19},{4,20},{5,21},{6,22},{7,23},{8,24},{9,... | collective-permute-start | bytes 135176 | tf_op jit(solution)/shard_map/ppermute | solution.py:180
  46.9 1.5 %collective-permute-done.14.refs_0_ = bf16[176,128]{1,0:T(8,128)(2,1)S(1)} collective-permute-done((bf16[176,128]{1,0:T(8,128)(2,1)S(1)}, bf16[176,128]{1,0:T(8,128)(2,1)S(1)}, u32[]{:S(2)}, u32[]{:S(2)}) %collective-permute-start.14) | collective-permute-done | bytes 45088 | tf_op jit(solution)/shard_map/ppermute | solution.py:180
  49.2 3.4 %collective-permute-done.16.refs_2_ = bf16[176,128]{1,0:T(8,128)(2,1)S(1)} collective-permute-done((bf16[176,128]{1,0:T(8,128)(2,1)S(1)}, bf16[176,128]{1,0:T(8,128)(2,1)S(1)}, u32[]{:S(2)}, u32[]{:S(2)}) %collective-permute-start.16) | collective-permute-done | bytes 45088 | tf_op jit(solution)/shard_map/ppermute | solution.py:180
  52.7 2.2 %collective-permute-start.18 = (bf16[176,128]{1,0:T(8,128)(2,1)S(1)}, bf16[176,128]{1,0:T(8,128)(2,1)S(1)}, u32[]{:S(2)}, u32[]{:S(2)}) collective-permute-start(bf16[176,128]{1,0:T(8,128)(2,1)S(1)} %combine_last.1.refs_0_), channel_id=1, source_target_pairs={{0,16},{1,17},{2,18},{3,19},{4,20},{5,21},{6,22},{7,23},{8,24},{9,... | collective-permute-start | bytes 135176 | tf_op jit(solution)/shard_map/ppermute | solution.py:180
  54.9 2.1 %collective-permute-start.19 = (bf16[176,128]{1,0:T(8,128)(2,1)S(1)}, bf16[176,128]{1,0:T(8,128)(2,1)S(1)}, u32[]{:S(2)}, u32[]{:S(2)}) collective-permute-start(bf16[176,128]{1,0:T(8,128)(2,1)S(1)} %combine_last.1.refs_0_), channel_id=1, source_target_pairs={{0,24},{1,25},{2,26},{3,27},{4,28},{5,29},{6,30},{7,31},{8,16},{9,... | collective-permute-start | bytes 135176 | tf_op jit(solution)/shard_map/ppermute | solution.py:180
  57.8 2.9 %collective-permute-done.19.refs_3_ = bf16[176,128]{1,0:T(8,128)(2,1)S(1)} collective-permute-done((bf16[176,128]{1,0:T(8,128)(2,1)S(1)}, bf16[176,128]{1,0:T(8,128)(2,1)S(1)}, u32[]{:S(2)}, u32[]{:S(2)}) %collective-permute-start.19) | collective-permute-done | bytes 45088 | tf_op jit(solution)/shard_map/ppermute | solution.py:180
  60.8 1.0 %collective-permute-start.25 = (bf16[656,128]{1,0:T(8,128)(2,1)S(1)}, bf16[656,128]{1,0:T(8,128)(2,1)S(1)}, u32[]{:S(2)}, u32[]{:S(2)}) collective-permute-start(bf16[656,128]{1,0:T(8,128)(2,1)S(1)} %assemble.1.refs_0_), channel_id=1, source_target_pairs={{0,6},{1,7},{2,4},{3,5},{4,2},{5,3},{6,0},{7,1},{8,14},{9,15},{10,... | collective-permute-start | bytes 503816 | tf_op jit(solution)/shard_map/ppermute | solution.py:180
  62.8 1.6 %collective-permute-start.21 = (bf16[656,128]{1,0:T(8,128)(2,1)S(1)}, bf16[656,128]{1,0:T(8,128)(2,1)S(1)}, u32[]{:S(2)}, u32[]{:S(2)}) collective-permute-start(bf16[656,128]{1,0:T(8,128)(2,1)S(1)} %assemble.1.refs_0_), channel_id=1, source_target_pairs={{0,2},{1,3},{2,0},{3,1},{4,6},{5,7},{6,4},{7,5},{8,10},{9,11},{10,... | collective-permute-start | bytes 503816 | tf_op jit(solution)/shard_map/ppermute | solution.py:180
  64.3 1.0 %near_input_gradient.1.part_ref = f32[1024,192]{1,0:T(8,128)S(1)} custom-call(bf16[1024,192]{1,0:T(8,128)(2,1)S(1)} %get-tuple-element.43.source.x_ref.pre_ref, bf16[3,3,192,192]{3,2,1,0:T(8,128)(2,1)S(1)} %copy-done.1, bf16[1536,128]{1,0:T(8,128)(2,1)S(1)} %collective-permute-done.8.rest_0_), custom_call_target="tpu_custom_call" | custom-call | flops 452984832 | bytes 2236416 | tf_op jit(solution)/shard_map/near_input_gradient/pallas_call | solution.py:22
  65.4 1.4 %input_gradient.1 = bf16[1024,192]{1,0:T(8,128)(2,1)} custom-call(f32[1024,192]{1,0:T(8,128)S(1)} %near_input_gradient.1.part_ref, bf16[3,3,192,192]{3,2,1,0:T(8,128)(2,1)S(1)} %copy-done.1, bf16[1536,128]{1,0:T(8,128)(2,1)S(1)} %collective-permute-done.11.rest_0_), custom_call_target="tpu_custom_call" | custom-call | flops 226492416 | bytes 2236416 | tf_op jit(solution)/shard_map/input_gradient/pallas_call | solution.py:22
  66.8 1.7 %collective-permute-done.25.refs_3_ = bf16[656,128]{1,0:T(8,128)(2,1)S(1)} collective-permute-done((bf16[656,128]{1,0:T(8,128)(2,1)S(1)}, bf16[656,128]{1,0:T(8,128)(2,1)S(1)}, u32[]{:S(2)}, u32[]{:S(2)}) %collective-permute-start.25) | collective-permute-done | bytes 167968 | tf_op jit(solution)/shard_map/ppermute | solution.py:180
  69.9 1.3 %unpack_gradients.2 = (f32[3,3,192,192]{3,2,1,0:T(8,128)}, f32[3,3,192,192]{3,2,1,0:T(8,128)}) custom-call(bf16[656,128]{1,0:T(8,128)(2,1)S(1)} %assemble.1.refs_0_, bf16[656,128]{1,0:T(8,128)(2,1)S(1)} %collective-permute-done.21.refs_1_, bf16[656,128]{1,0:T(8,128)(2,1)S(1)} %collective-permute-done.23.refs_2_, ...), custom_call_target="tpu_custom_call" | custom-call | bytes 3325952 | tf_op jit(solution)/shard_map/unpack_gradients/pallas_call | solution.py:22
  71.2 1.3 %unpack_gradients.3 = (f32[3,3,192,192]{3,2,1,0:T(8,128)}, f32[3,3,192,192]{3,2,1,0:T(8,128)}) custom-call(bf16[656,128]{1,0:T(8,128)(2,1)S(1)} %collective-permute-done.20.refs_0_, bf16[656,128]{1,0:T(8,128)(2,1)S(1)} %collective-permute-done.22.refs_1_, ...), custom_call_target="tpu_custom_call", output_to_operand_aliasing={{0}: (4, {}), {1}: (5, {})} | custom-call | bytes 5980160 | tf_op jit(solution)/shard_map/unpack_gradients/pallas_call | solution.py:22
  (51 shorter events, 9.8 us)
Async XLA Ops:
  0.6 22.1 %copy-start.1 = (bf16[3,3,192,192]{3,2,1,0:T(8,128)(2,1)S(1)}, bf16[3,3,192,192]{3,2,1,0:T(8,128)(2,1)}, u32[]{:S(2)}) copy-start(bf16[3,3,192,192]{3,2,1,0:T(8,128)(2,1)} %w_ref.11) | copy-start | bytes 1990660
  0.6 1.1 %copy-start.4 = (bf16[32,32,192]{2,1,0:T(8,128)(2,1)S(1)}, bf16[32,32,192]{2,1,0:T(8,128)(2,1)}, u32[]{:S(2)}) copy-start(bf16[32,32,192]{2,1,0:T(8,128)(2,1)} %param.5) | copy-start | bytes 1179652
  1.9 12.4 %collective-permute-start = (bf16[896,128]{1,0:T(8,128)(2,1)S(1)}, bf16[896,128]{1,0:T(8,128)(2,1)S(1)}, u32[]{:S(2)}, u32[]{:S(2)}) collective-permute-start(bf16[896,128]{1,0:T(8,128)(2,1)S(1)} %get-tuple-element.35), channel_id=1, source_target_pairs={{0,2},{1,3},{2,0},{3,1},{4,6},{5,7},{6,4},{7,5},{8,10},{9,11},{10,... | collective-permute-start | bytes 688136 | tf_op jit(solution)/shard_map/ppermute | solution.py:315
  6.0 8.3 %collective-permute-start.3 = (bf16[752,128]{1,0:T(8,128)(2,1)S(1)}, bf16[752,128]{1,0:T(8,128)(2,1)S(1)}, u32[]{:S(2)}, u32[]{:S(2)}) collective-permute-start(bf16[752,128]{1,0:T(8,128)(2,1)S(1)} %get-tuple-element.40), channel_id=1, source_target_pairs={{0,1},{1,0},{2,3},{3,2},{4,5},{5,4},{6,7},{7,6},{8,9},{9,8},{10,11... | collective-permute-start | bytes 577544 | tf_op jit(solution)/shard_map/ppermute | solution.py:325
  6.1 11.8 %collective-permute-start.2 = (bf16[784,128]{1,0:T(8,128)(2,1)S(1)}, bf16[784,128]{1,0:T(8,128)(2,1)S(1)}, u32[]{:S(2)}, u32[]{:S(2)}) collective-permute-start(bf16[784,128]{1,0:T(8,128)(2,1)S(1)} %get-tuple-element.39), channel_id=1, source_target_pairs={{0,1},{1,0},{2,3},{3,2},{4,5},{5,4},{6,7},{7,6},{8,9},{9,8},{10,11... | collective-permute-start | bytes 602120 | tf_op jit(solution)/shard_map/ppermute | solution.py:325
  6.6 16.1 %collective-permute-start.4 = (bf16[784,128]{1,0:T(8,128)(2,1)S(1)}, bf16[784,128]{1,0:T(8,128)(2,1)S(1)}, u32[]{:S(2)}, u32[]{:S(2)}) collective-permute-start(bf16[784,128]{1,0:T(8,128)(2,1)S(1)} %get-tuple-element.39), channel_id=1, source_target_pairs={{0,31},{1,2},{2,1},{3,4},{4,3},{5,6},{6,5},{7,8},{8,7},{9,10},{10,... | collective-permute-start | bytes 602120 | tf_op jit(solution)/shard_map/ppermute | solution.py:326
  10.8 11.8 %collective-permute-start.5 = (bf16[752,128]{1,0:T(8,128)(2,1)S(1)}, bf16[752,128]{1,0:T(8,128)(2,1)S(1)}, u32[]{:S(2)}, u32[]{:S(2)}) collective-permute-start(bf16[752,128]{1,0:T(8,128)(2,1)S(1)} %get-tuple-element.40), channel_id=1, source_target_pairs={{0,31},{1,2},{2,1},{3,4},{4,3},{5,6},{6,5},{7,8},{8,7},{9,10},{10,... | collective-permute-start | bytes 577544 | tf_op jit(solution)/shard_map/ppermute | solution.py:326
  14.3 12.6 %collective-permute-start.6 = (bf16[896,128]{1,0:T(8,128)(2,1)S(1)}, bf16[896,128]{1,0:T(8,128)(2,1)S(1)}, u32[]{:S(2)}, u32[]{:S(2)}) collective-permute-start(bf16[896,128]{1,0:T(8,128)(2,1)S(1)} %collective-permute-done.rest_0_), channel_id=1, source_target_pairs={{0,4},{1,5},{2,30},{3,31},{4,8},{5,9},{6,2},{7,3},{8,12},{9,13},{1... | collective-permute-start | bytes 688136 | tf_op jit(solution)/shard_map/ppermute | solution.py:317
  14.3 10.0 %collective-permute-start.1 = (bf16[640,128]{1,0:T(8,128)(2,1)S(1)}, bf16[640,128]{1,0:T(8,128)(2,1)S(1)}, u32[]{:S(2)}, u32[]{:S(2)}) collective-permute-start(bf16[640,128]{1,0:T(8,128)(2,1)S(1)} %get-tuple-element.36), channel_id=1, source_target_pairs={{0,2},{1,3},{2,0},{3,1},{4,6},{5,7},{6,4},{7,5},{8,10},{9,11},{10,... | collective-permute-start | bytes 491528 | tf_op jit(solution)/shard_map/ppermute | solution.py:315
  17.9 9.0 %collective-permute-start.7 = (bf16[640,128]{1,0:T(8,128)(2,1)S(1)}, bf16[640,128]{1,0:T(8,128)(2,1)S(1)}, u32[]{:S(2)}, u32[]{:S(2)}) collective-permute-start(bf16[640,128]{1,0:T(8,128)(2,1)S(1)} %get-tuple-element.36), channel_id=1, source_target_pairs={{0,30},{1,31},{2,4},{3,5},{4,2},{5,3},{6,8},{7,9},{8,6},{9,7},{10,... | collective-permute-start | bytes 491528 | tf_op jit(solution)/shard_map/ppermute | solution.py:318
  20.5 1.2 %copy-start = (bf16[3,3,192,192]{3,2,1,0:T(8,128)(2,1)S(1)}, bf16[3,3,192,192]{3,2,1,0:T(8,128)(2,1)}, u32[]{:S(2)}) copy-start(bf16[3,3,192,192]{3,2,1,0:T(8,128)(2,1)} %w_ref.11) | copy-start | bytes 1990660
  21.7 2.7 %copy-start.2 = (bf16[3,3,192,192]{3,2,1,0:T(8,128)(2,1)S(1)}, bf16[3,3,192,192]{3,2,1,0:T(8,128)(2,1)}, u32[]{:S(2)}) copy-start(bf16[3,3,192,192]{3,2,1,0:T(8,128)(2,1)} %w_ref.9) | copy-start | bytes 1990660
  21.7 2.7 %copy-start.5 = (bf16[32,32,192]{2,1,0:T(8,128)(2,1)S(1)}, bf16[32,32,192]{2,1,0:T(8,128)(2,1)}, u32[]{:S(2)}) copy-start(bf16[32,32,192]{2,1,0:T(8,128)(2,1)} %param.5) | copy-start | bytes 1179652
  28.8 2.2 %collective-permute-start.9 = (bf16[2624,128]{1,0:T(8,128)(2,1)S(1)}, bf16[2624,128]{1,0:T(8,128)(2,1)S(1)}, u32[]{:S(2)}, u32[]{:S(2)}) collective-permute-start(bf16[2624,128]{1,0:T(8,128)(2,1)S(1)} %sibling_kernel_gradient.1), channel_id=1, source_target_pairs={{0,1},{1,0},{2,3},{3,2},{4,5},{5,4},{6,7},{7,6},{8,9},{9,8},{10,11... | collective-permute-start | bytes 2015240 | tf_op jit(solution)/shard_map/ppermute | solution.py:180
  31.1 8.1 %collective-permute-start.10 = (bf16[656,128]{1,0:T(8,128)(2,1)S(1)}, bf16[656,128]{1,0:T(8,128)(2,1)S(1)}, u32[]{:S(2)}, u32[]{:S(2)}) collective-permute-start(bf16[656,128]{1,0:T(8,128)(2,1)S(1)} %get-tuple-element.51), channel_id=1, source_target_pairs={{0,6},{1,7},{2,4},{3,5},{4,2},{5,3},{6,0},{7,1},{8,14},{9,15},{10,... | collective-permute-start | bytes 503816 | tf_op jit(solution)/shard_map/ppermute | solution.py:180
  32.2 32.2 %collective-permute-start.8 = (bf16[1536,128]{1,0:T(8,128)(2,1)S(1)}, bf16[1536,128]{1,0:T(8,128)(2,1)S(1)}, u32[]{:S(2)}, u32[]{:S(2)}) collective-permute-start(bf16[1536,128]{1,0:T(8,128)(2,1)S(1)} %pack.5), channel_id=1, source_target_pairs={{0,1},{1,0},{2,3},{3,2},{4,5},{5,4},{6,7},{7,6},{8,9},{9,8},{10,11... | collective-permute-start | bytes 1179656 | tf_op jit(solution)/shard_map/ppermute | solution.py:477
  32.2 10.2 %collective-permute-start.12 = (bf16[656,128]{1,0:T(8,128)(2,1)S(1)}, bf16[656,128]{1,0:T(8,128)(2,1)S(1)}, u32[]{:S(2)}, u32[]{:S(2)}) collective-permute-start(bf16[656,128]{1,0:T(8,128)(2,1)S(1)} %get-tuple-element.54), channel_id=1, source_target_pairs={{0,2},{1,3},{2,0},{3,1},{4,6},{5,7},{6,4},{7,5},{8,10},{9,11},{10,... | collective-permute-start | bytes 503816 | tf_op jit(solution)/shard_map/ppermute | solution.py:180
  34.7 7.7 %collective-permute-start.13 = (bf16[656,128]{1,0:T(8,128)(2,1)S(1)}, bf16[656,128]{1,0:T(8,128)(2,1)S(1)}, u32[]{:S(2)}, u32[]{:S(2)}) collective-permute-start(bf16[656,128]{1,0:T(8,128)(2,1)S(1)} %get-tuple-element.55), channel_id=1, source_target_pairs={{0,4},{1,5},{2,6},{3,7},{4,0},{5,1},{6,2},{7,3},{8,12},{9,13},{10,... | collective-permute-start | bytes 503816 | tf_op jit(solution)/shard_map/ppermute | solution.py:180
  39.2 26.2 %collective-permute-start.11 = (bf16[1536,128]{1,0:T(8,128)(2,1)S(1)}, bf16[1536,128]{1,0:T(8,128)(2,1)S(1)}, u32[]{:S(2)}, u32[]{:S(2)}) collective-permute-start(bf16[1536,128]{1,0:T(8,128)(2,1)S(1)} %pack.5), channel_id=1, source_target_pairs={{0,31},{1,2},{2,1},{3,4},{4,3},{5,6},{6,5},{7,8},{8,7},{9,10},{10,... | collective-permute-start | bytes 1179656 | tf_op jit(solution)/shard_map/ppermute | solution.py:478
  42.5 6.0 %collective-permute-start.14 = (bf16[176,128]{1,0:T(8,128)(2,1)S(1)}, bf16[176,128]{1,0:T(8,128)(2,1)S(1)}, u32[]{:S(2)}, u32[]{:S(2)}) collective-permute-start(bf16[176,128]{1,0:T(8,128)(2,1)S(1)} %get-tuple-element.57), channel_id=1, source_target_pairs={{0,8},{1,9},{2,10},{3,11},{4,12},{5,13},{6,14},{7,15},{8,0},{9,1},... | collective-permute-start | bytes 135176 | tf_op jit(solution)/shard_map/ppermute | solution.py:180
  44.1 5.1 %collective-permute-start.15 = (bf16[176,128]{1,0:T(8,128)(2,1)S(1)}, bf16[176,128]{1,0:T(8,128)(2,1)S(1)}, u32[]{:S(2)}, u32[]{:S(2)}) collective-permute-start(bf16[176,128]{1,0:T(8,128)(2,1)S(1)} %get-tuple-element.58), channel_id=1, source_target_pairs={{0,16},{1,17},{2,18},{3,19},{4,20},{5,21},{6,22},{7,23},{8,24},{9,... | collective-permute-start | bytes 135176 | tf_op jit(solution)/shard_map/ppermute | solution.py:180
  46.7 5.8 %collective-permute-start.16 = (bf16[176,128]{1,0:T(8,128)(2,1)S(1)}, bf16[176,128]{1,0:T(8,128)(2,1)S(1)}, u32[]{:S(2)}, u32[]{:S(2)}) collective-permute-start(bf16[176,128]{1,0:T(8,128)(2,1)S(1)} %get-tuple-element.59), channel_id=1, source_target_pairs={{0,24},{1,25},{2,26},{3,27},{4,28},{5,29},{6,30},{7,31},{8,16},{9,... | collective-permute-start | bytes 135176 | tf_op jit(solution)/shard_map/ppermute | solution.py:180
  52.6 4.5 %collective-permute-start.17 = (bf16[176,128]{1,0:T(8,128)(2,1)S(1)}, bf16[176,128]{1,0:T(8,128)(2,1)S(1)}, u32[]{:S(2)}, u32[]{:S(2)}) collective-permute-start(bf16[176,128]{1,0:T(8,128)(2,1)S(1)} %combine_last.1.refs_0_), channel_id=1, source_target_pairs={{0,8},{1,9},{2,10},{3,11},{4,12},{5,13},{6,14},{7,15},{8,0},{9,1},... | collective-permute-start | bytes 135176 | tf_op jit(solution)/shard_map/ppermute | solution.py:180
  52.7 5.1 %collective-permute-start.18 = (bf16[176,128]{1,0:T(8,128)(2,1)S(1)}, bf16[176,128]{1,0:T(8,128)(2,1)S(1)}, u32[]{:S(2)}, u32[]{:S(2)}) collective-permute-start(bf16[176,128]{1,0:T(8,128)(2,1)S(1)} %combine_last.1.refs_0_), channel_id=1, source_target_pairs={{0,16},{1,17},{2,18},{3,19},{4,20},{5,21},{6,22},{7,23},{8,24},{9,... | collective-permute-start | bytes 135176 | tf_op jit(solution)/shard_map/ppermute | solution.py:180
  54.9 5.8 %collective-permute-start.19 = (bf16[176,128]{1,0:T(8,128)(2,1)S(1)}, bf16[176,128]{1,0:T(8,128)(2,1)S(1)}, u32[]{:S(2)}, u32[]{:S(2)}) collective-permute-start(bf16[176,128]{1,0:T(8,128)(2,1)S(1)} %combine_last.1.refs_0_), channel_id=1, source_target_pairs={{0,24},{1,25},{2,26},{3,27},{4,28},{5,29},{6,30},{7,31},{8,16},{9,... | collective-permute-start | bytes 135176 | tf_op jit(solution)/shard_map/ppermute | solution.py:180
  60.8 7.7 %collective-permute-start.25 = (bf16[656,128]{1,0:T(8,128)(2,1)S(1)}, bf16[656,128]{1,0:T(8,128)(2,1)S(1)}, u32[]{:S(2)}, u32[]{:S(2)}) collective-permute-start(bf16[656,128]{1,0:T(8,128)(2,1)S(1)} %assemble.1.refs_0_), channel_id=1, source_target_pairs={{0,6},{1,7},{2,4},{3,5},{4,2},{5,3},{6,0},{7,1},{8,14},{9,15},{10,... | collective-permute-start | bytes 503816 | tf_op jit(solution)/shard_map/ppermute | solution.py:180
  61.8 7.5 %collective-permute-start.23 = (bf16[656,128]{1,0:T(8,128)(2,1)S(1)}, bf16[656,128]{1,0:T(8,128)(2,1)S(1)}, u32[]{:S(2)}, u32[]{:S(2)}) collective-permute-start(bf16[656,128]{1,0:T(8,128)(2,1)S(1)} %assemble.1.refs_0_), channel_id=1, source_target_pairs={{0,4},{1,5},{2,6},{3,7},{4,0},{5,1},{6,2},{7,3},{8,12},{9,13},{10,... | collective-permute-start | bytes 503816 | tf_op jit(solution)/shard_map/ppermute | solution.py:180
  62.8 6.6 %collective-permute-start.21 = (bf16[656,128]{1,0:T(8,128)(2,1)S(1)}, bf16[656,128]{1,0:T(8,128)(2,1)S(1)}, u32[]{:S(2)}, u32[]{:S(2)}) collective-permute-start(bf16[656,128]{1,0:T(8,128)(2,1)S(1)} %assemble.1.refs_0_), channel_id=1, source_target_pairs={{0,2},{1,3},{2,0},{3,1},{4,6},{5,7},{6,4},{7,5},{8,10},{9,11},{10,... | collective-permute-start | bytes 503816 | tf_op jit(solution)/shard_map/ppermute | solution.py:180
  65.3 5.9 %collective-permute-start.20 = (bf16[656,128]{1,0:T(8,128)(2,1)S(1)}, bf16[656,128]{1,0:T(8,128)(2,1)S(1)}, u32[]{:S(2)}, u32[]{:S(2)}) collective-permute-start(bf16[656,128]{1,0:T(8,128)(2,1)S(1)} %assemble.1.refs_0_), channel_id=1, source_target_pairs={{0,1},{1,0},{2,3},{3,2},{4,5},{5,4},{6,7},{7,6},{8,9},{9,8},{10,11... | collective-permute-start | bytes 503816 | tf_op jit(solution)/shard_map/ppermute | solution.py:180
  68.5 2.7 %collective-permute-start.26 = (bf16[656,128]{1,0:T(8,128)(2,1)S(1)}, bf16[656,128]{1,0:T(8,128)(2,1)S(1)}, u32[]{:S(2)}, u32[]{:S(2)}) collective-permute-start(bf16[656,128]{1,0:T(8,128)(2,1)S(1)} %collective-permute-done.25.refs_3_), channel_id=1, source_target_pairs={{0,1},{1,0},{2,3},{3,2},{4,5},{5,4},{6,7},{7,6},{8,9},{9,8},{10,11... | collective-permute-start | bytes 503816 | tf_op jit(solution)/shard_map/ppermute | solution.py:180
  69.3 1.9 %collective-permute-start.24 = (bf16[656,128]{1,0:T(8,128)(2,1)S(1)}, bf16[656,128]{1,0:T(8,128)(2,1)S(1)}, u32[]{:S(2)}, u32[]{:S(2)}) collective-permute-start(bf16[656,128]{1,0:T(8,128)(2,1)S(1)} %collective-permute-done.23.refs_2_), channel_id=1, source_target_pairs={{0,1},{1,0},{2,3},{3,2},{4,5},{5,4},{6,7},{7,6},{8,9},{9,8},{10,11... | collective-permute-start | bytes 503816 | tf_op jit(solution)/shard_map/ppermute | solution.py:180
  69.4 1.9 %collective-permute-start.22 = (bf16[656,128]{1,0:T(8,128)(2,1)S(1)}, bf16[656,128]{1,0:T(8,128)(2,1)S(1)}, u32[]{:S(2)}, u32[]{:S(2)}) collective-permute-start(bf16[656,128]{1,0:T(8,128)(2,1)S(1)} %collective-permute-done.21.refs_1_), channel_id=1, source_target_pairs={{0,1},{1,0},{2,3},{3,2},{4,5},{5,4},{6,7},{7,6},{8,9},{9,8},{10,11... | collective-permute-start | bytes 503816 | tf_op jit(solution)/shard_map/ppermute | solution.py:180
  (1 other events, 1.0 us)
